TPU v7x, 768 devices: a whole 4x8x12 slice. The times are simulated.
768 devices in a mesh: dp: 48 (over z_lo, y), mx: 8 (over x, z_hi), my: 2 (over core).
Axes of the slice: x: 4, y: 8, z: 12 (z_hi: 2, z_lo: 6; z = z_hi * 6 + z_lo), core: 2. Of those that a mesh axis runs over, the one named last changes fastest.
Arguments:
- normed: bfloat16 [18432, 6144], P(('dp', 'mx'), 'my'), may hold values from -24 to 24
- weight: bfloat16 [6144, 3072], P('my', 'mx'), may hold values from -0.078125 to 0.078125
- cotangent: bfloat16 [18432, 3072], P('dp', 'mx'), may hold values from -6 to 6
- head_gain: float32 [128], replicated, may hold values from 0.1 to 1.9
Outputs:
- input_grad: bfloat16 [18432, 6144], P(('dp', 'mx'), 'my')
- weight_grad: float32 [6144, 3072], P(('my', 'dp'), 'mx')
All inputs are finite; a program needn't handle non-finite values.
Results may differ from a plain program's by a relative error of at most 0.0049.
Values may be sent and summed in bfloat16 or wider, within the bound.
No kernel may reach another device: no remote copies, remote signals or barrier semaphores. Data moves between devices by JAX's collectives and lax.ppermute only.
A program may use at most 64 MiB of HBM per device.

v0:
```python
import math

import jax
import jax.numpy as jnp
from jax import lax
from jax.sharding import PartitionSpec as P


def head_backward(pre, cot, gain):
    rows = pre.shape[0]
    pre3 = pre.reshape(rows, -1, gain.shape[0])
    centred = pre3 - jnp.mean(pre3, axis=-1, keepdims=True)
    inverse = lax.rsqrt(jnp.mean(centred * centred, axis=-1, keepdims=True) + 1e-06)
    unit = centred * inverse
    scaled = cot.astype(jnp.float32).reshape(pre3.shape) * gain
    result = inverse * (
        scaled
        - jnp.mean(scaled, axis=-1, keepdims=True)
        - unit * jnp.mean(scaled * unit, axis=-1, keepdims=True)
    )
    return result.reshape(rows, -1).astype(jnp.bfloat16)


def body(normed, weight, cotangent, head_gain):
    gathered = lax.all_gather(normed, "mx", axis=0, tiled=True)
    partial_value = jnp.dot(gathered, weight, preferred_element_type=jnp.float32)
    summed = lax.psum(partial_value, "my")
    head_rows = head_backward(summed, cotangent, head_gain)
    total_tokens = normed.shape[0] * lax.axis_size("dp") * lax.axis_size("mx")
    factor = 1.0 / math.sqrt(total_tokens)
    term = lax.dot_general(
        gathered, head_rows, (((0,), (0,)), ((), ())), preferred_element_type=jnp.float32
    )
    weight_grad = lax.psum_scatter(term * factor, "dp", scatter_dimension=0, tiled=True)
    input_grad = lax.psum_scatter(
        lax.dot_general(
            head_rows, weight, (((1,), (1,)), ((), ())), preferred_element_type=jnp.float32
        ),
        "mx",
        scatter_dimension=0,
        tiled=True,
    ).astype(jnp.bfloat16)
    return (input_grad, weight_grad)


def solution(mesh):
    return jax.shard_map(
        body,
        mesh=mesh,
        in_specs=(P(("dp", "mx"), "my"), P("my", "mx"), P("dp", "mx"), P()),
        out_specs=(P(("dp", "mx"), "my"), P(("my", "dp"), "mx")),
        check_vma=False,
    )
```

profile of v0, /device:TPU:6, one launch (start us, length us, event | category | flops | bytes accessed | tf_op | source)
XLA Modules:
  0.0 687.3 jit_solution(15035524367011240223)
XLA Ops:
  7.2 0.0 copy-start
  7.2 0.0 all-gather.2.cloned.1.call-start
  7.2 0.7 all-gather.2.cloned.1.call-update
  7.9 0.0 copy-start.2
  7.9 0.0 copy-start.4
  7.9 0.0 all-reduce.2.cloned.1.call-start
  8.0 120.6 %all-gather.2.cloned.1.call-done = bf16[384,3072]{1,0:T(8,128)(2,1)} async-done(((bf16[48,3072]{1,0:T(8,128)(2,1)}), bf16[384,3072]{1,0:T(8,128)(2,1)}) %all-gather.2.cloned.1.call-update) | async-done | bytes 2359312 | tf_op jit(solution)/shard_map/all_gather | solution.py:25
  128.6 0.0 copy-done
  128.6 3.9 fusion
  132.4 0.0 all-reduce.2.cloned.1.call-update
  132.5 0.0 reduce-scatter.5.cloned.1.call-start
  132.5 0.0 copy-done.2
  132.5 0.2 copy.16
  132.7 0.0 copy-done.4
  132.7 0.6 broadcast_bitcast_fusion
  133.3 33.4 %all-reduce.2.cloned.1.call-done = f32[384,384]{1,0:T(8,128)} async-done(((f32[384,384]{1,0:T(8,128)}), f32[384,384]{1,0:T(8,128)}) %all-reduce.2.cloned.1.call-update) | async-done | bytes 589840 | tf_op jit(solution)/shard_map/psum | solution.py:27
  166.7 1.3 copy.15
  168.0 0.1 multiply_reduce_fusion.1
  168.1 0.9 mul.64
  169.0 2.1 copy.21
  171.1 0.9 sub.28
  172.0 2.1 copy.18
  174.2 0.8 multiply_reduce_fusion.2
  175.0 0.0 copy-start.1
  175.0 0.0 copy-start.3
  175.1 1.1 copy.20
  176.2 1.1 copy.17
  177.2 0.0 copy-done.1
  177.2 0.0 copy-done.3
  177.3 1.8 multiply_convert_fusion
  179.1 3.5 fusion.1
  182.6 0.0 reduce-scatter.5.cloned.1.call-update
  182.7 0.0 reduce-scatter.7.cloned.1.call-start
  182.7 5.3 multiply_bitcast_fusion
  188.0 6.1 copy.23
  194.2 0.0 reduce-scatter.7.cloned.1.call-update
  194.2 171.3 %reduce-scatter.5.cloned.1.call-done = f32[48,3072]{1,0:T(8,128)} async-done(((f32[384,3072]{1,0:T(8,128)}), f32[48,3072]{1,0:T(8,128)}) %reduce-scatter.5.cloned.1.call-update) | async-done | bytes 589840 | tf_op jit(solution)/shard_map/reduce_scatter | solution.py:35
  365.5 1.8 convert_element_type.11
  367.3 313.5 %reduce-scatter.7.cloned.1.call-done = f32[64,384]{1,0:T(8,128)} async-done(((f32[3072,384]{1,0:T(8,128)}), f32[64,384]{1,0:T(8,128)}) %reduce-scatter.7.cloned.1.call-update) | async-done | bytes 98320
  (6 shorter events, 0.1 us)
Async XLA Ops:
  7.2 121.4 %copy-start = (bf16[3072,384]{1,0:T(8,128)(2,1)S(1)}, bf16[3072,384]{1,0:T(8,128)(2,1)}, u32[]{:S(2)}) copy-start(bf16[3072,384]{1,0:T(8,128)(2,1)} %param.5) | copy-start | bytes 7077892
  7.2 121.4 %all-gather.2.cloned.1.call-start = ((), (), s32[]{:S(2)}) async-start(), calls=%async_computation.2 | async-start | bytes 2654208 | tf_op jit(solution)/shard_map/all_gather | solution.py:25
  7.9 124.6 %copy-start.2 = (bf16[384,384]{1,0:T(8,128)(2,1)S(1)}, bf16[384,384]{1,0:T(8,128)(2,1)}, u32[]{:S(2)}) copy-start(bf16[384,384]{1,0:T(8,128)(2,1)} %param.6) | copy-start | bytes 884740
  7.9 124.8 %copy-start.4 = (f32[128]{0:T(128)S(1)}, f32[128]{0:T(128)}, u32[]{:S(2)}) copy-start(f32[128]{0:T(128)} %param.7) | copy-start | bytes 1540
  7.9 158.8 %all-reduce.2.cloned.1.call-start = ((), (), s32[]{:S(2)}) async-start(), calls=%async_computation.3 | async-start | bytes 1179648 | tf_op jit(solution)/shard_map/psum | solution.py:27
  132.5 233.0 %reduce-scatter.5.cloned.1.call-start = ((), (), s32[]{:S(2)}) async-start(), calls=%async_computation.4 | async-start | bytes 5308416 | tf_op jit(solution)/shard_map/reduce_scatter | solution.py:35
  175.0 2.3 copy-start.1
  175.0 2.2 copy-start.3
  182.7 498.1 %reduce-scatter.7.cloned.1.call-start = ((), (), s32[]{:S(2)}) async-start(), calls=%async_computation.5 | async-start | bytes 4816896
Sparse Core Ops, SparseCore 0:
  11.8 116.7 all-gather.1
  132.6 34.0 all-reduce.1
  182.8 182.6 reduce-scatter.4
  369.0 311.7 reduce-scatter.6
where the time goes:
time: 688 us; the launch traced here: 687 us
  waiting for transfers between devices  639 us (93%)
  local copies, waits for them, and re-layouts  16.4 us (2%)
  between operations  13.9 us (2%)
  matrix products  12.7 us (2%)
    unnamed x5, waiting for transfers between devices  314 us
    reduce_scatter x1, waiting for transfers between devices, body(): lax.psum_scatter(lax.dot_general(head_rows, weight, (((1,), (1,)), ((), (...  171 us
    all_gather x1, waiting for transfers between devices, body(): gathered = lax.all_gather(normed, 'mx', axis=0, tiled=True)  121 us
    psum x1, waiting for transfers between devices, body(): summed = lax.psum(partial_value, 'my')  33.4 us
  transfers between devices with their start and end apart: 4, of which 4 were waited for; matrix products, arithmetic and copies ran while one was open for 2% of the time, Pallas kernels for 0%

commit v1 on v0

v1 whole, which is shorter than its diff:
```python
import math

import jax
import jax.numpy as jnp
from jax import lax
from jax.sharding import Mesh, PartitionSpec as P

F32 = jnp.float32
BF16 = jnp.bfloat16


def head_backward(pre, cot, gain):
    rows = pre.shape[0]
    pre3 = pre.reshape(rows, -1, gain.shape[0])
    centred = pre3 - jnp.mean(pre3, axis=-1, keepdims=True)
    inverse = lax.rsqrt(jnp.mean(centred * centred, axis=-1, keepdims=True) + 1e-06)
    unit = centred * inverse
    scaled = cot.astype(F32).reshape(pre3.shape) * gain
    result = inverse * (
        scaled
        - jnp.mean(scaled, axis=-1, keepdims=True)
        - unit * jnp.mean(scaled * unit, axis=-1, keepdims=True)
    )
    return result.reshape(rows, -1).astype(BF16)


def shift(value, axis, by):
    size = lax.axis_size(axis)
    return lax.ppermute(value, axis, [(i, (i + by) % size) for i in range(size)])


def body(normed, weight, cotangent, head_gain):
    nx, ny, nz, nh = (lax.axis_size(a) for a in ("x", "y", "zl", "zh"))
    rows, width = normed.shape
    heads = weight.shape[1]
    x, y, zl, zh = (lax.axis_index(a) for a in ("x", "y", "zl", "zh"))

    peer = shift(normed, "zh", 1)
    own = [normed] + [shift(normed, "x", k) for k in range(1, nx)]
    other = [peer] + [shift(peer, "x", k) for k in range(1, nx)]
    gathered = jnp.concatenate([p for pair in zip(own, other) for p in pair], axis=0)

    cot = cotangent.reshape(nx, nh, rows, heads)
    order_x = (x - jnp.arange(nx)) % nx
    order_h = (zh + jnp.arange(nh)) % nh
    cot = cot[order_x][:, order_h].reshape(nx * nh * rows, heads)

    partial_value = jnp.dot(gathered, weight, preferred_element_type=F32)
    summed = partial_value + shift(partial_value, "c", 1)
    head_rows = head_backward(summed, cot, head_gain)

    factor = 1.0 / math.sqrt(rows * nx * nh * ny * nz)
    term = lax.dot_general(
        gathered, head_rows, (((0,), (0,)), ((), ())), preferred_element_type=F32
    )
    term = (term * factor).astype(BF16).reshape(nz, ny, -1, heads).swapaxes(0, 1)
    over_y = lax.psum_scatter(term, "y", scatter_dimension=0, tiled=True)[0]

    back = lax.dot_general(
        head_rows, weight, (((1,), (1,)), ((), ())), preferred_element_type=F32
    ).astype(BF16).reshape(nx, nh, rows, width)
    total = back[0].astype(F32)
    for k in range(1, nx):
        total = total + shift(back[k], "x", -k).astype(F32)
    input_grad = (total[0] + shift(total[1].astype(BF16), "zh", 1).astype(F32)).astype(BF16)

    weight_grad = lax.dynamic_index_in_dim(over_y, zl, 0, False).astype(F32)
    for k in range(1, nz):
        chunk = lax.dynamic_index_in_dim(over_y, (zl + k) % nz, 0, False)
        weight_grad = weight_grad + shift(chunk, "zl", k).astype(F32)
    return (input_grad, weight_grad)


def spread(fine):
    return jax.shard_map(
        body,
        mesh=fine,
        in_specs=(
            P(("zl", "y", "x", "zh"), "c"),
            P("c", ("x", "zh")),
            P(("zl", "y"), ("x", "zh")),
            P(),
        ),
        out_specs=(P(("zl", "y", "x", "zh"), "c"), P(("c", "zl", "y"), ("x", "zh"))),
        check_vma=False,
    )


def solution(mesh):
    return spread(Mesh(mesh.devices.reshape(6, 8, 4, 2, 2), ("zl", "y", "x", "zh", "c")))
```

time: 688 us -> 180 us (0.26)
  waiting for transfers between devices: 639 us -> 45.5 us
  starting transfers between devices: 0.16 us -> 79.8 us
  other arithmetic: 4.64 us -> 15.5 us
    unnamed x5 -> x1, waiting for transfers between devices: 314 us -> 0.02 us
    reduce_scatter x1, waiting for transfers between devices: 171 us -> 7.12 us  [body(): over_y = lax.psum_scatter(term, 'y', scatter_dimension=0, tiled=True)[0]]
    all_gather x1 -> x0, waiting for transfers between devices: 121 us -> none  [body(): gathered = lax.all_gather(normed, 'mx', axis=0, tiled=True)]
    ppermute x0 -> x17, starting transfers between devices: none -> 79.8 us  [shift(): lax.ppermute(value, axis, [(i, (i + by) % size) for i in range(size)])]
    ppermute x0 -> x17, waiting for transfers between devices: none -> 38.3 us  [shift(): lax.ppermute(value, axis, [(i, (i + by) % size) for i in range(size)])]
    psum x1 -> x0, waiting for transfers between devices: 33.4 us -> none  [body(): summed = lax.psum(partial_value, 'my')]
  transfers between devices with their start and end apart: 4 -> 18, of which waited for: 4 -> 8; matrix products, arithmetic and copies ran while one was open for 2% -> 5% of each run, Pallas kernels for 0% -> 0%
where the time goes in v1:
time: 180 us; the launch traced here: 179 us
  starting transfers between devices  79.8 us (44%)
  waiting for transfers between devices  45.5 us (25%)
  local copies, waits for them, and re-layouts  16.5 us (9%)
  other arithmetic  15.5 us (9%)
  between operations  14.5 us (8%)
  matrix products  7.16 us (4%)
    ppermute x17, starting transfers between devices, shift(): lax.ppermute(value, axis, [(i, (i + by) % size) for i in range(size)])  79.8 us
    ppermute x17, waiting for transfers between devices, shift(): lax.ppermute(value, axis, [(i, (i + by) % size) for i in range(size)])  38.3 us
    reduce_scatter x1, waiting for transfers between devices, body(): over_y = lax.psum_scatter(term, 'y', scatter_dimension=0, tiled=True)[0]  7.12 us
    reduce_sum x1, other arithmetic, head_backward(): jnp.mean(scaled, axis=-1, keepdims=True)  4.26 us
  transfers between devices with their start and end apart: 18, of which 8 were waited for; matrix products, arithmetic and copies ran while one was open for 5% of the time, Pallas kernels for 0%

profile of v1, /device:TPU:6, one launch (start us, length us, event | category | flops | bytes accessed | tf_op | source)
XLA Modules:
  0.0 179.0 jit_solution(4019846252164270238)
XLA Ops:
  7.2 0.0 copy-start
  7.2 0.0 reduce-scatter.2.cloned.1.call-start
  7.2 15.3 %collective-permute-start = (bf16[48,3072]{1,0:T(8,128)(2,1)}, bf16[48,3072]{1,0:T(8,128)(2,1)S(1)}, u32[]{:S(2)}, u32[]{:S(2)}) collective-permute-start(bf16[48,3072]{1,0:T(8,128)(2,1)} %param.4), channel_id=1, source_target_pairs={{0,2},{2,0},{1,3},{3,1},{4,6},{6,4},{5,7},{7,5},{8,10},{10,8},{9,1... | collective-permute-start | bytes 884744 | tf_op jit(solution)/shard_map/ppermute | solution.py:29
  22.5 2.4 %collective-permute-start.1 = (bf16[48,3072]{1,0:T(8,128)(2,1)}, bf16[48,3072]{1,0:T(8,128)(2,1)S(1)}, u32[]{:S(2)}, u32[]{:S(2)}) collective-permute-start(bf16[48,3072]{1,0:T(8,128)(2,1)} %param.4), channel_id=1, source_target_pairs={{0,4},{4,8},{8,12},{12,0},{1,5},{5,9},{9,13},{13,1},{2,6},{6,10},{... | collective-permute-start | bytes 884744 | tf_op jit(solution)/shard_map/ppermute | solution.py:29
  24.9 4.3 %collective-permute-start.3 = (bf16[48,3072]{1,0:T(8,128)(2,1)}, bf16[48,3072]{1,0:T(8,128)(2,1)S(1)}, u32[]{:S(2)}, u32[]{:S(2)}) collective-permute-start(bf16[48,3072]{1,0:T(8,128)(2,1)} %param.4), channel_id=1, source_target_pairs={{0,8},{4,12},{8,0},{12,4},{1,9},{5,13},{9,1},{13,5},{2,10},{6,14},... | collective-permute-start | bytes 884744 | tf_op jit(solution)/shard_map/ppermute | solution.py:29
  29.2 1.9 %collective-permute-start.5 = (bf16[48,3072]{1,0:T(8,128)(2,1)}, bf16[48,3072]{1,0:T(8,128)(2,1)S(1)}, u32[]{:S(2)}, u32[]{:S(2)}) collective-permute-start(bf16[48,3072]{1,0:T(8,128)(2,1)} %param.4), channel_id=1, source_target_pairs={{0,12},{4,0},{8,4},{12,8},{1,13},{5,1},{9,5},{13,9},{2,14},{6,2},{... | collective-permute-start | bytes 884744 | tf_op jit(solution)/shard_map/ppermute | solution.py:29
  31.2 1.0 constant_dynamic-update-slice_fusion.7
  32.2 5.1 %collective-permute-start.2 = (bf16[48,3072]{1,0:T(8,128)(2,1)S(1)}, bf16[48,3072]{1,0:T(8,128)(2,1)S(1)}, u32[]{:S(2)}, u32[]{:S(2)}) collective-permute-start(bf16[48,3072]{1,0:T(8,128)(2,1)S(1)} %collective-permute-done), channel_id=1, source_target_pairs={{0,4},{4,8},{8,12},{12,0},{1,5},{5,9},{9,13},{13,1},{2,6},{6,10},{... | collective-permute-start | bytes 884744 | tf_op jit(solution)/shard_map/ppermute | solution.py:29
  37.4 1.9 %collective-permute-start.4 = (bf16[48,3072]{1,0:T(8,128)(2,1)S(1)}, bf16[48,3072]{1,0:T(8,128)(2,1)S(1)}, u32[]{:S(2)}, u32[]{:S(2)}) collective-permute-start(bf16[48,3072]{1,0:T(8,128)(2,1)S(1)} %collective-permute-done), channel_id=1, source_target_pairs={{0,8},{4,12},{8,0},{12,4},{1,9},{5,13},{9,1},{13,5},{2,10},{6,14},... | collective-permute-start | bytes 884744 | tf_op jit(solution)/shard_map/ppermute | solution.py:29
  39.3 0.0 collective-permute-done.1
  39.3 3.3 %collective-permute-start.6 = (bf16[48,3072]{1,0:T(8,128)(2,1)S(1)}, bf16[48,3072]{1,0:T(8,128)(2,1)S(1)}, u32[]{:S(2)}, u32[]{:S(2)}) collective-permute-start(bf16[48,3072]{1,0:T(8,128)(2,1)S(1)} %collective-permute-done), channel_id=1, source_target_pairs={{0,12},{4,0},{8,4},{12,8},{1,13},{5,1},{9,5},{13,9},{2,14},{6,2},{... | collective-permute-start | bytes 884744 | tf_op jit(solution)/shard_map/ppermute | solution.py:29
  42.7 4.5 %collective-permute-done.2 = bf16[48,3072]{1,0:T(8,128)(2,1)S(1)} collective-permute-done((bf16[48,3072]{1,0:T(8,128)(2,1)S(1)}, bf16[48,3072]{1,0:T(8,128)(2,1)S(1)}, u32[]{:S(2)}, u32[]{:S(2)}) %collective-permute-start.2) | collective-permute-done | bytes 294944 | tf_op jit(solution)/shard_map/ppermute | solution.py:29
  47.2 0.0 collective-permute-done.3
  47.2 3.5 %collective-permute-done.4 = bf16[48,3072]{1,0:T(8,128)(2,1)S(1)} collective-permute-done((bf16[48,3072]{1,0:T(8,128)(2,1)S(1)}, bf16[48,3072]{1,0:T(8,128)(2,1)S(1)}, u32[]{:S(2)}, u32[]{:S(2)}) %collective-permute-start.4) | collective-permute-done | bytes 294944 | tf_op jit(solution)/shard_map/ppermute | solution.py:29
  50.8 0.0 collective-permute-done.5
  50.8 4.9 %collective-permute-done.6 = bf16[48,3072]{1,0:T(8,128)(2,1)S(1)} collective-permute-done((bf16[48,3072]{1,0:T(8,128)(2,1)S(1)}, bf16[48,3072]{1,0:T(8,128)(2,1)S(1)}, u32[]{:S(2)}, u32[]{:S(2)}) %collective-permute-start.6) | collective-permute-done | bytes 294944 | tf_op jit(solution)/shard_map/ppermute | solution.py:29
  55.7 0.0 copy-start.1
  55.7 2.3 %fusion.17 = f32[384,384]{0,1:T(8,128)} fusion(bf16[384,3072]{1,0:T(8,128)(2,1)S(1)} %constant_dynamic-update-slice_fusion, bf16[3072,384]{1,0:T(8,128)(2,1)S(1)} %copy-done), kind=kOutput, calls=%fused_computation.62 | convolution fusion | flops 905969664 | bytes 5308416 | tf_op jit(solution)/shard_map/dot_general | solution.py:48
  58.0 1.9 %collective-permute-start.7 = (f32[384,384]{0,1:T(8,128)}, f32[384,384]{0,1:T(8,128)}, u32[]{:S(2)}, u32[]{:S(2)}) collective-permute-start(f32[384,384]{0,1:T(8,128)} %fusion.17), channel_id=1, source_target_pairs={{0,1},{1,0},{2,3},{3,2},{4,5},{5,4},{6,7},{7,6},{8,9},{9,8},{10,11... | collective-permute-start | bytes 1769480 | tf_op jit(solution)/shard_map/ppermute | solution.py:29
  60.0 0.6 gather_fusion
  60.6 0.6 gather_fusion.1
  61.2 0.0 copy-start.5
  61.3 1.1 reshape.177
  62.4 0.2 copy.31
  62.7 0.6 broadcast_bitcast_fusion
  63.2 1.3 add.152
  64.5 1.2 copy.26
  65.8 0.8 copy.25
  66.6 2.7 %multiply_reduce_fusion.1 = f32[384,3]{1,0:T(8,128)} fusion(f32[384,3,128]{2,1,0:T(4,128)} %copy.26, f32[384,3]{1,0:T(8,128)} %copy.25), kind=kLoop, calls=%fused_computation.11 | loop fusion | flops 441216 | bytes 599040 | tf_op jit(solution)/shard_map/reduce_sum | solution.py:16
  69.3 1.6 copy.27
  71.0 0.7 add_rsqrt_fusion
  71.7 0.8 copy.28
  72.5 4.3 %multiply_reduce_fusion.2 = (f32[384,3]{1,0:T(8,128)}, f32[384,3]{1,0:T(8,128)}) fusion(f32[384,3,128]{2,1,0:T(4,128)} %reshape.177, f32[128]{0:T(128)} %param.7, f32[384,3]{1,0:T(8,128)} %copy.28, f32[384,3,128]{2,1,0:T(4,128)} %copy.26, f32[384,3]{1,0:T(8,128)} %copy.25), kind=kLoop, calls=%fused_computation.12 | loop fusion | flops 882432 | bytes 1198592 | tf_op jit(solution)/shard_map/reduce_sum | solution.py:21
  76.8 1.6 copy.35
  78.4 1.3 broadcast_multiply_fusion
  79.7 1.6 copy.33
  81.3 0.7 broadcast_multiply_fusion.1
  82.0 0.9 fusion.4
  82.9 0.0 copy-start.2
  82.9 3.4 %multiply_convert_fusion = bf16[3072,384]{1,0:T(8,128)(2,1)S(1)} fusion(bf16[384,3072]{1,0:T(8,128)(2,1)} %copy-done.4, bf16[384,384]{0,1:T(8,128)(2,1)S(1)} %fusion.4), kind=kOutput, calls=%fused_computation.2 | convolution fusion | flops 908328960 | bytes 5013504 | tf_op jit(solution)/shard_map/dot_general | solution.py:53
  86.3 1.7 copy.40
  88.0 0.0 reduce-scatter.2.cloned.1.call-update
  88.1 0.9 copy-done.3
  89.0 1.4 convolution_convert_fusion
  90.4 0.2 fusion.16
  90.6 2.5 %collective-permute-start.10 = (bf16[2,48,3072]{2,1,0:T(8,128)(2,1)S(1)}, bf16[2,48,3072]{2,1,0:T(8,128)(2,1)S(1)}, u32[]{:S(2)}, u32[]{:S(2)}) collective-permute-start(bf16[2,48,3072]{2,1,0:T(8,128)(2,1)S(1)} %bitcast.78), channel_id=1, source_target_pairs={{0,4},{4,8},{8,12},{12,0},{1,5},{5,9},{9,13},{13,1},{2,6},{6,10},{... | collective-permute-start | bytes 1769480 | tf_op jit(solution)/shard_map/ppermute | solution.py:29
  93.1 3.3 %collective-permute-start.8 = (bf16[2,48,3072]{2,1,0:T(8,128)(2,1)S(1)}, bf16[2,48,3072]{2,1,0:T(8,128)(2,1)S(1)}, u32[]{:S(2)}, u32[]{:S(2)}) collective-permute-start(bf16[2,48,3072]{2,1,0:T(8,128)(2,1)S(1)} %bitcast.77), channel_id=1, source_target_pairs={{0,12},{4,0},{8,4},{12,8},{1,13},{5,1},{9,5},{13,9},{2,14},{6,2},{... | collective-permute-start | bytes 1769480 | tf_op jit(solution)/shard_map/ppermute | solution.py:29
  96.5 4.3 %collective-permute-start.9 = (bf16[2,48,3072]{2,1,0:T(8,128)(2,1)S(1)}, bf16[2,48,3072]{2,1,0:T(8,128)(2,1)S(1)}, u32[]{:S(2)}, u32[]{:S(2)}) collective-permute-start(bf16[2,48,3072]{2,1,0:T(8,128)(2,1)S(1)} %bitcast.76), channel_id=1, source_target_pairs={{0,8},{4,12},{8,0},{12,4},{1,9},{5,13},{9,1},{13,5},{2,10},{6,14},... | collective-permute-start | bytes 1769480 | tf_op jit(solution)/shard_map/ppermute | solution.py:29
  100.8 7.8 %collective-permute-done.10 = bf16[2,48,3072]{2,1,0:T(8,128)(2,1)S(1)} collective-permute-done((bf16[2,48,3072]{2,1,0:T(8,128)(2,1)S(1)}, bf16[2,48,3072]{2,1,0:T(8,128)(2,1)S(1)}, u32[]{:S(2)}, u32[]{:S(2)}) %collective-permute-start.10) | collective-permute-done | bytes 589856 | tf_op jit(solution)/shard_map/ppermute | solution.py:29
  108.6 3.2 %collective-permute-done.8 = bf16[2,48,3072]{2,1,0:T(8,128)(2,1)S(1)} collective-permute-done((bf16[2,48,3072]{2,1,0:T(8,128)(2,1)S(1)}, bf16[2,48,3072]{2,1,0:T(8,128)(2,1)S(1)}, u32[]{:S(2)}, u32[]{:S(2)}) %collective-permute-start.8) | collective-permute-done | bytes 589856 | tf_op jit(solution)/shard_map/ppermute | solution.py:29
  111.8 13.1 %collective-permute-done.9 = bf16[2,48,3072]{2,1,0:T(8,128)(2,1)S(1)} collective-permute-done((bf16[2,48,3072]{2,1,0:T(8,128)(2,1)S(1)}, bf16[2,48,3072]{2,1,0:T(8,128)(2,1)S(1)}, u32[]{:S(2)}, u32[]{:S(2)}) %collective-permute-start.9) | collective-permute-done | bytes 589856 | tf_op jit(solution)/shard_map/ppermute | solution.py:29
  124.9 0.3 fusion.1
  125.2 0.7 fusion.7
  126.0 11.1 %collective-permute-start.11 = (bf16[48,3072]{1,0:T(8,128)(2,1)}, bf16[48,3072]{1,0:T(8,128)(2,1)}, u32[]{:S(2)}, u32[]{:S(2)}) collective-permute-start(bf16[48,3072]{1,0:T(8,128)(2,1)} %fusion.7), channel_id=1, source_target_pairs={{0,2},{2,0},{1,3},{3,1},{4,6},{6,4},{5,7},{7,5},{8,10},{10,8},{9,1... | collective-permute-start | bytes 884744 | tf_op jit(solution)/shard_map/ppermute | solution.py:29
  137.2 7.1 %reduce-scatter.2.cloned.1.call-done = bf16[1,6,64,384]{3,2,1,0:T(8,128)(2,1)} async-done(((bf16[8,6,64,384]{3,2,1,0:T(8,128)(2,1)}), bf16[1,6,64,384]{3,2,1,0:T(8,128)(2,1)}) %reduce-scatter.2.cloned.1.call-update) | async-done | bytes 294928 | tf_op jit(solution)/shard_map/reduce_scatter | solution.py:57
  144.3 0.9 dynamic-slice_bitcast_fusion.4
  145.2 3.5 %collective-permute-start.12 = (bf16[64,384]{1,0:T(8,128)(2,1)S(1)}, bf16[64,384]{1,0:T(8,128)(2,1)S(1)}, u32[]{:S(2)}, u32[]{:S(2)}) collective-permute-start(bf16[64,384]{1,0:T(8,128)(2,1)S(1)} %get-tuple-element.8), channel_id=1, source_target_pairs={{0,128},{128,256},{256,384},{384,512},{512,640},{640,0},{1,129},{1... | collective-permute-start | bytes 147464 | tf_op jit(solution)/shard_map/ppermute | solution.py:29
  148.7 4.8 %collective-permute-start.13 = (bf16[64,384]{1,0:T(8,128)(2,1)S(1)}, bf16[64,384]{1,0:T(8,128)(2,1)S(1)}, u32[]{:S(2)}, u32[]{:S(2)}) collective-permute-start(bf16[64,384]{1,0:T(8,128)(2,1)S(1)} %get-tuple-element.12), channel_id=1, source_target_pairs={{0,256},{128,384},{256,512},{384,640},{512,0},{640,128},{1,257},{1... | collective-permute-start | bytes 147464 | tf_op jit(solution)/shard_map/ppermute | solution.py:29
  153.5 5.1 %collective-permute-start.14 = (bf16[64,384]{1,0:T(8,128)(2,1)S(1)}, bf16[64,384]{1,0:T(8,128)(2,1)S(1)}, u32[]{:S(2)}, u32[]{:S(2)}) collective-permute-start(bf16[64,384]{1,0:T(8,128)(2,1)S(1)} %get-tuple-element.11), channel_id=1, source_target_pairs={{0,384},{128,512},{256,640},{384,0},{512,128},{640,256},{1,385},{1... | collective-permute-start | bytes 147464 | tf_op jit(solution)/shard_map/ppermute | solution.py:29
  158.7 6.0 %collective-permute-start.15 = (bf16[64,384]{1,0:T(8,128)(2,1)S(1)}, bf16[64,384]{1,0:T(8,128)(2,1)S(1)}, u32[]{:S(2)}, u32[]{:S(2)}) collective-permute-start(bf16[64,384]{1,0:T(8,128)(2,1)S(1)} %get-tuple-element.10), channel_id=1, source_target_pairs={{0,512},{128,640},{256,0},{384,128},{512,256},{640,384},{1,513},{1... | collective-permute-start | bytes 147464 | tf_op jit(solution)/shard_map/ppermute | solution.py:29
  164.7 2.9 %collective-permute-start.16 = (bf16[64,384]{1,0:T(8,128)(2,1)S(1)}, bf16[64,384]{1,0:T(8,128)(2,1)S(1)}, u32[]{:S(2)}, u32[]{:S(2)}) collective-permute-start(bf16[64,384]{1,0:T(8,128)(2,1)S(1)} %get-tuple-element.9), channel_id=1, source_target_pairs={{0,640},{128,0},{256,128},{384,256},{512,384},{640,512},{1,641},{1... | collective-permute-start | bytes 147464 | tf_op jit(solution)/shard_map/ppermute | solution.py:29
  167.6 1.7 fusion.6
  169.3 1.3 collective-permute-done.16
  170.7 1.5 fusion.11
  (28 shorter events, 0.3 us)
Async XLA Ops:
  7.2 48.5 %copy-start = (bf16[3072,384]{1,0:T(8,128)(2,1)S(1)}, bf16[3072,384]{1,0:T(8,128)(2,1)}, u32[]{:S(2)}) copy-start(bf16[3072,384]{1,0:T(8,128)(2,1)} %param.5) | copy-start | bytes 7077892
  7.2 137.1 %reduce-scatter.2.cloned.1.call-start = ((), (), s32[]{:S(2)}) async-start(), calls=%async_computation.1 | async-start | bytes 2654208 | tf_op jit(solution)/shard_map/reduce_scatter | solution.py:57
  7.2 25.0 %collective-permute-start = (bf16[48,3072]{1,0:T(8,128)(2,1)}, bf16[48,3072]{1,0:T(8,128)(2,1)S(1)}, u32[]{:S(2)}, u32[]{:S(2)}) collective-permute-start(bf16[48,3072]{1,0:T(8,128)(2,1)} %param.4), channel_id=1, source_target_pairs={{0,2},{2,0},{1,3},{3,1},{4,6},{6,4},{5,7},{7,5},{8,10},{10,8},{9,1... | collective-permute-start | bytes 884744 | tf_op jit(solution)/shard_map/ppermute | solution.py:29
  22.5 16.8 %collective-permute-start.1 = (bf16[48,3072]{1,0:T(8,128)(2,1)}, bf16[48,3072]{1,0:T(8,128)(2,1)S(1)}, u32[]{:S(2)}, u32[]{:S(2)}) collective-permute-start(bf16[48,3072]{1,0:T(8,128)(2,1)} %param.4), channel_id=1, source_target_pairs={{0,4},{4,8},{8,12},{12,0},{1,5},{5,9},{9,13},{13,1},{2,6},{6,10},{... | collective-permute-start | bytes 884744 | tf_op jit(solution)/shard_map/ppermute | solution.py:29
  24.9 22.3 %collective-permute-start.3 = (bf16[48,3072]{1,0:T(8,128)(2,1)}, bf16[48,3072]{1,0:T(8,128)(2,1)S(1)}, u32[]{:S(2)}, u32[]{:S(2)}) collective-permute-start(bf16[48,3072]{1,0:T(8,128)(2,1)} %param.4), channel_id=1, source_target_pairs={{0,8},{4,12},{8,0},{12,4},{1,9},{5,13},{9,1},{13,5},{2,10},{6,14},... | collective-permute-start | bytes 884744 | tf_op jit(solution)/shard_map/ppermute | solution.py:29
  29.2 21.5 %collective-permute-start.5 = (bf16[48,3072]{1,0:T(8,128)(2,1)}, bf16[48,3072]{1,0:T(8,128)(2,1)S(1)}, u32[]{:S(2)}, u32[]{:S(2)}) collective-permute-start(bf16[48,3072]{1,0:T(8,128)(2,1)} %param.4), channel_id=1, source_target_pairs={{0,12},{4,0},{8,4},{12,8},{1,13},{5,1},{9,5},{13,9},{2,14},{6,2},{... | collective-permute-start | bytes 884744 | tf_op jit(solution)/shard_map/ppermute | solution.py:29
  32.2 15.0 %collective-permute-start.2 = (bf16[48,3072]{1,0:T(8,128)(2,1)S(1)}, bf16[48,3072]{1,0:T(8,128)(2,1)S(1)}, u32[]{:S(2)}, u32[]{:S(2)}) collective-permute-start(bf16[48,3072]{1,0:T(8,128)(2,1)S(1)} %collective-permute-done), channel_id=1, source_target_pairs={{0,4},{4,8},{8,12},{12,0},{1,5},{5,9},{9,13},{13,1},{2,6},{6,10},{... | collective-permute-start | bytes 884744 | tf_op jit(solution)/shard_map/ppermute | solution.py:29
  37.4 13.4 %collective-permute-start.4 = (bf16[48,3072]{1,0:T(8,128)(2,1)S(1)}, bf16[48,3072]{1,0:T(8,128)(2,1)S(1)}, u32[]{:S(2)}, u32[]{:S(2)}) collective-permute-start(bf16[48,3072]{1,0:T(8,128)(2,1)S(1)} %collective-permute-done), channel_id=1, source_target_pairs={{0,8},{4,12},{8,0},{12,4},{1,9},{5,13},{9,1},{13,5},{2,10},{6,14},... | collective-permute-start | bytes 884744 | tf_op jit(solution)/shard_map/ppermute | solution.py:29
  39.3 16.3 %collective-permute-start.6 = (bf16[48,3072]{1,0:T(8,128)(2,1)S(1)}, bf16[48,3072]{1,0:T(8,128)(2,1)S(1)}, u32[]{:S(2)}, u32[]{:S(2)}) collective-permute-start(bf16[48,3072]{1,0:T(8,128)(2,1)S(1)} %collective-permute-done), channel_id=1, source_target_pairs={{0,12},{4,0},{8,4},{12,8},{1,13},{5,1},{9,5},{13,9},{2,14},{6,2},{... | collective-permute-start | bytes 884744 | tf_op jit(solution)/shard_map/ppermute | solution.py:29
  55.7 2.3 %copy-start.4 = (bf16[384,3072]{1,0:T(8,128)(2,1)}, bf16[384,3072]{1,0:T(8,128)(2,1)S(1)}, u32[]{:S(2)}) copy-start(bf16[384,3072]{1,0:T(8,128)(2,1)S(1)} %constant_dynamic-update-slice_fusion) | copy-start | bytes 7077892
  55.7 4.3 %copy-start.1 = (bf16[384,384]{1,0:T(8,128)(2,1)S(1)}, bf16[384,384]{1,0:T(8,128)(2,1)}, u32[]{:S(2)}) copy-start(bf16[384,384]{1,0:T(8,128)(2,1)} %param.6) | copy-start | bytes 884740
  58.0 5.2 %collective-permute-start.7 = (f32[384,384]{0,1:T(8,128)}, f32[384,384]{0,1:T(8,128)}, u32[]{:S(2)}, u32[]{:S(2)}) collective-permute-start(f32[384,384]{0,1:T(8,128)} %fusion.17), channel_id=1, source_target_pairs={{0,1},{1,0},{2,3},{3,2},{4,5},{5,4},{6,7},{7,6},{8,9},{9,8},{10,11... | collective-permute-start | bytes 1769480 | tf_op jit(solution)/shard_map/ppermute | solution.py:29
  61.2 1.5 copy-start.5
  82.9 3.5 %copy-start.2 = (bf16[384,384]{0,1:T(8,128)(2,1)}, bf16[384,384]{0,1:T(8,128)(2,1)S(1)}, u32[]{:S(2)}) copy-start(bf16[384,384]{0,1:T(8,128)(2,1)S(1)} %fusion.4) | copy-start | bytes 884740
  88.0 1.0 copy-start.3
  90.6 18.0 %collective-permute-start.10 = (bf16[2,48,3072]{2,1,0:T(8,128)(2,1)S(1)}, bf16[2,48,3072]{2,1,0:T(8,128)(2,1)S(1)}, u32[]{:S(2)}, u32[]{:S(2)}) collective-permute-start(bf16[2,48,3072]{2,1,0:T(8,128)(2,1)S(1)} %bitcast.78), channel_id=1, source_target_pairs={{0,4},{4,8},{8,12},{12,0},{1,5},{5,9},{9,13},{13,1},{2,6},{6,10},{... | collective-permute-start | bytes 1769480 | tf_op jit(solution)/shard_map/ppermute | solution.py:29
  93.1 18.7 %collective-permute-start.8 = (bf16[2,48,3072]{2,1,0:T(8,128)(2,1)S(1)}, bf16[2,48,3072]{2,1,0:T(8,128)(2,1)S(1)}, u32[]{:S(2)}, u32[]{:S(2)}) collective-permute-start(bf16[2,48,3072]{2,1,0:T(8,128)(2,1)S(1)} %bitcast.77), channel_id=1, source_target_pairs={{0,12},{4,0},{8,4},{12,8},{1,13},{5,1},{9,5},{13,9},{2,14},{6,2},{... | collective-permute-start | bytes 1769480 | tf_op jit(solution)/shard_map/ppermute | solution.py:29
  96.5 28.5 %collective-permute-start.9 = (bf16[2,48,3072]{2,1,0:T(8,128)(2,1)S(1)}, bf16[2,48,3072]{2,1,0:T(8,128)(2,1)S(1)}, u32[]{:S(2)}, u32[]{:S(2)}) collective-permute-start(bf16[2,48,3072]{2,1,0:T(8,128)(2,1)S(1)} %bitcast.76), channel_id=1, source_target_pairs={{0,8},{4,12},{8,0},{12,4},{1,9},{5,13},{9,1},{13,5},{2,10},{6,14},... | collective-permute-start | bytes 1769480 | tf_op jit(solution)/shard_map/ppermute | solution.py:29
  126.0 38.7 %collective-permute-start.11 = (bf16[48,3072]{1,0:T(8,128)(2,1)}, bf16[48,3072]{1,0:T(8,128)(2,1)}, u32[]{:S(2)}, u32[]{:S(2)}) collective-permute-start(bf16[48,3072]{1,0:T(8,128)(2,1)} %fusion.7), channel_id=1, source_target_pairs={{0,2},{2,0},{1,3},{3,1},{4,6},{6,4},{5,7},{7,5},{8,10},{10,8},{9,1... | collective-permute-start | bytes 884744 | tf_op jit(solution)/shard_map/ppermute | solution.py:29
  145.2 24.1 %collective-permute-start.12 = (bf16[64,384]{1,0:T(8,128)(2,1)S(1)}, bf16[64,384]{1,0:T(8,128)(2,1)S(1)}, u32[]{:S(2)}, u32[]{:S(2)}) collective-permute-start(bf16[64,384]{1,0:T(8,128)(2,1)S(1)} %get-tuple-element.8), channel_id=1, source_target_pairs={{0,128},{128,256},{256,384},{384,512},{512,640},{640,0},{1,129},{1... | collective-permute-start | bytes 147464 | tf_op jit(solution)/shard_map/ppermute | solution.py:29
  148.7 20.6 %collective-permute-start.13 = (bf16[64,384]{1,0:T(8,128)(2,1)S(1)}, bf16[64,384]{1,0:T(8,128)(2,1)S(1)}, u32[]{:S(2)}, u32[]{:S(2)}) collective-permute-start(bf16[64,384]{1,0:T(8,128)(2,1)S(1)} %get-tuple-element.12), channel_id=1, source_target_pairs={{0,256},{128,384},{256,512},{384,640},{512,0},{640,128},{1,257},{1... | collective-permute-start | bytes 147464 | tf_op jit(solution)/shard_map/ppermute | solution.py:29
  153.5 15.8 %collective-permute-start.14 = (bf16[64,384]{1,0:T(8,128)(2,1)S(1)}, bf16[64,384]{1,0:T(8,128)(2,1)S(1)}, u32[]{:S(2)}, u32[]{:S(2)}) collective-permute-start(bf16[64,384]{1,0:T(8,128)(2,1)S(1)} %get-tuple-element.11), channel_id=1, source_target_pairs={{0,384},{128,512},{256,640},{384,0},{512,128},{640,256},{1,385},{1... | collective-permute-start | bytes 147464 | tf_op jit(solution)/shard_map/ppermute | solution.py:29
  158.7 10.6 %collective-permute-start.15 = (bf16[64,384]{1,0:T(8,128)(2,1)S(1)}, bf16[64,384]{1,0:T(8,128)(2,1)S(1)}, u32[]{:S(2)}, u32[]{:S(2)}) collective-permute-start(bf16[64,384]{1,0:T(8,128)(2,1)S(1)} %get-tuple-element.10), channel_id=1, source_target_pairs={{0,512},{128,640},{256,0},{384,128},{512,256},{640,384},{1,513},{1... | collective-permute-start | bytes 147464 | tf_op jit(solution)/shard_map/ppermute | solution.py:29
  164.7 6.0 %collective-permute-start.16 = (bf16[64,384]{1,0:T(8,128)(2,1)S(1)}, bf16[64,384]{1,0:T(8,128)(2,1)S(1)}, u32[]{:S(2)}, u32[]{:S(2)}) collective-permute-start(bf16[64,384]{1,0:T(8,128)(2,1)S(1)} %get-tuple-element.9), channel_id=1, source_target_pairs={{0,640},{128,0},{256,128},{384,256},{512,384},{640,512},{1,641},{1... | collective-permute-start | bytes 147464 | tf_op jit(solution)/shard_map/ppermute | solution.py:29
Sparse Core Ops, SparseCore 0:
  88.2 56.0 reduce-scatter.1

commit v2 on v1

v2 whole, which is shorter than its diff:
```python
import functools
import math

import jax
import jax.numpy as jnp
from jax import lax
from jax.experimental import pallas as pl
from jax.experimental.pallas import tpu as pltpu
from jax.sharding import Mesh, PartitionSpec as P

F32 = jnp.float32
BF16 = jnp.bfloat16


def mean(value):
    return jnp.mean(value, axis=-1, keepdims=True)


def rows_kernel(sizes, factor, where, mine, theirs, cot, gain, tokens, rows_out, *rest):
    nx, nh, ny, nz = sizes
    outs, term = rest[:-1], rest[-1]
    x, zh, y = where[0], where[1], where[2]
    count = tokens.shape[0] // (nx * nh)
    heads = mine.shape[1]
    hd = gain.shape[1]
    for kx in range(nx):
        for kh in range(nh):
            block = lax.rem(x - kx + nx, nx) * nh + lax.rem(zh + kh, nh)
            span = pl.ds((kx * nh + kh) * count, count)
            for h in range(0, heads, hd):
                pre = mine[span, h : h + hd] + theirs[span, h : h + hd]
                centred = pre - mean(pre)
                inverse = lax.rsqrt(mean(centred * centred) + 1e-06)
                unit = centred * inverse
                scaled = cot[block, :, h : h + hd].astype(F32) * gain[...]
                result = inverse * (scaled - mean(scaled) - unit * mean(scaled * unit))
                rows_out[span, h : h + hd] = result.astype(BF16)
    rows = rows_out[...]
    part = tokens.shape[1] // nz
    blk = part // ny
    for z in range(nz):
        term[...] = factor * lax.dot_general(
            tokens[:, z * part : (z + 1) * part],
            rows,
            (((0,), (0,)), ((), ())),
            preferred_element_type=F32,
        )
        for k in range(ny):
            at = pl.multiple_of(lax.rem(y + k, ny) * blk, blk)
            outs[k][z] = term[pl.ds(at, blk), :].astype(BF16)


def rows_and_chunks(sizes, factor, where, mine, theirs, cot, gain, tokens):
    nx, nh, ny, nz = sizes
    heads = mine.shape[1]
    part = tokens.shape[1] // nz
    vmem = pl.BlockSpec(memory_space=pltpu.VMEM)
    chunk = jax.ShapeDtypeStruct((nz, part // ny, heads), BF16)
    return pl.pallas_call(
        functools.partial(rows_kernel, sizes, factor),
        out_shape=[jax.ShapeDtypeStruct(mine.shape, BF16)] + [chunk] * ny,
        in_specs=[pl.BlockSpec(memory_space=pltpu.SMEM)] + [vmem] * 5,
        out_specs=[vmem] * (ny + 1),
        scratch_shapes=[pltpu.VMEM((part, heads), F32)],
        compiler_params=pltpu.CompilerParams(vmem_limit_bytes=40 * 2**20),
        name="rows_and_chunks",
    )(where, mine, theirs, cot, gain, tokens)


def shift(value, axis, by):
    size = lax.axis_size(axis)
    return lax.ppermute(value, axis, [(i, (i + by) % size) for i in range(size)])


def add(*terms):
    total = terms[0].astype(F32)
    for t in terms[1:]:
        total = total + t.astype(F32)
    return total


def body(normed, weight, cotangent, head_gain):
    nx, ny, nz, nh = (lax.axis_size(a) for a in ("x", "y", "zl", "zh"))
    count, width = normed.shape
    heads = weight.shape[1]
    where = jnp.stack([lax.axis_index(a) for a in ("x", "zh", "y")]).astype(jnp.int32)

    peer = shift(normed, "zh", 1)
    own = [normed] + [shift(normed, "x", k) for k in range(1, nx)]
    other = [peer] + [shift(peer, "x", k) for k in range(1, nx)]
    tokens = jnp.concatenate([p for pair in zip(own, other) for p in pair], axis=0)

    mine = jnp.dot(tokens, weight, preferred_element_type=F32)
    theirs = shift(mine, "c", 1)
    factor = 1.0 / math.sqrt(count * nx * nh * ny * nz)
    rows, *c = rows_and_chunks(
        (nx, nh, ny, nz),
        factor,
        where,
        mine,
        theirs,
        cotangent.reshape(nx * nh, count, heads),
        head_gain.reshape(1, -1),
        tokens,
    )

    half = c[4].shape[1] // 2
    from3, from5 = shift(c[3], "y", 1), shift(c[5], "y", -1)
    low = shift(c[4][:, :half], "y", 2)
    high = shift(c[4][:, half:], "y", -2)
    near1, near7 = shift(c[1], "y", 1), shift(c[7], "y", -1)
    up = add(c[2], from3) + jnp.pad(low.astype(F32), ((0, 0), (0, half), (0, 0)))
    down = add(c[6], from5) + jnp.pad(high.astype(F32), ((0, 0), (half, 0), (0, 0)))
    near2, near6 = shift(up.astype(BF16), "y", 2), shift(down.astype(BF16), "y", -2)

    back = [
        lax.dot_general(
            rows[k * nh * count : (k + 1) * nh * count],
            weight,
            (((1,), (1,)), ((), ())),
            preferred_element_type=F32,
        ).astype(BF16)
        for k in range(nx)
    ]
    total = add(back[0], *[shift(back[k], "x", -k) for k in range(1, nx)])
    far = shift(total[count:].astype(BF16), "zh", 1)
    input_grad = add(total[:count], far).astype(BF16)

    over_y = add(c[0], near1, near7, near2, near6).astype(BF16)
    pieces = lax.all_to_all(over_y, "zl", 0, 0, tiled=True)
    weight_grad = jnp.sum(pieces.astype(F32), axis=0)
    return (input_grad, weight_grad)


def spread(fine):
    return jax.shard_map(
        body,
        mesh=fine,
        in_specs=(
            P(("zl", "y", "x", "zh"), "c"),
            P("c", ("x", "zh")),
            P(("zl", "y"), ("x", "zh")),
            P(),
        ),
        out_specs=(P(("zl", "y", "x", "zh"), "c"), P(("c", "zl", "y"), ("x", "zh"))),
        check_vma=False,
    )


def solution(mesh):
    return spread(Mesh(mesh.devices.reshape(6, 8, 4, 2, 2), ("zl", "y", "x", "zh", "c")))
```

time: 180 us -> 158 us (0.88)
  starting transfers between devices: 79.8 us -> 95.3 us
  between operations: 14.5 us -> 1.02 us
  local copies, waits for them, and re-layouts: 16.5 us -> 4.57 us
  other arithmetic: 15.5 us -> 4.56 us
  Pallas kernels: 0 us -> 3.04 us
  waiting for transfers between devices: 45.5 us -> 42.5 us
  matrix products: 7.16 us -> 4.85 us
    all_to_all x0 -> x1, starting transfers between devices: none -> 15.1 us  [body(): pieces = lax.all_to_all(over_y, 'zl', 0, 0, tiled=True)]
    all_to_all x0 -> x1, waiting for transfers between devices: none -> 12.3 us  [body(): pieces = lax.all_to_all(over_y, 'zl', 0, 0, tiled=True)]
    ppermute x17 -> x20, waiting for transfers between devices: 38.3 us -> 30.2 us  [shift(): lax.ppermute(value, axis, [(i, (i + by) % size) for i in range(size)])]
    reduce_scatter x1 -> x0, waiting for transfers between devices: 7.12 us -> none  [body(): over_y = lax.psum_scatter(term, 'y', scatter_dimension=0, tiled=True)[0]]
    reduce_sum x3 -> x1, other arithmetic: 7.05 us -> 1.65 us  [body(): weight_grad = jnp.sum(pieces.astype(F32), axis=0)]
    reduce_sum x3 -> x0, local copies, waits for them, and re-layouts: 4.88 us -> none  [the longest x1 1.63 us: head_backward(): jnp.mean(centred * centred, axis=-1, keepdims=True) + 1e-06]
    add x3 -> x0, other arithmetic: 3.09 us -> none  [the longest x1 1.48 us: body(): weight_grad = weight_grad + shift(chunk, 'zl', k).astype(F32)]
    pallas_call x0 -> x1, Pallas kernels: none -> 3.04 us  [rows_and_chunks(): pl.pallas_call(functools.partial(rows_kernel, sizes, factor), out_shape=[...]
  transfers between devices with their start and end apart: 18 -> 21, of which waited for: 8 -> 8; matrix products, arithmetic and copies ran while one was open for 5% -> 4% of each run, Pallas kernels for 0% -> 0%
where the time goes in v2:
time: 158 us; the launch traced here: 156 us
  starting transfers between devices  95.3 us (60%)
  waiting for transfers between devices  42.5 us (27%)
  matrix products  4.85 us (3%)
  local copies, waits for them, and re-layouts  4.57 us (3%)
  other arithmetic  4.56 us (3%)
  Pallas kernels  3.04 us (2%)
    ppermute x20, starting transfers between devices, shift(): lax.ppermute(value, axis, [(i, (i + by) % size) for i in range(size)])  80.2 us
    ppermute x20, waiting for transfers between devices, shift(): lax.ppermute(value, axis, [(i, (i + by) % size) for i in range(size)])  30.2 us
    all_to_all x1, starting transfers between devices, body(): pieces = lax.all_to_all(over_y, 'zl', 0, 0, tiled=True)  15.1 us
    all_to_all x1, waiting for transfers between devices, body(): pieces = lax.all_to_all(over_y, 'zl', 0, 0, tiled=True)  12.3 us
    unnamed x17, local copies, waits for them, and re-layouts  3.78 us
    dot_general x4, matrix products, body(): lax.dot_general(rows[k * nh * count:(k + 1) * nh * count], weight, (((1,)...  3.44 us
  transfers between devices with their start and end apart: 21, of which 8 were waited for; matrix products, arithmetic and copies ran while one was open for 4% of the time, Pallas kernels for 0%

profile of v2, /device:TPU:6, one launch (start us, length us, event | category | flops | bytes accessed | tf_op | source)
XLA Modules:
  0.0 155.8 jit_solution(14169549286091771311)
XLA Ops:
  0.6 0.0 copy-start
  0.6 15.3 %collective-permute-start = (bf16[48,3072]{1,0:T(8,128)(2,1)}, bf16[48,3072]{1,0:T(8,128)(2,1)S(1)}, u32[]{:S(2)}, u32[]{:S(2)}) collective-permute-start(bf16[48,3072]{1,0:T(8,128)(2,1)} %param.4), channel_id=1, source_target_pairs={{0,2},{2,0},{1,3},{3,1},{4,6},{6,4},{5,7},{7,5},{8,10},{10,8},{9,1... | collective-permute-start | bytes 884744 | tf_op jit(solution)/shard_map/ppermute | solution.py:72
  15.9 2.4 %collective-permute-start.1 = (bf16[48,3072]{1,0:T(8,128)(2,1)}, bf16[48,3072]{1,0:T(8,128)(2,1)S(1)}, u32[]{:S(2)}, u32[]{:S(2)}) collective-permute-start(bf16[48,3072]{1,0:T(8,128)(2,1)} %param.4), channel_id=1, source_target_pairs={{0,4},{4,8},{8,12},{12,0},{1,5},{5,9},{9,13},{13,1},{2,6},{6,10},{... | collective-permute-start | bytes 884744 | tf_op jit(solution)/shard_map/ppermute | solution.py:72
  18.3 4.3 %collective-permute-start.3 = (bf16[48,3072]{1,0:T(8,128)(2,1)}, bf16[48,3072]{1,0:T(8,128)(2,1)S(1)}, u32[]{:S(2)}, u32[]{:S(2)}) collective-permute-start(bf16[48,3072]{1,0:T(8,128)(2,1)} %param.4), channel_id=1, source_target_pairs={{0,8},{4,12},{8,0},{12,4},{1,9},{5,13},{9,1},{13,5},{2,10},{6,14},... | collective-permute-start | bytes 884744 | tf_op jit(solution)/shard_map/ppermute | solution.py:72
  22.6 1.9 %collective-permute-start.5 = (bf16[48,3072]{1,0:T(8,128)(2,1)}, bf16[48,3072]{1,0:T(8,128)(2,1)S(1)}, u32[]{:S(2)}, u32[]{:S(2)}) collective-permute-start(bf16[48,3072]{1,0:T(8,128)(2,1)} %param.4), channel_id=1, source_target_pairs={{0,12},{4,0},{8,4},{12,8},{1,13},{5,1},{9,5},{13,9},{2,14},{6,2},{... | collective-permute-start | bytes 884744 | tf_op jit(solution)/shard_map/ppermute | solution.py:72
  24.6 1.0 constant_dynamic-update-slice_fusion.7
  25.6 0.0 collective-permute-done
  25.6 5.1 %collective-permute-start.2 = (bf16[48,3072]{1,0:T(8,128)(2,1)S(1)}, bf16[48,3072]{1,0:T(8,128)(2,1)S(1)}, u32[]{:S(2)}, u32[]{:S(2)}) collective-permute-start(bf16[48,3072]{1,0:T(8,128)(2,1)S(1)} %collective-permute-done), channel_id=1, source_target_pairs={{0,4},{4,8},{8,12},{12,0},{1,5},{5,9},{9,13},{13,1},{2,6},{6,10},{... | collective-permute-start | bytes 884744 | tf_op jit(solution)/shard_map/ppermute | solution.py:72
  30.7 1.9 %collective-permute-start.4 = (bf16[48,3072]{1,0:T(8,128)(2,1)S(1)}, bf16[48,3072]{1,0:T(8,128)(2,1)S(1)}, u32[]{:S(2)}, u32[]{:S(2)}) collective-permute-start(bf16[48,3072]{1,0:T(8,128)(2,1)S(1)} %collective-permute-done), channel_id=1, source_target_pairs={{0,8},{4,12},{8,0},{12,4},{1,9},{5,13},{9,1},{13,5},{2,10},{6,14},... | collective-permute-start | bytes 884744 | tf_op jit(solution)/shard_map/ppermute | solution.py:72
  32.7 0.0 collective-permute-done.1
  32.7 3.3 %collective-permute-start.6 = (bf16[48,3072]{1,0:T(8,128)(2,1)S(1)}, bf16[48,3072]{1,0:T(8,128)(2,1)S(1)}, u32[]{:S(2)}, u32[]{:S(2)}) collective-permute-start(bf16[48,3072]{1,0:T(8,128)(2,1)S(1)} %collective-permute-done), channel_id=1, source_target_pairs={{0,12},{4,0},{8,4},{12,8},{1,13},{5,1},{9,5},{13,9},{2,14},{6,2},{... | collective-permute-start | bytes 884744 | tf_op jit(solution)/shard_map/ppermute | solution.py:72
  36.1 4.5 %collective-permute-done.2 = bf16[48,3072]{1,0:T(8,128)(2,1)S(1)} collective-permute-done((bf16[48,3072]{1,0:T(8,128)(2,1)S(1)}, bf16[48,3072]{1,0:T(8,128)(2,1)S(1)}, u32[]{:S(2)}, u32[]{:S(2)}) %collective-permute-start.2) | collective-permute-done | bytes 294944 | tf_op jit(solution)/shard_map/ppermute | solution.py:72
  40.6 0.0 collective-permute-done.3
  40.7 3.4 %collective-permute-done.4 = bf16[48,3072]{1,0:T(8,128)(2,1)S(1)} collective-permute-done((bf16[48,3072]{1,0:T(8,128)(2,1)S(1)}, bf16[48,3072]{1,0:T(8,128)(2,1)S(1)}, u32[]{:S(2)}, u32[]{:S(2)}) %collective-permute-start.4) | collective-permute-done | bytes 294944 | tf_op jit(solution)/shard_map/ppermute | solution.py:72
  44.1 0.0 collective-permute-done.5
  44.2 4.9 %collective-permute-done.6 = bf16[48,3072]{1,0:T(8,128)(2,1)S(1)} collective-permute-done((bf16[48,3072]{1,0:T(8,128)(2,1)S(1)}, bf16[48,3072]{1,0:T(8,128)(2,1)S(1)}, u32[]{:S(2)}, u32[]{:S(2)}) %collective-permute-start.6) | collective-permute-done | bytes 294944 | tf_op jit(solution)/shard_map/ppermute | solution.py:72
  49.1 0.0 copy-done
  49.1 0.0 copy-start.1
  49.1 0.0 copy-start.4
  49.1 1.4 fusion.10.mine
  50.5 0.0 copy-done.1
  50.6 1.9 %collective-permute-start.7 = (f32[384,384]{1,0:T(8,128)S(1)}, f32[384,384]{1,0:T(8,128)S(1)}, u32[]{:S(2)}, u32[]{:S(2)}) collective-permute-start(f32[384,384]{1,0:T(8,128)S(1)} %fusion.10.mine), channel_id=1, source_target_pairs={{0,1},{1,0},{2,3},{3,2},{4,5},{5,4},{6,7},{7,6},{8,9},{9,8},{10,11... | collective-permute-start | bytes 1769480 | tf_op jit(solution)/shard_map/ppermute | solution.py:72
  52.5 0.1 pad_add_fusion.where
  52.6 1.9 %collective-permute-done.7.theirs = f32[384,384]{1,0:T(8,128)S(1)} collective-permute-done((f32[384,384]{1,0:T(8,128)S(1)}, f32[384,384]{1,0:T(8,128)S(1)}, u32[]{:S(2)}, u32[]{:S(2)}) %collective-permute-start.7) | collective-permute-done | bytes 589856 | tf_op jit(solution)/shard_map/ppermute | solution.py:72
  54.4 0.0 copy-done.4
  54.5 1.7 %copy-done.2 = bf16[384,3072]{1,0:T(8,128)(2,1)S(1)} copy-done((bf16[384,3072]{1,0:T(8,128)(2,1)S(1)}, bf16[384,3072]{1,0:T(8,128)(2,1)}, u32[]{:S(2)}) %copy-start.2) | copy-done | bytes 2359320
  56.1 1.0 copy-done.3
  57.1 3.0 %rows_and_chunks.1 = (bf16[384,384]{1,0:T(8,128)(2,1)S(1)}, bf16[6,64,384]{2,1,0:T(8,128)(2,1)S(1)}, bf16[6,64,384]{2,1,0:T(8,128)(2,1)S(1)}, bf16[6,64,384]{2,1...) custom-call(s32[3]{0:T(128)S(1)} %pad_add_fusion.where, ...), custom_call_target="tpu_custom_call" | custom-call | tf_op jit(solution)/shard_map/rows_and_chunks/pallas_call | solution.py:59
  60.1 0.8 convolution_convert_fusion
  61.0 0.8 convolution_convert_fusion.2
  61.9 4.5 %collective-permute-start.15 = (bf16[6,32,384]{2,1,0:T(8,128)(2,1)S(1)}, bf16[6,32,384]{2,1,0:T(8,128)(2,1)S(1)}, u32[]{:S(2)}, u32[]{:S(2)}) collective-permute-start(bf16[6,32,384]{2,1,0:T(8,128)(2,1)S(1)} %get-tuple-element.20), channel_id=1, source_target_pairs={{0,32},{16,48},{32,64},{48,80},{64,96},{80,112},{96,0},{112,16},{1... | collective-permute-start | bytes 442376 | tf_op jit(solution)/shard_map/ppermute | solution.py:72
  66.4 3.5 %collective-permute-start.14 = (bf16[6,64,384]{2,1,0:T(8,128)(2,1)S(1)}, bf16[6,64,384]{2,1,0:T(8,128)(2,1)S(1)}, u32[]{:S(2)}, u32[]{:S(2)}) collective-permute-start(bf16[6,64,384]{2,1,0:T(8,128)(2,1)S(1)} %get-tuple-element.16), channel_id=1, source_target_pairs={{0,16},{16,32},{32,48},{48,64},{64,80},{80,96},{96,112},{112,0},{1... | collective-permute-start | bytes 884744 | tf_op jit(solution)/shard_map/ppermute | solution.py:72
  69.9 2.5 %collective-permute-start.10 = (bf16[96,3072]{1,0:T(8,128)(2,1)S(1)}, bf16[96,3072]{1,0:T(8,128)(2,1)S(1)}, u32[]{:S(2)}, u32[]{:S(2)}) collective-permute-start(bf16[96,3072]{1,0:T(8,128)(2,1)S(1)} %convolution_convert_fusion), channel_id=1, source_target_pairs={{0,4},{4,8},{8,12},{12,0},{1,5},{5,9},{9,13},{13,1},{2,6},{6,10},{... | collective-permute-start | bytes 1769480 | tf_op jit(solution)/shard_map/ppermute | solution.py:72
  72.4 3.3 %collective-permute-start.8 = (bf16[96,3072]{1,0:T(8,128)(2,1)S(1)}, bf16[96,3072]{1,0:T(8,128)(2,1)S(1)}, u32[]{:S(2)}, u32[]{:S(2)}) collective-permute-start(bf16[96,3072]{1,0:T(8,128)(2,1)S(1)} %convolution_convert_fusion.2), channel_id=1, source_target_pairs={{0,12},{4,0},{8,4},{12,8},{1,13},{5,1},{9,5},{13,9},{2,14},{6,2},{... | collective-permute-start | bytes 1769480 | tf_op jit(solution)/shard_map/ppermute | solution.py:72
  75.7 0.8 convolution_convert_fusion.1
  76.6 4.3 %collective-permute-start.9 = (bf16[96,3072]{1,0:T(8,128)(2,1)S(1)}, bf16[96,3072]{1,0:T(8,128)(2,1)S(1)}, u32[]{:S(2)}, u32[]{:S(2)}) collective-permute-start(bf16[96,3072]{1,0:T(8,128)(2,1)S(1)} %convolution_convert_fusion.1), channel_id=1, source_target_pairs={{0,8},{4,12},{8,0},{12,4},{1,9},{5,13},{9,1},{13,5},{2,10},{6,14},... | collective-permute-start | bytes 1769480 | tf_op jit(solution)/shard_map/ppermute | solution.py:72
  80.9 0.0 collective-permute-done.15
  80.9 3.6 %collective-permute-start.17 = (bf16[6,64,384]{2,1,0:T(8,128)(2,1)S(1)}, bf16[6,64,384]{2,1,0:T(8,128)(2,1)S(1)}, u32[]{:S(2)}, u32[]{:S(2)}) collective-permute-start(bf16[6,64,384]{2,1,0:T(8,128)(2,1)S(1)} %get-tuple-element.19), channel_id=1, source_target_pairs={{0,112},{16,0},{32,16},{48,32},{64,48},{80,64},{96,80},{112,96},{1... | collective-permute-start | bytes 884744 | tf_op jit(solution)/shard_map/ppermute | solution.py:72
  84.5 0.0 collective-permute-done.14
  84.5 2.5 %collective-permute-start.18 = (bf16[6,32,384]{2,1,0:T(8,128)(2,1)S(1)}, bf16[6,32,384]{2,1,0:T(8,128)(2,1)S(1)}, u32[]{:S(2)}, u32[]{:S(2)}) collective-permute-start(bf16[6,32,384]{2,1,0:T(8,128)(2,1)S(1)} %get-tuple-element.21), channel_id=1, source_target_pairs={{0,96},{16,112},{32,0},{48,16},{64,32},{80,48},{96,64},{112,80},{1... | collective-permute-start | bytes 442376 | tf_op jit(solution)/shard_map/ppermute | solution.py:72
  87.0 0.1 add_convert_fusion.2
  87.1 11.9 %collective-permute-done.18 = bf16[6,32,384]{2,1,0:T(8,128)(2,1)S(1)} collective-permute-done((bf16[6,32,384]{2,1,0:T(8,128)(2,1)S(1)}, bf16[6,32,384]{2,1,0:T(8,128)(2,1)S(1)}, u32[]{:S(2)}, u32[]{:S(2)}) %collective-permute-start.18) | collective-permute-done | bytes 147488 | tf_op jit(solution)/shard_map/ppermute | solution.py:72
  99.0 1.9 %collective-permute-start.12 = (bf16[6,64,384]{2,1,0:T(8,128)(2,1)S(1)}, bf16[6,64,384]{2,1,0:T(8,128)(2,1)S(1)}, u32[]{:S(2)}, u32[]{:S(2)}) collective-permute-start(bf16[6,64,384]{2,1,0:T(8,128)(2,1)S(1)} %get-tuple-element.13), channel_id=1, source_target_pairs={{0,16},{16,32},{32,48},{48,64},{64,80},{80,96},{96,112},{112,0},{1... | collective-permute-start | bytes 884744 | tf_op jit(solution)/shard_map/ppermute | solution.py:72
  100.9 0.0 collective-permute-done.17
  100.9 5.1 %collective-permute-start.13 = (bf16[6,64,384]{2,1,0:T(8,128)(2,1)S(1)}, bf16[6,64,384]{2,1,0:T(8,128)(2,1)S(1)}, u32[]{:S(2)}, u32[]{:S(2)}) collective-permute-start(bf16[6,64,384]{2,1,0:T(8,128)(2,1)S(1)} %get-tuple-element.14), channel_id=1, source_target_pairs={{0,112},{16,0},{32,16},{48,32},{64,48},{80,64},{96,80},{112,96},{1... | collective-permute-start | bytes 884744 | tf_op jit(solution)/shard_map/ppermute | solution.py:72
  106.1 0.1 add_convert_fusion.1
  106.2 0.0 collective-permute-done.10
  106.2 2.7 %collective-permute-start.16 = (bf16[6,64,384]{2,1,0:T(8,128)(2,1)S(1)}, bf16[6,64,384]{2,1,0:T(8,128)(2,1)S(1)}, u32[]{:S(2)}, u32[]{:S(2)}) collective-permute-start(bf16[6,64,384]{2,1,0:T(8,128)(2,1)S(1)} %add_convert_fusion.2), channel_id=1, source_target_pairs={{0,32},{16,48},{32,64},{48,80},{64,96},{80,112},{96,0},{112,16},{1... | collective-permute-start | bytes 884744 | tf_op jit(solution)/shard_map/ppermute | solution.py:72
  108.9 0.0 collective-permute-done.8
  108.9 5.3 %collective-permute-start.19 = (bf16[6,64,384]{2,1,0:T(8,128)(2,1)S(1)}, bf16[6,64,384]{2,1,0:T(8,128)(2,1)S(1)}, u32[]{:S(2)}, u32[]{:S(2)}) collective-permute-start(bf16[6,64,384]{2,1,0:T(8,128)(2,1)S(1)} %add_convert_fusion.1), channel_id=1, source_target_pairs={{0,96},{16,112},{32,0},{48,16},{64,32},{80,48},{96,64},{112,80},{1... | collective-permute-start | bytes 884744 | tf_op jit(solution)/shard_map/ppermute | solution.py:72
  114.2 0.0 collective-permute-done.9
  114.2 0.9 fusion.3
  115.1 0.7 slice.47
  115.8 4.8 %collective-permute-start.11 = (bf16[48,3072]{1,0:T(8,128)(2,1)}, bf16[48,3072]{1,0:T(8,128)(2,1)}, u32[]{:S(2)}, u32[]{:S(2)}) collective-permute-start(bf16[48,3072]{1,0:T(8,128)(2,1)} %slice.47), channel_id=1, source_target_pairs={{0,2},{2,0},{1,3},{3,1},{4,6},{6,4},{5,7},{7,5},{8,10},{10,8},{9,1... | collective-permute-start | bytes 884744 | tf_op jit(solution)/shard_map/ppermute | solution.py:72
  120.6 0.0 collective-permute-done.12
  120.6 0.0 collective-permute-done.13
  120.6 1.5 collective-permute-done.16
  122.1 2.1 %collective-permute-done.19 = bf16[6,64,384]{2,1,0:T(8,128)(2,1)S(1)} collective-permute-done((bf16[6,64,384]{2,1,0:T(8,128)(2,1)S(1)}, bf16[6,64,384]{2,1,0:T(8,128)(2,1)S(1)}, u32[]{:S(2)}, u32[]{:S(2)}) %collective-permute-start.19) | collective-permute-done | bytes 294944 | tf_op jit(solution)/shard_map/ppermute | solution.py:72
  124.2 0.9 add_convert_fusion
  125.1 15.1 %all-to-all-start = ((bf16[6,64,384]{2,1,0:T(8,128)(2,1)}), bf16[6,64,384]{2,1,0:T(8,128)(2,1)}, u32[]{:S(2)}, u32[]{:S(2)}) async-start(bf16[6,64,384]{2,1,0:T(8,128)(2,1)} %add_convert_fusion), calls=%async_computation | async-start | bytes 589824 | tf_op jit(solution)/shard_map/all_to_all | solution.py:130
  140.2 0.0 collective-permute-done.11
  140.2 1.7 %fusion.4 = bf16[48,3072]{1,0:T(8,128)(2,1)} fusion(f32[96,3072]{1,0:T(8,128)S(1)} %fusion.3, bf16[48,3072]{1,0:T(8,128)(2,1)} %collective-permute-done.11), kind=kLoop, calls=%fused_computation.10 | loop fusion | flops 442368 | bytes 1179648 | tf_op jit(solution)/shard_map/convert_element_type | solution.py:127
  141.9 12.3 %all-to-all-done = bf16[6,64,384]{2,1,0:T(8,128)(2,1)} async-done(((bf16[6,64,384]{2,1,0:T(8,128)(2,1)}), bf16[6,64,384]{2,1,0:T(8,128)(2,1)}, u32[]{:S(2)}, u32[]{:S(2)}) %all-to-all-start) | async-done | bytes 294944 | tf_op jit(solution)/shard_map/all_to_all | solution.py:130
  154.2 1.6 %convert_reduce_fusion = f32[64,384]{1,0:T(8,128)} fusion(bf16[6,64,384]{2,1,0:T(8,128)(2,1)} %all-to-all-done), kind=kLoop, calls=%fused_computation.11 | loop fusion | flops 270336 | bytes 393216 | tf_op jit(solution)/shard_map/reduce_sum | solution.py:131
  (10 shorter events, 0.2 us)
Async XLA Ops:
  0.6 48.5 %copy-start = (bf16[3072,384]{1,0:T(8,128)(2,1)S(1)}, bf16[3072,384]{1,0:T(8,128)(2,1)}, u32[]{:S(2)}) copy-start(bf16[3072,384]{1,0:T(8,128)(2,1)} %param.5) | copy-start | bytes 7077892
  0.6 24.9 %collective-permute-start = (bf16[48,3072]{1,0:T(8,128)(2,1)}, bf16[48,3072]{1,0:T(8,128)(2,1)S(1)}, u32[]{:S(2)}, u32[]{:S(2)}) collective-permute-start(bf16[48,3072]{1,0:T(8,128)(2,1)} %param.4), channel_id=1, source_target_pairs={{0,2},{2,0},{1,3},{3,1},{4,6},{6,4},{5,7},{7,5},{8,10},{10,8},{9,1... | collective-permute-start | bytes 884744 | tf_op jit(solution)/shard_map/ppermute | solution.py:72
  15.9 16.8 %collective-permute-start.1 = (bf16[48,3072]{1,0:T(8,128)(2,1)}, bf16[48,3072]{1,0:T(8,128)(2,1)S(1)}, u32[]{:S(2)}, u32[]{:S(2)}) collective-permute-start(bf16[48,3072]{1,0:T(8,128)(2,1)} %param.4), channel_id=1, source_target_pairs={{0,4},{4,8},{8,12},{12,0},{1,5},{5,9},{9,13},{13,1},{2,6},{6,10},{... | collective-permute-start | bytes 884744 | tf_op jit(solution)/shard_map/ppermute | solution.py:72
  18.3 22.3 %collective-permute-start.3 = (bf16[48,3072]{1,0:T(8,128)(2,1)}, bf16[48,3072]{1,0:T(8,128)(2,1)S(1)}, u32[]{:S(2)}, u32[]{:S(2)}) collective-permute-start(bf16[48,3072]{1,0:T(8,128)(2,1)} %param.4), channel_id=1, source_target_pairs={{0,8},{4,12},{8,0},{12,4},{1,9},{5,13},{9,1},{13,5},{2,10},{6,14},... | collective-permute-start | bytes 884744 | tf_op jit(solution)/shard_map/ppermute | solution.py:72
  22.6 21.5 %collective-permute-start.5 = (bf16[48,3072]{1,0:T(8,128)(2,1)}, bf16[48,3072]{1,0:T(8,128)(2,1)S(1)}, u32[]{:S(2)}, u32[]{:S(2)}) collective-permute-start(bf16[48,3072]{1,0:T(8,128)(2,1)} %param.4), channel_id=1, source_target_pairs={{0,12},{4,0},{8,4},{12,8},{1,13},{5,1},{9,5},{13,9},{2,14},{6,2},{... | collective-permute-start | bytes 884744 | tf_op jit(solution)/shard_map/ppermute | solution.py:72
  25.6 15.0 %collective-permute-start.2 = (bf16[48,3072]{1,0:T(8,128)(2,1)S(1)}, bf16[48,3072]{1,0:T(8,128)(2,1)S(1)}, u32[]{:S(2)}, u32[]{:S(2)}) collective-permute-start(bf16[48,3072]{1,0:T(8,128)(2,1)S(1)} %collective-permute-done), channel_id=1, source_target_pairs={{0,4},{4,8},{8,12},{12,0},{1,5},{5,9},{9,13},{13,1},{2,6},{6,10},{... | collective-permute-start | bytes 884744 | tf_op jit(solution)/shard_map/ppermute | solution.py:72
  30.7 13.4 %collective-permute-start.4 = (bf16[48,3072]{1,0:T(8,128)(2,1)S(1)}, bf16[48,3072]{1,0:T(8,128)(2,1)S(1)}, u32[]{:S(2)}, u32[]{:S(2)}) collective-permute-start(bf16[48,3072]{1,0:T(8,128)(2,1)S(1)} %collective-permute-done), channel_id=1, source_target_pairs={{0,8},{4,12},{8,0},{12,4},{1,9},{5,13},{9,1},{13,5},{2,10},{6,14},... | collective-permute-start | bytes 884744 | tf_op jit(solution)/shard_map/ppermute | solution.py:72
  32.7 16.4 %collective-permute-start.6 = (bf16[48,3072]{1,0:T(8,128)(2,1)S(1)}, bf16[48,3072]{1,0:T(8,128)(2,1)S(1)}, u32[]{:S(2)}, u32[]{:S(2)}) collective-permute-start(bf16[48,3072]{1,0:T(8,128)(2,1)S(1)} %collective-permute-done), channel_id=1, source_target_pairs={{0,12},{4,0},{8,4},{12,8},{1,13},{5,1},{9,5},{13,9},{2,14},{6,2},{... | collective-permute-start | bytes 884744 | tf_op jit(solution)/shard_map/ppermute | solution.py:72
  49.1 1.4 copy-start.1
  49.1 5.3 %copy-start.4 = (f32[128]{0:T(128)S(1)}, f32[128]{0:T(128)}, u32[]{:S(2)}) copy-start(f32[128]{0:T(128)} %param.7) | copy-start | bytes 1540
  50.6 3.9 %collective-permute-start.7 = (f32[384,384]{1,0:T(8,128)S(1)}, f32[384,384]{1,0:T(8,128)S(1)}, u32[]{:S(2)}, u32[]{:S(2)}) collective-permute-start(f32[384,384]{1,0:T(8,128)S(1)} %fusion.10.mine), channel_id=1, source_target_pairs={{0,1},{1,0},{2,3},{3,2},{4,5},{5,4},{6,7},{7,6},{8,9},{9,8},{10,11... | collective-permute-start | bytes 1769480 | tf_op jit(solution)/shard_map/ppermute | solution.py:72
  54.4 1.7 %copy-start.2 = (bf16[384,3072]{1,0:T(8,128)(2,1)S(1)}, bf16[384,3072]{1,0:T(8,128)(2,1)}, u32[]{:S(2)}) copy-start(bf16[384,3072]{1,0:T(8,128)(2,1)} %copy-done.1) | copy-start | bytes 7077892
  56.1 1.0 copy-start.3
  61.9 19.0 %collective-permute-start.15 = (bf16[6,32,384]{2,1,0:T(8,128)(2,1)S(1)}, bf16[6,32,384]{2,1,0:T(8,128)(2,1)S(1)}, u32[]{:S(2)}, u32[]{:S(2)}) collective-permute-start(bf16[6,32,384]{2,1,0:T(8,128)(2,1)S(1)} %get-tuple-element.20), channel_id=1, source_target_pairs={{0,32},{16,48},{32,64},{48,80},{64,96},{80,112},{96,0},{112,16},{1... | collective-permute-start | bytes 442376 | tf_op jit(solution)/shard_map/ppermute | solution.py:72
  66.4 18.1 %collective-permute-start.14 = (bf16[6,64,384]{2,1,0:T(8,128)(2,1)S(1)}, bf16[6,64,384]{2,1,0:T(8,128)(2,1)S(1)}, u32[]{:S(2)}, u32[]{:S(2)}) collective-permute-start(bf16[6,64,384]{2,1,0:T(8,128)(2,1)S(1)} %get-tuple-element.16), channel_id=1, source_target_pairs={{0,16},{16,32},{32,48},{48,64},{64,80},{80,96},{96,112},{112,0},{1... | collective-permute-start | bytes 884744 | tf_op jit(solution)/shard_map/ppermute | solution.py:72
  69.9 36.3 %collective-permute-start.10 = (bf16[96,3072]{1,0:T(8,128)(2,1)S(1)}, bf16[96,3072]{1,0:T(8,128)(2,1)S(1)}, u32[]{:S(2)}, u32[]{:S(2)}) collective-permute-start(bf16[96,3072]{1,0:T(8,128)(2,1)S(1)} %convolution_convert_fusion), channel_id=1, source_target_pairs={{0,4},{4,8},{8,12},{12,0},{1,5},{5,9},{9,13},{13,1},{2,6},{6,10},{... | collective-permute-start | bytes 1769480 | tf_op jit(solution)/shard_map/ppermute | solution.py:72
  72.4 36.5 %collective-permute-start.8 = (bf16[96,3072]{1,0:T(8,128)(2,1)S(1)}, bf16[96,3072]{1,0:T(8,128)(2,1)S(1)}, u32[]{:S(2)}, u32[]{:S(2)}) collective-permute-start(bf16[96,3072]{1,0:T(8,128)(2,1)S(1)} %convolution_convert_fusion.2), channel_id=1, source_target_pairs={{0,12},{4,0},{8,4},{12,8},{1,13},{5,1},{9,5},{13,9},{2,14},{6,2},{... | collective-permute-start | bytes 1769480 | tf_op jit(solution)/shard_map/ppermute | solution.py:72
  76.6 37.6 %collective-permute-start.9 = (bf16[96,3072]{1,0:T(8,128)(2,1)S(1)}, bf16[96,3072]{1,0:T(8,128)(2,1)S(1)}, u32[]{:S(2)}, u32[]{:S(2)}) collective-permute-start(bf16[96,3072]{1,0:T(8,128)(2,1)S(1)} %convolution_convert_fusion.1), channel_id=1, source_target_pairs={{0,8},{4,12},{8,0},{12,4},{1,9},{5,13},{9,1},{13,5},{2,10},{6,14},... | collective-permute-start | bytes 1769480 | tf_op jit(solution)/shard_map/ppermute | solution.py:72
  80.9 20.0 %collective-permute-start.17 = (bf16[6,64,384]{2,1,0:T(8,128)(2,1)S(1)}, bf16[6,64,384]{2,1,0:T(8,128)(2,1)S(1)}, u32[]{:S(2)}, u32[]{:S(2)}) collective-permute-start(bf16[6,64,384]{2,1,0:T(8,128)(2,1)S(1)} %get-tuple-element.19), channel_id=1, source_target_pairs={{0,112},{16,0},{32,16},{48,32},{64,48},{80,64},{96,80},{112,96},{1... | collective-permute-start | bytes 884744 | tf_op jit(solution)/shard_map/ppermute | solution.py:72
  84.5 14.5 %collective-permute-start.18 = (bf16[6,32,384]{2,1,0:T(8,128)(2,1)S(1)}, bf16[6,32,384]{2,1,0:T(8,128)(2,1)S(1)}, u32[]{:S(2)}, u32[]{:S(2)}) collective-permute-start(bf16[6,32,384]{2,1,0:T(8,128)(2,1)S(1)} %get-tuple-element.21), channel_id=1, source_target_pairs={{0,96},{16,112},{32,0},{48,16},{64,32},{80,48},{96,64},{112,80},{1... | collective-permute-start | bytes 442376 | tf_op jit(solution)/shard_map/ppermute | solution.py:72
  99.0 21.6 %collective-permute-start.12 = (bf16[6,64,384]{2,1,0:T(8,128)(2,1)S(1)}, bf16[6,64,384]{2,1,0:T(8,128)(2,1)S(1)}, u32[]{:S(2)}, u32[]{:S(2)}) collective-permute-start(bf16[6,64,384]{2,1,0:T(8,128)(2,1)S(1)} %get-tuple-element.13), channel_id=1, source_target_pairs={{0,16},{16,32},{32,48},{48,64},{64,80},{80,96},{96,112},{112,0},{1... | collective-permute-start | bytes 884744 | tf_op jit(solution)/shard_map/ppermute | solution.py:72
  100.9 19.7 %collective-permute-start.13 = (bf16[6,64,384]{2,1,0:T(8,128)(2,1)S(1)}, bf16[6,64,384]{2,1,0:T(8,128)(2,1)S(1)}, u32[]{:S(2)}, u32[]{:S(2)}) collective-permute-start(bf16[6,64,384]{2,1,0:T(8,128)(2,1)S(1)} %get-tuple-element.14), channel_id=1, source_target_pairs={{0,112},{16,0},{32,16},{48,32},{64,48},{80,64},{96,80},{112,96},{1... | collective-permute-start | bytes 884744 | tf_op jit(solution)/shard_map/ppermute | solution.py:72
  106.2 15.9 %collective-permute-start.16 = (bf16[6,64,384]{2,1,0:T(8,128)(2,1)S(1)}, bf16[6,64,384]{2,1,0:T(8,128)(2,1)S(1)}, u32[]{:S(2)}, u32[]{:S(2)}) collective-permute-start(bf16[6,64,384]{2,1,0:T(8,128)(2,1)S(1)} %add_convert_fusion.2), channel_id=1, source_target_pairs={{0,32},{16,48},{32,64},{48,80},{64,96},{80,112},{96,0},{112,16},{1... | collective-permute-start | bytes 884744 | tf_op jit(solution)/shard_map/ppermute | solution.py:72
  108.9 15.3 %collective-permute-start.19 = (bf16[6,64,384]{2,1,0:T(8,128)(2,1)S(1)}, bf16[6,64,384]{2,1,0:T(8,128)(2,1)S(1)}, u32[]{:S(2)}, u32[]{:S(2)}) collective-permute-start(bf16[6,64,384]{2,1,0:T(8,128)(2,1)S(1)} %add_convert_fusion.1), channel_id=1, source_target_pairs={{0,96},{16,112},{32,0},{48,16},{64,32},{80,48},{96,64},{112,80},{1... | collective-permute-start | bytes 884744 | tf_op jit(solution)/shard_map/ppermute | solution.py:72
  115.8 24.4 %collective-permute-start.11 = (bf16[48,3072]{1,0:T(8,128)(2,1)}, bf16[48,3072]{1,0:T(8,128)(2,1)}, u32[]{:S(2)}, u32[]{:S(2)}) collective-permute-start(bf16[48,3072]{1,0:T(8,128)(2,1)} %slice.47), channel_id=1, source_target_pairs={{0,2},{2,0},{1,3},{3,1},{4,6},{6,4},{5,7},{7,5},{8,10},{10,8},{9,1... | collective-permute-start | bytes 884744 | tf_op jit(solution)/shard_map/ppermute | solution.py:72
  125.1 29.1 %all-to-all-start = ((bf16[6,64,384]{2,1,0:T(8,128)(2,1)}), bf16[6,64,384]{2,1,0:T(8,128)(2,1)}, u32[]{:S(2)}, u32[]{:S(2)}) async-start(bf16[6,64,384]{2,1,0:T(8,128)(2,1)} %add_convert_fusion), calls=%async_computation | async-start | bytes 589824 | tf_op jit(solution)/shard_map/all_to_all | solution.py:130

commit v3 on v2

--- a/solution.py
+++ b/solution.py
@@ -10,6 +10,7 @@
 
 F32 = jnp.float32
 BF16 = jnp.bfloat16
+ORDER = ((3, 1), (5, 7), (4,), (2,), (6,), (0,))
 
 
 def mean(value):
@@ -45,9 +46,10 @@
             (((0,), (0,)), ((), ())),
             preferred_element_type=F32,
         )
-        for k in range(ny):
-            at = pl.multiple_of(lax.rem(y + k, ny) * blk, blk)
-            outs[k][z] = term[pl.ds(at, blk), :].astype(BF16)
+        for out, ks in zip(outs, ORDER):
+            for i, k in enumerate(ks):
+                at = pl.multiple_of(lax.rem(y + k, ny) * blk, blk)
+                out[i, z] = term[pl.ds(at, blk), :].astype(BF16)
 
 
 def rows_and_chunks(sizes, factor, where, mine, theirs, cot, gain, tokens):
@@ -55,14 +57,14 @@
     heads = mine.shape[1]
     part = tokens.shape[1] // nz
     vmem = pl.BlockSpec(memory_space=pltpu.VMEM)
-    chunk = jax.ShapeDtypeStruct((nz, part // ny, heads), BF16)
+    chunks = [jax.ShapeDtypeStruct((len(ks), nz, part // ny, heads), BF16) for ks in ORDER]
     return pl.pallas_call(
         functools.partial(rows_kernel, sizes, factor),
-        out_shape=[jax.ShapeDtypeStruct(mine.shape, BF16)] + [chunk] * ny,
+        out_shape=[jax.ShapeDtypeStruct(mine.shape, BF16)] + chunks,
         in_specs=[pl.BlockSpec(memory_space=pltpu.SMEM)] + [vmem] * 5,
-        out_specs=[vmem] * (ny + 1),
+        out_specs=[vmem] * (len(ORDER) + 1),
         scratch_shapes=[pltpu.VMEM((part, heads), F32)],
-        compiler_params=pltpu.CompilerParams(vmem_limit_bytes=40 * 2**20),
+        compiler_params=pltpu.CompilerParams(vmem_limit_bytes=8 * 2**20),
         name="rows_and_chunks",
     )(where, mine, theirs, cot, gain, tokens)
 
@@ -86,9 +88,11 @@
     where = jnp.stack([lax.axis_index(a) for a in ("x", "zh", "y")]).astype(jnp.int32)
 
     peer = shift(normed, "zh", 1)
-    own = [normed] + [shift(normed, "x", k) for k in range(1, nx)]
-    other = [peer] + [shift(peer, "x", k) for k in range(1, nx)]
-    tokens = jnp.concatenate([p for pair in zip(own, other) for p in pair], axis=0)
+    own1, own3 = shift(normed, "x", 1), shift(normed, "x", -1)
+    both = jnp.concatenate([normed, peer], axis=0)
+    both2 = shift(both, "x", 2)
+    peer1, peer3 = shift(peer, "x", 1), shift(peer, "x", -1)
+    tokens = jnp.concatenate([both, own1, peer1, both2, own3, peer3], axis=0)
 
     mine = jnp.dot(tokens, weight, preferred_element_type=F32)
     theirs = shift(mine, "c", 1)
@@ -104,14 +108,16 @@
         tokens,
     )
 
-    half = c[4].shape[1] // 2
-    from3, from5 = shift(c[3], "y", 1), shift(c[5], "y", -1)
-    low = shift(c[4][:, :half], "y", 2)
-    high = shift(c[4][:, half:], "y", -2)
-    near1, near7 = shift(c[1], "y", 1), shift(c[7], "y", -1)
-    up = add(c[2], from3) + jnp.pad(low.astype(F32), ((0, 0), (0, half), (0, 0)))
-    down = add(c[6], from5) + jnp.pad(high.astype(F32), ((0, 0), (half, 0), (0, 0)))
-    near2, near6 = shift(up.astype(BF16), "y", 2), shift(down.astype(BF16), "y", -2)
+    up, down, across, two, six, own = c
+    core = lax.axis_index("c")
+    turn = [
+        (i * 2 + j, (i + (2, -2)[j]) % ny * 2 + j) for i in range(ny) for j in range(2)
+    ]
+    got_up, got_down = shift(up, "y", 1), shift(down, "y", -1)
+    got4 = lax.ppermute(across[0], ("y", "c"), turn).astype(F32)
+    two = add(two[0], got_up[0], jnp.where(core == 0, got4, 0.0)).astype(BF16)
+    six = add(six[0], got_down[0], jnp.where(core == 1, got4, 0.0)).astype(BF16)
+    got2, got6 = shift(two, "y", 2), shift(six, "y", -2)
 
     back = [
         lax.dot_general(
@@ -119,16 +125,29 @@
             weight,
             (((1,), (1,)), ((), ())),
             preferred_element_type=F32,
-        ).astype(BF16)
+        )
         for k in range(nx)
     ]
-    total = add(back[0], *[shift(back[k], "x", -k) for k in range(1, nx)])
-    far = shift(total[count:].astype(BF16), "zh", 1)
-    input_grad = add(total[:count], far).astype(BF16)
+    terms = [back[0]] + [shift(back[k].astype(BF16), "x", -k) for k in (2, 1, 3)]
+    far = shift(add(*[t[count:] for t in terms]).astype(BF16), "zh", 1)
+    input_grad = add(*[t[:count] for t in terms], far).astype(BF16)
 
-    over_y = add(c[0], near1, near7, near2, near6).astype(BF16)
-    pieces = lax.all_to_all(over_y, "zl", 0, 0, tiled=True)
-    weight_grad = jnp.sum(pieces.astype(F32), axis=0)
+    over_y = add(own[0], got_up[1], got_down[1], got2, got6)
+    third = nz // 2
+    zl = lax.axis_index("zl")
+    over_y = over_y.reshape(2, third, -1, heads)
+    place = zl % third
+
+    def of_third(k):
+        return lax.dynamic_index_in_dim(over_y, (place + k) % third, 1, False)
+
+    kept = of_third(0)
+    for k in range(1, third):
+        hop = [(i, i // third * third + (i + k) % third) for i in range(nz)]
+        kept = add(kept, lax.ppermute(of_third(k).astype(BF16), "zl", hop))
+    side = zl // third
+    last = shift(lax.dynamic_index_in_dim(kept, 1 - side, 0, False).astype(BF16), "zl", third)
+    weight_grad = add(lax.dynamic_index_in_dim(kept, side, 0, False), last)
     return (input_grad, weight_grad)
 
 

time: 158 us -> 165 us (1.044)
  the two profiles are of different devices: /device:TPU:6 before, /device:TPU:17 now
where the time goes in v3:
time: 165 us; the launch traced here: 164 us
  starting transfers between devices  92.7 us (56%)
  waiting for transfers between devices  55.5 us (34%)
  matrix products  4.81 us (3%)
  local copies, waits for them, and re-layouts  3.85 us (2%)
  other arithmetic  3.21 us (2%)
  Pallas kernels  3.07 us (2%)
    ppermute x16, starting transfers between devices, shift(): lax.ppermute(value, axis, [(i, (i + by) % size) for i in range(size)])  73 us
    ppermute x16, waiting for transfers between devices, shift(): lax.ppermute(value, axis, [(i, (i + by) % size) for i in range(size)])  44.7 us
    ppermute x2, starting transfers between devices, body(): kept = add(kept, lax.ppermute(of_third(k).astype(BF16), 'zl', hop))  15.9 us
    ppermute x1, waiting for transfers between devices, body(): got4 = lax.ppermute(across[0], ('y', 'c'), turn).astype(F32)  10.8 us
    unnamed x16, local copies, waits for them, and re-layouts  3.77 us
    ppermute x1, starting transfers between devices, body(): got4 = lax.ppermute(across[0], ('y', 'c'), turn).astype(F32)  3.7 us
    dot_general x4, matrix products, body(): lax.dot_general(rows[k * nh * count:(k + 1) * nh * count], weight, (((1,)...  3.41 us
  transfers between devices with their start and end apart: 19, of which 7 were waited for; matrix products, arithmetic and copies ran while one was open for 4% of the time, Pallas kernels for 0%

profile of v3, /device:TPU:17, one launch (start us, length us, event | category | flops | bytes accessed | tf_op | source)
XLA Modules:
  0.0 164.2 jit_solution(3493012543574297735)
XLA Ops:
  0.6 0.0 copy-start
  0.6 15.0 %collective-permute-start = (bf16[48,3072]{1,0:T(8,128)(2,1)}, bf16[48,3072]{1,0:T(8,128)(2,1)S(1)}, u32[]{:S(2)}, u32[]{:S(2)}) collective-permute-start(bf16[48,3072]{1,0:T(8,128)(2,1)} %param.4), channel_id=1, source_target_pairs={{0,2},{2,0},{1,3},{3,1},{4,6},{6,4},{5,7},{7,5},{8,10},{10,8},{9,1... | collective-permute-start | bytes 884744 | tf_op jit(solution)/shard_map/ppermute | solution.py:74
  15.6 3.1 %collective-permute-start.1 = (bf16[48,3072]{1,0:T(8,128)(2,1)}, bf16[48,3072]{1,0:T(8,128)(2,1)S(1)}, u32[]{:S(2)}, u32[]{:S(2)}) collective-permute-start(bf16[48,3072]{1,0:T(8,128)(2,1)} %param.4), channel_id=1, source_target_pairs={{0,4},{4,8},{8,12},{12,0},{1,5},{5,9},{9,13},{13,1},{2,6},{6,10},{... | collective-permute-start | bytes 884744 | tf_op jit(solution)/shard_map/ppermute | solution.py:74
  18.8 3.4 %collective-permute-start.4 = (bf16[48,3072]{1,0:T(8,128)(2,1)}, bf16[48,3072]{1,0:T(8,128)(2,1)S(1)}, u32[]{:S(2)}, u32[]{:S(2)}) collective-permute-start(bf16[48,3072]{1,0:T(8,128)(2,1)} %param.4), channel_id=1, source_target_pairs={{0,12},{4,0},{8,4},{12,8},{1,13},{5,1},{9,5},{13,9},{2,14},{6,2},{... | collective-permute-start | bytes 884744 | tf_op jit(solution)/shard_map/ppermute | solution.py:74
  22.2 1.0 constant_dynamic-update-slice_fusion.6
  23.2 0.0 collective-permute-done
  23.2 1.0 pad_maximum_fusion
  24.2 4.1 %collective-permute-start.3 = (bf16[96,3072]{1,0:T(8,128)(2,1)S(1)}, bf16[96,3072]{1,0:T(8,128)(2,1)S(1)}, u32[]{:S(2)}, u32[]{:S(2)}) collective-permute-start(bf16[96,3072]{1,0:T(8,128)(2,1)S(1)} %pad_maximum_fusion), channel_id=1, source_target_pairs={{0,8},{4,12},{8,0},{12,4},{1,9},{5,13},{9,1},{13,5},{2,10},{6,14},... | collective-permute-start | bytes 1769480 | tf_op jit(solution)/shard_map/ppermute | solution.py:74
  28.2 2.2 %collective-permute-start.2 = (bf16[48,3072]{1,0:T(8,128)(2,1)S(1)}, bf16[48,3072]{1,0:T(8,128)(2,1)S(1)}, u32[]{:S(2)}, u32[]{:S(2)}) collective-permute-start(bf16[48,3072]{1,0:T(8,128)(2,1)S(1)} %collective-permute-done), channel_id=1, source_target_pairs={{0,4},{4,8},{8,12},{12,0},{1,5},{5,9},{9,13},{13,1},{2,6},{6,10},{... | collective-permute-start | bytes 884744 | tf_op jit(solution)/shard_map/ppermute | solution.py:74
  30.5 4.3 %collective-permute-start.5 = (bf16[48,3072]{1,0:T(8,128)(2,1)S(1)}, bf16[48,3072]{1,0:T(8,128)(2,1)S(1)}, u32[]{:S(2)}, u32[]{:S(2)}) collective-permute-start(bf16[48,3072]{1,0:T(8,128)(2,1)S(1)} %collective-permute-done), channel_id=1, source_target_pairs={{0,12},{4,0},{8,4},{12,8},{1,13},{5,1},{9,5},{13,9},{2,14},{6,2},{... | collective-permute-start | bytes 884744 | tf_op jit(solution)/shard_map/ppermute | solution.py:74
  34.8 0.0 collective-permute-done.1
  34.8 14.3 %collective-permute-done.2 = bf16[48,3072]{1,0:T(8,128)(2,1)S(1)} collective-permute-done((bf16[48,3072]{1,0:T(8,128)(2,1)S(1)}, bf16[48,3072]{1,0:T(8,128)(2,1)S(1)}, u32[]{:S(2)}, u32[]{:S(2)}) %collective-permute-start.2) | collective-permute-done | bytes 294944 | tf_op jit(solution)/shard_map/ppermute | solution.py:74
  49.2 0.0 collective-permute-done.3
  49.2 0.0 collective-permute-done.4
  49.3 0.0 collective-permute-done.5
  49.3 0.0 copy-done
  49.3 0.0 copy-start.1
  49.3 0.0 copy-start.4
  49.3 1.4 fusion.21.mine
  50.7 0.0 copy-done.1
  50.8 2.4 %collective-permute-start.6 = (f32[384,384]{1,0:T(8,128)S(1)}, f32[384,384]{1,0:T(8,128)S(1)}, u32[]{:S(2)}, u32[]{:S(2)}) collective-permute-start(f32[384,384]{1,0:T(8,128)S(1)} %fusion.21.mine), channel_id=1, source_target_pairs={{0,1},{1,0},{2,3},{3,2},{4,5},{5,4},{6,7},{7,6},{8,9},{9,8},{10,11... | collective-permute-start | bytes 1769480 | tf_op jit(solution)/shard_map/ppermute | solution.py:74
  53.3 0.1 pad_add_fusion.where
  53.3 1.4 collective-permute-done.6.theirs
  54.8 0.0 copy-done.4
  54.8 0.0 copy-start.2
  54.8 1.7 %copy-done.2 = bf16[384,3072]{1,0:T(8,128)(2,1)S(1)} copy-done((bf16[384,3072]{1,0:T(8,128)(2,1)S(1)}, bf16[384,3072]{1,0:T(8,128)(2,1)}, u32[]{:S(2)}) %copy-start.2) | copy-done | bytes 2359320
  56.4 0.0 copy-start.3
  56.4 1.0 copy-done.3
  57.4 3.1 %rows_and_chunks.1 = (bf16[384,384]{1,0:T(8,128)(2,1)S(1)}, bf16[2,6,64,384]{3,2,1,0:T(8,128)(2,1)S(1)}, bf16[2,6,64,384]{3,2,1,0:T(8,128)(2,1)S(1)}, bf16[1,6,6...) custom-call(s32[3]{0:T(128)S(1)} %pad_add_fusion.where, ...), custom_call_target="tpu_custom_call" | custom-call | tf_op jit(solution)/shard_map/rows_and_chunks/pallas_call | solution.py:61
  60.5 3.2 %collective-permute-start.11 = (bf16[2,6,64,384]{3,2,1,0:T(8,128)(2,1)S(1)}, bf16[2,6,64,384]{3,2,1,0:T(8,128)(2,1)S(1)}, u32[]{:S(2)}, u32[]{:S(2)}) collective-permute-start(bf16[2,6,64,384]{3,2,1,0:T(8,128)(2,1)S(1)} %get-tuple-element.11), channel_id=1, source_target_pairs={{0,16},{16,32},{32,48},{48,64},{64,80},{80,96},{96,112},{112,0},{1... | collective-permute-start | bytes 1769480 | tf_op jit(solution)/shard_map/ppermute | solution.py:74
  63.7 2.1 %collective-permute-start.12 = (bf16[2,6,64,384]{3,2,1,0:T(8,128)(2,1)S(1)}, bf16[2,6,64,384]{3,2,1,0:T(8,128)(2,1)S(1)}, u32[]{:S(2)}, u32[]{:S(2)}) collective-permute-start(bf16[2,6,64,384]{3,2,1,0:T(8,128)(2,1)S(1)} %get-tuple-element.12), channel_id=1, source_target_pairs={{0,112},{16,0},{32,16},{48,32},{64,48},{80,64},{96,80},{112,96},{1... | collective-permute-start | bytes 1769480 | tf_op jit(solution)/shard_map/ppermute | solution.py:74
  65.8 3.7 %collective-permute-start.13 = (bf16[6,64,384]{2,1,0:T(8,128)(2,1)S(1)}, bf16[6,64,384]{2,1,0:T(8,128)(2,1)S(1)}, u32[]{:S(2)}, u32[]{:S(2)}) collective-permute-start(bf16[6,64,384]{2,1,0:T(8,128)(2,1)S(1)} %bitcast.43), channel_id=1, source_target_pairs={{0,32},{1,97},{16,48},{17,113},{32,64},{33,1},{48,80},{49,17},{64,... | collective-permute-start | bytes 884744 | tf_op jit(solution)/shard_map/ppermute | solution.py:117
  69.5 0.9 convolution_convert_fusion.2
  70.3 4.1 %collective-permute-start.7 = (bf16[96,3072]{1,0:T(8,128)(2,1)S(1)}, bf16[96,3072]{1,0:T(8,128)(2,1)S(1)}, u32[]{:S(2)}, u32[]{:S(2)}) collective-permute-start(bf16[96,3072]{1,0:T(8,128)(2,1)S(1)} %convolution_convert_fusion.2), channel_id=1, source_target_pairs={{0,8},{4,12},{8,0},{12,4},{1,9},{5,13},{9,1},{13,5},{2,10},{6,14},... | collective-permute-start | bytes 1769480 | tf_op jit(solution)/shard_map/ppermute | solution.py:74
  74.4 0.9 convolution_convert_fusion.1
  75.3 3.5 %collective-permute-start.8 = (bf16[96,3072]{1,0:T(8,128)(2,1)S(1)}, bf16[96,3072]{1,0:T(8,128)(2,1)S(1)}, u32[]{:S(2)}, u32[]{:S(2)}) collective-permute-start(bf16[96,3072]{1,0:T(8,128)(2,1)S(1)} %convolution_convert_fusion.1), channel_id=1, source_target_pairs={{0,12},{4,0},{8,4},{12,8},{1,13},{5,1},{9,5},{13,9},{2,14},{6,2},{... | collective-permute-start | bytes 1769480 | tf_op jit(solution)/shard_map/ppermute | solution.py:74
  78.8 0.9 convolution_convert_fusion
  79.6 10.8 %collective-permute-done.13 = bf16[6,64,384]{2,1,0:T(8,128)(2,1)S(1)} collective-permute-done((bf16[6,64,384]{2,1,0:T(8,128)(2,1)S(1)}, bf16[6,64,384]{2,1,0:T(8,128)(2,1)S(1)}, u32[]{:S(2)}, u32[]{:S(2)}) %collective-permute-start.13) | collective-permute-done | bytes 294944 | tf_op jit(solution)/shard_map/ppermute | solution.py:117
  90.4 3.2 %collective-permute-start.9 = (bf16[96,3072]{1,0:T(8,128)(2,1)S(1)}, bf16[96,3072]{1,0:T(8,128)(2,1)S(1)}, u32[]{:S(2)}, u32[]{:S(2)}) collective-permute-start(bf16[96,3072]{1,0:T(8,128)(2,1)S(1)} %convolution_convert_fusion), channel_id=1, source_target_pairs={{0,4},{4,8},{8,12},{12,0},{1,5},{5,9},{9,13},{13,1},{2,6},{6,10},{... | collective-permute-start | bytes 1769480 | tf_op jit(solution)/shard_map/ppermute | solution.py:74
  93.6 0.0 collective-permute-done.11
  93.6 0.0 collective-permute-done.12
  93.7 0.3 fusion.1
  93.9 1.9 %collective-permute-start.14 = (bf16[6,64,384]{2,1,0:T(8,128)(2,1)S(1)}, bf16[6,64,384]{2,1,0:T(8,128)(2,1)S(1)}, u32[]{:S(2)}, u32[]{:S(2)}) collective-permute-start(bf16[6,64,384]{2,1,0:T(8,128)(2,1)S(1)} %get-tuple-element.18), channel_id=1, source_target_pairs={{0,32},{16,48},{32,64},{48,80},{64,96},{80,112},{96,0},{112,16},{1... | collective-permute-start | bytes 884744 | tf_op jit(solution)/shard_map/ppermute | solution.py:74
  95.8 4.3 %collective-permute-start.15 = (bf16[6,64,384]{2,1,0:T(8,128)(2,1)S(1)}, bf16[6,64,384]{2,1,0:T(8,128)(2,1)S(1)}, u32[]{:S(2)}, u32[]{:S(2)}) collective-permute-start(bf16[6,64,384]{2,1,0:T(8,128)(2,1)S(1)} %get-tuple-element.19), channel_id=1, source_target_pairs={{0,96},{16,112},{32,0},{48,16},{64,32},{80,48},{96,64},{112,80},{1... | collective-permute-start | bytes 884744 | tf_op jit(solution)/shard_map/ppermute | solution.py:74
  100.1 0.9 fusion.18
  101.0 7.8 %collective-permute-done.14 = bf16[6,64,384]{2,1,0:T(8,128)(2,1)S(1)} collective-permute-done((bf16[6,64,384]{2,1,0:T(8,128)(2,1)S(1)}, bf16[6,64,384]{2,1,0:T(8,128)(2,1)S(1)}, u32[]{:S(2)}, u32[]{:S(2)}) %collective-permute-start.14) | collective-permute-done | bytes 294944 | tf_op jit(solution)/shard_map/ppermute | solution.py:74
  108.8 4.2 %collective-permute-done.15 = bf16[6,64,384]{2,1,0:T(8,128)(2,1)S(1)} collective-permute-done((bf16[6,64,384]{2,1,0:T(8,128)(2,1)S(1)}, bf16[6,64,384]{2,1,0:T(8,128)(2,1)S(1)}, u32[]{:S(2)}, u32[]{:S(2)}) %collective-permute-start.15) | collective-permute-done | bytes 294944 | tf_op jit(solution)/shard_map/ppermute | solution.py:74
  113.0 0.2 fusion.11
  113.2 14.0 %collective-permute-start.16 = (bf16[2,64,384]{2,1,0:T(8,128)(2,1)S(1)}, bf16[2,64,384]{2,1,0:T(8,128)(2,1)S(1)}, u32[]{:S(2)}, u32[]{:S(2)}) collective-permute-start(bf16[2,64,384]{2,1,0:T(8,128)(2,1)S(1)} %get-tuple-element.16), channel_id=1, source_target_pairs={{0,128},{128,256},{256,0},{384,512},{512,640},{640,384},{1,129},{1... | collective-permute-start | bytes 294920 | tf_op jit(solution)/shard_map/ppermute | solution.py:147
  127.2 1.9 %collective-permute-start.17 = (bf16[2,64,384]{2,1,0:T(8,128)(2,1)S(1)}, bf16[2,64,384]{2,1,0:T(8,128)(2,1)S(1)}, u32[]{:S(2)}, u32[]{:S(2)}) collective-permute-start(bf16[2,64,384]{2,1,0:T(8,128)(2,1)S(1)} %get-tuple-element.17), channel_id=1, source_target_pairs={{0,256},{128,0},{256,128},{384,640},{512,384},{640,512},{1,257},{1... | collective-permute-start | bytes 294920 | tf_op jit(solution)/shard_map/ppermute | solution.py:147
  129.2 0.0 collective-permute-done.7
  129.2 0.0 collective-permute-done.8
  129.2 0.0 collective-permute-done.9
  129.2 0.1 fusion.6
  129.3 9.9 %collective-permute-start.10 = (bf16[48,3072]{1,0:T(8,128)(2,1)S(1)}, bf16[48,3072]{1,0:T(8,128)(2,1)S(1)}, u32[]{:S(2)}, u32[]{:S(2)}) collective-permute-start(bf16[48,3072]{1,0:T(8,128)(2,1)S(1)} %fusion.6), channel_id=1, source_target_pairs={{0,2},{2,0},{1,3},{3,1},{4,6},{6,4},{5,7},{7,5},{8,10},{10,8},{9,1... | collective-permute-start | bytes 884744 | tf_op jit(solution)/shard_map/ppermute | solution.py:74
  139.2 0.0 collective-permute-done.16
  139.2 0.0 collective-permute-done.17
  139.3 6.5 %collective-permute-start.18 = (bf16[64,384]{1,0:T(8,128)(2,1)S(1)}, bf16[64,384]{1,0:T(8,128)(2,1)S(1)}, u32[]{:S(2)}, u32[]{:S(2)}) collective-permute-start(bf16[64,384]{1,0:T(8,128)(2,1)S(1)} %fusion.20), channel_id=1, source_target_pairs={{0,384},{128,512},{256,640},{384,0},{512,128},{640,256},{1,385},{1... | collective-permute-start | bytes 147464 | tf_op jit(solution)/shard_map/ppermute | solution.py:74
  145.8 0.9 collective-permute-done.10
  146.7 0.9 fusion.10
  147.6 16.0 %collective-permute-done.18 = bf16[64,384]{1,0:T(8,128)(2,1)S(1)} collective-permute-done((bf16[64,384]{1,0:T(8,128)(2,1)S(1)}, bf16[64,384]{1,0:T(8,128)(2,1)S(1)}, u32[]{:S(2)}, u32[]{:S(2)}) %collective-permute-start.18) | collective-permute-done | bytes 49184 | tf_op jit(solution)/shard_map/ppermute | solution.py:74
  163.6 0.7 bitcast_add_fusion.2
  (9 shorter events, 0.2 us)
Async XLA Ops:
  0.6 48.7 %copy-start = (bf16[3072,384]{1,0:T(8,128)(2,1)S(1)}, bf16[3072,384]{1,0:T(8,128)(2,1)}, u32[]{:S(2)}) copy-start(bf16[3072,384]{1,0:T(8,128)(2,1)} %param.5) | copy-start | bytes 7077892
  0.6 22.5 %collective-permute-start = (bf16[48,3072]{1,0:T(8,128)(2,1)}, bf16[48,3072]{1,0:T(8,128)(2,1)S(1)}, u32[]{:S(2)}, u32[]{:S(2)}) collective-permute-start(bf16[48,3072]{1,0:T(8,128)(2,1)} %param.4), channel_id=1, source_target_pairs={{0,2},{2,0},{1,3},{3,1},{4,6},{6,4},{5,7},{7,5},{8,10},{10,8},{9,1... | collective-permute-start | bytes 884744 | tf_op jit(solution)/shard_map/ppermute | solution.py:74
  15.6 19.1 %collective-permute-start.1 = (bf16[48,3072]{1,0:T(8,128)(2,1)}, bf16[48,3072]{1,0:T(8,128)(2,1)S(1)}, u32[]{:S(2)}, u32[]{:S(2)}) collective-permute-start(bf16[48,3072]{1,0:T(8,128)(2,1)} %param.4), channel_id=1, source_target_pairs={{0,4},{4,8},{8,12},{12,0},{1,5},{5,9},{9,13},{13,1},{2,6},{6,10},{... | collective-permute-start | bytes 884744 | tf_op jit(solution)/shard_map/ppermute | solution.py:74
  18.8 30.4 %collective-permute-start.4 = (bf16[48,3072]{1,0:T(8,128)(2,1)}, bf16[48,3072]{1,0:T(8,128)(2,1)S(1)}, u32[]{:S(2)}, u32[]{:S(2)}) collective-permute-start(bf16[48,3072]{1,0:T(8,128)(2,1)} %param.4), channel_id=1, source_target_pairs={{0,12},{4,0},{8,4},{12,8},{1,13},{5,1},{9,5},{13,9},{2,14},{6,2},{... | collective-permute-start | bytes 884744 | tf_op jit(solution)/shard_map/ppermute | solution.py:74
  24.2 25.0 %collective-permute-start.3 = (bf16[96,3072]{1,0:T(8,128)(2,1)S(1)}, bf16[96,3072]{1,0:T(8,128)(2,1)S(1)}, u32[]{:S(2)}, u32[]{:S(2)}) collective-permute-start(bf16[96,3072]{1,0:T(8,128)(2,1)S(1)} %pad_maximum_fusion), channel_id=1, source_target_pairs={{0,8},{4,12},{8,0},{12,4},{1,9},{5,13},{9,1},{13,5},{2,10},{6,14},... | collective-permute-start | bytes 1769480 | tf_op jit(solution)/shard_map/ppermute | solution.py:74
  28.2 20.9 %collective-permute-start.2 = (bf16[48,3072]{1,0:T(8,128)(2,1)S(1)}, bf16[48,3072]{1,0:T(8,128)(2,1)S(1)}, u32[]{:S(2)}, u32[]{:S(2)}) collective-permute-start(bf16[48,3072]{1,0:T(8,128)(2,1)S(1)} %collective-permute-done), channel_id=1, source_target_pairs={{0,4},{4,8},{8,12},{12,0},{1,5},{5,9},{9,13},{13,1},{2,6},{6,10},{... | collective-permute-start | bytes 884744 | tf_op jit(solution)/shard_map/ppermute | solution.py:74
  30.5 18.8 %collective-permute-start.5 = (bf16[48,3072]{1,0:T(8,128)(2,1)S(1)}, bf16[48,3072]{1,0:T(8,128)(2,1)S(1)}, u32[]{:S(2)}, u32[]{:S(2)}) collective-permute-start(bf16[48,3072]{1,0:T(8,128)(2,1)S(1)} %collective-permute-done), channel_id=1, source_target_pairs={{0,12},{4,0},{8,4},{12,8},{1,13},{5,1},{9,5},{13,9},{2,14},{6,2},{... | collective-permute-start | bytes 884744 | tf_op jit(solution)/shard_map/ppermute | solution.py:74
  49.3 1.4 copy-start.1
  49.3 5.4 %copy-start.4 = (f32[128]{0:T(128)S(1)}, f32[128]{0:T(128)}, u32[]{:S(2)}) copy-start(f32[128]{0:T(128)} %param.7) | copy-start | bytes 1540
  50.8 4.0 %collective-permute-start.6 = (f32[384,384]{1,0:T(8,128)S(1)}, f32[384,384]{1,0:T(8,128)S(1)}, u32[]{:S(2)}, u32[]{:S(2)}) collective-permute-start(f32[384,384]{1,0:T(8,128)S(1)} %fusion.21.mine), channel_id=1, source_target_pairs={{0,1},{1,0},{2,3},{3,2},{4,5},{5,4},{6,7},{7,6},{8,9},{9,8},{10,11... | collective-permute-start | bytes 1769480 | tf_op jit(solution)/shard_map/ppermute | solution.py:74
  54.8 1.7 %copy-start.2 = (bf16[384,3072]{1,0:T(8,128)(2,1)S(1)}, bf16[384,3072]{1,0:T(8,128)(2,1)}, u32[]{:S(2)}) copy-start(bf16[384,3072]{1,0:T(8,128)(2,1)} %copy-done.1) | copy-start | bytes 7077892
  56.4 1.0 copy-start.3
  60.5 33.2 %collective-permute-start.11 = (bf16[2,6,64,384]{3,2,1,0:T(8,128)(2,1)S(1)}, bf16[2,6,64,384]{3,2,1,0:T(8,128)(2,1)S(1)}, u32[]{:S(2)}, u32[]{:S(2)}) collective-permute-start(bf16[2,6,64,384]{3,2,1,0:T(8,128)(2,1)S(1)} %get-tuple-element.11), channel_id=1, source_target_pairs={{0,16},{16,32},{32,48},{48,64},{64,80},{80,96},{96,112},{112,0},{1... | collective-permute-start | bytes 1769480 | tf_op jit(solution)/shard_map/ppermute | solution.py:74
  63.7 30.0 %collective-permute-start.12 = (bf16[2,6,64,384]{3,2,1,0:T(8,128)(2,1)S(1)}, bf16[2,6,64,384]{3,2,1,0:T(8,128)(2,1)S(1)}, u32[]{:S(2)}, u32[]{:S(2)}) collective-permute-start(bf16[2,6,64,384]{3,2,1,0:T(8,128)(2,1)S(1)} %get-tuple-element.12), channel_id=1, source_target_pairs={{0,112},{16,0},{32,16},{48,32},{64,48},{80,64},{96,80},{112,96},{1... | collective-permute-start | bytes 1769480 | tf_op jit(solution)/shard_map/ppermute | solution.py:74
  65.8 24.6 %collective-permute-start.13 = (bf16[6,64,384]{2,1,0:T(8,128)(2,1)S(1)}, bf16[6,64,384]{2,1,0:T(8,128)(2,1)S(1)}, u32[]{:S(2)}, u32[]{:S(2)}) collective-permute-start(bf16[6,64,384]{2,1,0:T(8,128)(2,1)S(1)} %bitcast.43), channel_id=1, source_target_pairs={{0,32},{1,97},{16,48},{17,113},{32,64},{33,1},{48,80},{49,17},{64,... | collective-permute-start | bytes 884744 | tf_op jit(solution)/shard_map/ppermute | solution.py:117
  70.3 58.8 %collective-permute-start.7 = (bf16[96,3072]{1,0:T(8,128)(2,1)S(1)}, bf16[96,3072]{1,0:T(8,128)(2,1)S(1)}, u32[]{:S(2)}, u32[]{:S(2)}) collective-permute-start(bf16[96,3072]{1,0:T(8,128)(2,1)S(1)} %convolution_convert_fusion.2), channel_id=1, source_target_pairs={{0,8},{4,12},{8,0},{12,4},{1,9},{5,13},{9,1},{13,5},{2,10},{6,14},... | collective-permute-start | bytes 1769480 | tf_op jit(solution)/shard_map/ppermute | solution.py:74
  75.3 53.9 %collective-permute-start.8 = (bf16[96,3072]{1,0:T(8,128)(2,1)S(1)}, bf16[96,3072]{1,0:T(8,128)(2,1)S(1)}, u32[]{:S(2)}, u32[]{:S(2)}) collective-permute-start(bf16[96,3072]{1,0:T(8,128)(2,1)S(1)} %convolution_convert_fusion.1), channel_id=1, source_target_pairs={{0,12},{4,0},{8,4},{12,8},{1,13},{5,1},{9,5},{13,9},{2,14},{6,2},{... | collective-permute-start | bytes 1769480 | tf_op jit(solution)/shard_map/ppermute | solution.py:74
  90.4 38.8 %collective-permute-start.9 = (bf16[96,3072]{1,0:T(8,128)(2,1)S(1)}, bf16[96,3072]{1,0:T(8,128)(2,1)S(1)}, u32[]{:S(2)}, u32[]{:S(2)}) collective-permute-start(bf16[96,3072]{1,0:T(8,128)(2,1)S(1)} %convolution_convert_fusion), channel_id=1, source_target_pairs={{0,4},{4,8},{8,12},{12,0},{1,5},{5,9},{9,13},{13,1},{2,6},{6,10},{... | collective-permute-start | bytes 1769480 | tf_op jit(solution)/shard_map/ppermute | solution.py:74
  93.9 14.9 %collective-permute-start.14 = (bf16[6,64,384]{2,1,0:T(8,128)(2,1)S(1)}, bf16[6,64,384]{2,1,0:T(8,128)(2,1)S(1)}, u32[]{:S(2)}, u32[]{:S(2)}) collective-permute-start(bf16[6,64,384]{2,1,0:T(8,128)(2,1)S(1)} %get-tuple-element.18), channel_id=1, source_target_pairs={{0,32},{16,48},{32,64},{48,80},{64,96},{80,112},{96,0},{112,16},{1... | collective-permute-start | bytes 884744 | tf_op jit(solution)/shard_map/ppermute | solution.py:74
  95.8 17.1 %collective-permute-start.15 = (bf16[6,64,384]{2,1,0:T(8,128)(2,1)S(1)}, bf16[6,64,384]{2,1,0:T(8,128)(2,1)S(1)}, u32[]{:S(2)}, u32[]{:S(2)}) collective-permute-start(bf16[6,64,384]{2,1,0:T(8,128)(2,1)S(1)} %get-tuple-element.19), channel_id=1, source_target_pairs={{0,96},{16,112},{32,0},{48,16},{64,32},{80,48},{96,64},{112,80},{1... | collective-permute-start | bytes 884744 | tf_op jit(solution)/shard_map/ppermute | solution.py:74
  113.2 26.0 %collective-permute-start.16 = (bf16[2,64,384]{2,1,0:T(8,128)(2,1)S(1)}, bf16[2,64,384]{2,1,0:T(8,128)(2,1)S(1)}, u32[]{:S(2)}, u32[]{:S(2)}) collective-permute-start(bf16[2,64,384]{2,1,0:T(8,128)(2,1)S(1)} %get-tuple-element.16), channel_id=1, source_target_pairs={{0,128},{128,256},{256,0},{384,512},{512,640},{640,384},{1,129},{1... | collective-permute-start | bytes 294920 | tf_op jit(solution)/shard_map/ppermute | solution.py:147
  127.2 12.0 %collective-permute-start.17 = (bf16[2,64,384]{2,1,0:T(8,128)(2,1)S(1)}, bf16[2,64,384]{2,1,0:T(8,128)(2,1)S(1)}, u32[]{:S(2)}, u32[]{:S(2)}) collective-permute-start(bf16[2,64,384]{2,1,0:T(8,128)(2,1)S(1)} %get-tuple-element.17), channel_id=1, source_target_pairs={{0,256},{128,0},{256,128},{384,640},{512,384},{640,512},{1,257},{1... | collective-permute-start | bytes 294920 | tf_op jit(solution)/shard_map/ppermute | solution.py:147
  129.3 17.4 %collective-permute-start.10 = (bf16[48,3072]{1,0:T(8,128)(2,1)S(1)}, bf16[48,3072]{1,0:T(8,128)(2,1)S(1)}, u32[]{:S(2)}, u32[]{:S(2)}) collective-permute-start(bf16[48,3072]{1,0:T(8,128)(2,1)S(1)} %fusion.6), channel_id=1, source_target_pairs={{0,2},{2,0},{1,3},{3,1},{4,6},{6,4},{5,7},{7,5},{8,10},{10,8},{9,1... | collective-permute-start | bytes 884744 | tf_op jit(solution)/shard_map/ppermute | solution.py:74
  139.3 24.3 %collective-permute-start.18 = (bf16[64,384]{1,0:T(8,128)(2,1)S(1)}, bf16[64,384]{1,0:T(8,128)(2,1)S(1)}, u32[]{:S(2)}, u32[]{:S(2)}) collective-permute-start(bf16[64,384]{1,0:T(8,128)(2,1)S(1)} %fusion.20), channel_id=1, source_target_pairs={{0,384},{128,512},{256,640},{384,0},{512,128},{640,256},{1,385},{1... | collective-permute-start | bytes 147464 | tf_op jit(solution)/shard_map/ppermute | solution.py:74

commit v4 on v3

--- a/solution.py
+++ b/solution.py
@@ -17,31 +17,35 @@
     return jnp.mean(value, axis=-1, keepdims=True)
 
 
-def rows_kernel(sizes, factor, where, mine, theirs, cot, gain, tokens, rows_out, *rest):
+def rows_kernel(sizes, factor, where, mine, theirs, cot, cot_far, gain, tokens, rows_out, *rest):
     nx, nh, ny, nz = sizes
-    outs, term = rest[:-1], rest[-1]
-    x, zh, y = where[0], where[1], where[2]
-    count = tokens.shape[0] // (nx * nh)
+    outs, (held, term, sem) = rest[:-3], rest[-3:]
+    x, y = where[0], where[1]
+    copy = pltpu.make_async_copy(tokens, held, sem)
+    copy.start()
+    count = cot.shape[1]
     heads = mine.shape[1]
     hd = gain.shape[1]
     for kx in range(nx):
+        block = lax.rem(x - kx + nx, nx)
         for kh in range(nh):
-            block = lax.rem(x - kx + nx, nx) * nh + lax.rem(zh + kh, nh)
             span = pl.ds((kx * nh + kh) * count, count)
+            side = (cot, cot_far)[kh]
             for h in range(0, heads, hd):
                 pre = mine[span, h : h + hd] + theirs[span, h : h + hd]
                 centred = pre - mean(pre)
                 inverse = lax.rsqrt(mean(centred * centred) + 1e-06)
                 unit = centred * inverse
-                scaled = cot[block, :, h : h + hd].astype(F32) * gain[...]
+                scaled = side[block, :, h : h + hd].astype(F32) * gain[...]
                 result = inverse * (scaled - mean(scaled) - unit * mean(scaled * unit))
                 rows_out[span, h : h + hd] = result.astype(BF16)
     rows = rows_out[...]
-    part = tokens.shape[1] // nz
+    part = held.shape[1] // nz
     blk = part // ny
+    copy.wait()
     for z in range(nz):
         term[...] = factor * lax.dot_general(
-            tokens[:, z * part : (z + 1) * part],
+            held[:, z * part : (z + 1) * part],
             rows,
             (((0,), (0,)), ((), ())),
             preferred_element_type=F32,
@@ -52,7 +56,7 @@
                 out[i, z] = term[pl.ds(at, blk), :].astype(BF16)
 
 
-def rows_and_chunks(sizes, factor, where, mine, theirs, cot, gain, tokens):
+def rows_and_chunks(sizes, factor, where, mine, theirs, cot, cot_far, gain, tokens):
     nx, nh, ny, nz = sizes
     heads = mine.shape[1]
     part = tokens.shape[1] // nz
@@ -61,12 +65,18 @@
     return pl.pallas_call(
         functools.partial(rows_kernel, sizes, factor),
         out_shape=[jax.ShapeDtypeStruct(mine.shape, BF16)] + chunks,
-        in_specs=[pl.BlockSpec(memory_space=pltpu.SMEM)] + [vmem] * 5,
+        in_specs=[pl.BlockSpec(memory_space=pltpu.SMEM)]
+        + [vmem] * 5
+        + [pl.BlockSpec(memory_space=pl.ANY)],
         out_specs=[vmem] * (len(ORDER) + 1),
-        scratch_shapes=[pltpu.VMEM((part, heads), F32)],
-        compiler_params=pltpu.CompilerParams(vmem_limit_bytes=8 * 2**20),
+        scratch_shapes=[
+            pltpu.VMEM(tokens.shape, BF16),
+            pltpu.VMEM((part, heads), F32),
+            pltpu.SemaphoreType.DMA,
+        ],
+        compiler_params=pltpu.CompilerParams(vmem_limit_bytes=12 * 2**20),
         name="rows_and_chunks",
-    )(where, mine, theirs, cot, gain, tokens)
+    )(where, mine, theirs, cot, cot_far, gain, tokens)
 
 
 def shift(value, axis, by):
@@ -85,14 +95,21 @@
     nx, ny, nz, nh = (lax.axis_size(a) for a in ("x", "y", "zl", "zh"))
     count, width = normed.shape
     heads = weight.shape[1]
-    where = jnp.stack([lax.axis_index(a) for a in ("x", "zh", "y")]).astype(jnp.int32)
+    where = jnp.stack([lax.axis_index(a) for a in ("x", "y")]).astype(jnp.int32)
+    zh = lax.axis_index("zh")
 
-    peer = shift(normed, "zh", 1)
-    own1, own3 = shift(normed, "x", 1), shift(normed, "x", -1)
-    both = jnp.concatenate([normed, peer], axis=0)
-    both2 = shift(both, "x", 2)
-    peer1, peer3 = shift(peer, "x", 1), shift(peer, "x", -1)
-    tokens = jnp.concatenate([both, own1, peer1, both2, own3, peer3], axis=0)
+    def mirror(value):
+        ends = [(i, nz * nh - 1 - i) for i in range(nz * nh)]
+        return lax.ppermute(value, ("zl", "zh"), ends)
+
+    peer = mirror(normed)
+    own = [normed] + [shift(normed, "x", k) for k in (1, 2, 3)]
+    cot = cotangent.reshape(nx, nh, count, heads)
+    cot_far = lax.dynamic_index_in_dim(cot, 1 - zh, 1, False)
+    cot_far = lax.ppermute(cot_far, "zl", [(i, nz - 1 - i) for i in range(nz)])
+    cot = lax.dynamic_index_in_dim(cot, zh, 1, False)
+    other = [peer] + [shift(peer, "x", k) for k in (1, 2, 3)]
+    tokens = jnp.concatenate([p for pair in zip(own, other) for p in pair], axis=0)
 
     mine = jnp.dot(tokens, weight, preferred_element_type=F32)
     theirs = shift(mine, "c", 1)
@@ -103,7 +120,8 @@
         where,
         mine,
         theirs,
-        cotangent.reshape(nx * nh, count, heads),
+        cot,
+        cot_far,
         head_gain.reshape(1, -1),
         tokens,
     )
@@ -129,7 +147,7 @@
         for k in range(nx)
     ]
     terms = [back[0]] + [shift(back[k].astype(BF16), "x", -k) for k in (2, 1, 3)]
-    far = shift(add(*[t[count:] for t in terms]).astype(BF16), "zh", 1)
+    far = mirror(add(*[t[count:] for t in terms]).astype(BF16))
     input_grad = add(*[t[:count] for t in terms], far).astype(BF16)
 
     over_y = add(own[0], got_up[1], got_down[1], got2, got6)

time: 165 us -> 168 us (1.018)
  the two profiles are of different devices: /device:TPU:17 before, /device:TPU:6 now
where the time goes in v4:
time: 168 us; the launch traced here: 164 us
  starting transfers between devices  77.9 us (46%)
  waiting for transfers between devices  69.1 us (41%)
  Pallas kernels  5.72 us (3%)
  matrix products  4.82 us (3%)
  local copies, waits for them, and re-layouts  3.58 us (2%)
  other arithmetic  2.2 us (1%)
    ppermute x15, starting transfers between devices, shift(): lax.ppermute(value, axis, [(i, (i + by) % size) for i in range(size)])  48.6 us
    ppermute x2, waiting for transfers between devices, mirror(): return lax.ppermute(value, ('zl', 'zh'), ends)  28.8 us
    ppermute x15, waiting for transfers between devices, shift(): lax.ppermute(value, axis, [(i, (i + by) % size) for i in range(size)])  24.8 us
    ppermute x2, starting transfers between devices, mirror(): return lax.ppermute(value, ('zl', 'zh'), ends)  17.6 us
    ppermute x1, waiting for transfers between devices, body(): cot_far = lax.ppermute(cot_far, 'zl', [(i, nz - 1 - i) for i in range(nz)])  11 us
    ppermute x2, starting transfers between devices, body(): kept = add(kept, lax.ppermute(of_third(k).astype(BF16), 'zl', hop))  6.74 us
    pallas_call x1, Pallas kernels, rows_and_chunks(): pl.pallas_call(functools.partial(rows_kernel, sizes, factor), out_shape=[...  5.72 us
    ppermute x1, waiting for transfers between devices, body(): got4 = lax.ppermute(across[0], ('y', 'c'), turn).astype(F32)  3.8 us
  transfers between devices with their start and end apart: 21, of which 10 were waited for; matrix products, arithmetic and copies ran while one was open for 4% of the time, Pallas kernels for 0%

profile of v4, /device:TPU:6, one launch (start us, length us, event | category | flops | bytes accessed | tf_op | source)
XLA Modules:
  0.0 164.5 jit_solution(18262683923606221158)
XLA Ops:
  0.6 0.0 copy-start
  0.6 14.7 %collective-permute-start = (bf16[48,3072]{1,0:T(8,128)(2,1)}, bf16[48,3072]{1,0:T(8,128)(2,1)S(1)}, u32[]{:S(2)}, u32[]{:S(2)}) collective-permute-start(bf16[48,3072]{1,0:T(8,128)(2,1)} %param.4), channel_id=1, source_target_pairs={{0,642},{2,640},{128,514},{130,512},{256,386},{258,384},{384,258},... | collective-permute-start | bytes 884744 | tf_op jit(solution)/shard_map/ppermute | solution.py:103
  15.4 2.4 %collective-permute-start.1 = (bf16[48,3072]{1,0:T(8,128)(2,1)}, bf16[48,3072]{1,0:T(8,128)(2,1)S(1)}, u32[]{:S(2)}, u32[]{:S(2)}) collective-permute-start(bf16[48,3072]{1,0:T(8,128)(2,1)} %param.4), channel_id=1, source_target_pairs={{0,4},{4,8},{8,12},{12,0},{1,5},{5,9},{9,13},{13,1},{2,6},{6,10},{... | collective-permute-start | bytes 884744 | tf_op jit(solution)/shard_map/ppermute | solution.py:84
  17.8 4.3 %collective-permute-start.3 = (bf16[48,3072]{1,0:T(8,128)(2,1)}, bf16[48,3072]{1,0:T(8,128)(2,1)S(1)}, u32[]{:S(2)}, u32[]{:S(2)}) collective-permute-start(bf16[48,3072]{1,0:T(8,128)(2,1)} %param.4), channel_id=1, source_target_pairs={{0,8},{4,12},{8,0},{12,4},{1,9},{5,13},{9,1},{13,5},{2,10},{6,14},... | collective-permute-start | bytes 884744 | tf_op jit(solution)/shard_map/ppermute | solution.py:84
  22.1 1.9 %collective-permute-start.5 = (bf16[48,3072]{1,0:T(8,128)(2,1)}, bf16[48,3072]{1,0:T(8,128)(2,1)S(1)}, u32[]{:S(2)}, u32[]{:S(2)}) collective-permute-start(bf16[48,3072]{1,0:T(8,128)(2,1)} %param.4), channel_id=1, source_target_pairs={{0,12},{4,0},{8,4},{12,8},{1,13},{5,1},{9,5},{13,9},{2,14},{6,2},{... | collective-permute-start | bytes 884744 | tf_op jit(solution)/shard_map/ppermute | solution.py:84
  24.0 1.0 constant_dynamic-update-slice_fusion.7
  25.0 10.2 %collective-permute-done = bf16[48,3072]{1,0:T(8,128)(2,1)S(1)} collective-permute-done((bf16[48,3072]{1,0:T(8,128)(2,1)}, bf16[48,3072]{1,0:T(8,128)(2,1)S(1)}, u32[]{:S(2)}, u32[]{:S(2)}) %collective-permute-start) | collective-permute-done | bytes 294944 | tf_op jit(solution)/shard_map/ppermute | solution.py:103
  35.2 2.4 %collective-permute-start.2 = (bf16[48,3072]{1,0:T(8,128)(2,1)S(1)}, bf16[48,3072]{1,0:T(8,128)(2,1)S(1)}, u32[]{:S(2)}, u32[]{:S(2)}) collective-permute-start(bf16[48,3072]{1,0:T(8,128)(2,1)S(1)} %collective-permute-done), channel_id=1, source_target_pairs={{0,4},{4,8},{8,12},{12,0},{1,5},{5,9},{9,13},{13,1},{2,6},{6,10},{... | collective-permute-start | bytes 884744 | tf_op jit(solution)/shard_map/ppermute | solution.py:84
  37.6 4.3 %collective-permute-start.4 = (bf16[48,3072]{1,0:T(8,128)(2,1)S(1)}, bf16[48,3072]{1,0:T(8,128)(2,1)S(1)}, u32[]{:S(2)}, u32[]{:S(2)}) collective-permute-start(bf16[48,3072]{1,0:T(8,128)(2,1)S(1)} %collective-permute-done), channel_id=1, source_target_pairs={{0,8},{4,12},{8,0},{12,4},{1,9},{5,13},{9,1},{13,5},{2,10},{6,14},... | collective-permute-start | bytes 884744 | tf_op jit(solution)/shard_map/ppermute | solution.py:84
  41.9 0.0 collective-permute-done.1
  41.9 1.9 %collective-permute-start.6 = (bf16[48,3072]{1,0:T(8,128)(2,1)S(1)}, bf16[48,3072]{1,0:T(8,128)(2,1)S(1)}, u32[]{:S(2)}, u32[]{:S(2)}) collective-permute-start(bf16[48,3072]{1,0:T(8,128)(2,1)S(1)} %collective-permute-done), channel_id=1, source_target_pairs={{0,12},{4,0},{8,4},{12,8},{1,13},{5,1},{9,5},{13,9},{2,14},{6,2},{... | collective-permute-start | bytes 884744 | tf_op jit(solution)/shard_map/ppermute | solution.py:84
  43.9 3.0 %collective-permute-done.2 = bf16[48,3072]{1,0:T(8,128)(2,1)S(1)} collective-permute-done((bf16[48,3072]{1,0:T(8,128)(2,1)S(1)}, bf16[48,3072]{1,0:T(8,128)(2,1)S(1)}, u32[]{:S(2)}, u32[]{:S(2)}) %collective-permute-start.2) | collective-permute-done | bytes 294944 | tf_op jit(solution)/shard_map/ppermute | solution.py:84
  47.0 0.0 collective-permute-done.3
  47.0 3.9 %collective-permute-done.4 = bf16[48,3072]{1,0:T(8,128)(2,1)S(1)} collective-permute-done((bf16[48,3072]{1,0:T(8,128)(2,1)S(1)}, bf16[48,3072]{1,0:T(8,128)(2,1)S(1)}, u32[]{:S(2)}, u32[]{:S(2)}) %collective-permute-start.4) | collective-permute-done | bytes 294944 | tf_op jit(solution)/shard_map/ppermute | solution.py:84
  50.9 0.0 collective-permute-done.5
  50.9 5.0 %collective-permute-done.6 = bf16[48,3072]{1,0:T(8,128)(2,1)S(1)} collective-permute-done((bf16[48,3072]{1,0:T(8,128)(2,1)S(1)}, bf16[48,3072]{1,0:T(8,128)(2,1)S(1)}, u32[]{:S(2)}, u32[]{:S(2)}) %collective-permute-start.6) | collective-permute-done | bytes 294944 | tf_op jit(solution)/shard_map/ppermute | solution.py:84
  56.0 0.0 copy-done
  56.0 0.0 copy-start.1
  56.0 0.0 copy-start.4
  56.0 0.0 copy-start.3
  56.0 1.4 fusion.21.mine
  57.4 0.0 copy-done.1
  57.4 1.9 %collective-permute-start.7 = (f32[384,384]{1,0:T(8,128)S(1)}, f32[384,384]{1,0:T(8,128)}, u32[]{:S(2)}, u32[]{:S(2)}) collective-permute-start(f32[384,384]{1,0:T(8,128)S(1)} %fusion.21.mine), channel_id=1, source_target_pairs={{0,1},{1,0},{2,3},{3,2},{4,5},{5,4},{6,7},{7,6},{8,9},{9,8},{10,11... | collective-permute-start | bytes 1769480 | tf_op jit(solution)/shard_map/ppermute | solution.py:84
  59.4 0.0 copy-done.4
  59.4 0.7 dynamic-slice_bitcast_fusion
  60.1 1.9 %collective-permute-start.8 = (bf16[4,48,384]{2,1,0:T(8,128)(2,1)}, bf16[4,48,384]{2,1,0:T(8,128)(2,1)S(1)}, u32[]{:S(2)}, u32[]{:S(2)}) collective-permute-start(bf16[4,48,384]{2,1,0:T(8,128)(2,1)} %get-tuple-element.20), channel_id=1, source_target_pairs={{0,640},{128,512},{256,384},{384,256},{512,128},{640,0},{1,641},{1... | collective-permute-start | bytes 442376 | tf_op jit(solution)/shard_map/ppermute | solution.py:109
  62.1 0.1 pad_add_fusion.where
  62.2 11.0 %collective-permute-done.8.cot_far = bf16[4,48,384]{2,1,0:T(8,128)(2,1)S(1)} collective-permute-done((bf16[4,48,384]{2,1,0:T(8,128)(2,1)}, bf16[4,48,384]{2,1,0:T(8,128)(2,1)S(1)}, u32[]{:S(2)}, u32[]{:S(2)}) %collective-permute-start.8) | collective-permute-done | bytes 147488 | tf_op jit(solution)/shard_map/ppermute | solution.py:109
  73.2 0.0 collective-permute-done.7.theirs
  73.3 1.7 %copy-done.2 = bf16[384,3072]{1,0:T(8,128)(2,1)S(1)} copy-done((bf16[384,3072]{1,0:T(8,128)(2,1)S(1)}, bf16[384,3072]{1,0:T(8,128)(2,1)}, u32[]{:S(2)}) %copy-start.2) | copy-done | bytes 2359320
  74.9 5.7 %rows_and_chunks.1 = (bf16[384,384]{1,0:T(8,128)(2,1)S(1)}, bf16[2,6,64,384]{3,2,1,0:T(8,128)(2,1)S(1)}, bf16[2,6,64,384]{3,2,1,0:T(8,128)(2,1)S(1)}, bf16[1,6,6...) custom-call(s32[2]{0:T(128)S(1)} %pad_add_fusion.where, ...), custom_call_target="tpu_custom_call" | custom-call | tf_op jit(solution)/shard_map/rows_and_chunks/pallas_call | solution.py:65
  80.6 3.5 %collective-permute-start.13 = (bf16[2,6,64,384]{3,2,1,0:T(8,128)(2,1)S(1)}, bf16[2,6,64,384]{3,2,1,0:T(8,128)(2,1)S(1)}, u32[]{:S(2)}, u32[]{:S(2)}) collective-permute-start(bf16[2,6,64,384]{3,2,1,0:T(8,128)(2,1)S(1)} %get-tuple-element.11), channel_id=1, source_target_pairs={{0,16},{16,32},{32,48},{48,64},{64,80},{80,96},{96,112},{112,0},{1... | collective-permute-start | bytes 1769480 | tf_op jit(solution)/shard_map/ppermute | solution.py:84
  84.1 3.8 %collective-permute-start.14 = (bf16[2,6,64,384]{3,2,1,0:T(8,128)(2,1)S(1)}, bf16[2,6,64,384]{3,2,1,0:T(8,128)(2,1)S(1)}, u32[]{:S(2)}, u32[]{:S(2)}) collective-permute-start(bf16[2,6,64,384]{3,2,1,0:T(8,128)(2,1)S(1)} %get-tuple-element.12), channel_id=1, source_target_pairs={{0,112},{16,0},{32,16},{48,32},{64,48},{80,64},{96,80},{112,96},{1... | collective-permute-start | bytes 1769480 | tf_op jit(solution)/shard_map/ppermute | solution.py:84
  88.0 3.0 %collective-permute-start.15 = (bf16[6,64,384]{2,1,0:T(8,128)(2,1)S(1)}, bf16[6,64,384]{2,1,0:T(8,128)(2,1)S(1)}, u32[]{:S(2)}, u32[]{:S(2)}) collective-permute-start(bf16[6,64,384]{2,1,0:T(8,128)(2,1)S(1)} %bitcast.49), channel_id=1, source_target_pairs={{0,32},{1,97},{16,48},{17,113},{32,64},{33,1},{48,80},{49,17},{64,... | collective-permute-start | bytes 884744 | tf_op jit(solution)/shard_map/ppermute | solution.py:135
  91.0 0.9 convolution_convert_fusion.1
  91.9 2.9 %collective-permute-start.10 = (bf16[96,3072]{1,0:T(8,128)(2,1)S(1)}, bf16[96,3072]{1,0:T(8,128)(2,1)S(1)}, u32[]{:S(2)}, u32[]{:S(2)}) collective-permute-start(bf16[96,3072]{1,0:T(8,128)(2,1)S(1)} %convolution_convert_fusion.1), channel_id=1, source_target_pairs={{0,12},{4,0},{8,4},{12,8},{1,13},{5,1},{9,5},{13,9},{2,14},{6,2},{... | collective-permute-start | bytes 1769480 | tf_op jit(solution)/shard_map/ppermute | solution.py:84
  94.7 0.9 convolution_convert_fusion
  95.6 4.2 %collective-permute-start.11 = (bf16[96,3072]{1,0:T(8,128)(2,1)S(1)}, bf16[96,3072]{1,0:T(8,128)(2,1)S(1)}, u32[]{:S(2)}, u32[]{:S(2)}) collective-permute-start(bf16[96,3072]{1,0:T(8,128)(2,1)S(1)} %convolution_convert_fusion), channel_id=1, source_target_pairs={{0,4},{4,8},{8,12},{12,0},{1,5},{5,9},{9,13},{13,1},{2,6},{6,10},{... | collective-permute-start | bytes 1769480 | tf_op jit(solution)/shard_map/ppermute | solution.py:84
  99.8 0.9 convolution_convert_fusion.2
  100.6 3.8 %collective-permute-done.15 = bf16[6,64,384]{2,1,0:T(8,128)(2,1)S(1)} collective-permute-done((bf16[6,64,384]{2,1,0:T(8,128)(2,1)S(1)}, bf16[6,64,384]{2,1,0:T(8,128)(2,1)S(1)}, u32[]{:S(2)}, u32[]{:S(2)}) %collective-permute-start.15) | collective-permute-done | bytes 294944 | tf_op jit(solution)/shard_map/ppermute | solution.py:135
  104.4 4.3 %collective-permute-start.9 = (bf16[96,3072]{1,0:T(8,128)(2,1)S(1)}, bf16[96,3072]{1,0:T(8,128)(2,1)S(1)}, u32[]{:S(2)}, u32[]{:S(2)}) collective-permute-start(bf16[96,3072]{1,0:T(8,128)(2,1)S(1)} %convolution_convert_fusion.2), channel_id=1, source_target_pairs={{0,8},{4,12},{8,0},{12,4},{1,9},{5,13},{9,1},{13,5},{2,10},{6,14},... | collective-permute-start | bytes 1769480 | tf_op jit(solution)/shard_map/ppermute | solution.py:84
  108.8 0.0 collective-permute-done.13
  108.8 0.0 collective-permute-done.14
  108.8 0.2 fusion.1
  109.0 2.8 %collective-permute-start.16 = (bf16[6,64,384]{2,1,0:T(8,128)(2,1)S(1)}, bf16[6,64,384]{2,1,0:T(8,128)(2,1)S(1)}, u32[]{:S(2)}, u32[]{:S(2)}) collective-permute-start(bf16[6,64,384]{2,1,0:T(8,128)(2,1)S(1)} %get-tuple-element.18), channel_id=1, source_target_pairs={{0,32},{16,48},{32,64},{48,80},{64,96},{80,112},{96,0},{112,16},{1... | collective-permute-start | bytes 884744 | tf_op jit(solution)/shard_map/ppermute | solution.py:84
  111.8 5.2 %collective-permute-start.17 = (bf16[6,64,384]{2,1,0:T(8,128)(2,1)S(1)}, bf16[6,64,384]{2,1,0:T(8,128)(2,1)S(1)}, u32[]{:S(2)}, u32[]{:S(2)}) collective-permute-start(bf16[6,64,384]{2,1,0:T(8,128)(2,1)S(1)} %get-tuple-element.19), channel_id=1, source_target_pairs={{0,96},{16,112},{32,0},{48,16},{64,32},{80,48},{96,64},{112,80},{1... | collective-permute-start | bytes 884744 | tf_op jit(solution)/shard_map/ppermute | solution.py:84
  117.0 0.9 fusion.18
  117.9 4.6 %collective-permute-done.16 = bf16[6,64,384]{2,1,0:T(8,128)(2,1)S(1)} collective-permute-done((bf16[6,64,384]{2,1,0:T(8,128)(2,1)S(1)}, bf16[6,64,384]{2,1,0:T(8,128)(2,1)S(1)}, u32[]{:S(2)}, u32[]{:S(2)}) %collective-permute-start.16) | collective-permute-done | bytes 294944 | tf_op jit(solution)/shard_map/ppermute | solution.py:84
  122.5 8.2 %collective-permute-done.17 = bf16[6,64,384]{2,1,0:T(8,128)(2,1)S(1)} collective-permute-done((bf16[6,64,384]{2,1,0:T(8,128)(2,1)S(1)}, bf16[6,64,384]{2,1,0:T(8,128)(2,1)S(1)}, u32[]{:S(2)}, u32[]{:S(2)}) %collective-permute-start.17) | collective-permute-done | bytes 294944 | tf_op jit(solution)/shard_map/ppermute | solution.py:84
  130.7 0.2 fusion.11
  130.9 1.9 %collective-permute-start.18 = (bf16[2,64,384]{2,1,0:T(8,128)(2,1)S(1)}, bf16[2,64,384]{2,1,0:T(8,128)(2,1)S(1)}, u32[]{:S(2)}, u32[]{:S(2)}) collective-permute-start(bf16[2,64,384]{2,1,0:T(8,128)(2,1)S(1)} %get-tuple-element.16), channel_id=1, source_target_pairs={{0,128},{128,256},{256,0},{384,512},{512,640},{640,384},{1,129},{1... | collective-permute-start | bytes 294920 | tf_op jit(solution)/shard_map/ppermute | solution.py:165
  132.9 4.8 %collective-permute-start.19 = (bf16[2,64,384]{2,1,0:T(8,128)(2,1)S(1)}, bf16[2,64,384]{2,1,0:T(8,128)(2,1)S(1)}, u32[]{:S(2)}, u32[]{:S(2)}) collective-permute-start(bf16[2,64,384]{2,1,0:T(8,128)(2,1)S(1)} %get-tuple-element.17), channel_id=1, source_target_pairs={{0,256},{128,0},{256,128},{384,640},{512,384},{640,512},{1,257},{1... | collective-permute-start | bytes 294920 | tf_op jit(solution)/shard_map/ppermute | solution.py:165
  137.7 0.0 collective-permute-done.10
  137.7 0.0 collective-permute-done.11
  137.7 0.0 collective-permute-done.9
  137.7 0.1 fusion.6
  137.9 2.9 %collective-permute-start.12 = (bf16[48,3072]{1,0:T(8,128)(2,1)S(1)}, bf16[48,3072]{1,0:T(8,128)(2,1)S(1)}, u32[]{:S(2)}, u32[]{:S(2)}) collective-permute-start(bf16[48,3072]{1,0:T(8,128)(2,1)S(1)} %fusion.6), channel_id=1, source_target_pairs={{0,642},{2,640},{128,514},{130,512},{256,386},{258,384},{384,258},... | collective-permute-start | bytes 884744 | tf_op jit(solution)/shard_map/ppermute | solution.py:103
  140.8 0.0 collective-permute-done.18
  140.8 0.7 collective-permute-done.19
  141.5 2.8 %collective-permute-start.20 = (bf16[64,384]{1,0:T(8,128)(2,1)S(1)}, bf16[64,384]{1,0:T(8,128)(2,1)S(1)}, u32[]{:S(2)}, u32[]{:S(2)}) collective-permute-start(bf16[64,384]{1,0:T(8,128)(2,1)S(1)} %fusion.20), channel_id=1, source_target_pairs={{0,384},{128,512},{256,640},{384,0},{512,128},{640,256},{1,385},{1... | collective-permute-start | bytes 147464 | tf_op jit(solution)/shard_map/ppermute | solution.py:84
  144.3 18.6 %collective-permute-done.12 = bf16[48,3072]{1,0:T(8,128)(2,1)S(1)} collective-permute-done((bf16[48,3072]{1,0:T(8,128)(2,1)S(1)}, bf16[48,3072]{1,0:T(8,128)(2,1)S(1)}, u32[]{:S(2)}, u32[]{:S(2)}) %collective-permute-start.12) | collective-permute-done | bytes 294944 | tf_op jit(solution)/shard_map/ppermute | solution.py:103
  162.9 0.9 fusion.10
  163.8 0.0 collective-permute-done.20
  163.8 0.7 bitcast_add_fusion.2
  (12 shorter events, 0.2 us)
Async XLA Ops:
  0.6 55.4 %copy-start = (bf16[3072,384]{1,0:T(8,128)(2,1)S(1)}, bf16[3072,384]{1,0:T(8,128)(2,1)}, u32[]{:S(2)}) copy-start(bf16[3072,384]{1,0:T(8,128)(2,1)} %param.5) | copy-start | bytes 7077892
  0.6 34.5 %collective-permute-start = (bf16[48,3072]{1,0:T(8,128)(2,1)}, bf16[48,3072]{1,0:T(8,128)(2,1)S(1)}, u32[]{:S(2)}, u32[]{:S(2)}) collective-permute-start(bf16[48,3072]{1,0:T(8,128)(2,1)} %param.4), channel_id=1, source_target_pairs={{0,642},{2,640},{128,514},{130,512},{256,386},{258,384},{384,258},... | collective-permute-start | bytes 884744 | tf_op jit(solution)/shard_map/ppermute | solution.py:103
  15.4 26.6 %collective-permute-start.1 = (bf16[48,3072]{1,0:T(8,128)(2,1)}, bf16[48,3072]{1,0:T(8,128)(2,1)S(1)}, u32[]{:S(2)}, u32[]{:S(2)}) collective-permute-start(bf16[48,3072]{1,0:T(8,128)(2,1)} %param.4), channel_id=1, source_target_pairs={{0,4},{4,8},{8,12},{12,0},{1,5},{5,9},{9,13},{13,1},{2,6},{6,10},{... | collective-permute-start | bytes 884744 | tf_op jit(solution)/shard_map/ppermute | solution.py:84
  17.8 29.2 %collective-permute-start.3 = (bf16[48,3072]{1,0:T(8,128)(2,1)}, bf16[48,3072]{1,0:T(8,128)(2,1)S(1)}, u32[]{:S(2)}, u32[]{:S(2)}) collective-permute-start(bf16[48,3072]{1,0:T(8,128)(2,1)} %param.4), channel_id=1, source_target_pairs={{0,8},{4,12},{8,0},{12,4},{1,9},{5,13},{9,1},{13,5},{2,10},{6,14},... | collective-permute-start | bytes 884744 | tf_op jit(solution)/shard_map/ppermute | solution.py:84
  22.1 28.8 %collective-permute-start.5 = (bf16[48,3072]{1,0:T(8,128)(2,1)}, bf16[48,3072]{1,0:T(8,128)(2,1)S(1)}, u32[]{:S(2)}, u32[]{:S(2)}) collective-permute-start(bf16[48,3072]{1,0:T(8,128)(2,1)} %param.4), channel_id=1, source_target_pairs={{0,12},{4,0},{8,4},{12,8},{1,13},{5,1},{9,5},{13,9},{2,14},{6,2},{... | collective-permute-start | bytes 884744 | tf_op jit(solution)/shard_map/ppermute | solution.py:84
  35.2 11.8 %collective-permute-start.2 = (bf16[48,3072]{1,0:T(8,128)(2,1)S(1)}, bf16[48,3072]{1,0:T(8,128)(2,1)S(1)}, u32[]{:S(2)}, u32[]{:S(2)}) collective-permute-start(bf16[48,3072]{1,0:T(8,128)(2,1)S(1)} %collective-permute-done), channel_id=1, source_target_pairs={{0,4},{4,8},{8,12},{12,0},{1,5},{5,9},{9,13},{13,1},{2,6},{6,10},{... | collective-permute-start | bytes 884744 | tf_op jit(solution)/shard_map/ppermute | solution.py:84
  37.6 13.3 %collective-permute-start.4 = (bf16[48,3072]{1,0:T(8,128)(2,1)S(1)}, bf16[48,3072]{1,0:T(8,128)(2,1)S(1)}, u32[]{:S(2)}, u32[]{:S(2)}) collective-permute-start(bf16[48,3072]{1,0:T(8,128)(2,1)S(1)} %collective-permute-done), channel_id=1, source_target_pairs={{0,8},{4,12},{8,0},{12,4},{1,9},{5,13},{9,1},{13,5},{2,10},{6,14},... | collective-permute-start | bytes 884744 | tf_op jit(solution)/shard_map/ppermute | solution.py:84
  41.9 14.0 %collective-permute-start.6 = (bf16[48,3072]{1,0:T(8,128)(2,1)S(1)}, bf16[48,3072]{1,0:T(8,128)(2,1)S(1)}, u32[]{:S(2)}, u32[]{:S(2)}) collective-permute-start(bf16[48,3072]{1,0:T(8,128)(2,1)S(1)} %collective-permute-done), channel_id=1, source_target_pairs={{0,12},{4,0},{8,4},{12,8},{1,13},{5,1},{9,5},{13,9},{2,14},{6,2},{... | collective-permute-start | bytes 884744 | tf_op jit(solution)/shard_map/ppermute | solution.py:84
  56.0 1.4 copy-start.1
  56.0 3.4 %copy-start.4 = (bf16[384,384]{1,0:T(8,128)(2,1)S(1)}, bf16[384,384]{1,0:T(8,128)(2,1)}, u32[]{:S(2)}) copy-start(bf16[384,384]{1,0:T(8,128)(2,1)} %param.6) | copy-start | bytes 884740
  56.0 17.2 %copy-start.3 = (f32[128]{0:T(128)S(1)}, f32[128]{0:T(128)}, u32[]{:S(2)}) copy-start(f32[128]{0:T(128)} %param.7) | copy-start | bytes 1540
  57.4 15.8 %collective-permute-start.7 = (f32[384,384]{1,0:T(8,128)S(1)}, f32[384,384]{1,0:T(8,128)}, u32[]{:S(2)}, u32[]{:S(2)}) collective-permute-start(f32[384,384]{1,0:T(8,128)S(1)} %fusion.21.mine), channel_id=1, source_target_pairs={{0,1},{1,0},{2,3},{3,2},{4,5},{5,4},{6,7},{7,6},{8,9},{9,8},{10,11... | collective-permute-start | bytes 1769480 | tf_op jit(solution)/shard_map/ppermute | solution.py:84
  60.1 13.1 %collective-permute-start.8 = (bf16[4,48,384]{2,1,0:T(8,128)(2,1)}, bf16[4,48,384]{2,1,0:T(8,128)(2,1)S(1)}, u32[]{:S(2)}, u32[]{:S(2)}) collective-permute-start(bf16[4,48,384]{2,1,0:T(8,128)(2,1)} %get-tuple-element.20), channel_id=1, source_target_pairs={{0,640},{128,512},{256,384},{384,256},{512,128},{640,0},{1,641},{1... | collective-permute-start | bytes 442376 | tf_op jit(solution)/shard_map/ppermute | solution.py:109
  73.2 1.7 %copy-start.2 = (bf16[384,3072]{1,0:T(8,128)(2,1)S(1)}, bf16[384,3072]{1,0:T(8,128)(2,1)}, u32[]{:S(2)}) copy-start(bf16[384,3072]{1,0:T(8,128)(2,1)} %copy-done.1) | copy-start | bytes 7077892
  80.6 28.1 %collective-permute-start.13 = (bf16[2,6,64,384]{3,2,1,0:T(8,128)(2,1)S(1)}, bf16[2,6,64,384]{3,2,1,0:T(8,128)(2,1)S(1)}, u32[]{:S(2)}, u32[]{:S(2)}) collective-permute-start(bf16[2,6,64,384]{3,2,1,0:T(8,128)(2,1)S(1)} %get-tuple-element.11), channel_id=1, source_target_pairs={{0,16},{16,32},{32,48},{48,64},{64,80},{80,96},{96,112},{112,0},{1... | collective-permute-start | bytes 1769480 | tf_op jit(solution)/shard_map/ppermute | solution.py:84
  84.1 24.6 %collective-permute-start.14 = (bf16[2,6,64,384]{3,2,1,0:T(8,128)(2,1)S(1)}, bf16[2,6,64,384]{3,2,1,0:T(8,128)(2,1)S(1)}, u32[]{:S(2)}, u32[]{:S(2)}) collective-permute-start(bf16[2,6,64,384]{3,2,1,0:T(8,128)(2,1)S(1)} %get-tuple-element.12), channel_id=1, source_target_pairs={{0,112},{16,0},{32,16},{48,32},{64,48},{80,64},{96,80},{112,96},{1... | collective-permute-start | bytes 1769480 | tf_op jit(solution)/shard_map/ppermute | solution.py:84
  88.0 16.5 %collective-permute-start.15 = (bf16[6,64,384]{2,1,0:T(8,128)(2,1)S(1)}, bf16[6,64,384]{2,1,0:T(8,128)(2,1)S(1)}, u32[]{:S(2)}, u32[]{:S(2)}) collective-permute-start(bf16[6,64,384]{2,1,0:T(8,128)(2,1)S(1)} %bitcast.49), channel_id=1, source_target_pairs={{0,32},{1,97},{16,48},{17,113},{32,64},{33,1},{48,80},{49,17},{64,... | collective-permute-start | bytes 884744 | tf_op jit(solution)/shard_map/ppermute | solution.py:135
  91.9 45.8 %collective-permute-start.10 = (bf16[96,3072]{1,0:T(8,128)(2,1)S(1)}, bf16[96,3072]{1,0:T(8,128)(2,1)S(1)}, u32[]{:S(2)}, u32[]{:S(2)}) collective-permute-start(bf16[96,3072]{1,0:T(8,128)(2,1)S(1)} %convolution_convert_fusion.1), channel_id=1, source_target_pairs={{0,12},{4,0},{8,4},{12,8},{1,13},{5,1},{9,5},{13,9},{2,14},{6,2},{... | collective-permute-start | bytes 1769480 | tf_op jit(solution)/shard_map/ppermute | solution.py:84
  95.6 42.1 %collective-permute-start.11 = (bf16[96,3072]{1,0:T(8,128)(2,1)S(1)}, bf16[96,3072]{1,0:T(8,128)(2,1)S(1)}, u32[]{:S(2)}, u32[]{:S(2)}) collective-permute-start(bf16[96,3072]{1,0:T(8,128)(2,1)S(1)} %convolution_convert_fusion), channel_id=1, source_target_pairs={{0,4},{4,8},{8,12},{12,0},{1,5},{5,9},{9,13},{13,1},{2,6},{6,10},{... | collective-permute-start | bytes 1769480 | tf_op jit(solution)/shard_map/ppermute | solution.py:84
  104.4 33.3 %collective-permute-start.9 = (bf16[96,3072]{1,0:T(8,128)(2,1)S(1)}, bf16[96,3072]{1,0:T(8,128)(2,1)S(1)}, u32[]{:S(2)}, u32[]{:S(2)}) collective-permute-start(bf16[96,3072]{1,0:T(8,128)(2,1)S(1)} %convolution_convert_fusion.2), channel_id=1, source_target_pairs={{0,8},{4,12},{8,0},{12,4},{1,9},{5,13},{9,1},{13,5},{2,10},{6,14},... | collective-permute-start | bytes 1769480 | tf_op jit(solution)/shard_map/ppermute | solution.py:84
  109.0 13.4 %collective-permute-start.16 = (bf16[6,64,384]{2,1,0:T(8,128)(2,1)S(1)}, bf16[6,64,384]{2,1,0:T(8,128)(2,1)S(1)}, u32[]{:S(2)}, u32[]{:S(2)}) collective-permute-start(bf16[6,64,384]{2,1,0:T(8,128)(2,1)S(1)} %get-tuple-element.18), channel_id=1, source_target_pairs={{0,32},{16,48},{32,64},{48,80},{64,96},{80,112},{96,0},{112,16},{1... | collective-permute-start | bytes 884744 | tf_op jit(solution)/shard_map/ppermute | solution.py:84
  111.8 18.9 %collective-permute-start.17 = (bf16[6,64,384]{2,1,0:T(8,128)(2,1)S(1)}, bf16[6,64,384]{2,1,0:T(8,128)(2,1)S(1)}, u32[]{:S(2)}, u32[]{:S(2)}) collective-permute-start(bf16[6,64,384]{2,1,0:T(8,128)(2,1)S(1)} %get-tuple-element.19), channel_id=1, source_target_pairs={{0,96},{16,112},{32,0},{48,16},{64,32},{80,48},{96,64},{112,80},{1... | collective-permute-start | bytes 884744 | tf_op jit(solution)/shard_map/ppermute | solution.py:84
  130.9 9.8 %collective-permute-start.18 = (bf16[2,64,384]{2,1,0:T(8,128)(2,1)S(1)}, bf16[2,64,384]{2,1,0:T(8,128)(2,1)S(1)}, u32[]{:S(2)}, u32[]{:S(2)}) collective-permute-start(bf16[2,64,384]{2,1,0:T(8,128)(2,1)S(1)} %get-tuple-element.16), channel_id=1, source_target_pairs={{0,128},{128,256},{256,0},{384,512},{512,640},{640,384},{1,129},{1... | collective-permute-start | bytes 294920 | tf_op jit(solution)/shard_map/ppermute | solution.py:165
  132.9 8.6 %collective-permute-start.19 = (bf16[2,64,384]{2,1,0:T(8,128)(2,1)S(1)}, bf16[2,64,384]{2,1,0:T(8,128)(2,1)S(1)}, u32[]{:S(2)}, u32[]{:S(2)}) collective-permute-start(bf16[2,64,384]{2,1,0:T(8,128)(2,1)S(1)} %get-tuple-element.17), channel_id=1, source_target_pairs={{0,256},{128,0},{256,128},{384,640},{512,384},{640,512},{1,257},{1... | collective-permute-start | bytes 294920 | tf_op jit(solution)/shard_map/ppermute | solution.py:165
  137.9 25.1 %collective-permute-start.12 = (bf16[48,3072]{1,0:T(8,128)(2,1)S(1)}, bf16[48,3072]{1,0:T(8,128)(2,1)S(1)}, u32[]{:S(2)}, u32[]{:S(2)}) collective-permute-start(bf16[48,3072]{1,0:T(8,128)(2,1)S(1)} %fusion.6), channel_id=1, source_target_pairs={{0,642},{2,640},{128,514},{130,512},{256,386},{258,384},{384,258},... | collective-permute-start | bytes 884744 | tf_op jit(solution)/shard_map/ppermute | solution.py:103
  141.5 22.3 %collective-permute-start.20 = (bf16[64,384]{1,0:T(8,128)(2,1)S(1)}, bf16[64,384]{1,0:T(8,128)(2,1)S(1)}, u32[]{:S(2)}, u32[]{:S(2)}) collective-permute-start(bf16[64,384]{1,0:T(8,128)(2,1)S(1)} %fusion.20), channel_id=1, source_target_pairs={{0,384},{128,512},{256,640},{384,0},{512,128},{640,256},{1,385},{1... | collective-permute-start | bytes 147464 | tf_op jit(solution)/shard_map/ppermute | solution.py:84

commit v5 on v4

--- a/solution.py
+++ b/solution.py
@@ -19,10 +19,8 @@
 
 def rows_kernel(sizes, factor, where, mine, theirs, cot, cot_far, gain, tokens, rows_out, *rest):
     nx, nh, ny, nz = sizes
-    outs, (held, term, sem) = rest[:-3], rest[-3:]
+    outs, term = rest[:-1], rest[-1]
     x, y = where[0], where[1]
-    copy = pltpu.make_async_copy(tokens, held, sem)
-    copy.start()
     count = cot.shape[1]
     heads = mine.shape[1]
     hd = gain.shape[1]
@@ -40,12 +38,11 @@
                 result = inverse * (scaled - mean(scaled) - unit * mean(scaled * unit))
                 rows_out[span, h : h + hd] = result.astype(BF16)
     rows = rows_out[...]
-    part = held.shape[1] // nz
+    part = tokens.shape[1] // nz
     blk = part // ny
-    copy.wait()
     for z in range(nz):
         term[...] = factor * lax.dot_general(
-            held[:, z * part : (z + 1) * part],
+            tokens[:, z * part : (z + 1) * part],
             rows,
             (((0,), (0,)), ((), ())),
             preferred_element_type=F32,
@@ -65,18 +62,71 @@
     return pl.pallas_call(
         functools.partial(rows_kernel, sizes, factor),
         out_shape=[jax.ShapeDtypeStruct(mine.shape, BF16)] + chunks,
-        in_specs=[pl.BlockSpec(memory_space=pltpu.SMEM)]
-        + [vmem] * 5
-        + [pl.BlockSpec(memory_space=pl.ANY)],
+        in_specs=[pl.BlockSpec(memory_space=pltpu.SMEM)] + [vmem] * 6,
         out_specs=[vmem] * (len(ORDER) + 1),
-        scratch_shapes=[
-            pltpu.VMEM(tokens.shape, BF16),
-            pltpu.VMEM((part, heads), F32),
-            pltpu.SemaphoreType.DMA,
-        ],
-        compiler_params=pltpu.CompilerParams(vmem_limit_bytes=12 * 2**20),
+        scratch_shapes=[pltpu.VMEM((part, heads), F32)],
+        compiler_params=pltpu.CompilerParams(vmem_limit_bytes=8 * 2**20),
         name="rows_and_chunks",
     )(where, mine, theirs, cot, cot_far, gain, tokens)
+
+
+def small_call(kernel, out_shape, *operands, where=None):
+    vmem = pl.BlockSpec(memory_space=pltpu.VMEM)
+    scalars = () if where is None else (where,)
+    return pl.pallas_call(
+        kernel,
+        out_shape=out_shape,
+        in_specs=[pl.BlockSpec(memory_space=pltpu.SMEM)] * len(scalars) + [vmem] * len(operands),
+        out_specs=[vmem] * len(out_shape),
+        compiler_params=pltpu.CompilerParams(vmem_limit_bytes=8 * 2**20),
+        cost_estimate=pl.CostEstimate(flops=0, transcendentals=0, bytes_accessed=0),
+    )(*scalars, *operands)
+
+
+def backs_kernel(rows, weight, *outs):
+    count = outs[0].shape[0]
+    for k, out in enumerate(outs):
+        out[...] = lax.dot_general(
+            rows[k * count : (k + 1) * count, :],
+            weight[...],
+            (((1,), (1,)), ((), ())),
+            preferred_element_type=F32,
+        ).astype(out.dtype)
+
+
+def back_sum_kernel(first, *rest):
+    terms, (near, far) = rest[:-2], rest[-2:]
+    count = near.shape[0]
+    for span, out in ((pl.ds(0, count), near), (pl.ds(count, count), far)):
+        total = first[span, :]
+        for t in terms:
+            total = total + t[span, :].astype(F32)
+        out[...] = total.astype(out.dtype)
+
+
+def over_y_kernel(where, own, up, down, got2, got4, got6, kept, *sends):
+    count, third = kept.shape[0], len(sends) + 1
+    for k in range(third):
+        place = lax.rem(where[0] + k, third)
+        for i in range(count):
+            z = i * third + place
+            total = own[0, z].astype(F32) + got4[z].astype(F32)
+            total = total + (up[1, z].astype(F32) + down[1, z].astype(F32))
+            total = total + (got2[z].astype(F32) + got6[z].astype(F32))
+            if k:
+                sends[k - 1][i] = total.astype(BF16)
+            else:
+                kept[i] = total
+
+
+def over_third_kernel(where, kept, *rest):
+    got, (stay, send) = rest[:-2], rest[-2:]
+    side = where[1]
+    for at, out in ((side, stay), (1 - side, send)):
+        total = kept[at]
+        for g in got:
+            total = total + g[at].astype(F32)
+        out[...] = total.astype(out.dtype)
 
 
 def shift(value, axis, by):
@@ -108,6 +158,7 @@
     cot_far = lax.dynamic_index_in_dim(cot, 1 - zh, 1, False)
     cot_far = lax.ppermute(cot_far, "zl", [(i, nz - 1 - i) for i in range(nz)])
     cot = lax.dynamic_index_in_dim(cot, zh, 1, False)
+    peer, cot_far = lax.optimization_barrier((peer, cot_far))
     other = [peer] + [shift(peer, "x", k) for k in (1, 2, 3)]
     tokens = jnp.concatenate([p for pair in zip(own, other) for p in pair], axis=0)
 
@@ -127,45 +178,57 @@
     )
 
     up, down, across, two, six, own = c
-    core = lax.axis_index("c")
     turn = [
-        (i * 2 + j, (i + (2, -2)[j]) % ny * 2 + j) for i in range(ny) for j in range(2)
+        (i * 2 + j, (i + (4, -4)[j]) % ny * 2 + j) for i in range(ny) for j in range(2)
     ]
     got_up, got_down = shift(up, "y", 1), shift(down, "y", -1)
-    got4 = lax.ppermute(across[0], ("y", "c"), turn).astype(F32)
-    two = add(two[0], got_up[0], jnp.where(core == 0, got4, 0.0)).astype(BF16)
-    six = add(six[0], got_down[0], jnp.where(core == 1, got4, 0.0)).astype(BF16)
+    got4 = lax.ppermute(across[0], ("y", "c"), turn)
+    two = add(two[0], got_up[0]).astype(BF16)
+    six = add(six[0], got_down[0]).astype(BF16)
     got2, got6 = shift(two, "y", 2), shift(six, "y", -2)
 
-    back = [
-        lax.dot_general(
-            rows[k * nh * count : (k + 1) * nh * count],
-            weight,
-            (((1,), (1,)), ((), ())),
-            preferred_element_type=F32,
-        )
-        for k in range(nx)
-    ]
-    terms = [back[0]] + [shift(back[k].astype(BF16), "x", -k) for k in (2, 1, 3)]
-    far = mirror(add(*[t[count:] for t in terms]).astype(BF16))
-    input_grad = add(*[t[:count] for t in terms], far).astype(BF16)
-
-    over_y = add(own[0], got_up[1], got_down[1], got2, got6)
+    block = (nh * count, width)
+    back = small_call(
+        backs_kernel,
+        [jax.ShapeDtypeStruct(block, F32)] + [jax.ShapeDtypeStruct(block, BF16)] * (nx - 1),
+        rows,
+        weight,
+    )
+    near, far = small_call(
+        back_sum_kernel,
+        [jax.ShapeDtypeStruct((count, width), t) for t in (F32, BF16)],
+        back[0],
+        *[shift(back[k], "x", -k) for k in (2, 1, 3)],
+    )
+    input_grad = add(near, mirror(far)).astype(BF16)
+
     third = nz // 2
     zl = lax.axis_index("zl")
-    over_y = over_y.reshape(2, third, -1, heads)
-    place = zl % third
-
-    def of_third(k):
-        return lax.dynamic_index_in_dim(over_y, (place + k) % third, 1, False)
-
-    kept = of_third(0)
+    spot = jnp.stack([zl % third, zl // third]).astype(jnp.int32)
+    blk = own.shape[2]
+    kept, *sends = small_call(
+        over_y_kernel,
+        [jax.ShapeDtypeStruct((2, blk, heads), t) for t in (F32, *[BF16] * (third - 1))],
+        own,
+        got_up,
+        got_down,
+        got2,
+        got4,
+        got6,
+        where=spot,
+    )
+    got = []
     for k in range(1, third):
         hop = [(i, i // third * third + (i + k) % third) for i in range(nz)]
-        kept = add(kept, lax.ppermute(of_third(k).astype(BF16), "zl", hop))
-    side = zl // third
-    last = shift(lax.dynamic_index_in_dim(kept, 1 - side, 0, False).astype(BF16), "zl", third)
-    weight_grad = add(lax.dynamic_index_in_dim(kept, side, 0, False), last)
+        got.append(lax.ppermute(sends[k - 1], "zl", hop))
+    stay, send = small_call(
+        over_third_kernel,
+        [jax.ShapeDtypeStruct((blk, heads), t) for t in (F32, BF16)],
+        kept,
+        *got,
+        where=spot,
+    )
+    weight_grad = add(stay, shift(send, "zl", third))
     return (input_grad, weight_grad)
 
 

time: 168 us -> 152 us (0.905)
  the two profiles are of different devices: /device:TPU:6 before, /device:TPU:128 now
where the time goes in v5:
time: 152 us; the launch traced here: 151 us
  starting transfers between devices  78.1 us (51%)
  waiting for transfers between devices  54.3 us (36%)
  Pallas kernels  8.98 us (6%)
  other arithmetic  4.11 us (3%)
  local copies, waits for them, and re-layouts  3.13 us (2%)
    ppermute x15, starting transfers between devices, shift(): lax.ppermute(value, axis, [(i, (i + by) % size) for i in range(size)])  48.1 us
    ppermute x15, waiting for transfers between devices, shift(): lax.ppermute(value, axis, [(i, (i + by) % size) for i in range(size)])  31.9 us
    ppermute x2, starting transfers between devices, mirror(): return lax.ppermute(value, ('zl', 'zh'), ends)  14.7 us
    ppermute x2, waiting for transfers between devices, body(): got.append(lax.ppermute(sends[k - 1], 'zl', hop))  13.3 us
    ppermute x1, waiting for transfers between devices, body(): cot_far = lax.ppermute(cot_far, 'zl', [(i, nz - 1 - i) for i in range(nz)])  9.16 us
    ppermute x1, starting transfers between devices, body(): got4 = lax.ppermute(across[0], ('y', 'c'), turn)  6.28 us
    ppermute x2, starting transfers between devices, body(): got.append(lax.ppermute(sends[k - 1], 'zl', hop))  5.84 us
    pallas_call x4, Pallas kernels, small_call(): pl.pallas_call(kernel, out_shape=out_shape, in_specs=[pl.BlockSpec(memory...  4.66 us
  transfers between devices with their start and end apart: 21, of which 9 were waited for; matrix products, arithmetic and copies ran while one was open for 4% of the time, Pallas kernels for 3%

profile of v5, /device:TPU:128, one launch (start us, length us, event | category | flops | bytes accessed | tf_op | source)
XLA Modules:
  0.0 151.1 jit_solution(633220476873709101)
XLA Ops:
  0.6 12.7 %collective-permute-start = (bf16[48,3072]{1,0:T(8,128)(2,1)}, bf16[48,3072]{1,0:T(8,128)(2,1)S(1)}, u32[]{:S(2)}, u32[]{:S(2)}) collective-permute-start(bf16[48,3072]{1,0:T(8,128)(2,1)} %param.4), channel_id=1, source_target_pairs={{0,642},{2,640},{128,514},{130,512},{256,386},{258,384},{384,258},... | collective-permute-start | bytes 884744 | tf_op jit(solution)/shard_map/ppermute | solution.py:153
  13.4 3.4 %collective-permute-start.2 = (bf16[48,3072]{1,0:T(8,128)(2,1)}, bf16[48,3072]{1,0:T(8,128)(2,1)}, u32[]{:S(2)}, u32[]{:S(2)}) collective-permute-start(bf16[48,3072]{1,0:T(8,128)(2,1)} %param.4), channel_id=1, source_target_pairs={{0,4},{4,8},{8,12},{12,0},{1,5},{5,9},{9,13},{13,1},{2,6},{6,10},{... | collective-permute-start | bytes 884744 | tf_op jit(solution)/shard_map/ppermute | solution.py:134
  16.8 4.6 %collective-permute-start.4 = (bf16[48,3072]{1,0:T(8,128)(2,1)}, bf16[48,3072]{1,0:T(8,128)(2,1)S(1)}, u32[]{:S(2)}, u32[]{:S(2)}) collective-permute-start(bf16[48,3072]{1,0:T(8,128)(2,1)} %param.4), channel_id=1, source_target_pairs={{0,8},{4,12},{8,0},{12,4},{1,9},{5,13},{9,1},{13,5},{2,10},{6,14},... | collective-permute-start | bytes 884744 | tf_op jit(solution)/shard_map/ppermute | solution.py:134
  21.4 3.3 %collective-permute-start.6 = (bf16[48,3072]{1,0:T(8,128)(2,1)}, bf16[48,3072]{1,0:T(8,128)(2,1)S(1)}, u32[]{:S(2)}, u32[]{:S(2)}) collective-permute-start(bf16[48,3072]{1,0:T(8,128)(2,1)} %param.4), channel_id=1, source_target_pairs={{0,12},{4,0},{8,4},{12,8},{1,13},{5,1},{9,5},{13,9},{2,14},{6,2},{... | collective-permute-start | bytes 884744 | tf_op jit(solution)/shard_map/ppermute | solution.py:134
  24.8 1.0 dynamic-slice_bitcast_fusion
  25.8 0.0 copy-start
  25.8 3.2 %collective-permute-start.1 = (bf16[4,48,384]{2,1,0:T(8,128)(2,1)S(1)}, bf16[4,48,384]{2,1,0:T(8,128)(2,1)S(1)}, u32[]{:S(2)}, u32[]{:S(2)}) collective-permute-start(bf16[4,48,384]{2,1,0:T(8,128)(2,1)S(1)} %get-tuple-element.43), channel_id=1, source_target_pairs={{0,640},{128,512},{256,384},{384,256},{512,128},{640,0},{1,641},{1... | collective-permute-start | bytes 442376 | tf_op jit(solution)/shard_map/ppermute | solution.py:159
  29.0 1.0 constant_dynamic-update-slice_fusion.7
  30.0 9.2 %collective-permute-done.1.cot_far = bf16[4,48,384]{2,1,0:T(8,128)(2,1)S(1)} collective-permute-done((bf16[4,48,384]{2,1,0:T(8,128)(2,1)S(1)}, bf16[4,48,384]{2,1,0:T(8,128)(2,1)S(1)}, u32[]{:S(2)}, u32[]{:S(2)}) %collective-permute-start.1) | collective-permute-done | bytes 147488 | tf_op jit(solution)/shard_map/ppermute | solution.py:159
  39.2 0.0 collective-permute-done
  39.2 2.5 %collective-permute-start.3 = (bf16[48,3072]{1,0:T(8,128)(2,1)S(1)}, bf16[48,3072]{1,0:T(8,128)(2,1)S(1)}, u32[]{:S(2)}, u32[]{:S(2)}) collective-permute-start(bf16[48,3072]{1,0:T(8,128)(2,1)S(1)} %collective-permute-done), channel_id=1, source_target_pairs={{0,4},{4,8},{8,12},{12,0},{1,5},{5,9},{9,13},{13,1},{2,6},{6,10},{... | collective-permute-start | bytes 884744 | tf_op jit(solution)/shard_map/ppermute | solution.py:134
  41.7 2.9 %collective-permute-start.5 = (bf16[48,3072]{1,0:T(8,128)(2,1)S(1)}, bf16[48,3072]{1,0:T(8,128)(2,1)S(1)}, u32[]{:S(2)}, u32[]{:S(2)}) collective-permute-start(bf16[48,3072]{1,0:T(8,128)(2,1)S(1)} %collective-permute-done), channel_id=1, source_target_pairs={{0,8},{4,12},{8,0},{12,4},{1,9},{5,13},{9,1},{13,5},{2,10},{6,14},... | collective-permute-start | bytes 884744 | tf_op jit(solution)/shard_map/ppermute | solution.py:134
  44.7 0.0 collective-permute-done.2
  44.7 3.6 %collective-permute-start.7 = (bf16[48,3072]{1,0:T(8,128)(2,1)S(1)}, bf16[48,3072]{1,0:T(8,128)(2,1)S(1)}, u32[]{:S(2)}, u32[]{:S(2)}) collective-permute-start(bf16[48,3072]{1,0:T(8,128)(2,1)S(1)} %collective-permute-done), channel_id=1, source_target_pairs={{0,12},{4,0},{8,4},{12,8},{1,13},{5,1},{9,5},{13,9},{2,14},{6,2},{... | collective-permute-start | bytes 884744 | tf_op jit(solution)/shard_map/ppermute | solution.py:134
  48.3 1.0 constant_dynamic-update-slice_fusion.5
  49.2 5.8 %collective-permute-done.3 = bf16[48,3072]{1,0:T(8,128)(2,1)S(1)} collective-permute-done((bf16[48,3072]{1,0:T(8,128)(2,1)S(1)}, bf16[48,3072]{1,0:T(8,128)(2,1)S(1)}, u32[]{:S(2)}, u32[]{:S(2)}) %collective-permute-start.3) | collective-permute-done | bytes 294944 | tf_op jit(solution)/shard_map/ppermute | solution.py:134
  55.1 0.0 collective-permute-done.4
  55.1 0.0 collective-permute-done.5
  55.2 0.0 collective-permute-done.6
  55.2 2.3 %collective-permute-done.7 = bf16[48,3072]{1,0:T(8,128)(2,1)S(1)} collective-permute-done((bf16[48,3072]{1,0:T(8,128)(2,1)S(1)}, bf16[48,3072]{1,0:T(8,128)(2,1)S(1)}, u32[]{:S(2)}, u32[]{:S(2)}) %collective-permute-start.7) | collective-permute-done | bytes 294944 | tf_op jit(solution)/shard_map/ppermute | solution.py:134
  57.6 0.0 copy-done
  57.6 0.0 copy-start.2
  57.6 1.4 fusion.2.mine
  59.0 1.9 %collective-permute-start.8 = (f32[384,384]{1,0:T(8,128)S(1)}, f32[384,384]{1,0:T(8,128)}, u32[]{:S(2)}, u32[]{:S(2)}) collective-permute-start(f32[384,384]{1,0:T(8,128)S(1)} %fusion.2.mine), channel_id=1, source_target_pairs={{0,1},{1,0},{2,3},{3,2},{4,5},{5,4},{6,7},{7,6},{8,9},{9,8},{10,11... | collective-permute-start | bytes 1769480 | tf_op jit(solution)/shard_map/ppermute | solution.py:134
  60.9 0.0 copy-start.1
  60.9 0.1 pad_add_fusion.where
  61.0 2.0 %collective-permute-done.8.theirs = f32[384,384]{1,0:T(8,128)} collective-permute-done((f32[384,384]{1,0:T(8,128)S(1)}, f32[384,384]{1,0:T(8,128)}, u32[]{:S(2)}, u32[]{:S(2)}) %collective-permute-start.8) | collective-permute-done | bytes 589856 | tf_op jit(solution)/shard_map/ppermute | solution.py:134
  63.0 0.0 copy-done.2
  63.0 4.3 %rows_and_chunks.1 = (bf16[384,384]{1,0:T(8,128)(2,1)S(1)}, bf16[2,6,64,384]{3,2,1,0:T(8,128)(2,1)S(1)}, bf16[2,6,64,384]{3,2,1,0:T(8,128)(2,1)S(1)}, bf16[1,6,6...) custom-call(s32[2]{0:T(128)S(1)} %pad_add_fusion.where, ...), custom_call_target="tpu_custom_call" | custom-call | tf_op jit(solution)/shard_map/rows_and_chunks/pallas_call | solution.py:62
  67.4 5.4 %collective-permute-start.14 = (bf16[2,6,64,384]{3,2,1,0:T(8,128)(2,1)S(1)}, bf16[2,6,64,384]{3,2,1,0:T(8,128)(2,1)S(1)}, u32[]{:S(2)}, u32[]{:S(2)}) collective-permute-start(bf16[2,6,64,384]{3,2,1,0:T(8,128)(2,1)S(1)} %get-tuple-element.33), channel_id=1, source_target_pairs={{0,112},{16,0},{32,16},{48,32},{64,48},{80,64},{96,80},{112,96},{1... | collective-permute-start | bytes 1769480 | tf_op jit(solution)/shard_map/ppermute | solution.py:134
  72.7 1.9 %collective-permute-start.13 = (bf16[2,6,64,384]{3,2,1,0:T(8,128)(2,1)S(1)}, bf16[2,6,64,384]{3,2,1,0:T(8,128)(2,1)S(1)}, u32[]{:S(2)}, u32[]{:S(2)}) collective-permute-start(bf16[2,6,64,384]{3,2,1,0:T(8,128)(2,1)S(1)} %get-tuple-element.32), channel_id=1, source_target_pairs={{0,16},{16,32},{32,48},{48,64},{64,80},{80,96},{96,112},{112,0},{1... | collective-permute-start | bytes 1769480 | tf_op jit(solution)/shard_map/ppermute | solution.py:134
  74.7 0.0 copy-done.1
  74.7 3.0 %shard_map.59 = (f32[96,3072]{1,0:T(8,128)S(1)}, bf16[96,3072]{1,0:T(8,128)(2,1)S(1)}, bf16[96,3072]{1,0:T(8,128)(2,1)S(1)}, bf16[96,3072]{1,0:T(8,128)(2,1)S(1)}) custom-call(bf16[384,384]{1,0:T(8,128)(2,1)S(1)} %get-tuple-element.24.rows, bf16[3072,384]{1,0:T(8,128)(2,1)S(1)} %copy-done.1), custom_call_target="tpu_custom_call" | custom-call | tf_op jit(solution)/shard_map/pallas_call | solution.py:76
  77.7 4.6 %collective-permute-start.10 = (bf16[96,3072]{1,0:T(8,128)(2,1)S(1)}, bf16[96,3072]{1,0:T(8,128)(2,1)S(1)}, u32[]{:S(2)}, u32[]{:S(2)}) collective-permute-start(bf16[96,3072]{1,0:T(8,128)(2,1)S(1)} %get-tuple-element.27), channel_id=1, source_target_pairs={{0,12},{4,0},{8,4},{12,8},{1,13},{5,1},{9,5},{13,9},{2,14},{6,2},{... | collective-permute-start | bytes 1769480 | tf_op jit(solution)/shard_map/ppermute | solution.py:134
  82.3 6.3 %collective-permute-start.16 = (bf16[6,64,384]{2,1,0:T(8,128)(2,1)}, bf16[6,64,384]{2,1,0:T(8,128)(2,1)S(1)}, u32[]{:S(2)}, u32[]{:S(2)}) collective-permute-start(bf16[6,64,384]{2,1,0:T(8,128)(2,1)} %bitcast.9), channel_id=1, source_target_pairs={{0,64},{1,65},{16,80},{17,81},{32,96},{33,97},{48,112},{49,113},{6... | collective-permute-start | bytes 884744 | tf_op jit(solution)/shard_map/ppermute | solution.py:185
  88.6 1.9 %collective-permute-start.11 = (bf16[96,3072]{1,0:T(8,128)(2,1)S(1)}, bf16[96,3072]{1,0:T(8,128)(2,1)S(1)}, u32[]{:S(2)}, u32[]{:S(2)}) collective-permute-start(bf16[96,3072]{1,0:T(8,128)(2,1)S(1)} %get-tuple-element.28), channel_id=1, source_target_pairs={{0,4},{4,8},{8,12},{12,0},{1,5},{5,9},{9,13},{13,1},{2,6},{6,10},{... | collective-permute-start | bytes 1769480 | tf_op jit(solution)/shard_map/ppermute | solution.py:134
  90.5 0.0 collective-permute-done.14.down
  90.5 3.4 %collective-permute-start.9 = (bf16[96,3072]{1,0:T(8,128)(2,1)S(1)}, bf16[96,3072]{1,0:T(8,128)(2,1)S(1)}, u32[]{:S(2)}, u32[]{:S(2)}) collective-permute-start(bf16[96,3072]{1,0:T(8,128)(2,1)S(1)} %get-tuple-element.26), channel_id=1, source_target_pairs={{0,8},{4,12},{8,0},{12,4},{1,9},{5,13},{9,1},{13,5},{2,10},{6,14},... | collective-permute-start | bytes 1769480 | tf_op jit(solution)/shard_map/ppermute | solution.py:134
  93.9 0.8 fusion.1
  94.7 5.6 %collective-permute-done.13.up = bf16[2,6,64,384]{3,2,1,0:T(8,128)(2,1)S(1)} collective-permute-done((bf16[2,6,64,384]{3,2,1,0:T(8,128)(2,1)S(1)}, bf16[2,6,64,384]{3,2,1,0:T(8,128)(2,1)S(1)}, u32[]{:S(2)}, u32[]{:S(2)}) %collective-permute-start.13) | collective-permute-done | bytes 589856 | tf_op jit(solution)/shard_map/ppermute | solution.py:134
  100.3 1.9 %collective-permute-start.17 = (bf16[6,64,384]{2,1,0:T(8,128)(2,1)}, bf16[6,64,384]{2,1,0:T(8,128)(2,1)S(1)}, u32[]{:S(2)}, u32[]{:S(2)}) collective-permute-start(bf16[6,64,384]{2,1,0:T(8,128)(2,1)} %fusion.1), channel_id=1, source_target_pairs={{0,96},{16,112},{32,0},{48,16},{64,32},{80,48},{96,64},{112,80},{1... | collective-permute-start | bytes 884744 | tf_op jit(solution)/shard_map/ppermute | solution.py:134
  102.2 0.8 fusion
  103.0 0.0 collective-permute-done.10.rest_1_
  103.0 4.8 %collective-permute-start.15 = (bf16[6,64,384]{2,1,0:T(8,128)(2,1)}, bf16[6,64,384]{2,1,0:T(8,128)(2,1)S(1)}, u32[]{:S(2)}, u32[]{:S(2)}) collective-permute-start(bf16[6,64,384]{2,1,0:T(8,128)(2,1)} %fusion), channel_id=1, source_target_pairs={{0,32},{16,48},{32,64},{48,80},{64,96},{80,112},{96,0},{112,16},{1... | collective-permute-start | bytes 884744 | tf_op jit(solution)/shard_map/ppermute | solution.py:134
  107.8 10.7 %collective-permute-done.11.rest_2_ = bf16[96,3072]{1,0:T(8,128)(2,1)S(1)} collective-permute-done((bf16[96,3072]{1,0:T(8,128)(2,1)S(1)}, bf16[96,3072]{1,0:T(8,128)(2,1)S(1)}, u32[]{:S(2)}, u32[]{:S(2)}) %collective-permute-start.11) | collective-permute-done | bytes 589856 | tf_op jit(solution)/shard_map/ppermute | solution.py:134
  118.5 0.0 collective-permute-done.9.rest_0_
  118.5 0.3 shard_map.60
  118.8 1.9 %collective-permute-start.12 = (bf16[48,3072]{1,0:T(8,128)(2,1)S(1)}, bf16[48,3072]{1,0:T(8,128)(2,1)}, u32[]{:S(2)}, u32[]{:S(2)}) collective-permute-start(bf16[48,3072]{1,0:T(8,128)(2,1)S(1)} %get-tuple-element.30), channel_id=1, source_target_pairs={{0,642},{2,640},{128,514},{130,512},{256,386},{258,384},{384,258},... | collective-permute-start | bytes 884744 | tf_op jit(solution)/shard_map/ppermute | solution.py:153
  120.8 0.1 pad_add_fusion.1.where
  120.9 0.0 collective-permute-done.16.got4
  120.9 0.0 collective-permute-done.17.got6
  120.9 0.0 collective-permute-done.15.got2
  120.9 0.8 shard_map.61
  121.7 1.9 %collective-permute-start.18 = (bf16[2,64,384]{2,1,0:T(8,128)(2,1)S(1)}, bf16[2,64,384]{2,1,0:T(8,128)(2,1)S(1)}, u32[]{:S(2)}, u32[]{:S(2)}) collective-permute-start(bf16[2,64,384]{2,1,0:T(8,128)(2,1)S(1)} %get-tuple-element.38), channel_id=1, source_target_pairs={{0,128},{128,256},{256,0},{384,512},{512,640},{640,384},{1,129},{1... | collective-permute-start | bytes 294920 | tf_op jit(solution)/shard_map/ppermute | solution.py:223
  123.6 3.9 %collective-permute-start.19 = (bf16[2,64,384]{2,1,0:T(8,128)(2,1)S(1)}, bf16[2,64,384]{2,1,0:T(8,128)(2,1)S(1)}, u32[]{:S(2)}, u32[]{:S(2)}) collective-permute-start(bf16[2,64,384]{2,1,0:T(8,128)(2,1)S(1)} %get-tuple-element.39), channel_id=1, source_target_pairs={{0,256},{128,0},{256,128},{384,640},{512,384},{640,512},{1,257},{1... | collective-permute-start | bytes 294920 | tf_op jit(solution)/shard_map/ppermute | solution.py:223
  127.5 2.2 %collective-permute-done.18.rest_0_ = bf16[2,64,384]{2,1,0:T(8,128)(2,1)S(1)} collective-permute-done((bf16[2,64,384]{2,1,0:T(8,128)(2,1)S(1)}, bf16[2,64,384]{2,1,0:T(8,128)(2,1)S(1)}, u32[]{:S(2)}, u32[]{:S(2)}) %collective-permute-start.18) | collective-permute-done | bytes 98336 | tf_op jit(solution)/shard_map/ppermute | solution.py:223
  129.7 11.1 %collective-permute-done.19.rest_1_ = bf16[2,64,384]{2,1,0:T(8,128)(2,1)S(1)} collective-permute-done((bf16[2,64,384]{2,1,0:T(8,128)(2,1)S(1)}, bf16[2,64,384]{2,1,0:T(8,128)(2,1)S(1)}, u32[]{:S(2)}, u32[]{:S(2)}) %collective-permute-start.19) | collective-permute-done | bytes 98336 | tf_op jit(solution)/shard_map/ppermute | solution.py:223
  140.8 0.6 shard_map.62
  141.4 1.9 %collective-permute-start.20 = (bf16[64,384]{1,0:T(8,128)(2,1)S(1)}, bf16[64,384]{1,0:T(8,128)(2,1)S(1)}, u32[]{:S(2)}, u32[]{:S(2)}) collective-permute-start(bf16[64,384]{1,0:T(8,128)(2,1)S(1)} %get-tuple-element.41), channel_id=1, source_target_pairs={{0,384},{128,512},{256,640},{384,0},{512,128},{640,256},{1,385},{1... | collective-permute-start | bytes 147464 | tf_op jit(solution)/shard_map/ppermute | solution.py:134
  143.3 0.0 collective-permute-done.12
  143.3 1.7 %add_convert_fusion.2 = bf16[48,3072]{1,0:T(8,128)(2,1)} fusion(f32[48,3072]{1,0:T(8,128)S(1)} %get-tuple-element.29, bf16[48,3072]{1,0:T(8,128)(2,1)} %collective-permute-done.12), kind=kLoop, calls=%fused_computation.2 | loop fusion | flops 442368 | bytes 1179648 | tf_op jit(solution)/shard_map/convert_element_type | solution.py:203
  145.1 5.3 %collective-permute-done.20 = bf16[64,384]{1,0:T(8,128)(2,1)S(1)} collective-permute-done((bf16[64,384]{1,0:T(8,128)(2,1)S(1)}, bf16[64,384]{1,0:T(8,128)(2,1)S(1)}, u32[]{:S(2)}, u32[]{:S(2)}) %collective-permute-start.20) | collective-permute-done | bytes 49184 | tf_op jit(solution)/shard_map/ppermute | solution.py:134
  150.4 0.7 convert_add_fusion
  (6 shorter events, 0.1 us)
Async XLA Ops:
  0.6 38.6 %collective-permute-start = (bf16[48,3072]{1,0:T(8,128)(2,1)}, bf16[48,3072]{1,0:T(8,128)(2,1)S(1)}, u32[]{:S(2)}, u32[]{:S(2)}) collective-permute-start(bf16[48,3072]{1,0:T(8,128)(2,1)} %param.4), channel_id=1, source_target_pairs={{0,642},{2,640},{128,514},{130,512},{256,386},{258,384},{384,258},... | collective-permute-start | bytes 884744 | tf_op jit(solution)/shard_map/ppermute | solution.py:153
  13.4 31.3 %collective-permute-start.2 = (bf16[48,3072]{1,0:T(8,128)(2,1)}, bf16[48,3072]{1,0:T(8,128)(2,1)}, u32[]{:S(2)}, u32[]{:S(2)}) collective-permute-start(bf16[48,3072]{1,0:T(8,128)(2,1)} %param.4), channel_id=1, source_target_pairs={{0,4},{4,8},{8,12},{12,0},{1,5},{5,9},{9,13},{13,1},{2,6},{6,10},{... | collective-permute-start | bytes 884744 | tf_op jit(solution)/shard_map/ppermute | solution.py:134
  16.8 38.3 %collective-permute-start.4 = (bf16[48,3072]{1,0:T(8,128)(2,1)}, bf16[48,3072]{1,0:T(8,128)(2,1)S(1)}, u32[]{:S(2)}, u32[]{:S(2)}) collective-permute-start(bf16[48,3072]{1,0:T(8,128)(2,1)} %param.4), channel_id=1, source_target_pairs={{0,8},{4,12},{8,0},{12,4},{1,9},{5,13},{9,1},{13,5},{2,10},{6,14},... | collective-permute-start | bytes 884744 | tf_op jit(solution)/shard_map/ppermute | solution.py:134
  21.4 33.7 %collective-permute-start.6 = (bf16[48,3072]{1,0:T(8,128)(2,1)}, bf16[48,3072]{1,0:T(8,128)(2,1)S(1)}, u32[]{:S(2)}, u32[]{:S(2)}) collective-permute-start(bf16[48,3072]{1,0:T(8,128)(2,1)} %param.4), channel_id=1, source_target_pairs={{0,12},{4,0},{8,4},{12,8},{1,13},{5,1},{9,5},{13,9},{2,14},{6,2},{... | collective-permute-start | bytes 884744 | tf_op jit(solution)/shard_map/ppermute | solution.py:134
  25.8 31.7 %copy-start = (bf16[3072,384]{1,0:T(8,128)(2,1)S(1)}, bf16[3072,384]{1,0:T(8,128)(2,1)}, u32[]{:S(2)}) copy-start(bf16[3072,384]{1,0:T(8,128)(2,1)} %weight.1) | copy-start | bytes 7077892
  25.8 13.4 %collective-permute-start.1 = (bf16[4,48,384]{2,1,0:T(8,128)(2,1)S(1)}, bf16[4,48,384]{2,1,0:T(8,128)(2,1)S(1)}, u32[]{:S(2)}, u32[]{:S(2)}) collective-permute-start(bf16[4,48,384]{2,1,0:T(8,128)(2,1)S(1)} %get-tuple-element.43), channel_id=1, source_target_pairs={{0,640},{128,512},{256,384},{384,256},{512,128},{640,0},{1,641},{1... | collective-permute-start | bytes 442376 | tf_op jit(solution)/shard_map/ppermute | solution.py:159
  39.2 15.9 %collective-permute-start.3 = (bf16[48,3072]{1,0:T(8,128)(2,1)S(1)}, bf16[48,3072]{1,0:T(8,128)(2,1)S(1)}, u32[]{:S(2)}, u32[]{:S(2)}) collective-permute-start(bf16[48,3072]{1,0:T(8,128)(2,1)S(1)} %collective-permute-done), channel_id=1, source_target_pairs={{0,4},{4,8},{8,12},{12,0},{1,5},{5,9},{9,13},{13,1},{2,6},{6,10},{... | collective-permute-start | bytes 884744 | tf_op jit(solution)/shard_map/ppermute | solution.py:134
  41.7 13.4 %collective-permute-start.5 = (bf16[48,3072]{1,0:T(8,128)(2,1)S(1)}, bf16[48,3072]{1,0:T(8,128)(2,1)S(1)}, u32[]{:S(2)}, u32[]{:S(2)}) collective-permute-start(bf16[48,3072]{1,0:T(8,128)(2,1)S(1)} %collective-permute-done), channel_id=1, source_target_pairs={{0,8},{4,12},{8,0},{12,4},{1,9},{5,13},{9,1},{13,5},{2,10},{6,14},... | collective-permute-start | bytes 884744 | tf_op jit(solution)/shard_map/ppermute | solution.py:134
  44.7 12.9 %collective-permute-start.7 = (bf16[48,3072]{1,0:T(8,128)(2,1)S(1)}, bf16[48,3072]{1,0:T(8,128)(2,1)S(1)}, u32[]{:S(2)}, u32[]{:S(2)}) collective-permute-start(bf16[48,3072]{1,0:T(8,128)(2,1)S(1)} %collective-permute-done), channel_id=1, source_target_pairs={{0,12},{4,0},{8,4},{12,8},{1,13},{5,1},{9,5},{13,9},{2,14},{6,2},{... | collective-permute-start | bytes 884744 | tf_op jit(solution)/shard_map/ppermute | solution.py:134
  57.6 5.5 %copy-start.2 = (f32[128]{0:T(128)S(1)}, f32[128]{0:T(128)}, u32[]{:S(2)}) copy-start(f32[128]{0:T(128)} %param.7) | copy-start | bytes 1540
  59.0 4.0 %collective-permute-start.8 = (f32[384,384]{1,0:T(8,128)S(1)}, f32[384,384]{1,0:T(8,128)}, u32[]{:S(2)}, u32[]{:S(2)}) collective-permute-start(f32[384,384]{1,0:T(8,128)S(1)} %fusion.2.mine), channel_id=1, source_target_pairs={{0,1},{1,0},{2,3},{3,2},{4,5},{5,4},{6,7},{7,6},{8,9},{9,8},{10,11... | collective-permute-start | bytes 1769480 | tf_op jit(solution)/shard_map/ppermute | solution.py:134
  60.9 13.7 %copy-start.1 = (bf16[3072,384]{1,0:T(8,128)(2,1)S(1)}, bf16[3072,384]{1,0:T(8,128)(2,1)}, u32[]{:S(2)}) copy-start(bf16[3072,384]{1,0:T(8,128)(2,1)} %weight.1) | copy-start | bytes 7077892
  67.4 23.1 %collective-permute-start.14 = (bf16[2,6,64,384]{3,2,1,0:T(8,128)(2,1)S(1)}, bf16[2,6,64,384]{3,2,1,0:T(8,128)(2,1)S(1)}, u32[]{:S(2)}, u32[]{:S(2)}) collective-permute-start(bf16[2,6,64,384]{3,2,1,0:T(8,128)(2,1)S(1)} %get-tuple-element.33), channel_id=1, source_target_pairs={{0,112},{16,0},{32,16},{48,32},{64,48},{80,64},{96,80},{112,96},{1... | collective-permute-start | bytes 1769480 | tf_op jit(solution)/shard_map/ppermute | solution.py:134
  72.7 27.6 %collective-permute-start.13 = (bf16[2,6,64,384]{3,2,1,0:T(8,128)(2,1)S(1)}, bf16[2,6,64,384]{3,2,1,0:T(8,128)(2,1)S(1)}, u32[]{:S(2)}, u32[]{:S(2)}) collective-permute-start(bf16[2,6,64,384]{3,2,1,0:T(8,128)(2,1)S(1)} %get-tuple-element.32), channel_id=1, source_target_pairs={{0,16},{16,32},{32,48},{48,64},{64,80},{80,96},{96,112},{112,0},{1... | collective-permute-start | bytes 1769480 | tf_op jit(solution)/shard_map/ppermute | solution.py:134
  77.7 25.3 %collective-permute-start.10 = (bf16[96,3072]{1,0:T(8,128)(2,1)S(1)}, bf16[96,3072]{1,0:T(8,128)(2,1)S(1)}, u32[]{:S(2)}, u32[]{:S(2)}) collective-permute-start(bf16[96,3072]{1,0:T(8,128)(2,1)S(1)} %get-tuple-element.27), channel_id=1, source_target_pairs={{0,12},{4,0},{8,4},{12,8},{1,13},{5,1},{9,5},{13,9},{2,14},{6,2},{... | collective-permute-start | bytes 1769480 | tf_op jit(solution)/shard_map/ppermute | solution.py:134
  82.3 38.6 %collective-permute-start.16 = (bf16[6,64,384]{2,1,0:T(8,128)(2,1)}, bf16[6,64,384]{2,1,0:T(8,128)(2,1)S(1)}, u32[]{:S(2)}, u32[]{:S(2)}) collective-permute-start(bf16[6,64,384]{2,1,0:T(8,128)(2,1)} %bitcast.9), channel_id=1, source_target_pairs={{0,64},{1,65},{16,80},{17,81},{32,96},{33,97},{48,112},{49,113},{6... | collective-permute-start | bytes 884744 | tf_op jit(solution)/shard_map/ppermute | solution.py:185
  88.6 30.0 %collective-permute-start.11 = (bf16[96,3072]{1,0:T(8,128)(2,1)S(1)}, bf16[96,3072]{1,0:T(8,128)(2,1)S(1)}, u32[]{:S(2)}, u32[]{:S(2)}) collective-permute-start(bf16[96,3072]{1,0:T(8,128)(2,1)S(1)} %get-tuple-element.28), channel_id=1, source_target_pairs={{0,4},{4,8},{8,12},{12,0},{1,5},{5,9},{9,13},{13,1},{2,6},{6,10},{... | collective-permute-start | bytes 1769480 | tf_op jit(solution)/shard_map/ppermute | solution.py:134
  90.5 28.1 %collective-permute-start.9 = (bf16[96,3072]{1,0:T(8,128)(2,1)S(1)}, bf16[96,3072]{1,0:T(8,128)(2,1)S(1)}, u32[]{:S(2)}, u32[]{:S(2)}) collective-permute-start(bf16[96,3072]{1,0:T(8,128)(2,1)S(1)} %get-tuple-element.26), channel_id=1, source_target_pairs={{0,8},{4,12},{8,0},{12,4},{1,9},{5,13},{9,1},{13,5},{2,10},{6,14},... | collective-permute-start | bytes 1769480 | tf_op jit(solution)/shard_map/ppermute | solution.py:134
  100.3 20.6 %collective-permute-start.17 = (bf16[6,64,384]{2,1,0:T(8,128)(2,1)}, bf16[6,64,384]{2,1,0:T(8,128)(2,1)S(1)}, u32[]{:S(2)}, u32[]{:S(2)}) collective-permute-start(bf16[6,64,384]{2,1,0:T(8,128)(2,1)} %fusion.1), channel_id=1, source_target_pairs={{0,96},{16,112},{32,0},{48,16},{64,32},{80,48},{96,64},{112,80},{1... | collective-permute-start | bytes 884744 | tf_op jit(solution)/shard_map/ppermute | solution.py:134
  103.0 17.9 %collective-permute-start.15 = (bf16[6,64,384]{2,1,0:T(8,128)(2,1)}, bf16[6,64,384]{2,1,0:T(8,128)(2,1)S(1)}, u32[]{:S(2)}, u32[]{:S(2)}) collective-permute-start(bf16[6,64,384]{2,1,0:T(8,128)(2,1)} %fusion), channel_id=1, source_target_pairs={{0,32},{16,48},{32,64},{48,80},{64,96},{80,112},{96,0},{112,16},{1... | collective-permute-start | bytes 884744 | tf_op jit(solution)/shard_map/ppermute | solution.py:134
  118.8 24.5 %collective-permute-start.12 = (bf16[48,3072]{1,0:T(8,128)(2,1)S(1)}, bf16[48,3072]{1,0:T(8,128)(2,1)}, u32[]{:S(2)}, u32[]{:S(2)}) collective-permute-start(bf16[48,3072]{1,0:T(8,128)(2,1)S(1)} %get-tuple-element.30), channel_id=1, source_target_pairs={{0,642},{2,640},{128,514},{130,512},{256,386},{258,384},{384,258},... | collective-permute-start | bytes 884744 | tf_op jit(solution)/shard_map/ppermute | solution.py:153
  121.7 8.1 %collective-permute-start.18 = (bf16[2,64,384]{2,1,0:T(8,128)(2,1)S(1)}, bf16[2,64,384]{2,1,0:T(8,128)(2,1)S(1)}, u32[]{:S(2)}, u32[]{:S(2)}) collective-permute-start(bf16[2,64,384]{2,1,0:T(8,128)(2,1)S(1)} %get-tuple-element.38), channel_id=1, source_target_pairs={{0,128},{128,256},{256,0},{384,512},{512,640},{640,384},{1,129},{1... | collective-permute-start | bytes 294920 | tf_op jit(solution)/shard_map/ppermute | solution.py:223
  123.6 17.2 %collective-permute-start.19 = (bf16[2,64,384]{2,1,0:T(8,128)(2,1)S(1)}, bf16[2,64,384]{2,1,0:T(8,128)(2,1)S(1)}, u32[]{:S(2)}, u32[]{:S(2)}) collective-permute-start(bf16[2,64,384]{2,1,0:T(8,128)(2,1)S(1)} %get-tuple-element.39), channel_id=1, source_target_pairs={{0,256},{128,0},{256,128},{384,640},{512,384},{640,512},{1,257},{1... | collective-permute-start | bytes 294920 | tf_op jit(solution)/shard_map/ppermute | solution.py:223
  141.4 9.0 %collective-permute-start.20 = (bf16[64,384]{1,0:T(8,128)(2,1)S(1)}, bf16[64,384]{1,0:T(8,128)(2,1)S(1)}, u32[]{:S(2)}, u32[]{:S(2)}) collective-permute-start(bf16[64,384]{1,0:T(8,128)(2,1)S(1)} %get-tuple-element.41), channel_id=1, source_target_pairs={{0,384},{128,512},{256,640},{384,0},{512,128},{640,256},{1,385},{1... | collective-permute-start | bytes 147464 | tf_op jit(solution)/shard_map/ppermute | solution.py:134

commit v6 on v5

--- a/solution.py
+++ b/solution.py
@@ -24,11 +24,10 @@
     count = cot.shape[1]
     heads = mine.shape[1]
     hd = gain.shape[1]
-    for kx in range(nx):
-        block = lax.rem(x - kx + nx, nx)
-        for kh in range(nh):
-            span = pl.ds((kx * nh + kh) * count, count)
-            side = (cot, cot_far)[kh]
+    for kh, side in enumerate((cot, cot_far)):
+        for kx in range(nx):
+            block = lax.rem(x - kx + nx, nx)
+            span = pl.ds((kh * nx + kx) * count, count)
             for h in range(0, heads, hd):
                 pre = mine[span, h : h + hd] + theirs[span, h : h + hd]
                 centred = pre - mean(pre)
@@ -83,35 +82,39 @@
     )(*scalars, *operands)
 
 
-def backs_kernel(rows, weight, *outs):
+def backs_kernel(base, rows, weight, *outs):
     count = outs[0].shape[0]
     for k, out in enumerate(outs):
         out[...] = lax.dot_general(
-            rows[k * count : (k + 1) * count, :],
+            rows[base + k * count : base + (k + 1) * count, :],
             weight[...],
             (((1,), (1,)), ((), ())),
             preferred_element_type=F32,
         ).astype(out.dtype)
 
 
-def back_sum_kernel(first, *rest):
-    terms, (near, far) = rest[:-2], rest[-2:]
-    count = near.shape[0]
-    for span, out in ((pl.ds(0, count), near), (pl.ds(count, count), far)):
-        total = first[span, :]
-        for t in terms:
-            total = total + t[span, :].astype(F32)
-        out[...] = total.astype(out.dtype)
-
-
-def over_y_kernel(where, own, up, down, got2, got4, got6, kept, *sends):
+def sum_kernel(*refs):
+    total = refs[0][...].astype(F32)
+    for t in refs[1:-1]:
+        total = total + t[...].astype(F32)
+    refs[-1][...] = total.astype(refs[-1].dtype)
+
+
+def relay_kernel(where, two, six, up, down, across, out_two, out_six):
+    core = where[0]
+    from4 = across[...].astype(F32)
+    keep = jnp.where(core == 0, 1.0, 0.0)
+    out_two[...] = (two[0].astype(F32) + up[0].astype(F32) + keep * from4).astype(BF16)
+    out_six[...] = (six[0].astype(F32) + down[0].astype(F32) + (1.0 - keep) * from4).astype(BF16)
+
+
+def over_y_kernel(where, own, up, down, got2, got6, kept, *sends):
     count, third = kept.shape[0], len(sends) + 1
     for k in range(third):
         place = lax.rem(where[0] + k, third)
         for i in range(count):
             z = i * third + place
-            total = own[0, z].astype(F32) + got4[z].astype(F32)
-            total = total + (up[1, z].astype(F32) + down[1, z].astype(F32))
+            total = own[0, z].astype(F32) + (up[1, z].astype(F32) + down[1, z].astype(F32))
             total = total + (got2[z].astype(F32) + got6[z].astype(F32))
             if k:
                 sends[k - 1][i] = total.astype(BF16)
@@ -160,7 +163,7 @@
     cot = lax.dynamic_index_in_dim(cot, zh, 1, False)
     peer, cot_far = lax.optimization_barrier((peer, cot_far))
     other = [peer] + [shift(peer, "x", k) for k in (1, 2, 3)]
-    tokens = jnp.concatenate([p for pair in zip(own, other) for p in pair], axis=0)
+    tokens = jnp.concatenate(own + other, axis=0)
 
     mine = jnp.dot(tokens, weight, preferred_element_type=F32)
     theirs = shift(mine, "c", 1)
@@ -179,28 +182,33 @@
 
     up, down, across, two, six, own = c
     turn = [
-        (i * 2 + j, (i + (4, -4)[j]) % ny * 2 + j) for i in range(ny) for j in range(2)
+        (i * 2 + j, (i + (2, -2)[j]) % ny * 2 + j) for i in range(ny) for j in range(2)
     ]
     got_up, got_down = shift(up, "y", 1), shift(down, "y", -1)
     got4 = lax.ppermute(across[0], ("y", "c"), turn)
-    two = add(two[0], got_up[0]).astype(BF16)
-    six = add(six[0], got_down[0]).astype(BF16)
+    core = lax.axis_index("c").astype(jnp.int32).reshape(1)
+    chunk = jax.ShapeDtypeStruct(got4.shape, BF16)
+    relay = small_call(
+        relay_kernel, [chunk, chunk], two, six, got_up, got_down, got4, where=core
+    )
+
+    block = (count, width)
+
+    def over_x(rows, base):
+        back = small_call(
+            functools.partial(backs_kernel, base),
+            [jax.ShapeDtypeStruct(block, F32)] + [jax.ShapeDtypeStruct(block, BF16)] * (nx - 1),
+            rows,
+            weight,
+        )
+        return [back[0]] + [shift(back[k], "x", -k) for k in (2, 1, 3)]
+
+    total = jax.ShapeDtypeStruct(block, BF16)
+    far = small_call(sum_kernel, [total], *over_x(rows, nx * count))[0]
+    rows, two, six = lax.optimization_barrier((rows, *relay))
     got2, got6 = shift(two, "y", 2), shift(six, "y", -2)
-
-    block = (nh * count, width)
-    back = small_call(
-        backs_kernel,
-        [jax.ShapeDtypeStruct(block, F32)] + [jax.ShapeDtypeStruct(block, BF16)] * (nx - 1),
-        rows,
-        weight,
-    )
-    near, far = small_call(
-        back_sum_kernel,
-        [jax.ShapeDtypeStruct((count, width), t) for t in (F32, BF16)],
-        back[0],
-        *[shift(back[k], "x", -k) for k in (2, 1, 3)],
-    )
-    input_grad = add(near, mirror(far)).astype(BF16)
+    near = over_x(rows, 0)
+    far = mirror(far)
 
     third = nz // 2
     zl = lax.axis_index("zl")
@@ -213,10 +221,10 @@
         got_up,
         got_down,
         got2,
-        got4,
         got6,
         where=spot,
     )
+    near[1], *sends = lax.optimization_barrier((near[1], *sends))
     got = []
     for k in range(1, third):
         hop = [(i, i // third * third + (i + k) % third) for i in range(nz)]
@@ -228,6 +236,7 @@
         *got,
         where=spot,
     )
+    input_grad = small_call(sum_kernel, [total], *near, far)[0]
     weight_grad = add(stay, shift(send, "zl", third))
     return (input_grad, weight_grad)
 

time: 152 us -> 162 us (1.066)
  the two profiles are of different devices: /device:TPU:128 before, /device:TPU:136 now
where the time goes in v6:
time: 162 us; the launch traced here: 160 us
  starting transfers between devices  95.8 us (59%)
  waiting for transfers between devices  29.5 us (18%)
  Pallas kernels  17 us (10%)
  local copies, waits for them, and re-layouts  14.8 us (9%)
    ppermute x18, starting transfers between devices, shift(): lax.ppermute(value, axis, [(i, (i + by) % size) for i in range(size)])  66.4 us
    ppermute x2, starting transfers between devices, mirror(): return lax.ppermute(value, ('zl', 'zh'), ends)  14.7 us
    unnamed x47, local copies, waits for them, and re-layouts  13.8 us
    pallas_call x7, Pallas kernels, small_call(): pl.pallas_call(kernel, out_shape=out_shape, in_specs=[pl.BlockSpec(memory...  12.3 us
    ppermute x18, waiting for transfers between devices, shift(): lax.ppermute(value, axis, [(i, (i + by) % size) for i in range(size)])  11.4 us
    ppermute x1, waiting for transfers between devices, body(): cot_far = lax.ppermute(cot_far, 'zl', [(i, nz - 1 - i) for i in range(nz)])  9.16 us
    ppermute x2, starting transfers between devices, body(): got.append(lax.ppermute(sends[k - 1], 'zl', hop))  5.84 us
    ppermute x1, starting transfers between devices, body(): got4 = lax.ppermute(across[0], ('y', 'c'), turn)  5.71 us
  transfers between devices with their start and end apart: 24, of which 8 were waited for; matrix products, arithmetic and copies ran while one was open for 2% of the time, Pallas kernels for 8%

profile of v6, /device:TPU:136, one launch (start us, length us, event | category | flops | bytes accessed | tf_op | source)
XLA Modules:
  0.0 160.5 jit_solution(11617007127359666367)
XLA Ops:
  0.6 12.7 %collective-permute-start.3 = (bf16[48,3072]{1,0:T(8,128)(2,1)}, bf16[48,3072]{1,0:T(8,128)(2,1)S(1)}, u32[]{:S(2)}, u32[]{:S(2)}) collective-permute-start(bf16[48,3072]{1,0:T(8,128)(2,1)} %param.4), channel_id=1, source_target_pairs={{0,642},{2,640},{128,514},{130,512},{256,386},{258,384},{384,258},... | collective-permute-start | bytes 884744 | tf_op jit(solution)/shard_map/ppermute | solution.py:156
  13.4 3.4 %collective-permute-start = (bf16[48,3072]{1,0:T(8,128)(2,1)}, bf16[48,3072]{1,0:T(8,128)(2,1)}, u32[]{:S(2)}, u32[]{:S(2)}) collective-permute-start(bf16[48,3072]{1,0:T(8,128)(2,1)} %param.4), channel_id=1, source_target_pairs={{0,4},{4,8},{8,12},{12,0},{1,5},{5,9},{9,13},{13,1},{2,6},{6,10},{... | collective-permute-start | bytes 884744 | tf_op jit(solution)/shard_map/ppermute | solution.py:137
  16.8 4.6 %collective-permute-start.1 = (bf16[48,3072]{1,0:T(8,128)(2,1)}, bf16[48,3072]{1,0:T(8,128)(2,1)S(1)}, u32[]{:S(2)}, u32[]{:S(2)}) collective-permute-start(bf16[48,3072]{1,0:T(8,128)(2,1)} %param.4), channel_id=1, source_target_pairs={{0,8},{4,12},{8,0},{12,4},{1,9},{5,13},{9,1},{13,5},{2,10},{6,14},... | collective-permute-start | bytes 884744 | tf_op jit(solution)/shard_map/ppermute | solution.py:137
  21.4 3.3 %collective-permute-start.2 = (bf16[48,3072]{1,0:T(8,128)(2,1)}, bf16[48,3072]{1,0:T(8,128)(2,1)S(1)}, u32[]{:S(2)}, u32[]{:S(2)}) collective-permute-start(bf16[48,3072]{1,0:T(8,128)(2,1)} %param.4), channel_id=1, source_target_pairs={{0,12},{4,0},{8,4},{12,8},{1,13},{5,1},{9,5},{13,9},{2,14},{6,2},{... | collective-permute-start | bytes 884744 | tf_op jit(solution)/shard_map/ppermute | solution.py:137
  24.8 1.0 dynamic-slice_bitcast_fusion
  25.8 0.0 copy-start
  25.8 3.2 %collective-permute-start.4 = (bf16[4,48,384]{2,1,0:T(8,128)(2,1)S(1)}, bf16[4,48,384]{2,1,0:T(8,128)(2,1)S(1)}, u32[]{:S(2)}, u32[]{:S(2)}) collective-permute-start(bf16[4,48,384]{2,1,0:T(8,128)(2,1)S(1)} %get-tuple-element.63), channel_id=1, source_target_pairs={{0,640},{128,512},{256,384},{384,256},{512,128},{640,0},{1,641},{1... | collective-permute-start | bytes 442376 | tf_op jit(solution)/shard_map/ppermute | solution.py:162
  29.0 1.0 constant_dynamic-update-slice_fusion.7
  30.0 9.2 %collective-permute-done.4.cot_far = bf16[4,48,384]{2,1,0:T(8,128)(2,1)S(1)} collective-permute-done((bf16[4,48,384]{2,1,0:T(8,128)(2,1)S(1)}, bf16[4,48,384]{2,1,0:T(8,128)(2,1)S(1)}, u32[]{:S(2)}, u32[]{:S(2)}) %collective-permute-start.4) | collective-permute-done | bytes 147488 | tf_op jit(solution)/shard_map/ppermute | solution.py:162
  39.2 0.0 collective-permute-done.3
  39.2 2.5 %collective-permute-start.5 = (bf16[48,3072]{1,0:T(8,128)(2,1)S(1)}, bf16[48,3072]{1,0:T(8,128)(2,1)S(1)}, u32[]{:S(2)}, u32[]{:S(2)}) collective-permute-start(bf16[48,3072]{1,0:T(8,128)(2,1)S(1)} %collective-permute-done.3), channel_id=1, source_target_pairs={{0,4},{4,8},{8,12},{12,0},{1,5},{5,9},{9,13},{13,1},{2,6},{6,10},{... | collective-permute-start | bytes 884744 | tf_op jit(solution)/shard_map/ppermute | solution.py:137
  41.7 2.9 %collective-permute-start.6 = (bf16[48,3072]{1,0:T(8,128)(2,1)S(1)}, bf16[48,3072]{1,0:T(8,128)(2,1)S(1)}, u32[]{:S(2)}, u32[]{:S(2)}) collective-permute-start(bf16[48,3072]{1,0:T(8,128)(2,1)S(1)} %collective-permute-done.3), channel_id=1, source_target_pairs={{0,8},{4,12},{8,0},{12,4},{1,9},{5,13},{9,1},{13,5},{2,10},{6,14},... | collective-permute-start | bytes 884744 | tf_op jit(solution)/shard_map/ppermute | solution.py:137
  44.6 0.0 collective-permute-done
  44.6 3.6 %collective-permute-start.7 = (bf16[48,3072]{1,0:T(8,128)(2,1)S(1)}, bf16[48,3072]{1,0:T(8,128)(2,1)S(1)}, u32[]{:S(2)}, u32[]{:S(2)}) collective-permute-start(bf16[48,3072]{1,0:T(8,128)(2,1)S(1)} %collective-permute-done.3), channel_id=1, source_target_pairs={{0,12},{4,0},{8,4},{12,8},{1,13},{5,1},{9,5},{13,9},{2,14},{6,2},{... | collective-permute-start | bytes 884744 | tf_op jit(solution)/shard_map/ppermute | solution.py:137
  48.2 1.0 constant_dynamic-update-slice_fusion.6
  49.3 5.7 %collective-permute-done.5 = bf16[48,3072]{1,0:T(8,128)(2,1)S(1)} collective-permute-done((bf16[48,3072]{1,0:T(8,128)(2,1)S(1)}, bf16[48,3072]{1,0:T(8,128)(2,1)S(1)}, u32[]{:S(2)}, u32[]{:S(2)}) %collective-permute-start.5) | collective-permute-done | bytes 294944 | tf_op jit(solution)/shard_map/ppermute | solution.py:137
  55.1 2.4 %collective-permute-done.7 = bf16[48,3072]{1,0:T(8,128)(2,1)S(1)} collective-permute-done((bf16[48,3072]{1,0:T(8,128)(2,1)S(1)}, bf16[48,3072]{1,0:T(8,128)(2,1)S(1)}, u32[]{:S(2)}, u32[]{:S(2)}) %collective-permute-start.7) | collective-permute-done | bytes 294944 | tf_op jit(solution)/shard_map/ppermute | solution.py:137
  57.6 0.0 copy-start.17
  57.6 1.4 fusion.mine
  59.0 1.9 %collective-permute-start.8 = (f32[384,384]{1,0:T(8,128)S(1)}, f32[384,384]{1,0:T(8,128)}, u32[]{:S(2)}, u32[]{:S(2)}) collective-permute-start(f32[384,384]{1,0:T(8,128)S(1)} %fusion.mine), channel_id=1, source_target_pairs={{0,1},{1,0},{2,3},{3,2},{4,5},{5,4},{6,7},{7,6},{8,9},{9,8},{10,11... | collective-permute-start | bytes 1769480 | tf_op jit(solution)/shard_map/ppermute | solution.py:137
  61.0 0.1 pad_add_fusion.where
  61.0 2.0 %collective-permute-done.8.theirs = f32[384,384]{1,0:T(8,128)} collective-permute-done((f32[384,384]{1,0:T(8,128)S(1)}, f32[384,384]{1,0:T(8,128)}, u32[]{:S(2)}, u32[]{:S(2)}) %collective-permute-start.8) | collective-permute-done | bytes 589856 | tf_op jit(solution)/shard_map/ppermute | solution.py:137
  63.1 1.7 %copy-done.2 = bf16[384,3072]{1,0:T(8,128)(2,1)S(1)} copy-done((bf16[384,3072]{1,0:T(8,128)(2,1)S(1)}, bf16[384,3072]{1,0:T(8,128)(2,1)}, u32[]{:S(2)}) %copy-start.2) | copy-done | bytes 2359320
  64.7 4.6 %rows_and_chunks.1 = (bf16[384,384]{1,0:T(8,128)(2,1)S(1)}, bf16[2,6,64,384]{3,2,1,0:T(8,128)(2,1)}, bf16[2,6,64,384]{3,2,1,0:T(8,128)(2,1)}, bf16[1,6,64,384]{3...) custom-call(s32[2]{0:T(128)S(1)} %pad_add_fusion.where, ...), custom_call_target="tpu_custom_call" | custom-call | tf_op jit(solution)/shard_map/rows_and_chunks/pallas_call | solution.py:61
  69.4 0.7 copy-done.9
  70.1 2.3 %collective-permute-start.10 = (bf16[2,6,64,384]{3,2,1,0:T(8,128)(2,1)}, bf16[2,6,64,384]{3,2,1,0:T(8,128)(2,1)S(1)}, u32[]{:S(2)}, u32[]{:S(2)}) collective-permute-start(bf16[2,6,64,384]{3,2,1,0:T(8,128)(2,1)} %get-tuple-element.38), channel_id=1, source_target_pairs={{0,112},{16,0},{32,16},{48,32},{64,48},{80,64},{96,80},{112,96},{1... | collective-permute-start | bytes 1769480 | tf_op jit(solution)/shard_map/ppermute | solution.py:137
  72.4 3.5 %collective-permute-start.9 = (bf16[2,6,64,384]{3,2,1,0:T(8,128)(2,1)}, bf16[2,6,64,384]{3,2,1,0:T(8,128)(2,1)S(1)}, u32[]{:S(2)}, u32[]{:S(2)}) collective-permute-start(bf16[2,6,64,384]{3,2,1,0:T(8,128)(2,1)} %get-tuple-element.37), channel_id=1, source_target_pairs={{0,16},{16,32},{32,48},{48,64},{64,80},{80,96},{96,112},{112,0},{1... | collective-permute-start | bytes 1769480 | tf_op jit(solution)/shard_map/ppermute | solution.py:137
  75.9 5.7 %collective-permute-start.11 = (bf16[6,64,384]{2,1,0:T(8,128)(2,1)}, bf16[6,64,384]{2,1,0:T(8,128)(2,1)}, u32[]{:S(2)}, u32[]{:S(2)}) collective-permute-start(bf16[6,64,384]{2,1,0:T(8,128)(2,1)} %bitcast.7), channel_id=1, source_target_pairs={{0,32},{1,97},{16,48},{17,113},{32,64},{33,1},{48,80},{49,17},{64,... | collective-permute-start | bytes 884744 | tf_op jit(solution)/shard_map/ppermute | solution.py:188
  81.6 3.0 %shard_map.62 = (f32[48,3072]{1,0:T(8,128)S(1)}, bf16[48,3072]{1,0:T(8,128)(2,1)S(1)}, bf16[48,3072]{1,0:T(8,128)(2,1)}, bf16[48,3072]{1,0:T(8,128)(2,1)S(1)}) custom-call(bf16[384,384]{1,0:T(8,128)(2,1)S(1)} %get-tuple-element.42.rows, bf16[3072,384]{1,0:T(8,128)(2,1)S(1)} %copy-done), custom_call_target="tpu_custom_call" | custom-call | tf_op jit(solution)/shard_map/pallas_call | solution.py:75
  84.7 0.7 copy-done.3
  85.4 0.8 copy-done.5
  86.2 0.7 copy-done.18
  86.9 0.7 copy-done.19
  87.6 3.0 %collective-permute-start.17 = (bf16[48,3072]{1,0:T(8,128)(2,1)}, bf16[48,3072]{1,0:T(8,128)(2,1)}, u32[]{:S(2)}, u32[]{:S(2)}) collective-permute-start(bf16[48,3072]{1,0:T(8,128)(2,1)} %get-tuple-element.54), channel_id=1, source_target_pairs={{0,8},{4,12},{8,0},{12,4},{1,9},{5,13},{9,1},{13,5},{2,10},{6,14},... | collective-permute-start | bytes 884744 | tf_op jit(solution)/shard_map/ppermute | solution.py:137
  90.6 4.0 %collective-permute-start.18 = (bf16[48,3072]{1,0:T(8,128)(2,1)}, bf16[48,3072]{1,0:T(8,128)(2,1)S(1)}, u32[]{:S(2)}, u32[]{:S(2)}) collective-permute-start(bf16[48,3072]{1,0:T(8,128)(2,1)} %copy-done.19), channel_id=1, source_target_pairs={{0,12},{4,0},{8,4},{12,8},{1,13},{5,1},{9,5},{13,9},{2,14},{6,2},{... | collective-permute-start | bytes 884744 | tf_op jit(solution)/shard_map/ppermute | solution.py:137
  94.6 5.5 %collective-permute-done.11.across = bf16[6,64,384]{2,1,0:T(8,128)(2,1)} collective-permute-done((bf16[6,64,384]{2,1,0:T(8,128)(2,1)}, bf16[6,64,384]{2,1,0:T(8,128)(2,1)}, u32[]{:S(2)}, u32[]{:S(2)}) %collective-permute-start.11) | collective-permute-done | bytes 294944 | tf_op jit(solution)/shard_map/ppermute | solution.py:188
  100.2 2.4 %collective-permute-start.19 = (bf16[48,3072]{1,0:T(8,128)(2,1)}, bf16[48,3072]{1,0:T(8,128)(2,1)S(1)}, u32[]{:S(2)}, u32[]{:S(2)}) collective-permute-start(bf16[48,3072]{1,0:T(8,128)(2,1)} %copy-done.18), channel_id=1, source_target_pairs={{0,4},{4,8},{8,12},{12,0},{1,5},{5,9},{9,13},{13,1},{2,6},{6,10},{... | collective-permute-start | bytes 884744 | tf_op jit(solution)/shard_map/ppermute | solution.py:137
  102.6 1.0 copy-done.14
  103.6 1.0 copy-done.16
  104.5 1.9 %shard_map.59 = (bf16[6,64,384]{2,1,0:T(8,128)(2,1)S(1)}, bf16[6,64,384]{2,1,0:T(8,128)(2,1)}) custom-call(s32[1]{0:T(128)} %bitcast.6.where, bf16[1,6,64,384]{3,2,1,0:T(8,128)(2,1)S(1)} %copy-done.14, bf16[1,6,64,384]{3,2,1,0:T(8,128)(2,1)S(1)} %copy-done.16, bf16[2,6,64,384]{3,2,1,0:T(8,128)(2,1)S(1)} %collective-permute-done.9.up, ...), custom_call_target="tpu_custom_call" | custom-call | tf_op jit(solution)/shard_map/pallas_call | solution.py:75
  106.4 1.9 %collective-permute-start.13 = (bf16[6,64,384]{2,1,0:T(8,128)(2,1)S(1)}, bf16[6,64,384]{2,1,0:T(8,128)(2,1)S(1)}, u32[]{:S(2)}, u32[]{:S(2)}) collective-permute-start(bf16[6,64,384]{2,1,0:T(8,128)(2,1)S(1)} %get-tuple-element.46), channel_id=1, source_target_pairs={{0,32},{16,48},{32,64},{48,80},{64,96},{80,112},{96,0},{112,16},{1... | collective-permute-start | bytes 884744 | tf_op jit(solution)/shard_map/ppermute | solution.py:137
  108.3 6.0 %collective-permute-start.14 = (bf16[6,64,384]{2,1,0:T(8,128)(2,1)}, bf16[6,64,384]{2,1,0:T(8,128)(2,1)}, u32[]{:S(2)}, u32[]{:S(2)}) collective-permute-start(bf16[6,64,384]{2,1,0:T(8,128)(2,1)} %get-tuple-element.47), channel_id=1, source_target_pairs={{0,96},{16,112},{32,0},{48,16},{64,32},{80,48},{96,64},{112,80},{1... | collective-permute-start | bytes 884744 | tf_op jit(solution)/shard_map/ppermute | solution.py:137
  114.4 1.0 copy-done.4
  115.3 3.7 %shard_map.60 = (f32[48,3072]{1,0:T(8,128)S(1)}, bf16[48,3072]{1,0:T(8,128)(2,1)}, bf16[48,3072]{1,0:T(8,128)(2,1)}, bf16[48,3072]{1,0:T(8,128)(2,1)}) custom-call(bf16[384,384]{1,0:T(8,128)(2,1)S(1)} %copy-done.4, bf16[3072,384]{1,0:T(8,128)(2,1)S(1)} %copy-done), custom_call_target="tpu_custom_call" | custom-call | tf_op jit(solution)/shard_map/pallas_call | solution.py:75
  119.0 0.8 copy-done.7
  119.9 5.6 %collective-permute-start.12 = (bf16[48,3072]{1,0:T(8,128)(2,1)}, bf16[48,3072]{1,0:T(8,128)(2,1)S(1)}, u32[]{:S(2)}, u32[]{:S(2)}) collective-permute-start(bf16[48,3072]{1,0:T(8,128)(2,1)} %get-tuple-element.44), channel_id=1, source_target_pairs={{0,8},{4,12},{8,0},{12,4},{1,9},{5,13},{9,1},{13,5},{2,10},{6,14},... | collective-permute-start | bytes 884744 | tf_op jit(solution)/shard_map/ppermute | solution.py:137
  125.5 1.1 shard_map.63
  126.6 1.9 %collective-permute-start.20 = (bf16[48,3072]{1,0:T(8,128)(2,1)S(1)}, bf16[48,3072]{1,0:T(8,128)(2,1)S(1)}, u32[]{:S(2)}, u32[]{:S(2)}) collective-permute-start(bf16[48,3072]{1,0:T(8,128)(2,1)S(1)} %shard_map.63), channel_id=1, source_target_pairs={{0,642},{2,640},{128,514},{130,512},{256,386},{258,384},{384,258},... | collective-permute-start | bytes 884744 | tf_op jit(solution)/shard_map/ppermute | solution.py:156
  128.6 1.9 %collective-permute-start.15 = (bf16[48,3072]{1,0:T(8,128)(2,1)}, bf16[48,3072]{1,0:T(8,128)(2,1)S(1)}, u32[]{:S(2)}, u32[]{:S(2)}) collective-permute-start(bf16[48,3072]{1,0:T(8,128)(2,1)} %get-tuple-element.51), channel_id=1, source_target_pairs={{0,12},{4,0},{8,4},{12,8},{1,13},{5,1},{9,5},{13,9},{2,14},{6,2},{... | collective-permute-start | bytes 884744 | tf_op jit(solution)/shard_map/ppermute | solution.py:137
  130.5 0.7 copy-done.11
  131.2 3.9 %collective-permute-start.16 = (bf16[48,3072]{1,0:T(8,128)(2,1)}, bf16[48,3072]{1,0:T(8,128)(2,1)S(1)}, u32[]{:S(2)}, u32[]{:S(2)}) collective-permute-start(bf16[48,3072]{1,0:T(8,128)(2,1)} %get-tuple-element.52), channel_id=1, source_target_pairs={{0,4},{4,8},{8,12},{12,0},{1,5},{5,9},{9,13},{13,1},{2,6},{6,10},{... | collective-permute-start | bytes 884744 | tf_op jit(solution)/shard_map/ppermute | solution.py:137
  135.2 0.1 pad_add_fusion.1.where
  135.3 1.0 copy-done.10
  136.2 1.0 copy-done.12
  137.2 1.2 shard_map.61
  138.4 1.9 %collective-permute-start.21 = (bf16[2,64,384]{2,1,0:T(8,128)(2,1)S(1)}, bf16[2,64,384]{2,1,0:T(8,128)(2,1)S(1)}, u32[]{:S(2)}, u32[]{:S(2)}) collective-permute-start(bf16[2,64,384]{2,1,0:T(8,128)(2,1)S(1)} %get-tuple-element.58), channel_id=1, source_target_pairs={{0,128},{128,256},{256,0},{384,512},{512,640},{640,384},{1,129},{1... | collective-permute-start | bytes 294920 | tf_op jit(solution)/shard_map/ppermute | solution.py:231
  140.3 3.9 %collective-permute-start.22 = (bf16[2,64,384]{2,1,0:T(8,128)(2,1)S(1)}, bf16[2,64,384]{2,1,0:T(8,128)(2,1)S(1)}, u32[]{:S(2)}, u32[]{:S(2)}) collective-permute-start(bf16[2,64,384]{2,1,0:T(8,128)(2,1)S(1)} %get-tuple-element.59), channel_id=1, source_target_pairs={{0,256},{128,0},{256,128},{384,640},{512,384},{640,512},{1,257},{1... | collective-permute-start | bytes 294920 | tf_op jit(solution)/shard_map/ppermute | solution.py:231
  144.2 0.7 collective-permute-done.21.rest_0_
  144.9 2.8 %collective-permute-done.22.rest_1_ = bf16[2,64,384]{2,1,0:T(8,128)(2,1)S(1)} collective-permute-done((bf16[2,64,384]{2,1,0:T(8,128)(2,1)S(1)}, bf16[2,64,384]{2,1,0:T(8,128)(2,1)S(1)}, u32[]{:S(2)}, u32[]{:S(2)}) %collective-permute-start.22) | collective-permute-done | bytes 98336 | tf_op jit(solution)/shard_map/ppermute | solution.py:231
  147.7 0.6 shard_map.65
  148.3 9.5 %collective-permute-start.23 = (bf16[64,384]{1,0:T(8,128)(2,1)S(1)}, bf16[64,384]{1,0:T(8,128)(2,1)S(1)}, u32[]{:S(2)}, u32[]{:S(2)}) collective-permute-start(bf16[64,384]{1,0:T(8,128)(2,1)S(1)} %get-tuple-element.61), channel_id=1, source_target_pairs={{0,384},{128,512},{256,640},{384,0},{512,128},{640,256},{1,385},{1... | collective-permute-start | bytes 147464 | tf_op jit(solution)/shard_map/ppermute | solution.py:137
  157.8 0.9 shard_map.64
  158.7 1.1 collective-permute-done.23
  159.8 0.7 convert_add_fusion
  (45 shorter events, 0.2 us)
Async XLA Ops:
  0.6 38.6 %collective-permute-start.3 = (bf16[48,3072]{1,0:T(8,128)(2,1)}, bf16[48,3072]{1,0:T(8,128)(2,1)S(1)}, u32[]{:S(2)}, u32[]{:S(2)}) collective-permute-start(bf16[48,3072]{1,0:T(8,128)(2,1)} %param.4), channel_id=1, source_target_pairs={{0,642},{2,640},{128,514},{130,512},{256,386},{258,384},{384,258},... | collective-permute-start | bytes 884744 | tf_op jit(solution)/shard_map/ppermute | solution.py:156
  13.4 31.2 %collective-permute-start = (bf16[48,3072]{1,0:T(8,128)(2,1)}, bf16[48,3072]{1,0:T(8,128)(2,1)}, u32[]{:S(2)}, u32[]{:S(2)}) collective-permute-start(bf16[48,3072]{1,0:T(8,128)(2,1)} %param.4), channel_id=1, source_target_pairs={{0,4},{4,8},{8,12},{12,0},{1,5},{5,9},{9,13},{13,1},{2,6},{6,10},{... | collective-permute-start | bytes 884744 | tf_op jit(solution)/shard_map/ppermute | solution.py:137
  16.8 32.4 %collective-permute-start.1 = (bf16[48,3072]{1,0:T(8,128)(2,1)}, bf16[48,3072]{1,0:T(8,128)(2,1)S(1)}, u32[]{:S(2)}, u32[]{:S(2)}) collective-permute-start(bf16[48,3072]{1,0:T(8,128)(2,1)} %param.4), channel_id=1, source_target_pairs={{0,8},{4,12},{8,0},{12,4},{1,9},{5,13},{9,1},{13,5},{2,10},{6,14},... | collective-permute-start | bytes 884744 | tf_op jit(solution)/shard_map/ppermute | solution.py:137
  21.4 27.8 %collective-permute-start.2 = (bf16[48,3072]{1,0:T(8,128)(2,1)}, bf16[48,3072]{1,0:T(8,128)(2,1)S(1)}, u32[]{:S(2)}, u32[]{:S(2)}) collective-permute-start(bf16[48,3072]{1,0:T(8,128)(2,1)} %param.4), channel_id=1, source_target_pairs={{0,12},{4,0},{8,4},{12,8},{1,13},{5,1},{9,5},{13,9},{2,14},{6,2},{... | collective-permute-start | bytes 884744 | tf_op jit(solution)/shard_map/ppermute | solution.py:137
  25.8 31.7 %copy-start = (bf16[3072,384]{1,0:T(8,128)(2,1)S(1)}, bf16[3072,384]{1,0:T(8,128)(2,1)}, u32[]{:S(2)}) copy-start(bf16[3072,384]{1,0:T(8,128)(2,1)} %weight.3) | copy-start | bytes 7077892
  25.8 13.4 %collective-permute-start.4 = (bf16[4,48,384]{2,1,0:T(8,128)(2,1)S(1)}, bf16[4,48,384]{2,1,0:T(8,128)(2,1)S(1)}, u32[]{:S(2)}, u32[]{:S(2)}) collective-permute-start(bf16[4,48,384]{2,1,0:T(8,128)(2,1)S(1)} %get-tuple-element.63), channel_id=1, source_target_pairs={{0,640},{128,512},{256,384},{384,256},{512,128},{640,0},{1,641},{1... | collective-permute-start | bytes 442376 | tf_op jit(solution)/shard_map/ppermute | solution.py:162
  39.2 15.9 %collective-permute-start.5 = (bf16[48,3072]{1,0:T(8,128)(2,1)S(1)}, bf16[48,3072]{1,0:T(8,128)(2,1)S(1)}, u32[]{:S(2)}, u32[]{:S(2)}) collective-permute-start(bf16[48,3072]{1,0:T(8,128)(2,1)S(1)} %collective-permute-done.3), channel_id=1, source_target_pairs={{0,4},{4,8},{8,12},{12,0},{1,5},{5,9},{9,13},{13,1},{2,6},{6,10},{... | collective-permute-start | bytes 884744 | tf_op jit(solution)/shard_map/ppermute | solution.py:137
  41.7 13.4 %collective-permute-start.6 = (bf16[48,3072]{1,0:T(8,128)(2,1)S(1)}, bf16[48,3072]{1,0:T(8,128)(2,1)S(1)}, u32[]{:S(2)}, u32[]{:S(2)}) collective-permute-start(bf16[48,3072]{1,0:T(8,128)(2,1)S(1)} %collective-permute-done.3), channel_id=1, source_target_pairs={{0,8},{4,12},{8,0},{12,4},{1,9},{5,13},{9,1},{13,5},{2,10},{6,14},... | collective-permute-start | bytes 884744 | tf_op jit(solution)/shard_map/ppermute | solution.py:137
  44.6 12.9 %collective-permute-start.7 = (bf16[48,3072]{1,0:T(8,128)(2,1)S(1)}, bf16[48,3072]{1,0:T(8,128)(2,1)S(1)}, u32[]{:S(2)}, u32[]{:S(2)}) collective-permute-start(bf16[48,3072]{1,0:T(8,128)(2,1)S(1)} %collective-permute-done.3), channel_id=1, source_target_pairs={{0,12},{4,0},{8,4},{12,8},{1,13},{5,1},{9,5},{13,9},{2,14},{6,2},{... | collective-permute-start | bytes 884744 | tf_op jit(solution)/shard_map/ppermute | solution.py:137
  57.6 1.4 copy-start.1
  57.6 5.5 %copy-start.17 = (f32[128]{0:T(128)S(1)}, f32[128]{0:T(128)}, u32[]{:S(2)}) copy-start(f32[128]{0:T(128)} %param.7) | copy-start | bytes 1540
  59.0 4.0 %collective-permute-start.8 = (f32[384,384]{1,0:T(8,128)S(1)}, f32[384,384]{1,0:T(8,128)}, u32[]{:S(2)}, u32[]{:S(2)}) collective-permute-start(f32[384,384]{1,0:T(8,128)S(1)} %fusion.mine), channel_id=1, source_target_pairs={{0,1},{1,0},{2,3},{3,2},{4,5},{5,4},{6,7},{7,6},{8,9},{9,8},{10,11... | collective-permute-start | bytes 1769480 | tf_op jit(solution)/shard_map/ppermute | solution.py:137
  63.1 1.7 %copy-start.2 = (bf16[384,3072]{1,0:T(8,128)(2,1)S(1)}, bf16[384,3072]{1,0:T(8,128)(2,1)}, u32[]{:S(2)}) copy-start(bf16[384,3072]{1,0:T(8,128)(2,1)} %copy-done.1) | copy-start | bytes 7077892
  69.4 0.7 copy-start.9
  70.1 14.6 %copy-start.13 = (bf16[1,6,64,384]{3,2,1,0:T(8,128)(2,1)}, bf16[1,6,64,384]{3,2,1,0:T(8,128)(2,1)S(1)}, u32[]{:S(2)}) copy-start(bf16[1,6,64,384]{3,2,1,0:T(8,128)(2,1)S(1)} %get-tuple-element.35.two) | copy-start | bytes 884740
  70.1 17.6 %copy-start.15 = (bf16[1,6,64,384]{3,2,1,0:T(8,128)(2,1)}, bf16[1,6,64,384]{3,2,1,0:T(8,128)(2,1)S(1)}, u32[]{:S(2)}) copy-start(bf16[1,6,64,384]{3,2,1,0:T(8,128)(2,1)S(1)} %get-tuple-element.36.six) | copy-start | bytes 884740
  70.1 32.5 %collective-permute-start.10 = (bf16[2,6,64,384]{3,2,1,0:T(8,128)(2,1)}, bf16[2,6,64,384]{3,2,1,0:T(8,128)(2,1)S(1)}, u32[]{:S(2)}, u32[]{:S(2)}) collective-permute-start(bf16[2,6,64,384]{3,2,1,0:T(8,128)(2,1)} %get-tuple-element.38), channel_id=1, source_target_pairs={{0,112},{16,0},{32,16},{48,32},{64,48},{80,64},{96,80},{112,96},{1... | collective-permute-start | bytes 1769480 | tf_op jit(solution)/shard_map/ppermute | solution.py:137
  72.4 30.2 %collective-permute-start.9 = (bf16[2,6,64,384]{3,2,1,0:T(8,128)(2,1)}, bf16[2,6,64,384]{3,2,1,0:T(8,128)(2,1)S(1)}, u32[]{:S(2)}, u32[]{:S(2)}) collective-permute-start(bf16[2,6,64,384]{3,2,1,0:T(8,128)(2,1)} %get-tuple-element.37), channel_id=1, source_target_pairs={{0,16},{16,32},{32,48},{48,64},{64,80},{80,96},{96,112},{112,0},{1... | collective-permute-start | bytes 1769480 | tf_op jit(solution)/shard_map/ppermute | solution.py:137
  75.9 24.2 %collective-permute-start.11 = (bf16[6,64,384]{2,1,0:T(8,128)(2,1)}, bf16[6,64,384]{2,1,0:T(8,128)(2,1)}, u32[]{:S(2)}, u32[]{:S(2)}) collective-permute-start(bf16[6,64,384]{2,1,0:T(8,128)(2,1)} %bitcast.7), channel_id=1, source_target_pairs={{0,32},{1,97},{16,48},{17,113},{32,64},{33,1},{48,80},{49,17},{64,... | collective-permute-start | bytes 884744 | tf_op jit(solution)/shard_map/ppermute | solution.py:188
  84.7 0.7 copy-start.3
  85.4 0.8 copy-start.5
  86.2 0.7 copy-start.18
  86.9 0.7 copy-start.19
  87.6 32.2 %collective-permute-start.17 = (bf16[48,3072]{1,0:T(8,128)(2,1)}, bf16[48,3072]{1,0:T(8,128)(2,1)}, u32[]{:S(2)}, u32[]{:S(2)}) collective-permute-start(bf16[48,3072]{1,0:T(8,128)(2,1)} %get-tuple-element.54), channel_id=1, source_target_pairs={{0,8},{4,12},{8,0},{12,4},{1,9},{5,13},{9,1},{13,5},{2,10},{6,14},... | collective-permute-start | bytes 884744 | tf_op jit(solution)/shard_map/ppermute | solution.py:137
  90.6 34.9 %collective-permute-start.18 = (bf16[48,3072]{1,0:T(8,128)(2,1)}, bf16[48,3072]{1,0:T(8,128)(2,1)S(1)}, u32[]{:S(2)}, u32[]{:S(2)}) collective-permute-start(bf16[48,3072]{1,0:T(8,128)(2,1)} %copy-done.19), channel_id=1, source_target_pairs={{0,12},{4,0},{8,4},{12,8},{1,13},{5,1},{9,5},{13,9},{2,14},{6,2},{... | collective-permute-start | bytes 884744 | tf_op jit(solution)/shard_map/ppermute | solution.py:137
  100.2 25.4 %collective-permute-start.19 = (bf16[48,3072]{1,0:T(8,128)(2,1)}, bf16[48,3072]{1,0:T(8,128)(2,1)S(1)}, u32[]{:S(2)}, u32[]{:S(2)}) collective-permute-start(bf16[48,3072]{1,0:T(8,128)(2,1)} %copy-done.18), channel_id=1, source_target_pairs={{0,4},{4,8},{8,12},{12,0},{1,5},{5,9},{9,13},{13,1},{2,6},{6,10},{... | collective-permute-start | bytes 884744 | tf_op jit(solution)/shard_map/ppermute | solution.py:137
  102.6 1.0 copy-start.14
  103.6 1.0 copy-start.16
  104.5 21.0 %copy-start.6 = (f32[48,3072]{1,0:T(8,128)S(1)}, f32[48,3072]{1,0:T(8,128)}, u32[]{:S(2)}) copy-start(f32[48,3072]{1,0:T(8,128)} %copy-done.5) | copy-start | bytes 1769476
  106.4 24.1 %collective-permute-start.13 = (bf16[6,64,384]{2,1,0:T(8,128)(2,1)S(1)}, bf16[6,64,384]{2,1,0:T(8,128)(2,1)S(1)}, u32[]{:S(2)}, u32[]{:S(2)}) collective-permute-start(bf16[6,64,384]{2,1,0:T(8,128)(2,1)S(1)} %get-tuple-element.46), channel_id=1, source_target_pairs={{0,32},{16,48},{32,64},{48,80},{64,96},{80,112},{96,0},{112,16},{1... | collective-permute-start | bytes 884744 | tf_op jit(solution)/shard_map/ppermute | solution.py:137
  108.3 26.9 %collective-permute-start.14 = (bf16[6,64,384]{2,1,0:T(8,128)(2,1)}, bf16[6,64,384]{2,1,0:T(8,128)(2,1)}, u32[]{:S(2)}, u32[]{:S(2)}) collective-permute-start(bf16[6,64,384]{2,1,0:T(8,128)(2,1)} %get-tuple-element.47), channel_id=1, source_target_pairs={{0,96},{16,112},{32,0},{48,16},{64,32},{80,48},{96,64},{112,80},{1... | collective-permute-start | bytes 884744 | tf_op jit(solution)/shard_map/ppermute | solution.py:137
  114.3 1.0 copy-start.4
  119.0 0.8 copy-start.7
  119.9 37.9 %copy-start.8 = (f32[48,3072]{1,0:T(8,128)S(1)}, f32[48,3072]{1,0:T(8,128)}, u32[]{:S(2)}) copy-start(f32[48,3072]{1,0:T(8,128)} %copy-done.7) | copy-start | bytes 1769476
  119.9 18.5 %collective-permute-start.12 = (bf16[48,3072]{1,0:T(8,128)(2,1)}, bf16[48,3072]{1,0:T(8,128)(2,1)S(1)}, u32[]{:S(2)}, u32[]{:S(2)}) collective-permute-start(bf16[48,3072]{1,0:T(8,128)(2,1)} %get-tuple-element.44), channel_id=1, source_target_pairs={{0,8},{4,12},{8,0},{12,4},{1,9},{5,13},{9,1},{13,5},{2,10},{6,14},... | collective-permute-start | bytes 884744 | tf_op jit(solution)/shard_map/ppermute | solution.py:137
  126.6 31.1 %collective-permute-start.20 = (bf16[48,3072]{1,0:T(8,128)(2,1)S(1)}, bf16[48,3072]{1,0:T(8,128)(2,1)S(1)}, u32[]{:S(2)}, u32[]{:S(2)}) collective-permute-start(bf16[48,3072]{1,0:T(8,128)(2,1)S(1)} %shard_map.63), channel_id=1, source_target_pairs={{0,642},{2,640},{128,514},{130,512},{256,386},{258,384},{384,258},... | collective-permute-start | bytes 884744 | tf_op jit(solution)/shard_map/ppermute | solution.py:156
  128.6 29.2 %collective-permute-start.15 = (bf16[48,3072]{1,0:T(8,128)(2,1)}, bf16[48,3072]{1,0:T(8,128)(2,1)S(1)}, u32[]{:S(2)}, u32[]{:S(2)}) collective-permute-start(bf16[48,3072]{1,0:T(8,128)(2,1)} %get-tuple-element.51), channel_id=1, source_target_pairs={{0,12},{4,0},{8,4},{12,8},{1,13},{5,1},{9,5},{13,9},{2,14},{6,2},{... | collective-permute-start | bytes 884744 | tf_op jit(solution)/shard_map/ppermute | solution.py:137
  130.5 0.7 copy-start.11
  131.2 26.6 %collective-permute-start.16 = (bf16[48,3072]{1,0:T(8,128)(2,1)}, bf16[48,3072]{1,0:T(8,128)(2,1)S(1)}, u32[]{:S(2)}, u32[]{:S(2)}) collective-permute-start(bf16[48,3072]{1,0:T(8,128)(2,1)} %get-tuple-element.52), channel_id=1, source_target_pairs={{0,4},{4,8},{8,12},{12,0},{1,5},{5,9},{9,13},{13,1},{2,6},{6,10},{... | collective-permute-start | bytes 884744 | tf_op jit(solution)/shard_map/ppermute | solution.py:137
  135.2 1.0 copy-start.10
  136.2 1.0 copy-start.12
  138.4 6.5 %collective-permute-start.21 = (bf16[2,64,384]{2,1,0:T(8,128)(2,1)S(1)}, bf16[2,64,384]{2,1,0:T(8,128)(2,1)S(1)}, u32[]{:S(2)}, u32[]{:S(2)}) collective-permute-start(bf16[2,64,384]{2,1,0:T(8,128)(2,1)S(1)} %get-tuple-element.58), channel_id=1, source_target_pairs={{0,128},{128,256},{256,0},{384,512},{512,640},{640,384},{1,129},{1... | collective-permute-start | bytes 294920 | tf_op jit(solution)/shard_map/ppermute | solution.py:231
  140.3 7.4 %collective-permute-start.22 = (bf16[2,64,384]{2,1,0:T(8,128)(2,1)S(1)}, bf16[2,64,384]{2,1,0:T(8,128)(2,1)S(1)}, u32[]{:S(2)}, u32[]{:S(2)}) collective-permute-start(bf16[2,64,384]{2,1,0:T(8,128)(2,1)S(1)} %get-tuple-element.59), channel_id=1, source_target_pairs={{0,256},{128,0},{256,128},{384,640},{512,384},{640,512},{1,257},{1... | collective-permute-start | bytes 294920 | tf_op jit(solution)/shard_map/ppermute | solution.py:231
  148.3 11.5 %collective-permute-start.23 = (bf16[64,384]{1,0:T(8,128)(2,1)S(1)}, bf16[64,384]{1,0:T(8,128)(2,1)S(1)}, u32[]{:S(2)}, u32[]{:S(2)}) collective-permute-start(bf16[64,384]{1,0:T(8,128)(2,1)S(1)} %get-tuple-element.61), channel_id=1, source_target_pairs={{0,384},{128,512},{256,640},{384,0},{512,128},{640,256},{1,385},{1... | collective-permute-start | bytes 147464 | tf_op jit(solution)/shard_map/ppermute | solution.py:137

commit v7 on v5

--- a/solution.py
+++ b/solution.py
@@ -104,14 +104,20 @@
         out[...] = total.astype(out.dtype)
 
 
-def over_y_kernel(where, own, up, down, got2, got4, got6, kept, *sends):
+def relay_kernel(where, two, six, up, down, across, out_two, out_six):
+    keep = jnp.where(where[0] == 0, 1.0, 0.0)
+    from4 = across[...].astype(F32)
+    out_two[...] = (two[0].astype(F32) + up[0].astype(F32) + keep * from4).astype(BF16)
+    out_six[...] = (six[0].astype(F32) + down[0].astype(F32) + (1.0 - keep) * from4).astype(BF16)
+
+
+def over_y_kernel(where, own, up, down, got2, got6, kept, *sends):
     count, third = kept.shape[0], len(sends) + 1
     for k in range(third):
         place = lax.rem(where[0] + k, third)
         for i in range(count):
             z = i * third + place
-            total = own[0, z].astype(F32) + got4[z].astype(F32)
-            total = total + (up[1, z].astype(F32) + down[1, z].astype(F32))
+            total = own[0, z].astype(F32) + (up[1, z].astype(F32) + down[1, z].astype(F32))
             total = total + (got2[z].astype(F32) + got6[z].astype(F32))
             if k:
                 sends[k - 1][i] = total.astype(BF16)
@@ -179,12 +185,15 @@
 
     up, down, across, two, six, own = c
     turn = [
-        (i * 2 + j, (i + (4, -4)[j]) % ny * 2 + j) for i in range(ny) for j in range(2)
+        (i * 2 + j, (i + (2, -2)[j]) % ny * 2 + j) for i in range(ny) for j in range(2)
     ]
     got_up, got_down = shift(up, "y", 1), shift(down, "y", -1)
     got4 = lax.ppermute(across[0], ("y", "c"), turn)
-    two = add(two[0], got_up[0]).astype(BF16)
-    six = add(six[0], got_down[0]).astype(BF16)
+    core = lax.axis_index("c").astype(jnp.int32).reshape(1)
+    chunk = jax.ShapeDtypeStruct(got4.shape, BF16)
+    two, six = small_call(
+        relay_kernel, [chunk, chunk], two, six, got_up, got_down, got4, where=core
+    )
     got2, got6 = shift(two, "y", 2), shift(six, "y", -2)
 
     block = (nh * count, width)
@@ -213,7 +222,6 @@
         got_up,
         got_down,
         got2,
-        got4,
         got6,
         where=spot,
     )

time: 152 us -> 160 us (1.053)
  local copies, waits for them, and re-layouts: 3.13 us -> 9.63 us
  Pallas kernels: 8.98 us -> 13.3 us
  other arithmetic: 4.11 us -> 1.58 us
    unnamed x13 -> x33, local copies, waits for them, and re-layouts: 2.09 us -> 8.59 us
    pallas_call x4 -> x5, Pallas kernels: 4.66 us -> 8.66 us  [small_call(): pl.pallas_call(kernel, out_shape=out_shape, in_specs=[pl.BlockSpec(memory...]
    ppermute x2, waiting for transfers between devices: 13.3 us -> 15.2 us  [body(): got.append(lax.ppermute(sends[k - 1], 'zl', hop))]
    ppermute x1, starting transfers between devices: 6.28 us -> 4.48 us  [body(): got4 = lax.ppermute(across[0], ('y', 'c'), turn)]
  transfers between devices with their start and end apart: 21 -> 21, of which waited for: 9 -> 10; matrix products, arithmetic and copies ran while one was open for 4% -> 3% of each run, Pallas kernels for 3% -> 5%
where the time goes in v7:
time: 160 us; the launch traced here: 159 us
  starting transfers between devices  77.3 us (48%)
  waiting for transfers between devices  54.8 us (34%)
  Pallas kernels  13.3 us (8%)
  local copies, waits for them, and re-layouts  9.63 us (6%)
    ppermute x15, starting transfers between devices, shift(): lax.ppermute(value, axis, [(i, (i + by) % size) for i in range(size)])  49.1 us
    ppermute x15, waiting for transfers between devices, shift(): lax.ppermute(value, axis, [(i, (i + by) % size) for i in range(size)])  30.4 us
    ppermute x2, waiting for transfers between devices, body(): got.append(lax.ppermute(sends[k - 1], 'zl', hop))  15.2 us
    ppermute x2, starting transfers between devices, mirror(): return lax.ppermute(value, ('zl', 'zh'), ends)  14.7 us
    ppermute x1, waiting for transfers between devices, body(): cot_far = lax.ppermute(cot_far, 'zl', [(i, nz - 1 - i) for i in range(nz)])  9.16 us
    pallas_call x5, Pallas kernels, small_call(): pl.pallas_call(kernel, out_shape=out_shape, in_specs=[pl.BlockSpec(memory...  8.66 us
    unnamed x33, local copies, waits for them, and re-layouts  8.59 us
    ppermute x2, starting transfers between devices, body(): got.append(lax.ppermute(sends[k - 1], 'zl', hop))  5.84 us
  transfers between devices with their start and end apart: 21, of which 10 were waited for; matrix products, arithmetic and copies ran while one was open for 3% of the time, Pallas kernels for 5%

profile of v7, /device:TPU:128, one launch (start us, length us, event | category | flops | bytes accessed | tf_op | source)
XLA Modules:
  0.0 159.0 jit_solution(814727519839450216)
XLA Ops:
  0.6 12.7 %collective-permute-start = (bf16[48,3072]{1,0:T(8,128)(2,1)}, bf16[48,3072]{1,0:T(8,128)(2,1)S(1)}, u32[]{:S(2)}, u32[]{:S(2)}) collective-permute-start(bf16[48,3072]{1,0:T(8,128)(2,1)} %param.4), channel_id=1, source_target_pairs={{0,642},{2,640},{128,514},{130,512},{256,386},{258,384},{384,258},... | collective-permute-start | bytes 884744 | tf_op jit(solution)/shard_map/ppermute | solution.py:159
  13.4 3.4 %collective-permute-start.2 = (bf16[48,3072]{1,0:T(8,128)(2,1)}, bf16[48,3072]{1,0:T(8,128)(2,1)}, u32[]{:S(2)}, u32[]{:S(2)}) collective-permute-start(bf16[48,3072]{1,0:T(8,128)(2,1)} %param.4), channel_id=1, source_target_pairs={{0,4},{4,8},{8,12},{12,0},{1,5},{5,9},{9,13},{13,1},{2,6},{6,10},{... | collective-permute-start | bytes 884744 | tf_op jit(solution)/shard_map/ppermute | solution.py:140
  16.8 4.6 %collective-permute-start.4 = (bf16[48,3072]{1,0:T(8,128)(2,1)}, bf16[48,3072]{1,0:T(8,128)(2,1)S(1)}, u32[]{:S(2)}, u32[]{:S(2)}) collective-permute-start(bf16[48,3072]{1,0:T(8,128)(2,1)} %param.4), channel_id=1, source_target_pairs={{0,8},{4,12},{8,0},{12,4},{1,9},{5,13},{9,1},{13,5},{2,10},{6,14},... | collective-permute-start | bytes 884744 | tf_op jit(solution)/shard_map/ppermute | solution.py:140
  21.4 3.3 %collective-permute-start.6 = (bf16[48,3072]{1,0:T(8,128)(2,1)}, bf16[48,3072]{1,0:T(8,128)(2,1)S(1)}, u32[]{:S(2)}, u32[]{:S(2)}) collective-permute-start(bf16[48,3072]{1,0:T(8,128)(2,1)} %param.4), channel_id=1, source_target_pairs={{0,12},{4,0},{8,4},{12,8},{1,13},{5,1},{9,5},{13,9},{2,14},{6,2},{... | collective-permute-start | bytes 884744 | tf_op jit(solution)/shard_map/ppermute | solution.py:140
  24.8 1.0 dynamic-slice_bitcast_fusion
  25.8 0.0 copy-start
  25.8 3.2 %collective-permute-start.1 = (bf16[4,48,384]{2,1,0:T(8,128)(2,1)S(1)}, bf16[4,48,384]{2,1,0:T(8,128)(2,1)S(1)}, u32[]{:S(2)}, u32[]{:S(2)}) collective-permute-start(bf16[4,48,384]{2,1,0:T(8,128)(2,1)S(1)} %get-tuple-element.47), channel_id=1, source_target_pairs={{0,640},{128,512},{256,384},{384,256},{512,128},{640,0},{1,641},{1... | collective-permute-start | bytes 442376 | tf_op jit(solution)/shard_map/ppermute | solution.py:165
  29.0 1.0 constant_dynamic-update-slice_fusion.7
  30.0 9.2 %collective-permute-done.1.cot_far = bf16[4,48,384]{2,1,0:T(8,128)(2,1)S(1)} collective-permute-done((bf16[4,48,384]{2,1,0:T(8,128)(2,1)S(1)}, bf16[4,48,384]{2,1,0:T(8,128)(2,1)S(1)}, u32[]{:S(2)}, u32[]{:S(2)}) %collective-permute-start.1) | collective-permute-done | bytes 147488 | tf_op jit(solution)/shard_map/ppermute | solution.py:165
  39.2 0.0 collective-permute-done
  39.2 2.5 %collective-permute-start.3 = (bf16[48,3072]{1,0:T(8,128)(2,1)S(1)}, bf16[48,3072]{1,0:T(8,128)(2,1)S(1)}, u32[]{:S(2)}, u32[]{:S(2)}) collective-permute-start(bf16[48,3072]{1,0:T(8,128)(2,1)S(1)} %collective-permute-done), channel_id=1, source_target_pairs={{0,4},{4,8},{8,12},{12,0},{1,5},{5,9},{9,13},{13,1},{2,6},{6,10},{... | collective-permute-start | bytes 884744 | tf_op jit(solution)/shard_map/ppermute | solution.py:140
  41.7 2.9 %collective-permute-start.5 = (bf16[48,3072]{1,0:T(8,128)(2,1)S(1)}, bf16[48,3072]{1,0:T(8,128)(2,1)S(1)}, u32[]{:S(2)}, u32[]{:S(2)}) collective-permute-start(bf16[48,3072]{1,0:T(8,128)(2,1)S(1)} %collective-permute-done), channel_id=1, source_target_pairs={{0,8},{4,12},{8,0},{12,4},{1,9},{5,13},{9,1},{13,5},{2,10},{6,14},... | collective-permute-start | bytes 884744 | tf_op jit(solution)/shard_map/ppermute | solution.py:140
  44.7 0.0 collective-permute-done.2
  44.7 3.6 %collective-permute-start.7 = (bf16[48,3072]{1,0:T(8,128)(2,1)S(1)}, bf16[48,3072]{1,0:T(8,128)(2,1)S(1)}, u32[]{:S(2)}, u32[]{:S(2)}) collective-permute-start(bf16[48,3072]{1,0:T(8,128)(2,1)S(1)} %collective-permute-done), channel_id=1, source_target_pairs={{0,12},{4,0},{8,4},{12,8},{1,13},{5,1},{9,5},{13,9},{2,14},{6,2},{... | collective-permute-start | bytes 884744 | tf_op jit(solution)/shard_map/ppermute | solution.py:140
  48.3 1.0 constant_dynamic-update-slice_fusion.5
  49.2 5.8 %collective-permute-done.3 = bf16[48,3072]{1,0:T(8,128)(2,1)S(1)} collective-permute-done((bf16[48,3072]{1,0:T(8,128)(2,1)S(1)}, bf16[48,3072]{1,0:T(8,128)(2,1)S(1)}, u32[]{:S(2)}, u32[]{:S(2)}) %collective-permute-start.3) | collective-permute-done | bytes 294944 | tf_op jit(solution)/shard_map/ppermute | solution.py:140
  55.1 0.0 collective-permute-done.4
  55.1 0.0 collective-permute-done.5
  55.2 0.0 collective-permute-done.6
  55.2 2.3 %collective-permute-done.7 = bf16[48,3072]{1,0:T(8,128)(2,1)S(1)} collective-permute-done((bf16[48,3072]{1,0:T(8,128)(2,1)S(1)}, bf16[48,3072]{1,0:T(8,128)(2,1)S(1)}, u32[]{:S(2)}, u32[]{:S(2)}) %collective-permute-start.7) | collective-permute-done | bytes 294944 | tf_op jit(solution)/shard_map/ppermute | solution.py:140
  57.6 0.0 copy-start.12
  57.6 1.4 fusion.mine
  59.0 1.9 %collective-permute-start.8 = (f32[384,384]{1,0:T(8,128)S(1)}, f32[384,384]{1,0:T(8,128)}, u32[]{:S(2)}, u32[]{:S(2)}) collective-permute-start(f32[384,384]{1,0:T(8,128)S(1)} %fusion.mine), channel_id=1, source_target_pairs={{0,1},{1,0},{2,3},{3,2},{4,5},{5,4},{6,7},{7,6},{8,9},{9,8},{10,11... | collective-permute-start | bytes 1769480 | tf_op jit(solution)/shard_map/ppermute | solution.py:140
  60.9 0.0 copy-start.1
  60.9 0.1 pad_add_fusion.where
  61.0 2.0 %collective-permute-done.8.theirs = f32[384,384]{1,0:T(8,128)} collective-permute-done((f32[384,384]{1,0:T(8,128)S(1)}, f32[384,384]{1,0:T(8,128)}, u32[]{:S(2)}, u32[]{:S(2)}) %collective-permute-start.8) | collective-permute-done | bytes 589856 | tf_op jit(solution)/shard_map/ppermute | solution.py:140
  63.0 4.6 %rows_and_chunks.1 = (bf16[384,384]{1,0:T(8,128)(2,1)S(1)}, bf16[2,6,64,384]{3,2,1,0:T(8,128)(2,1)}, bf16[2,6,64,384]{3,2,1,0:T(8,128)(2,1)}, bf16[1,6,64,384]{3...) custom-call(s32[2]{0:T(128)S(1)} %pad_add_fusion.where, ...), custom_call_target="tpu_custom_call" | custom-call | tf_op jit(solution)/shard_map/rows_and_chunks/pallas_call | solution.py:62
  67.7 4.5 %collective-permute-start.15 = (bf16[6,64,384]{2,1,0:T(8,128)(2,1)S(1)}, bf16[6,64,384]{2,1,0:T(8,128)(2,1)S(1)}, u32[]{:S(2)}, u32[]{:S(2)}) collective-permute-start(bf16[6,64,384]{2,1,0:T(8,128)(2,1)S(1)} %bitcast.19), channel_id=1, source_target_pairs={{0,32},{1,97},{16,48},{17,113},{32,64},{33,1},{48,80},{49,17},{64,... | collective-permute-start | bytes 884744 | tf_op jit(solution)/shard_map/ppermute | solution.py:191
  72.1 3.5 %collective-permute-start.13 = (bf16[2,6,64,384]{3,2,1,0:T(8,128)(2,1)}, bf16[2,6,64,384]{3,2,1,0:T(8,128)(2,1)S(1)}, u32[]{:S(2)}, u32[]{:S(2)}) collective-permute-start(bf16[2,6,64,384]{3,2,1,0:T(8,128)(2,1)} %get-tuple-element.34), channel_id=1, source_target_pairs={{0,16},{16,32},{32,48},{48,64},{64,80},{80,96},{96,112},{112,0},{1... | collective-permute-start | bytes 1769480 | tf_op jit(solution)/shard_map/ppermute | solution.py:140
  75.6 3.6 %collective-permute-start.14 = (bf16[2,6,64,384]{3,2,1,0:T(8,128)(2,1)}, bf16[2,6,64,384]{3,2,1,0:T(8,128)(2,1)S(1)}, u32[]{:S(2)}, u32[]{:S(2)}) collective-permute-start(bf16[2,6,64,384]{3,2,1,0:T(8,128)(2,1)} %get-tuple-element.35), channel_id=1, source_target_pairs={{0,112},{16,0},{32,16},{48,32},{64,48},{80,64},{96,80},{112,96},{1... | collective-permute-start | bytes 1769480 | tf_op jit(solution)/shard_map/ppermute | solution.py:140
  79.2 3.9 %shard_map.59 = (f32[96,3072]{1,0:T(8,128)S(1)}, bf16[96,3072]{1,0:T(8,128)(2,1)}, bf16[96,3072]{1,0:T(8,128)(2,1)}, bf16[96,3072]{1,0:T(8,128)(2,1)}) custom-call(bf16[384,384]{1,0:T(8,128)(2,1)S(1)} %get-tuple-element.26.rows, bf16[3072,384]{1,0:T(8,128)(2,1)S(1)} %copy-done.1), custom_call_target="tpu_custom_call" | custom-call | tf_op jit(solution)/shard_map/pallas_call | solution.py:76
  83.1 4.6 %collective-permute-start.10 = (bf16[96,3072]{1,0:T(8,128)(2,1)}, bf16[96,3072]{1,0:T(8,128)(2,1)S(1)}, u32[]{:S(2)}, u32[]{:S(2)}) collective-permute-start(bf16[96,3072]{1,0:T(8,128)(2,1)} %get-tuple-element.29), channel_id=1, source_target_pairs={{0,12},{4,0},{8,4},{12,8},{1,13},{5,1},{9,5},{13,9},{2,14},{6,2},{... | collective-permute-start | bytes 1769480 | tf_op jit(solution)/shard_map/ppermute | solution.py:140
  87.7 1.9 %collective-permute-start.11 = (bf16[96,3072]{1,0:T(8,128)(2,1)}, bf16[96,3072]{1,0:T(8,128)(2,1)S(1)}, u32[]{:S(2)}, u32[]{:S(2)}) collective-permute-start(bf16[96,3072]{1,0:T(8,128)(2,1)} %get-tuple-element.30), channel_id=1, source_target_pairs={{0,4},{4,8},{8,12},{12,0},{1,5},{5,9},{9,13},{13,1},{2,6},{6,10},{... | collective-permute-start | bytes 1769480 | tf_op jit(solution)/shard_map/ppermute | solution.py:140
  89.6 0.0 collective-permute-done.15.across
  89.7 0.7 copy-done.10
  90.4 3.4 %collective-permute-start.9 = (bf16[96,3072]{1,0:T(8,128)(2,1)}, bf16[96,3072]{1,0:T(8,128)(2,1)}, u32[]{:S(2)}, u32[]{:S(2)}) collective-permute-start(bf16[96,3072]{1,0:T(8,128)(2,1)} %get-tuple-element.28), channel_id=1, source_target_pairs={{0,8},{4,12},{8,0},{12,4},{1,9},{5,13},{9,1},{13,5},{2,10},{6,14},... | collective-permute-start | bytes 1769480 | tf_op jit(solution)/shard_map/ppermute | solution.py:140
  93.8 0.5 collective-permute-done.13.up
  94.3 0.0 collective-permute-done.14.down
  94.3 1.0 copy-done.7
  95.2 1.0 copy-done.9
  96.2 1.0 copy-done.11
  97.2 1.0 shard_map.61
  98.2 4.0 %collective-permute-start.16 = (bf16[6,64,384]{2,1,0:T(8,128)(2,1)}, bf16[6,64,384]{2,1,0:T(8,128)(2,1)}, u32[]{:S(2)}, u32[]{:S(2)}) collective-permute-start(bf16[6,64,384]{2,1,0:T(8,128)(2,1)} %get-tuple-element.39), channel_id=1, source_target_pairs={{0,32},{16,48},{32,64},{48,80},{64,96},{80,112},{96,0},{112,16},{1... | collective-permute-start | bytes 884744 | tf_op jit(solution)/shard_map/ppermute | solution.py:140
  102.2 3.9 %collective-permute-start.17 = (bf16[6,64,384]{2,1,0:T(8,128)(2,1)}, bf16[6,64,384]{2,1,0:T(8,128)(2,1)}, u32[]{:S(2)}, u32[]{:S(2)}) collective-permute-start(bf16[6,64,384]{2,1,0:T(8,128)(2,1)} %get-tuple-element.40), channel_id=1, source_target_pairs={{0,96},{16,112},{32,0},{48,16},{64,32},{80,48},{96,64},{112,80},{1... | collective-permute-start | bytes 884744 | tf_op jit(solution)/shard_map/ppermute | solution.py:140
  106.1 8.2 %collective-permute-done.10.rest_1_ = bf16[96,3072]{1,0:T(8,128)(2,1)S(1)} collective-permute-done((bf16[96,3072]{1,0:T(8,128)(2,1)}, bf16[96,3072]{1,0:T(8,128)(2,1)S(1)}, u32[]{:S(2)}, u32[]{:S(2)}) %collective-permute-start.10) | collective-permute-done | bytes 589856 | tf_op jit(solution)/shard_map/ppermute | solution.py:140
  114.4 5.2 %collective-permute-done.11.rest_2_ = bf16[96,3072]{1,0:T(8,128)(2,1)S(1)} collective-permute-done((bf16[96,3072]{1,0:T(8,128)(2,1)}, bf16[96,3072]{1,0:T(8,128)(2,1)S(1)}, u32[]{:S(2)}, u32[]{:S(2)}) %collective-permute-start.11) | collective-permute-done | bytes 589856 | tf_op jit(solution)/shard_map/ppermute | solution.py:140
  119.6 0.8 copy-done.2
  120.4 0.0 collective-permute-done.9.rest_0_
  120.4 1.1 copy-done.3
  121.5 1.9 %shard_map.60 = (f32[48,3072]{1,0:T(8,128)S(1)}, bf16[48,3072]{1,0:T(8,128)(2,1)}) custom-call(f32[96,3072]{1,0:T(8,128)S(1)} %get-tuple-element.27.first, bf16[96,3072]{1,0:T(8,128)(2,1)} %collective-permute-done.9.rest_0_, bf16[96,3072]{1,0:T(8,128)(2,1)S(1)} %collective-permute-done.10.rest_1_, bf16[96,3072]{1,0:T(8,128)(2,1)S(1)} %copy-done.3), custom_call_target="tpu_custom_call" | custom-call | tf_op jit(solution)/shard_map/pallas_call | solution.py:76
  123.4 1.9 %collective-permute-start.12 = (bf16[48,3072]{1,0:T(8,128)(2,1)}, bf16[48,3072]{1,0:T(8,128)(2,1)S(1)}, u32[]{:S(2)}, u32[]{:S(2)}) collective-permute-start(bf16[48,3072]{1,0:T(8,128)(2,1)} %get-tuple-element.32), channel_id=1, source_target_pairs={{0,642},{2,640},{128,514},{130,512},{256,386},{258,384},{384,258},... | collective-permute-start | bytes 884744 | tf_op jit(solution)/shard_map/ppermute | solution.py:159
  125.4 0.1 pad_add_fusion.1.where
  125.5 0.0 collective-permute-done.17.got6
  125.5 1.0 copy-done.5
  126.4 1.3 shard_map.62
  127.7 1.9 %collective-permute-start.18 = (bf16[2,64,384]{2,1,0:T(8,128)(2,1)S(1)}, bf16[2,64,384]{2,1,0:T(8,128)(2,1)S(1)}, u32[]{:S(2)}, u32[]{:S(2)}) collective-permute-start(bf16[2,64,384]{2,1,0:T(8,128)(2,1)S(1)} %get-tuple-element.42), channel_id=1, source_target_pairs={{0,128},{128,256},{256,0},{384,512},{512,640},{640,384},{1,129},{1... | collective-permute-start | bytes 294920 | tf_op jit(solution)/shard_map/ppermute | solution.py:231
  129.6 3.9 %collective-permute-start.19 = (bf16[2,64,384]{2,1,0:T(8,128)(2,1)S(1)}, bf16[2,64,384]{2,1,0:T(8,128)(2,1)S(1)}, u32[]{:S(2)}, u32[]{:S(2)}) collective-permute-start(bf16[2,64,384]{2,1,0:T(8,128)(2,1)S(1)} %get-tuple-element.43), channel_id=1, source_target_pairs={{0,256},{128,0},{256,128},{384,640},{512,384},{640,512},{1,257},{1... | collective-permute-start | bytes 294920 | tf_op jit(solution)/shard_map/ppermute | solution.py:231
  133.5 6.9 %collective-permute-done.18.rest_0_ = bf16[2,64,384]{2,1,0:T(8,128)(2,1)S(1)} collective-permute-done((bf16[2,64,384]{2,1,0:T(8,128)(2,1)S(1)}, bf16[2,64,384]{2,1,0:T(8,128)(2,1)S(1)}, u32[]{:S(2)}, u32[]{:S(2)}) %collective-permute-start.18) | collective-permute-done | bytes 98336 | tf_op jit(solution)/shard_map/ppermute | solution.py:231
  140.4 8.4 %collective-permute-done.19.rest_1_ = bf16[2,64,384]{2,1,0:T(8,128)(2,1)S(1)} collective-permute-done((bf16[2,64,384]{2,1,0:T(8,128)(2,1)S(1)}, bf16[2,64,384]{2,1,0:T(8,128)(2,1)S(1)}, u32[]{:S(2)}, u32[]{:S(2)}) %collective-permute-start.19) | collective-permute-done | bytes 98336 | tf_op jit(solution)/shard_map/ppermute | solution.py:231
  148.8 0.6 shard_map.63
  149.4 1.9 %collective-permute-start.20 = (bf16[64,384]{1,0:T(8,128)(2,1)S(1)}, bf16[64,384]{1,0:T(8,128)(2,1)S(1)}, u32[]{:S(2)}, u32[]{:S(2)}) collective-permute-start(bf16[64,384]{1,0:T(8,128)(2,1)S(1)} %get-tuple-element.45), channel_id=1, source_target_pairs={{0,384},{128,512},{256,640},{384,0},{512,128},{640,256},{1,385},{1... | collective-permute-start | bytes 147464 | tf_op jit(solution)/shard_map/ppermute | solution.py:140
  151.3 0.8 add_convert_fusion
  152.1 6.3 %collective-permute-done.20 = bf16[64,384]{1,0:T(8,128)(2,1)S(1)} collective-permute-done((bf16[64,384]{1,0:T(8,128)(2,1)S(1)}, bf16[64,384]{1,0:T(8,128)(2,1)S(1)}, u32[]{:S(2)}, u32[]{:S(2)}) %collective-permute-start.20) | collective-permute-done | bytes 49184 | tf_op jit(solution)/shard_map/ppermute | solution.py:140
  158.4 0.7 convert_add_fusion
  (24 shorter events, 0.2 us)
Async XLA Ops:
  0.6 38.6 %collective-permute-start = (bf16[48,3072]{1,0:T(8,128)(2,1)}, bf16[48,3072]{1,0:T(8,128)(2,1)S(1)}, u32[]{:S(2)}, u32[]{:S(2)}) collective-permute-start(bf16[48,3072]{1,0:T(8,128)(2,1)} %param.4), channel_id=1, source_target_pairs={{0,642},{2,640},{128,514},{130,512},{256,386},{258,384},{384,258},... | collective-permute-start | bytes 884744 | tf_op jit(solution)/shard_map/ppermute | solution.py:159
  13.4 31.3 %collective-permute-start.2 = (bf16[48,3072]{1,0:T(8,128)(2,1)}, bf16[48,3072]{1,0:T(8,128)(2,1)}, u32[]{:S(2)}, u32[]{:S(2)}) collective-permute-start(bf16[48,3072]{1,0:T(8,128)(2,1)} %param.4), channel_id=1, source_target_pairs={{0,4},{4,8},{8,12},{12,0},{1,5},{5,9},{9,13},{13,1},{2,6},{6,10},{... | collective-permute-start | bytes 884744 | tf_op jit(solution)/shard_map/ppermute | solution.py:140
  16.8 38.3 %collective-permute-start.4 = (bf16[48,3072]{1,0:T(8,128)(2,1)}, bf16[48,3072]{1,0:T(8,128)(2,1)S(1)}, u32[]{:S(2)}, u32[]{:S(2)}) collective-permute-start(bf16[48,3072]{1,0:T(8,128)(2,1)} %param.4), channel_id=1, source_target_pairs={{0,8},{4,12},{8,0},{12,4},{1,9},{5,13},{9,1},{13,5},{2,10},{6,14},... | collective-permute-start | bytes 884744 | tf_op jit(solution)/shard_map/ppermute | solution.py:140
  21.4 33.7 %collective-permute-start.6 = (bf16[48,3072]{1,0:T(8,128)(2,1)}, bf16[48,3072]{1,0:T(8,128)(2,1)S(1)}, u32[]{:S(2)}, u32[]{:S(2)}) collective-permute-start(bf16[48,3072]{1,0:T(8,128)(2,1)} %param.4), channel_id=1, source_target_pairs={{0,12},{4,0},{8,4},{12,8},{1,13},{5,1},{9,5},{13,9},{2,14},{6,2},{... | collective-permute-start | bytes 884744 | tf_op jit(solution)/shard_map/ppermute | solution.py:140
  25.8 31.7 %copy-start = (bf16[3072,384]{1,0:T(8,128)(2,1)S(1)}, bf16[3072,384]{1,0:T(8,128)(2,1)}, u32[]{:S(2)}) copy-start(bf16[3072,384]{1,0:T(8,128)(2,1)} %weight.1) | copy-start | bytes 7077892
  25.8 13.4 %collective-permute-start.1 = (bf16[4,48,384]{2,1,0:T(8,128)(2,1)S(1)}, bf16[4,48,384]{2,1,0:T(8,128)(2,1)S(1)}, u32[]{:S(2)}, u32[]{:S(2)}) collective-permute-start(bf16[4,48,384]{2,1,0:T(8,128)(2,1)S(1)} %get-tuple-element.47), channel_id=1, source_target_pairs={{0,640},{128,512},{256,384},{384,256},{512,128},{640,0},{1,641},{1... | collective-permute-start | bytes 442376 | tf_op jit(solution)/shard_map/ppermute | solution.py:165
  39.2 15.9 %collective-permute-start.3 = (bf16[48,3072]{1,0:T(8,128)(2,1)S(1)}, bf16[48,3072]{1,0:T(8,128)(2,1)S(1)}, u32[]{:S(2)}, u32[]{:S(2)}) collective-permute-start(bf16[48,3072]{1,0:T(8,128)(2,1)S(1)} %collective-permute-done), channel_id=1, source_target_pairs={{0,4},{4,8},{8,12},{12,0},{1,5},{5,9},{9,13},{13,1},{2,6},{6,10},{... | collective-permute-start | bytes 884744 | tf_op jit(solution)/shard_map/ppermute | solution.py:140
  41.7 13.4 %collective-permute-start.5 = (bf16[48,3072]{1,0:T(8,128)(2,1)S(1)}, bf16[48,3072]{1,0:T(8,128)(2,1)S(1)}, u32[]{:S(2)}, u32[]{:S(2)}) collective-permute-start(bf16[48,3072]{1,0:T(8,128)(2,1)S(1)} %collective-permute-done), channel_id=1, source_target_pairs={{0,8},{4,12},{8,0},{12,4},{1,9},{5,13},{9,1},{13,5},{2,10},{6,14},... | collective-permute-start | bytes 884744 | tf_op jit(solution)/shard_map/ppermute | solution.py:140
  44.7 12.9 %collective-permute-start.7 = (bf16[48,3072]{1,0:T(8,128)(2,1)S(1)}, bf16[48,3072]{1,0:T(8,128)(2,1)S(1)}, u32[]{:S(2)}, u32[]{:S(2)}) collective-permute-start(bf16[48,3072]{1,0:T(8,128)(2,1)S(1)} %collective-permute-done), channel_id=1, source_target_pairs={{0,12},{4,0},{8,4},{12,8},{1,13},{5,1},{9,5},{13,9},{2,14},{6,2},{... | collective-permute-start | bytes 884744 | tf_op jit(solution)/shard_map/ppermute | solution.py:140
  57.6 5.5 %copy-start.12 = (f32[128]{0:T(128)S(1)}, f32[128]{0:T(128)}, u32[]{:S(2)}) copy-start(f32[128]{0:T(128)} %param.7) | copy-start | bytes 1540
  59.0 4.0 %collective-permute-start.8 = (f32[384,384]{1,0:T(8,128)S(1)}, f32[384,384]{1,0:T(8,128)}, u32[]{:S(2)}, u32[]{:S(2)}) collective-permute-start(f32[384,384]{1,0:T(8,128)S(1)} %fusion.mine), channel_id=1, source_target_pairs={{0,1},{1,0},{2,3},{3,2},{4,5},{5,4},{6,7},{7,6},{8,9},{9,8},{10,11... | collective-permute-start | bytes 1769480 | tf_op jit(solution)/shard_map/ppermute | solution.py:140
  60.9 18.3 %copy-start.1 = (bf16[3072,384]{1,0:T(8,128)(2,1)S(1)}, bf16[3072,384]{1,0:T(8,128)(2,1)}, u32[]{:S(2)}) copy-start(bf16[3072,384]{1,0:T(8,128)(2,1)} %weight.1) | copy-start | bytes 7077892
  67.6 20.0 %copy-start.4 = (bf16[1,6,64,384]{3,2,1,0:T(8,128)(2,1)}, bf16[1,6,64,384]{3,2,1,0:T(8,128)(2,1)S(1)}, u32[]{:S(2)}) copy-start(bf16[1,6,64,384]{3,2,1,0:T(8,128)(2,1)S(1)} %get-tuple-element.33.own) | copy-start | bytes 884740
  67.6 20.1 %copy-start.6 = (bf16[1,6,64,384]{3,2,1,0:T(8,128)(2,1)}, bf16[1,6,64,384]{3,2,1,0:T(8,128)(2,1)S(1)}, u32[]{:S(2)}) copy-start(bf16[1,6,64,384]{3,2,1,0:T(8,128)(2,1)S(1)} %get-tuple-element.36.two) | copy-start | bytes 884740
  67.7 22.0 %copy-start.8 = (bf16[1,6,64,384]{3,2,1,0:T(8,128)(2,1)}, bf16[1,6,64,384]{3,2,1,0:T(8,128)(2,1)S(1)}, u32[]{:S(2)}) copy-start(bf16[1,6,64,384]{3,2,1,0:T(8,128)(2,1)S(1)} %get-tuple-element.37.six) | copy-start | bytes 884740
  67.7 22.0 %collective-permute-start.15 = (bf16[6,64,384]{2,1,0:T(8,128)(2,1)S(1)}, bf16[6,64,384]{2,1,0:T(8,128)(2,1)S(1)}, u32[]{:S(2)}, u32[]{:S(2)}) collective-permute-start(bf16[6,64,384]{2,1,0:T(8,128)(2,1)S(1)} %bitcast.19), channel_id=1, source_target_pairs={{0,32},{1,97},{16,48},{17,113},{32,64},{33,1},{48,80},{49,17},{64,... | collective-permute-start | bytes 884744 | tf_op jit(solution)/shard_map/ppermute | solution.py:191
  72.1 22.1 %collective-permute-start.13 = (bf16[2,6,64,384]{3,2,1,0:T(8,128)(2,1)}, bf16[2,6,64,384]{3,2,1,0:T(8,128)(2,1)S(1)}, u32[]{:S(2)}, u32[]{:S(2)}) collective-permute-start(bf16[2,6,64,384]{3,2,1,0:T(8,128)(2,1)} %get-tuple-element.34), channel_id=1, source_target_pairs={{0,16},{16,32},{32,48},{48,64},{64,80},{80,96},{96,112},{112,0},{1... | collective-permute-start | bytes 1769480 | tf_op jit(solution)/shard_map/ppermute | solution.py:140
  75.6 18.6 %collective-permute-start.14 = (bf16[2,6,64,384]{3,2,1,0:T(8,128)(2,1)}, bf16[2,6,64,384]{3,2,1,0:T(8,128)(2,1)S(1)}, u32[]{:S(2)}, u32[]{:S(2)}) collective-permute-start(bf16[2,6,64,384]{3,2,1,0:T(8,128)(2,1)} %get-tuple-element.35), channel_id=1, source_target_pairs={{0,112},{16,0},{32,16},{48,32},{64,48},{80,64},{96,80},{112,96},{1... | collective-permute-start | bytes 1769480 | tf_op jit(solution)/shard_map/ppermute | solution.py:140
  83.1 31.3 %collective-permute-start.10 = (bf16[96,3072]{1,0:T(8,128)(2,1)}, bf16[96,3072]{1,0:T(8,128)(2,1)S(1)}, u32[]{:S(2)}, u32[]{:S(2)}) collective-permute-start(bf16[96,3072]{1,0:T(8,128)(2,1)} %get-tuple-element.29), channel_id=1, source_target_pairs={{0,12},{4,0},{8,4},{12,8},{1,13},{5,1},{9,5},{13,9},{2,14},{6,2},{... | collective-permute-start | bytes 1769480 | tf_op jit(solution)/shard_map/ppermute | solution.py:140
  87.7 31.9 %collective-permute-start.11 = (bf16[96,3072]{1,0:T(8,128)(2,1)}, bf16[96,3072]{1,0:T(8,128)(2,1)S(1)}, u32[]{:S(2)}, u32[]{:S(2)}) collective-permute-start(bf16[96,3072]{1,0:T(8,128)(2,1)} %get-tuple-element.30), channel_id=1, source_target_pairs={{0,4},{4,8},{8,12},{12,0},{1,5},{5,9},{9,13},{13,1},{2,6},{6,10},{... | collective-permute-start | bytes 1769480 | tf_op jit(solution)/shard_map/ppermute | solution.py:140
  89.7 0.7 copy-start.10
  90.4 30.0 %collective-permute-start.9 = (bf16[96,3072]{1,0:T(8,128)(2,1)}, bf16[96,3072]{1,0:T(8,128)(2,1)}, u32[]{:S(2)}, u32[]{:S(2)}) collective-permute-start(bf16[96,3072]{1,0:T(8,128)(2,1)} %get-tuple-element.28), channel_id=1, source_target_pairs={{0,8},{4,12},{8,0},{12,4},{1,9},{5,13},{9,1},{13,5},{2,10},{6,14},... | collective-permute-start | bytes 1769480 | tf_op jit(solution)/shard_map/ppermute | solution.py:140
  94.3 1.0 copy-start.7
  95.2 1.0 copy-start.9
  96.2 1.0 copy-start.11
  98.2 27.3 %collective-permute-start.16 = (bf16[6,64,384]{2,1,0:T(8,128)(2,1)}, bf16[6,64,384]{2,1,0:T(8,128)(2,1)}, u32[]{:S(2)}, u32[]{:S(2)}) collective-permute-start(bf16[6,64,384]{2,1,0:T(8,128)(2,1)} %get-tuple-element.39), channel_id=1, source_target_pairs={{0,32},{16,48},{32,64},{48,80},{64,96},{80,112},{96,0},{112,16},{1... | collective-permute-start | bytes 884744 | tf_op jit(solution)/shard_map/ppermute | solution.py:140
  102.2 23.3 %collective-permute-start.17 = (bf16[6,64,384]{2,1,0:T(8,128)(2,1)}, bf16[6,64,384]{2,1,0:T(8,128)(2,1)}, u32[]{:S(2)}, u32[]{:S(2)}) collective-permute-start(bf16[6,64,384]{2,1,0:T(8,128)(2,1)} %get-tuple-element.40), channel_id=1, source_target_pairs={{0,96},{16,112},{32,0},{48,16},{64,32},{80,48},{96,64},{112,80},{1... | collective-permute-start | bytes 884744 | tf_op jit(solution)/shard_map/ppermute | solution.py:140
  119.6 0.8 copy-start.2
  120.4 1.1 copy-start.3
  123.4 27.9 %collective-permute-start.12 = (bf16[48,3072]{1,0:T(8,128)(2,1)}, bf16[48,3072]{1,0:T(8,128)(2,1)S(1)}, u32[]{:S(2)}, u32[]{:S(2)}) collective-permute-start(bf16[48,3072]{1,0:T(8,128)(2,1)} %get-tuple-element.32), channel_id=1, source_target_pairs={{0,642},{2,640},{128,514},{130,512},{256,386},{258,384},{384,258},... | collective-permute-start | bytes 884744 | tf_op jit(solution)/shard_map/ppermute | solution.py:159
  125.5 1.0 copy-start.5
  127.7 12.7 %collective-permute-start.18 = (bf16[2,64,384]{2,1,0:T(8,128)(2,1)S(1)}, bf16[2,64,384]{2,1,0:T(8,128)(2,1)S(1)}, u32[]{:S(2)}, u32[]{:S(2)}) collective-permute-start(bf16[2,64,384]{2,1,0:T(8,128)(2,1)S(1)} %get-tuple-element.42), channel_id=1, source_target_pairs={{0,128},{128,256},{256,0},{384,512},{512,640},{640,384},{1,129},{1... | collective-permute-start | bytes 294920 | tf_op jit(solution)/shard_map/ppermute | solution.py:231
  129.6 19.2 %collective-permute-start.19 = (bf16[2,64,384]{2,1,0:T(8,128)(2,1)S(1)}, bf16[2,64,384]{2,1,0:T(8,128)(2,1)S(1)}, u32[]{:S(2)}, u32[]{:S(2)}) collective-permute-start(bf16[2,64,384]{2,1,0:T(8,128)(2,1)S(1)} %get-tuple-element.43), channel_id=1, source_target_pairs={{0,256},{128,0},{256,128},{384,640},{512,384},{640,512},{1,257},{1... | collective-permute-start | bytes 294920 | tf_op jit(solution)/shard_map/ppermute | solution.py:231
  149.4 9.0 %collective-permute-start.20 = (bf16[64,384]{1,0:T(8,128)(2,1)S(1)}, bf16[64,384]{1,0:T(8,128)(2,1)S(1)}, u32[]{:S(2)}, u32[]{:S(2)}) collective-permute-start(bf16[64,384]{1,0:T(8,128)(2,1)S(1)} %get-tuple-element.45), channel_id=1, source_target_pairs={{0,384},{128,512},{256,640},{384,0},{512,128},{640,256},{1,385},{1... | collective-permute-start | bytes 147464 | tf_op jit(solution)/shard_map/ppermute | solution.py:140

commit v8 on v5

--- a/solution.py
+++ b/solution.py
@@ -10,7 +10,13 @@
 
 F32 = jnp.float32
 BF16 = jnp.bfloat16
-ORDER = ((3, 1), (5, 7), (4,), (2,), (6,), (0,))
+ORDER = (
+    ((1, 0), (1, 1), (6, 0), (6, 1), (4, 0)),
+    ((7, 0), (7, 1), (2, 0), (2, 1), (4, 1)),
+    ((3, 0), (3, 1)),
+    ((5, 0), (5, 1)),
+    ((0, 0), (0, 1)),
+)
 
 
 def mean(value):
@@ -40,6 +46,7 @@
     rows = rows_out[...]
     part = tokens.shape[1] // nz
     blk = part // ny
+    half = blk // 2
     for z in range(nz):
         term[...] = factor * lax.dot_general(
             tokens[:, z * part : (z + 1) * part],
@@ -48,9 +55,9 @@
             preferred_element_type=F32,
         )
         for out, ks in zip(outs, ORDER):
-            for i, k in enumerate(ks):
-                at = pl.multiple_of(lax.rem(y + k, ny) * blk, blk)
-                out[i, z] = term[pl.ds(at, blk), :].astype(BF16)
+            for i, (k, h) in enumerate(ks):
+                at = pl.multiple_of(lax.rem(y + k, ny) * blk + h * half, half)
+                out[i, z] = term[pl.ds(at, half), :].astype(BF16)
 
 
 def rows_and_chunks(sizes, factor, where, mine, theirs, cot, cot_far, gain, tokens):
@@ -58,7 +65,7 @@
     heads = mine.shape[1]
     part = tokens.shape[1] // nz
     vmem = pl.BlockSpec(memory_space=pltpu.VMEM)
-    chunks = [jax.ShapeDtypeStruct((len(ks), nz, part // ny, heads), BF16) for ks in ORDER]
+    chunks = [jax.ShapeDtypeStruct((len(ks), nz, part // ny // 2, heads), BF16) for ks in ORDER]
     return pl.pallas_call(
         functools.partial(rows_kernel, sizes, factor),
         out_shape=[jax.ShapeDtypeStruct(mine.shape, BF16)] + chunks,
@@ -104,19 +111,18 @@
         out[...] = total.astype(out.dtype)
 
 
-def over_y_kernel(where, own, up, down, got2, got4, got6, kept, *sends):
+def over_y_kernel(where, own, up, down, got3, got5, kept, *sends):
     count, third = kept.shape[0], len(sends) + 1
+    half = own.shape[2]
     for k in range(third):
         place = lax.rem(where[0] + k, third)
         for i in range(count):
             z = i * third + place
-            total = own[0, z].astype(F32) + got4[z].astype(F32)
-            total = total + (up[1, z].astype(F32) + down[1, z].astype(F32))
-            total = total + (got2[z].astype(F32) + got6[z].astype(F32))
-            if k:
-                sends[k - 1][i] = total.astype(BF16)
-            else:
-                kept[i] = total
+            for h in range(2):
+                total = own[h, z].astype(F32) + (up[h, z].astype(F32) + down[h, z].astype(F32))
+                total = total + (got3[h, z].astype(F32) + got5[h, z].astype(F32))
+                out = sends[k - 1] if k else kept
+                out[i, h * half : (h + 1) * half] = total.astype(out.dtype)
 
 
 def over_third_kernel(where, kept, *rest):
@@ -177,15 +183,13 @@
         tokens,
     )
 
-    up, down, across, two, six, own = c
-    turn = [
-        (i * 2 + j, (i + (4, -4)[j]) % ny * 2 + j) for i in range(ny) for j in range(2)
-    ]
+    up, down, three, five, own = c
     got_up, got_down = shift(up, "y", 1), shift(down, "y", -1)
-    got4 = lax.ppermute(across[0], ("y", "c"), turn)
-    two = add(two[0], got_up[0]).astype(BF16)
-    six = add(six[0], got_down[0]).astype(BF16)
-    got2, got6 = shift(two, "y", 2), shift(six, "y", -2)
+    low = jnp.pad(got_up[4:].astype(F32), ((0, 1), (0, 0), (0, 0), (0, 0)))
+    high = jnp.pad(got_down[4:].astype(F32), ((1, 0), (0, 0), (0, 0), (0, 0)))
+    three = add(three, got_down[2:4], low).astype(BF16)
+    five = add(five, got_up[2:4], high).astype(BF16)
+    got3, got5 = shift(three, "y", 3), shift(five, "y", -3)
 
     block = (nh * count, width)
     back = small_call(
@@ -205,16 +209,15 @@
     third = nz // 2
     zl = lax.axis_index("zl")
     spot = jnp.stack([zl % third, zl // third]).astype(jnp.int32)
-    blk = own.shape[2]
+    blk = 2 * own.shape[2]
     kept, *sends = small_call(
         over_y_kernel,
         [jax.ShapeDtypeStruct((2, blk, heads), t) for t in (F32, *[BF16] * (third - 1))],
         own,
         got_up,
         got_down,
-        got2,
-        got4,
-        got6,
+        got3,
+        got5,
         where=spot,
     )
     got = []

time: 152 us -> 149 us (0.980)
  the two profiles are of different devices: /device:TPU:128 before, /device:TPU:6 now
where the time goes in v8:
time: 149 us; the launch traced here: 147 us
  starting transfers between devices  76.6 us (51%)
  waiting for transfers between devices  52.4 us (35%)
  Pallas kernels  8.22 us (6%)
  other arithmetic  4.15 us (3%)
  local copies, waits for them, and re-layouts  3.17 us (2%)
    ppermute x15, starting transfers between devices, shift(): lax.ppermute(value, axis, [(i, (i + by) % size) for i in range(size)])  49.9 us
    ppermute x15, waiting for transfers between devices, shift(): lax.ppermute(value, axis, [(i, (i + by) % size) for i in range(size)])  38.9 us
    ppermute x2, starting transfers between devices, mirror(): return lax.ppermute(value, ('zl', 'zh'), ends)  16.8 us
    ppermute x1, waiting for transfers between devices, body(): cot_far = lax.ppermute(cot_far, 'zl', [(i, nz - 1 - i) for i in range(nz)])  8.49 us
    ppermute x2, starting transfers between devices, body(): got.append(lax.ppermute(sends[k - 1], 'zl', hop))  7.32 us
    ppermute x2, waiting for transfers between devices, body(): got.append(lax.ppermute(sends[k - 1], 'zl', hop))  5.07 us
    pallas_call x4, Pallas kernels, small_call(): pl.pallas_call(kernel, out_shape=out_shape, in_specs=[pl.BlockSpec(memory...  4.61 us
    pallas_call x1, Pallas kernels, rows_and_chunks(): pl.pallas_call(functools.partial(rows_kernel, sizes, factor), out_shape=[...  3.61 us
  transfers between devices with their start and end apart: 20, of which 14 were waited for; matrix products, arithmetic and copies ran while one was open for 5% of the time, Pallas kernels for 3%

profile of v8, /device:TPU:6, one launch (start us, length us, event | category | flops | bytes accessed | tf_op | source)
XLA Modules:
  0.0 147.0 jit_solution(15713204472151984791)
XLA Ops:
  0.6 14.6 %collective-permute-start = (bf16[48,3072]{1,0:T(8,128)(2,1)}, bf16[48,3072]{1,0:T(8,128)(2,1)S(1)}, u32[]{:S(2)}, u32[]{:S(2)}) collective-permute-start(bf16[48,3072]{1,0:T(8,128)(2,1)} %param.4), channel_id=1, source_target_pairs={{0,642},{2,640},{128,514},{130,512},{256,386},{258,384},{384,258},... | collective-permute-start | bytes 884744 | tf_op jit(solution)/shard_map/ppermute | solution.py:159
  15.2 2.4 %collective-permute-start.2 = (bf16[48,3072]{1,0:T(8,128)(2,1)}, bf16[48,3072]{1,0:T(8,128)(2,1)}, u32[]{:S(2)}, u32[]{:S(2)}) collective-permute-start(bf16[48,3072]{1,0:T(8,128)(2,1)} %param.4), channel_id=1, source_target_pairs={{0,4},{4,8},{8,12},{12,0},{1,5},{5,9},{9,13},{13,1},{2,6},{6,10},{... | collective-permute-start | bytes 884744 | tf_op jit(solution)/shard_map/ppermute | solution.py:140
  17.6 4.3 %collective-permute-start.4 = (bf16[48,3072]{1,0:T(8,128)(2,1)}, bf16[48,3072]{1,0:T(8,128)(2,1)S(1)}, u32[]{:S(2)}, u32[]{:S(2)}) collective-permute-start(bf16[48,3072]{1,0:T(8,128)(2,1)} %param.4), channel_id=1, source_target_pairs={{0,8},{4,12},{8,0},{12,4},{1,9},{5,13},{9,1},{13,5},{2,10},{6,14},... | collective-permute-start | bytes 884744 | tf_op jit(solution)/shard_map/ppermute | solution.py:140
  22.0 1.9 %collective-permute-start.6 = (bf16[48,3072]{1,0:T(8,128)(2,1)}, bf16[48,3072]{1,0:T(8,128)(2,1)S(1)}, u32[]{:S(2)}, u32[]{:S(2)}) collective-permute-start(bf16[48,3072]{1,0:T(8,128)(2,1)} %param.4), channel_id=1, source_target_pairs={{0,12},{4,0},{8,4},{12,8},{1,13},{5,1},{9,5},{13,9},{2,14},{6,2},{... | collective-permute-start | bytes 884744 | tf_op jit(solution)/shard_map/ppermute | solution.py:140
  23.9 1.0 dynamic-slice_bitcast_fusion
  24.9 0.0 copy-start
  24.9 2.6 %collective-permute-start.1 = (bf16[4,48,384]{2,1,0:T(8,128)(2,1)S(1)}, bf16[4,48,384]{2,1,0:T(8,128)(2,1)S(1)}, u32[]{:S(2)}, u32[]{:S(2)}) collective-permute-start(bf16[4,48,384]{2,1,0:T(8,128)(2,1)S(1)} %get-tuple-element.41), channel_id=1, source_target_pairs={{0,640},{128,512},{256,384},{384,256},{512,128},{640,0},{1,641},{1... | collective-permute-start | bytes 442376 | tf_op jit(solution)/shard_map/ppermute | solution.py:165
  27.5 1.0 constant_dynamic-update-slice_fusion.7
  28.5 8.5 %collective-permute-done.1.cot_far = bf16[4,48,384]{2,1,0:T(8,128)(2,1)S(1)} collective-permute-done((bf16[4,48,384]{2,1,0:T(8,128)(2,1)S(1)}, bf16[4,48,384]{2,1,0:T(8,128)(2,1)S(1)}, u32[]{:S(2)}, u32[]{:S(2)}) %collective-permute-start.1) | collective-permute-done | bytes 147488 | tf_op jit(solution)/shard_map/ppermute | solution.py:165
  37.0 0.0 collective-permute-done
  37.0 5.1 %collective-permute-start.3 = (bf16[48,3072]{1,0:T(8,128)(2,1)S(1)}, bf16[48,3072]{1,0:T(8,128)(2,1)S(1)}, u32[]{:S(2)}, u32[]{:S(2)}) collective-permute-start(bf16[48,3072]{1,0:T(8,128)(2,1)S(1)} %collective-permute-done), channel_id=1, source_target_pairs={{0,4},{4,8},{8,12},{12,0},{1,5},{5,9},{9,13},{13,1},{2,6},{6,10},{... | collective-permute-start | bytes 884744 | tf_op jit(solution)/shard_map/ppermute | solution.py:140
  42.1 1.9 %collective-permute-start.5 = (bf16[48,3072]{1,0:T(8,128)(2,1)S(1)}, bf16[48,3072]{1,0:T(8,128)(2,1)S(1)}, u32[]{:S(2)}, u32[]{:S(2)}) collective-permute-start(bf16[48,3072]{1,0:T(8,128)(2,1)S(1)} %collective-permute-done), channel_id=1, source_target_pairs={{0,8},{4,12},{8,0},{12,4},{1,9},{5,13},{9,1},{13,5},{2,10},{6,14},... | collective-permute-start | bytes 884744 | tf_op jit(solution)/shard_map/ppermute | solution.py:140
  44.1 0.0 collective-permute-done.2
  44.1 3.3 %collective-permute-start.7 = (bf16[48,3072]{1,0:T(8,128)(2,1)S(1)}, bf16[48,3072]{1,0:T(8,128)(2,1)S(1)}, u32[]{:S(2)}, u32[]{:S(2)}) collective-permute-start(bf16[48,3072]{1,0:T(8,128)(2,1)S(1)} %collective-permute-done), channel_id=1, source_target_pairs={{0,12},{4,0},{8,4},{12,8},{1,13},{5,1},{9,5},{13,9},{2,14},{6,2},{... | collective-permute-start | bytes 884744 | tf_op jit(solution)/shard_map/ppermute | solution.py:140
  47.4 1.0 constant_dynamic-update-slice_fusion.5
  48.4 4.1 %collective-permute-done.3 = bf16[48,3072]{1,0:T(8,128)(2,1)S(1)} collective-permute-done((bf16[48,3072]{1,0:T(8,128)(2,1)S(1)}, bf16[48,3072]{1,0:T(8,128)(2,1)S(1)}, u32[]{:S(2)}, u32[]{:S(2)}) %collective-permute-start.3) | collective-permute-done | bytes 294944 | tf_op jit(solution)/shard_map/ppermute | solution.py:140
  52.6 0.0 collective-permute-done.4
  52.6 2.4 %collective-permute-done.5 = bf16[48,3072]{1,0:T(8,128)(2,1)S(1)} collective-permute-done((bf16[48,3072]{1,0:T(8,128)(2,1)S(1)}, bf16[48,3072]{1,0:T(8,128)(2,1)S(1)}, u32[]{:S(2)}, u32[]{:S(2)}) %collective-permute-start.5) | collective-permute-done | bytes 294944 | tf_op jit(solution)/shard_map/ppermute | solution.py:140
  55.1 0.0 collective-permute-done.6
  55.1 3.0 %collective-permute-done.7 = bf16[48,3072]{1,0:T(8,128)(2,1)S(1)} collective-permute-done((bf16[48,3072]{1,0:T(8,128)(2,1)S(1)}, bf16[48,3072]{1,0:T(8,128)(2,1)S(1)}, u32[]{:S(2)}, u32[]{:S(2)}) %collective-permute-start.7) | collective-permute-done | bytes 294944 | tf_op jit(solution)/shard_map/ppermute | solution.py:140
  58.2 0.0 copy-done
  58.2 0.0 copy-start.2
  58.2 1.4 fusion.mine
  59.6 1.9 %collective-permute-start.8 = (f32[384,384]{1,0:T(8,128)S(1)}, f32[384,384]{1,0:T(8,128)}, u32[]{:S(2)}, u32[]{:S(2)}) collective-permute-start(f32[384,384]{1,0:T(8,128)S(1)} %fusion.mine), channel_id=1, source_target_pairs={{0,1},{1,0},{2,3},{3,2},{4,5},{5,4},{6,7},{7,6},{8,9},{9,8},{10,11... | collective-permute-start | bytes 1769480 | tf_op jit(solution)/shard_map/ppermute | solution.py:140
  61.5 0.0 copy-start.1
  61.6 0.1 pad_add_fusion.where
  61.6 2.0 %collective-permute-done.8.theirs = f32[384,384]{1,0:T(8,128)} collective-permute-done((f32[384,384]{1,0:T(8,128)S(1)}, f32[384,384]{1,0:T(8,128)}, u32[]{:S(2)}, u32[]{:S(2)}) %collective-permute-start.8) | collective-permute-done | bytes 589856 | tf_op jit(solution)/shard_map/ppermute | solution.py:140
  63.6 0.0 copy-done.2
  63.6 3.6 %rows_and_chunks.1 = (bf16[384,384]{1,0:T(8,128)(2,1)S(1)}, bf16[5,6,32,384]{3,2,1,0:T(8,128)(2,1)S(1)}, bf16[5,6,32,384]{3,2,1,0:T(8,128)(2,1)S(1)}, bf16[2,6,3...) custom-call(s32[2]{0:T(128)S(1)} %pad_add_fusion.where, ...), custom_call_target="tpu_custom_call" | custom-call | tf_op jit(solution)/shard_map/rows_and_chunks/pallas_call | solution.py:69
  67.3 5.4 %collective-permute-start.14 = (bf16[5,6,32,384]{3,2,1,0:T(8,128)(2,1)S(1)}, bf16[5,6,32,384]{3,2,1,0:T(8,128)(2,1)S(1)}, u32[]{:S(2)}, u32[]{:S(2)}) collective-permute-start(bf16[5,6,32,384]{3,2,1,0:T(8,128)(2,1)S(1)} %get-tuple-element.32), channel_id=1, source_target_pairs={{0,112},{16,0},{32,16},{48,32},{64,48},{80,64},{96,80},{112,96},{1... | collective-permute-start | bytes 2211848 | tf_op jit(solution)/shard_map/ppermute | solution.py:140
  72.6 1.9 %collective-permute-start.13 = (bf16[5,6,32,384]{3,2,1,0:T(8,128)(2,1)S(1)}, bf16[5,6,32,384]{3,2,1,0:T(8,128)(2,1)S(1)}, u32[]{:S(2)}, u32[]{:S(2)}) collective-permute-start(bf16[5,6,32,384]{3,2,1,0:T(8,128)(2,1)S(1)} %get-tuple-element.31), channel_id=1, source_target_pairs={{0,16},{16,32},{32,48},{48,64},{64,80},{80,96},{96,112},{112,0},{1... | collective-permute-start | bytes 2211848 | tf_op jit(solution)/shard_map/ppermute | solution.py:140
  74.6 0.0 copy-done.1
  74.6 3.0 %shard_map.59 = (f32[96,3072]{1,0:T(8,128)S(1)}, bf16[96,3072]{1,0:T(8,128)(2,1)S(1)}, bf16[96,3072]{1,0:T(8,128)(2,1)S(1)}, bf16[96,3072]{1,0:T(8,128)(2,1)S(1)}) custom-call(bf16[384,384]{1,0:T(8,128)(2,1)S(1)} %get-tuple-element.23.rows, bf16[3072,384]{1,0:T(8,128)(2,1)S(1)} %copy-done.1), custom_call_target="tpu_custom_call" | custom-call | tf_op jit(solution)/shard_map/pallas_call | solution.py:83
  77.6 1.9 %collective-permute-start.10 = (bf16[96,3072]{1,0:T(8,128)(2,1)S(1)}, bf16[96,3072]{1,0:T(8,128)(2,1)S(1)}, u32[]{:S(2)}, u32[]{:S(2)}) collective-permute-start(bf16[96,3072]{1,0:T(8,128)(2,1)S(1)} %get-tuple-element.26), channel_id=1, source_target_pairs={{0,12},{4,0},{8,4},{12,8},{1,13},{5,1},{9,5},{13,9},{2,14},{6,2},{... | collective-permute-start | bytes 1769480 | tf_op jit(solution)/shard_map/ppermute | solution.py:140
  79.5 5.1 %collective-permute-start.11 = (bf16[96,3072]{1,0:T(8,128)(2,1)S(1)}, bf16[96,3072]{1,0:T(8,128)(2,1)S(1)}, u32[]{:S(2)}, u32[]{:S(2)}) collective-permute-start(bf16[96,3072]{1,0:T(8,128)(2,1)S(1)} %get-tuple-element.27), channel_id=1, source_target_pairs={{0,4},{4,8},{8,12},{12,0},{1,5},{5,9},{9,13},{13,1},{2,6},{6,10},{... | collective-permute-start | bytes 1769480 | tf_op jit(solution)/shard_map/ppermute | solution.py:140
  84.7 1.9 %collective-permute-start.9 = (bf16[96,3072]{1,0:T(8,128)(2,1)S(1)}, bf16[96,3072]{1,0:T(8,128)(2,1)S(1)}, u32[]{:S(2)}, u32[]{:S(2)}) collective-permute-start(bf16[96,3072]{1,0:T(8,128)(2,1)S(1)} %get-tuple-element.25), channel_id=1, source_target_pairs={{0,8},{4,12},{8,0},{12,4},{1,9},{5,13},{9,1},{13,5},{2,10},{6,14},... | collective-permute-start | bytes 1769480 | tf_op jit(solution)/shard_map/ppermute | solution.py:140
  86.6 2.1 %collective-permute-done.14.down = bf16[5,6,32,384]{3,2,1,0:T(8,128)(2,1)S(1)} collective-permute-done((bf16[5,6,32,384]{3,2,1,0:T(8,128)(2,1)S(1)}, bf16[5,6,32,384]{3,2,1,0:T(8,128)(2,1)S(1)}, u32[]{:S(2)}, u32[]{:S(2)}) %collective-permute-start.14) | collective-permute-done | bytes 737312 | tf_op jit(solution)/shard_map/ppermute | solution.py:140
  88.7 5.3 %collective-permute-done.13.up = bf16[5,6,32,384]{3,2,1,0:T(8,128)(2,1)S(1)} collective-permute-done((bf16[5,6,32,384]{3,2,1,0:T(8,128)(2,1)S(1)}, bf16[5,6,32,384]{3,2,1,0:T(8,128)(2,1)S(1)}, u32[]{:S(2)}, u32[]{:S(2)}) %collective-permute-start.13) | collective-permute-done | bytes 737312 | tf_op jit(solution)/shard_map/ppermute | solution.py:140
  94.0 0.8 add_convert_fusion
  94.8 3.6 %collective-permute-start.16 = (bf16[2,6,32,384]{3,2,1,0:T(8,128)(2,1)}, bf16[2,6,32,384]{3,2,1,0:T(8,128)(2,1)S(1)}, u32[]{:S(2)}, u32[]{:S(2)}) collective-permute-start(bf16[2,6,32,384]{3,2,1,0:T(8,128)(2,1)} %add_convert_fusion), channel_id=1, source_target_pairs={{0,80},{16,96},{32,112},{48,0},{64,16},{80,32},{96,48},{112,64},{1... | collective-permute-start | bytes 884744 | tf_op jit(solution)/shard_map/ppermute | solution.py:140
  98.4 0.8 add_convert_fusion.1
  99.3 4.0 %collective-permute-start.15 = (bf16[2,6,32,384]{3,2,1,0:T(8,128)(2,1)}, bf16[2,6,32,384]{3,2,1,0:T(8,128)(2,1)S(1)}, u32[]{:S(2)}, u32[]{:S(2)}) collective-permute-start(bf16[2,6,32,384]{3,2,1,0:T(8,128)(2,1)} %add_convert_fusion.1), channel_id=1, source_target_pairs={{0,48},{16,64},{32,80},{48,96},{64,112},{80,0},{96,16},{112,32},{1... | collective-permute-start | bytes 884744 | tf_op jit(solution)/shard_map/ppermute | solution.py:140
  103.3 5.2 %collective-permute-done.10.rest_1_ = bf16[96,3072]{1,0:T(8,128)(2,1)S(1)} collective-permute-done((bf16[96,3072]{1,0:T(8,128)(2,1)S(1)}, bf16[96,3072]{1,0:T(8,128)(2,1)S(1)}, u32[]{:S(2)}, u32[]{:S(2)}) %collective-permute-start.10) | collective-permute-done | bytes 589856 | tf_op jit(solution)/shard_map/ppermute | solution.py:140
  108.4 1.2 collective-permute-done.11.rest_2_
  109.6 0.0 collective-permute-done.9.rest_0_
  109.6 0.3 shard_map.60
  109.9 2.2 %collective-permute-start.12 = (bf16[48,3072]{1,0:T(8,128)(2,1)S(1)}, bf16[48,3072]{1,0:T(8,128)(2,1)}, u32[]{:S(2)}, u32[]{:S(2)}) collective-permute-start(bf16[48,3072]{1,0:T(8,128)(2,1)S(1)} %get-tuple-element.29), channel_id=1, source_target_pairs={{0,642},{2,640},{128,514},{130,512},{256,386},{258,384},{384,258},... | collective-permute-start | bytes 884744 | tf_op jit(solution)/shard_map/ppermute | solution.py:159
  112.2 0.1 pad_add_fusion.1.where
  112.3 4.6 %collective-permute-done.16.got5 = bf16[2,6,32,384]{3,2,1,0:T(8,128)(2,1)S(1)} collective-permute-done((bf16[2,6,32,384]{3,2,1,0:T(8,128)(2,1)}, bf16[2,6,32,384]{3,2,1,0:T(8,128)(2,1)S(1)}, u32[]{:S(2)}, u32[]{:S(2)}) %collective-permute-start.16) | collective-permute-done | bytes 294944 | tf_op jit(solution)/shard_map/ppermute | solution.py:140
  116.9 8.0 %collective-permute-done.15.got3 = bf16[2,6,32,384]{3,2,1,0:T(8,128)(2,1)S(1)} collective-permute-done((bf16[2,6,32,384]{3,2,1,0:T(8,128)(2,1)}, bf16[2,6,32,384]{3,2,1,0:T(8,128)(2,1)S(1)}, u32[]{:S(2)}, u32[]{:S(2)}) %collective-permute-start.15) | collective-permute-done | bytes 294944 | tf_op jit(solution)/shard_map/ppermute | solution.py:140
  124.8 0.7 shard_map.61
  125.6 5.4 %collective-permute-start.17 = (bf16[2,64,384]{2,1,0:T(8,128)(2,1)S(1)}, bf16[2,64,384]{2,1,0:T(8,128)(2,1)S(1)}, u32[]{:S(2)}, u32[]{:S(2)}) collective-permute-start(bf16[2,64,384]{2,1,0:T(8,128)(2,1)S(1)} %get-tuple-element.36), channel_id=1, source_target_pairs={{0,128},{128,256},{256,0},{384,512},{512,640},{640,384},{1,129},{1... | collective-permute-start | bytes 294920 | tf_op jit(solution)/shard_map/ppermute | solution.py:226
  131.0 2.0 %collective-permute-start.18 = (bf16[2,64,384]{2,1,0:T(8,128)(2,1)S(1)}, bf16[2,64,384]{2,1,0:T(8,128)(2,1)S(1)}, u32[]{:S(2)}, u32[]{:S(2)}) collective-permute-start(bf16[2,64,384]{2,1,0:T(8,128)(2,1)S(1)} %get-tuple-element.37), channel_id=1, source_target_pairs={{0,256},{128,0},{256,128},{384,640},{512,384},{640,512},{1,257},{1... | collective-permute-start | bytes 294920 | tf_op jit(solution)/shard_map/ppermute | solution.py:226
  132.9 0.7 collective-permute-done.17.rest_0_
  133.6 4.4 %collective-permute-done.18.rest_1_ = bf16[2,64,384]{2,1,0:T(8,128)(2,1)S(1)} collective-permute-done((bf16[2,64,384]{2,1,0:T(8,128)(2,1)S(1)}, bf16[2,64,384]{2,1,0:T(8,128)(2,1)S(1)}, u32[]{:S(2)}, u32[]{:S(2)}) %collective-permute-start.18) | collective-permute-done | bytes 98336 | tf_op jit(solution)/shard_map/ppermute | solution.py:226
  138.0 0.6 shard_map.62
  138.6 5.1 %collective-permute-start.19 = (bf16[64,384]{1,0:T(8,128)(2,1)S(1)}, bf16[64,384]{1,0:T(8,128)(2,1)S(1)}, u32[]{:S(2)}, u32[]{:S(2)}) collective-permute-start(bf16[64,384]{1,0:T(8,128)(2,1)S(1)} %get-tuple-element.39), channel_id=1, source_target_pairs={{0,384},{128,512},{256,640},{384,0},{512,128},{640,256},{1,385},{1... | collective-permute-start | bytes 147464 | tf_op jit(solution)/shard_map/ppermute | solution.py:140
  143.7 0.0 collective-permute-done.12
  143.7 1.7 %add_convert_fusion.2 = bf16[48,3072]{1,0:T(8,128)(2,1)} fusion(f32[48,3072]{1,0:T(8,128)S(1)} %get-tuple-element.28, bf16[48,3072]{1,0:T(8,128)(2,1)} %collective-permute-done.12), kind=kLoop, calls=%fused_computation.2 | loop fusion | flops 442368 | bytes 1179648 | tf_op jit(solution)/shard_map/convert_element_type | solution.py:207
  145.4 1.0 collective-permute-done.19
  146.4 0.7 convert_add_fusion
  (8 shorter events, 0.2 us)
Async XLA Ops:
  0.6 36.3 %collective-permute-start = (bf16[48,3072]{1,0:T(8,128)(2,1)}, bf16[48,3072]{1,0:T(8,128)(2,1)S(1)}, u32[]{:S(2)}, u32[]{:S(2)}) collective-permute-start(bf16[48,3072]{1,0:T(8,128)(2,1)} %param.4), channel_id=1, source_target_pairs={{0,642},{2,640},{128,514},{130,512},{256,386},{258,384},{384,258},... | collective-permute-start | bytes 884744 | tf_op jit(solution)/shard_map/ppermute | solution.py:159
  15.2 28.9 %collective-permute-start.2 = (bf16[48,3072]{1,0:T(8,128)(2,1)}, bf16[48,3072]{1,0:T(8,128)(2,1)}, u32[]{:S(2)}, u32[]{:S(2)}) collective-permute-start(bf16[48,3072]{1,0:T(8,128)(2,1)} %param.4), channel_id=1, source_target_pairs={{0,4},{4,8},{8,12},{12,0},{1,5},{5,9},{9,13},{13,1},{2,6},{6,10},{... | collective-permute-start | bytes 884744 | tf_op jit(solution)/shard_map/ppermute | solution.py:140
  17.6 34.9 %collective-permute-start.4 = (bf16[48,3072]{1,0:T(8,128)(2,1)}, bf16[48,3072]{1,0:T(8,128)(2,1)S(1)}, u32[]{:S(2)}, u32[]{:S(2)}) collective-permute-start(bf16[48,3072]{1,0:T(8,128)(2,1)} %param.4), channel_id=1, source_target_pairs={{0,8},{4,12},{8,0},{12,4},{1,9},{5,13},{9,1},{13,5},{2,10},{6,14},... | collective-permute-start | bytes 884744 | tf_op jit(solution)/shard_map/ppermute | solution.py:140
  22.0 33.1 %collective-permute-start.6 = (bf16[48,3072]{1,0:T(8,128)(2,1)}, bf16[48,3072]{1,0:T(8,128)(2,1)S(1)}, u32[]{:S(2)}, u32[]{:S(2)}) collective-permute-start(bf16[48,3072]{1,0:T(8,128)(2,1)} %param.4), channel_id=1, source_target_pairs={{0,12},{4,0},{8,4},{12,8},{1,13},{5,1},{9,5},{13,9},{2,14},{6,2},{... | collective-permute-start | bytes 884744 | tf_op jit(solution)/shard_map/ppermute | solution.py:140
  24.9 33.3 %copy-start = (bf16[3072,384]{1,0:T(8,128)(2,1)S(1)}, bf16[3072,384]{1,0:T(8,128)(2,1)}, u32[]{:S(2)}) copy-start(bf16[3072,384]{1,0:T(8,128)(2,1)} %weight.1) | copy-start | bytes 7077892
  24.9 12.0 %collective-permute-start.1 = (bf16[4,48,384]{2,1,0:T(8,128)(2,1)S(1)}, bf16[4,48,384]{2,1,0:T(8,128)(2,1)S(1)}, u32[]{:S(2)}, u32[]{:S(2)}) collective-permute-start(bf16[4,48,384]{2,1,0:T(8,128)(2,1)S(1)} %get-tuple-element.41), channel_id=1, source_target_pairs={{0,640},{128,512},{256,384},{384,256},{512,128},{640,0},{1,641},{1... | collective-permute-start | bytes 442376 | tf_op jit(solution)/shard_map/ppermute | solution.py:165
  37.0 15.6 %collective-permute-start.3 = (bf16[48,3072]{1,0:T(8,128)(2,1)S(1)}, bf16[48,3072]{1,0:T(8,128)(2,1)S(1)}, u32[]{:S(2)}, u32[]{:S(2)}) collective-permute-start(bf16[48,3072]{1,0:T(8,128)(2,1)S(1)} %collective-permute-done), channel_id=1, source_target_pairs={{0,4},{4,8},{8,12},{12,0},{1,5},{5,9},{9,13},{13,1},{2,6},{6,10},{... | collective-permute-start | bytes 884744 | tf_op jit(solution)/shard_map/ppermute | solution.py:140
  42.1 12.9 %collective-permute-start.5 = (bf16[48,3072]{1,0:T(8,128)(2,1)S(1)}, bf16[48,3072]{1,0:T(8,128)(2,1)S(1)}, u32[]{:S(2)}, u32[]{:S(2)}) collective-permute-start(bf16[48,3072]{1,0:T(8,128)(2,1)S(1)} %collective-permute-done), channel_id=1, source_target_pairs={{0,8},{4,12},{8,0},{12,4},{1,9},{5,13},{9,1},{13,5},{2,10},{6,14},... | collective-permute-start | bytes 884744 | tf_op jit(solution)/shard_map/ppermute | solution.py:140
  44.1 14.0 %collective-permute-start.7 = (bf16[48,3072]{1,0:T(8,128)(2,1)S(1)}, bf16[48,3072]{1,0:T(8,128)(2,1)S(1)}, u32[]{:S(2)}, u32[]{:S(2)}) collective-permute-start(bf16[48,3072]{1,0:T(8,128)(2,1)S(1)} %collective-permute-done), channel_id=1, source_target_pairs={{0,12},{4,0},{8,4},{12,8},{1,13},{5,1},{9,5},{13,9},{2,14},{6,2},{... | collective-permute-start | bytes 884744 | tf_op jit(solution)/shard_map/ppermute | solution.py:140
  58.2 5.5 %copy-start.2 = (f32[128]{0:T(128)S(1)}, f32[128]{0:T(128)}, u32[]{:S(2)}) copy-start(f32[128]{0:T(128)} %param.7) | copy-start | bytes 1540
  59.6 4.0 %collective-permute-start.8 = (f32[384,384]{1,0:T(8,128)S(1)}, f32[384,384]{1,0:T(8,128)}, u32[]{:S(2)}, u32[]{:S(2)}) collective-permute-start(f32[384,384]{1,0:T(8,128)S(1)} %fusion.mine), channel_id=1, source_target_pairs={{0,1},{1,0},{2,3},{3,2},{4,5},{5,4},{6,7},{7,6},{8,9},{9,8},{10,11... | collective-permute-start | bytes 1769480 | tf_op jit(solution)/shard_map/ppermute | solution.py:140
  61.5 13.0 %copy-start.1 = (bf16[3072,384]{1,0:T(8,128)(2,1)S(1)}, bf16[3072,384]{1,0:T(8,128)(2,1)}, u32[]{:S(2)}) copy-start(bf16[3072,384]{1,0:T(8,128)(2,1)} %weight.1) | copy-start | bytes 7077892
  67.3 21.4 %collective-permute-start.14 = (bf16[5,6,32,384]{3,2,1,0:T(8,128)(2,1)S(1)}, bf16[5,6,32,384]{3,2,1,0:T(8,128)(2,1)S(1)}, u32[]{:S(2)}, u32[]{:S(2)}) collective-permute-start(bf16[5,6,32,384]{3,2,1,0:T(8,128)(2,1)S(1)} %get-tuple-element.32), channel_id=1, source_target_pairs={{0,112},{16,0},{32,16},{48,32},{64,48},{80,64},{96,80},{112,96},{1... | collective-permute-start | bytes 2211848 | tf_op jit(solution)/shard_map/ppermute | solution.py:140
  72.6 21.4 %collective-permute-start.13 = (bf16[5,6,32,384]{3,2,1,0:T(8,128)(2,1)S(1)}, bf16[5,6,32,384]{3,2,1,0:T(8,128)(2,1)S(1)}, u32[]{:S(2)}, u32[]{:S(2)}) collective-permute-start(bf16[5,6,32,384]{3,2,1,0:T(8,128)(2,1)S(1)} %get-tuple-element.31), channel_id=1, source_target_pairs={{0,16},{16,32},{32,48},{48,64},{64,80},{80,96},{96,112},{112,0},{1... | collective-permute-start | bytes 2211848 | tf_op jit(solution)/shard_map/ppermute | solution.py:140
  77.6 30.8 %collective-permute-start.10 = (bf16[96,3072]{1,0:T(8,128)(2,1)S(1)}, bf16[96,3072]{1,0:T(8,128)(2,1)S(1)}, u32[]{:S(2)}, u32[]{:S(2)}) collective-permute-start(bf16[96,3072]{1,0:T(8,128)(2,1)S(1)} %get-tuple-element.26), channel_id=1, source_target_pairs={{0,12},{4,0},{8,4},{12,8},{1,13},{5,1},{9,5},{13,9},{2,14},{6,2},{... | collective-permute-start | bytes 1769480 | tf_op jit(solution)/shard_map/ppermute | solution.py:140
  79.5 30.1 %collective-permute-start.11 = (bf16[96,3072]{1,0:T(8,128)(2,1)S(1)}, bf16[96,3072]{1,0:T(8,128)(2,1)S(1)}, u32[]{:S(2)}, u32[]{:S(2)}) collective-permute-start(bf16[96,3072]{1,0:T(8,128)(2,1)S(1)} %get-tuple-element.27), channel_id=1, source_target_pairs={{0,4},{4,8},{8,12},{12,0},{1,5},{5,9},{9,13},{13,1},{2,6},{6,10},{... | collective-permute-start | bytes 1769480 | tf_op jit(solution)/shard_map/ppermute | solution.py:140
  84.7 25.0 %collective-permute-start.9 = (bf16[96,3072]{1,0:T(8,128)(2,1)S(1)}, bf16[96,3072]{1,0:T(8,128)(2,1)S(1)}, u32[]{:S(2)}, u32[]{:S(2)}) collective-permute-start(bf16[96,3072]{1,0:T(8,128)(2,1)S(1)} %get-tuple-element.25), channel_id=1, source_target_pairs={{0,8},{4,12},{8,0},{12,4},{1,9},{5,13},{9,1},{13,5},{2,10},{6,14},... | collective-permute-start | bytes 1769480 | tf_op jit(solution)/shard_map/ppermute | solution.py:140
  94.8 22.1 %collective-permute-start.16 = (bf16[2,6,32,384]{3,2,1,0:T(8,128)(2,1)}, bf16[2,6,32,384]{3,2,1,0:T(8,128)(2,1)S(1)}, u32[]{:S(2)}, u32[]{:S(2)}) collective-permute-start(bf16[2,6,32,384]{3,2,1,0:T(8,128)(2,1)} %add_convert_fusion), channel_id=1, source_target_pairs={{0,80},{16,96},{32,112},{48,0},{64,16},{80,32},{96,48},{112,64},{1... | collective-permute-start | bytes 884744 | tf_op jit(solution)/shard_map/ppermute | solution.py:140
  99.3 25.6 %collective-permute-start.15 = (bf16[2,6,32,384]{3,2,1,0:T(8,128)(2,1)}, bf16[2,6,32,384]{3,2,1,0:T(8,128)(2,1)S(1)}, u32[]{:S(2)}, u32[]{:S(2)}) collective-permute-start(bf16[2,6,32,384]{3,2,1,0:T(8,128)(2,1)} %add_convert_fusion.1), channel_id=1, source_target_pairs={{0,48},{16,64},{32,80},{48,96},{64,112},{80,0},{96,16},{112,32},{1... | collective-permute-start | bytes 884744 | tf_op jit(solution)/shard_map/ppermute | solution.py:140
  109.9 33.7 %collective-permute-start.12 = (bf16[48,3072]{1,0:T(8,128)(2,1)S(1)}, bf16[48,3072]{1,0:T(8,128)(2,1)}, u32[]{:S(2)}, u32[]{:S(2)}) collective-permute-start(bf16[48,3072]{1,0:T(8,128)(2,1)S(1)} %get-tuple-element.29), channel_id=1, source_target_pairs={{0,642},{2,640},{128,514},{130,512},{256,386},{258,384},{384,258},... | collective-permute-start | bytes 884744 | tf_op jit(solution)/shard_map/ppermute | solution.py:159
  125.6 8.0 %collective-permute-start.17 = (bf16[2,64,384]{2,1,0:T(8,128)(2,1)S(1)}, bf16[2,64,384]{2,1,0:T(8,128)(2,1)S(1)}, u32[]{:S(2)}, u32[]{:S(2)}) collective-permute-start(bf16[2,64,384]{2,1,0:T(8,128)(2,1)S(1)} %get-tuple-element.36), channel_id=1, source_target_pairs={{0,128},{128,256},{256,0},{384,512},{512,640},{640,384},{1,129},{1... | collective-permute-start | bytes 294920 | tf_op jit(solution)/shard_map/ppermute | solution.py:226
  131.0 7.0 %collective-permute-start.18 = (bf16[2,64,384]{2,1,0:T(8,128)(2,1)S(1)}, bf16[2,64,384]{2,1,0:T(8,128)(2,1)S(1)}, u32[]{:S(2)}, u32[]{:S(2)}) collective-permute-start(bf16[2,64,384]{2,1,0:T(8,128)(2,1)S(1)} %get-tuple-element.37), channel_id=1, source_target_pairs={{0,256},{128,0},{256,128},{384,640},{512,384},{640,512},{1,257},{1... | collective-permute-start | bytes 294920 | tf_op jit(solution)/shard_map/ppermute | solution.py:226
  138.6 7.8 %collective-permute-start.19 = (bf16[64,384]{1,0:T(8,128)(2,1)S(1)}, bf16[64,384]{1,0:T(8,128)(2,1)S(1)}, u32[]{:S(2)}, u32[]{:S(2)}) collective-permute-start(bf16[64,384]{1,0:T(8,128)(2,1)S(1)} %get-tuple-element.39), channel_id=1, source_target_pairs={{0,384},{128,512},{256,640},{384,0},{512,128},{640,256},{1,385},{1... | collective-permute-start | bytes 147464 | tf_op jit(solution)/shard_map/ppermute | solution.py:140

commit v9 on v8

--- a/solution.py
+++ b/solution.py
@@ -164,8 +164,8 @@
     cot_far = lax.dynamic_index_in_dim(cot, 1 - zh, 1, False)
     cot_far = lax.ppermute(cot_far, "zl", [(i, nz - 1 - i) for i in range(nz)])
     cot = lax.dynamic_index_in_dim(cot, zh, 1, False)
-    peer, cot_far = lax.optimization_barrier((peer, cot_far))
     other = [peer] + [shift(peer, "x", k) for k in (1, 2, 3)]
+    other[2], cot_far = lax.optimization_barrier((other[2], cot_far))
     tokens = jnp.concatenate([p for pair in zip(own, other) for p in pair], axis=0)
 
     mine = jnp.dot(tokens, weight, preferred_element_type=F32)

time: 149 us -> 141 us (0.946)
  waiting for transfers between devices: 52.4 us -> 49 us
  starting transfers between devices: 76.6 us -> 73.4 us
    ppermute x1, waiting for transfers between devices: 8.49 us -> 0.01 us  [body(): cot_far = lax.ppermute(cot_far, 'zl', [(i, nz - 1 - i) for i in range(nz)])]
    ppermute x2, waiting for transfers between devices: 0.01 us -> 6.57 us  [mirror(): return lax.ppermute(value, ('zl', 'zh'), ends)]
    ppermute x15, starting transfers between devices: 49.9 us -> 45.6 us  [shift(): lax.ppermute(value, axis, [(i, (i + by) % size) for i in range(size)])]
    ppermute x2, waiting for transfers between devices: 5.07 us -> 2.23 us  [body(): got.append(lax.ppermute(sends[k - 1], 'zl', hop))]
    ppermute x2, starting transfers between devices: 16.8 us -> 18.6 us  [mirror(): return lax.ppermute(value, ('zl', 'zh'), ends)]
where the time goes in v9:
time: 141 us; the launch traced here: 140 us
  starting transfers between devices  73.4 us (52%)
  waiting for transfers between devices  49 us (35%)
  Pallas kernels  8.22 us (6%)
  other arithmetic  4.15 us (3%)
  local copies, waits for them, and re-layouts  3.17 us (2%)
    ppermute x15, starting transfers between devices, shift(): lax.ppermute(value, axis, [(i, (i + by) % size) for i in range(size)])  45.6 us
    ppermute x15, waiting for transfers between devices, shift(): lax.ppermute(value, axis, [(i, (i + by) % size) for i in range(size)])  40.2 us
    ppermute x2, starting transfers between devices, mirror(): return lax.ppermute(value, ('zl', 'zh'), ends)  18.6 us
    ppermute x2, starting transfers between devices, body(): got.append(lax.ppermute(sends[k - 1], 'zl', hop))  6.74 us
    ppermute x2, waiting for transfers between devices, mirror(): return lax.ppermute(value, ('zl', 'zh'), ends)  6.57 us
    pallas_call x4, Pallas kernels, small_call(): pl.pallas_call(kernel, out_shape=out_shape, in_specs=[pl.BlockSpec(memory...  4.61 us
    pallas_call x1, Pallas kernels, rows_and_chunks(): pl.pallas_call(functools.partial(rows_kernel, sizes, factor), out_shape=[...  3.61 us
  transfers between devices with their start and end apart: 20, of which 14 were waited for; matrix products, arithmetic and copies ran while one was open for 5% of the time, Pallas kernels for 3%

profile of v9, /device:TPU:6, one launch (start us, length us, event | category | flops | bytes accessed | tf_op | source)
XLA Modules:
  0.0 140.4 jit_solution(17672054157165389988)
XLA Ops:
  0.6 14.6 %collective-permute-start = (bf16[48,3072]{1,0:T(8,128)(2,1)}, bf16[48,3072]{1,0:T(8,128)(2,1)S(1)}, u32[]{:S(2)}, u32[]{:S(2)}) collective-permute-start(bf16[48,3072]{1,0:T(8,128)(2,1)} %param.4), channel_id=1, source_target_pairs={{0,642},{2,640},{128,514},{130,512},{256,386},{258,384},{384,258},... | collective-permute-start | bytes 884744 | tf_op jit(solution)/shard_map/ppermute | solution.py:159
  15.2 2.4 %collective-permute-start.1 = (bf16[48,3072]{1,0:T(8,128)(2,1)}, bf16[48,3072]{1,0:T(8,128)(2,1)}, u32[]{:S(2)}, u32[]{:S(2)}) collective-permute-start(bf16[48,3072]{1,0:T(8,128)(2,1)} %param.4), channel_id=1, source_target_pairs={{0,4},{4,8},{8,12},{12,0},{1,5},{5,9},{9,13},{13,1},{2,6},{6,10},{... | collective-permute-start | bytes 884744 | tf_op jit(solution)/shard_map/ppermute | solution.py:140
  17.6 4.3 %collective-permute-start.3 = (bf16[48,3072]{1,0:T(8,128)(2,1)}, bf16[48,3072]{1,0:T(8,128)(2,1)S(1)}, u32[]{:S(2)}, u32[]{:S(2)}) collective-permute-start(bf16[48,3072]{1,0:T(8,128)(2,1)} %param.4), channel_id=1, source_target_pairs={{0,8},{4,12},{8,0},{12,4},{1,9},{5,13},{9,1},{13,5},{2,10},{6,14},... | collective-permute-start | bytes 884744 | tf_op jit(solution)/shard_map/ppermute | solution.py:140
  22.0 1.9 %collective-permute-start.6 = (bf16[48,3072]{1,0:T(8,128)(2,1)}, bf16[48,3072]{1,0:T(8,128)(2,1)S(1)}, u32[]{:S(2)}, u32[]{:S(2)}) collective-permute-start(bf16[48,3072]{1,0:T(8,128)(2,1)} %param.4), channel_id=1, source_target_pairs={{0,12},{4,0},{8,4},{12,8},{1,13},{5,1},{9,5},{13,9},{2,14},{6,2},{... | collective-permute-start | bytes 884744 | tf_op jit(solution)/shard_map/ppermute | solution.py:140
  23.9 1.0 dynamic-slice_bitcast_fusion
  24.9 0.0 copy-start
  24.9 2.6 %collective-permute-start.5 = (bf16[4,48,384]{2,1,0:T(8,128)(2,1)S(1)}, bf16[4,48,384]{2,1,0:T(8,128)(2,1)S(1)}, u32[]{:S(2)}, u32[]{:S(2)}) collective-permute-start(bf16[4,48,384]{2,1,0:T(8,128)(2,1)S(1)} %get-tuple-element.41), channel_id=1, source_target_pairs={{0,640},{128,512},{256,384},{384,256},{512,128},{640,0},{1,641},{1... | collective-permute-start | bytes 442376 | tf_op jit(solution)/shard_map/ppermute | solution.py:165
  27.5 1.0 constant_dynamic-update-slice_fusion.7
  28.5 6.6 %collective-permute-done = bf16[48,3072]{1,0:T(8,128)(2,1)S(1)} collective-permute-done((bf16[48,3072]{1,0:T(8,128)(2,1)}, bf16[48,3072]{1,0:T(8,128)(2,1)S(1)}, u32[]{:S(2)}, u32[]{:S(2)}) %collective-permute-start) | collective-permute-done | bytes 294944 | tf_op jit(solution)/shard_map/ppermute | solution.py:159
  35.0 3.3 %collective-permute-start.4 = (bf16[48,3072]{1,0:T(8,128)(2,1)S(1)}, bf16[48,3072]{1,0:T(8,128)(2,1)S(1)}, u32[]{:S(2)}, u32[]{:S(2)}) collective-permute-start(bf16[48,3072]{1,0:T(8,128)(2,1)S(1)} %collective-permute-done), channel_id=1, source_target_pairs={{0,8},{4,12},{8,0},{12,4},{1,9},{5,13},{9,1},{13,5},{2,10},{6,14},... | collective-permute-start | bytes 884744 | tf_op jit(solution)/shard_map/ppermute | solution.py:140
  38.4 0.0 collective-permute-done.1
  38.4 4.0 %collective-permute-start.2 = (bf16[48,3072]{1,0:T(8,128)(2,1)S(1)}, bf16[48,3072]{1,0:T(8,128)(2,1)S(1)}, u32[]{:S(2)}, u32[]{:S(2)}) collective-permute-start(bf16[48,3072]{1,0:T(8,128)(2,1)S(1)} %collective-permute-done), channel_id=1, source_target_pairs={{0,4},{4,8},{8,12},{12,0},{1,5},{5,9},{9,13},{13,1},{2,6},{6,10},{... | collective-permute-start | bytes 884744 | tf_op jit(solution)/shard_map/ppermute | solution.py:140
  42.4 1.0 constant_dynamic-update-slice_fusion.5
  43.4 0.0 collective-permute-done.5.cot_far
  43.4 1.9 %collective-permute-start.7 = (bf16[48,3072]{1,0:T(8,128)(2,1)S(1)}, bf16[48,3072]{1,0:T(8,128)(2,1)S(1)}, u32[]{:S(2)}, u32[]{:S(2)}) collective-permute-start(bf16[48,3072]{1,0:T(8,128)(2,1)S(1)} %collective-permute-done), channel_id=1, source_target_pairs={{0,12},{4,0},{8,4},{12,8},{1,13},{5,1},{9,5},{13,9},{2,14},{6,2},{... | collective-permute-start | bytes 884744 | tf_op jit(solution)/shard_map/ppermute | solution.py:140
  45.3 2.0 %collective-permute-done.4 = bf16[48,3072]{1,0:T(8,128)(2,1)S(1)} collective-permute-done((bf16[48,3072]{1,0:T(8,128)(2,1)S(1)}, bf16[48,3072]{1,0:T(8,128)(2,1)S(1)}, u32[]{:S(2)}, u32[]{:S(2)}) %collective-permute-start.4) | collective-permute-done | bytes 294944 | tf_op jit(solution)/shard_map/ppermute | solution.py:140
  47.4 4.1 %collective-permute-done.2 = bf16[48,3072]{1,0:T(8,128)(2,1)S(1)} collective-permute-done((bf16[48,3072]{1,0:T(8,128)(2,1)S(1)}, bf16[48,3072]{1,0:T(8,128)(2,1)S(1)}, u32[]{:S(2)}, u32[]{:S(2)}) %collective-permute-start.2) | collective-permute-done | bytes 294944 | tf_op jit(solution)/shard_map/ppermute | solution.py:140
  51.5 0.0 collective-permute-done.3
  51.6 0.0 collective-permute-done.6
  51.6 3.3 %collective-permute-done.7 = bf16[48,3072]{1,0:T(8,128)(2,1)S(1)} collective-permute-done((bf16[48,3072]{1,0:T(8,128)(2,1)S(1)}, bf16[48,3072]{1,0:T(8,128)(2,1)S(1)}, u32[]{:S(2)}, u32[]{:S(2)}) %collective-permute-start.7) | collective-permute-done | bytes 294944 | tf_op jit(solution)/shard_map/ppermute | solution.py:140
  54.9 0.0 copy-done
  54.9 0.0 copy-start.2
  54.9 1.4 fusion.mine
  56.3 1.9 %collective-permute-start.8 = (f32[384,384]{1,0:T(8,128)S(1)}, f32[384,384]{1,0:T(8,128)}, u32[]{:S(2)}, u32[]{:S(2)}) collective-permute-start(f32[384,384]{1,0:T(8,128)S(1)} %fusion.mine), channel_id=1, source_target_pairs={{0,1},{1,0},{2,3},{3,2},{4,5},{5,4},{6,7},{7,6},{8,9},{9,8},{10,11... | collective-permute-start | bytes 1769480 | tf_op jit(solution)/shard_map/ppermute | solution.py:140
  58.3 0.0 copy-start.1
  58.3 0.1 pad_add_fusion.where
  58.4 2.0 %collective-permute-done.8.theirs = f32[384,384]{1,0:T(8,128)} collective-permute-done((f32[384,384]{1,0:T(8,128)S(1)}, f32[384,384]{1,0:T(8,128)}, u32[]{:S(2)}, u32[]{:S(2)}) %collective-permute-start.8) | collective-permute-done | bytes 589856 | tf_op jit(solution)/shard_map/ppermute | solution.py:140
  60.4 0.0 copy-done.2
  60.4 3.6 %rows_and_chunks.1 = (bf16[384,384]{1,0:T(8,128)(2,1)S(1)}, bf16[5,6,32,384]{3,2,1,0:T(8,128)(2,1)S(1)}, bf16[5,6,32,384]{3,2,1,0:T(8,128)(2,1)S(1)}, bf16[2,6,3...) custom-call(s32[2]{0:T(128)S(1)} %pad_add_fusion.where, ...), custom_call_target="tpu_custom_call" | custom-call | tf_op jit(solution)/shard_map/rows_and_chunks/pallas_call | solution.py:69
  64.0 5.4 %collective-permute-start.14 = (bf16[5,6,32,384]{3,2,1,0:T(8,128)(2,1)S(1)}, bf16[5,6,32,384]{3,2,1,0:T(8,128)(2,1)S(1)}, u32[]{:S(2)}, u32[]{:S(2)}) collective-permute-start(bf16[5,6,32,384]{3,2,1,0:T(8,128)(2,1)S(1)} %get-tuple-element.32), channel_id=1, source_target_pairs={{0,112},{16,0},{32,16},{48,32},{64,48},{80,64},{96,80},{112,96},{1... | collective-permute-start | bytes 2211848 | tf_op jit(solution)/shard_map/ppermute | solution.py:140
  69.4 1.9 %collective-permute-start.13 = (bf16[5,6,32,384]{3,2,1,0:T(8,128)(2,1)S(1)}, bf16[5,6,32,384]{3,2,1,0:T(8,128)(2,1)S(1)}, u32[]{:S(2)}, u32[]{:S(2)}) collective-permute-start(bf16[5,6,32,384]{3,2,1,0:T(8,128)(2,1)S(1)} %get-tuple-element.31), channel_id=1, source_target_pairs={{0,16},{16,32},{32,48},{48,64},{64,80},{80,96},{96,112},{112,0},{1... | collective-permute-start | bytes 2211848 | tf_op jit(solution)/shard_map/ppermute | solution.py:140
  71.3 0.0 copy-done.1
  71.3 3.0 %shard_map.59 = (f32[96,3072]{1,0:T(8,128)S(1)}, bf16[96,3072]{1,0:T(8,128)(2,1)S(1)}, bf16[96,3072]{1,0:T(8,128)(2,1)S(1)}, bf16[96,3072]{1,0:T(8,128)(2,1)S(1)}) custom-call(bf16[384,384]{1,0:T(8,128)(2,1)S(1)} %get-tuple-element.23.rows, bf16[3072,384]{1,0:T(8,128)(2,1)S(1)} %copy-done.1), custom_call_target="tpu_custom_call" | custom-call | tf_op jit(solution)/shard_map/pallas_call | solution.py:83
  74.3 1.9 %collective-permute-start.10 = (bf16[96,3072]{1,0:T(8,128)(2,1)S(1)}, bf16[96,3072]{1,0:T(8,128)(2,1)S(1)}, u32[]{:S(2)}, u32[]{:S(2)}) collective-permute-start(bf16[96,3072]{1,0:T(8,128)(2,1)S(1)} %get-tuple-element.26), channel_id=1, source_target_pairs={{0,12},{4,0},{8,4},{12,8},{1,13},{5,1},{9,5},{13,9},{2,14},{6,2},{... | collective-permute-start | bytes 1769480 | tf_op jit(solution)/shard_map/ppermute | solution.py:140
  76.3 5.1 %collective-permute-start.11 = (bf16[96,3072]{1,0:T(8,128)(2,1)S(1)}, bf16[96,3072]{1,0:T(8,128)(2,1)S(1)}, u32[]{:S(2)}, u32[]{:S(2)}) collective-permute-start(bf16[96,3072]{1,0:T(8,128)(2,1)S(1)} %get-tuple-element.27), channel_id=1, source_target_pairs={{0,4},{4,8},{8,12},{12,0},{1,5},{5,9},{9,13},{13,1},{2,6},{6,10},{... | collective-permute-start | bytes 1769480 | tf_op jit(solution)/shard_map/ppermute | solution.py:140
  81.4 1.9 %collective-permute-start.9 = (bf16[96,3072]{1,0:T(8,128)(2,1)S(1)}, bf16[96,3072]{1,0:T(8,128)(2,1)S(1)}, u32[]{:S(2)}, u32[]{:S(2)}) collective-permute-start(bf16[96,3072]{1,0:T(8,128)(2,1)S(1)} %get-tuple-element.25), channel_id=1, source_target_pairs={{0,8},{4,12},{8,0},{12,4},{1,9},{5,13},{9,1},{13,5},{2,10},{6,14},... | collective-permute-start | bytes 1769480 | tf_op jit(solution)/shard_map/ppermute | solution.py:140
  83.3 2.1 %collective-permute-done.14.down = bf16[5,6,32,384]{3,2,1,0:T(8,128)(2,1)S(1)} collective-permute-done((bf16[5,6,32,384]{3,2,1,0:T(8,128)(2,1)S(1)}, bf16[5,6,32,384]{3,2,1,0:T(8,128)(2,1)S(1)}, u32[]{:S(2)}, u32[]{:S(2)}) %collective-permute-start.14) | collective-permute-done | bytes 737312 | tf_op jit(solution)/shard_map/ppermute | solution.py:140
  85.4 5.3 %collective-permute-done.13.up = bf16[5,6,32,384]{3,2,1,0:T(8,128)(2,1)S(1)} collective-permute-done((bf16[5,6,32,384]{3,2,1,0:T(8,128)(2,1)S(1)}, bf16[5,6,32,384]{3,2,1,0:T(8,128)(2,1)S(1)}, u32[]{:S(2)}, u32[]{:S(2)}) %collective-permute-start.13) | collective-permute-done | bytes 737312 | tf_op jit(solution)/shard_map/ppermute | solution.py:140
  90.7 0.8 add_convert_fusion
  91.5 3.6 %collective-permute-start.16 = (bf16[2,6,32,384]{3,2,1,0:T(8,128)(2,1)}, bf16[2,6,32,384]{3,2,1,0:T(8,128)(2,1)S(1)}, u32[]{:S(2)}, u32[]{:S(2)}) collective-permute-start(bf16[2,6,32,384]{3,2,1,0:T(8,128)(2,1)} %add_convert_fusion), channel_id=1, source_target_pairs={{0,80},{16,96},{32,112},{48,0},{64,16},{80,32},{96,48},{112,64},{1... | collective-permute-start | bytes 884744 | tf_op jit(solution)/shard_map/ppermute | solution.py:140
  95.2 0.8 add_convert_fusion.1
  96.0 4.0 %collective-permute-start.15 = (bf16[2,6,32,384]{3,2,1,0:T(8,128)(2,1)}, bf16[2,6,32,384]{3,2,1,0:T(8,128)(2,1)S(1)}, u32[]{:S(2)}, u32[]{:S(2)}) collective-permute-start(bf16[2,6,32,384]{3,2,1,0:T(8,128)(2,1)} %add_convert_fusion.1), channel_id=1, source_target_pairs={{0,48},{16,64},{32,80},{48,96},{64,112},{80,0},{96,16},{112,32},{1... | collective-permute-start | bytes 884744 | tf_op jit(solution)/shard_map/ppermute | solution.py:140
  100.0 5.2 %collective-permute-done.10.rest_1_ = bf16[96,3072]{1,0:T(8,128)(2,1)S(1)} collective-permute-done((bf16[96,3072]{1,0:T(8,128)(2,1)S(1)}, bf16[96,3072]{1,0:T(8,128)(2,1)S(1)}, u32[]{:S(2)}, u32[]{:S(2)}) %collective-permute-start.10) | collective-permute-done | bytes 589856 | tf_op jit(solution)/shard_map/ppermute | solution.py:140
  105.2 1.2 collective-permute-done.11.rest_2_
  106.3 0.0 collective-permute-done.9.rest_0_
  106.4 0.3 shard_map.60
  106.6 4.0 %collective-permute-start.12 = (bf16[48,3072]{1,0:T(8,128)(2,1)S(1)}, bf16[48,3072]{1,0:T(8,128)(2,1)}, u32[]{:S(2)}, u32[]{:S(2)}) collective-permute-start(bf16[48,3072]{1,0:T(8,128)(2,1)S(1)} %get-tuple-element.29), channel_id=1, source_target_pairs={{0,642},{2,640},{128,514},{130,512},{256,386},{258,384},{384,258},... | collective-permute-start | bytes 884744 | tf_op jit(solution)/shard_map/ppermute | solution.py:159
  110.7 0.1 pad_add_fusion.1.where
  110.7 3.0 %collective-permute-done.16.got5 = bf16[2,6,32,384]{3,2,1,0:T(8,128)(2,1)S(1)} collective-permute-done((bf16[2,6,32,384]{3,2,1,0:T(8,128)(2,1)}, bf16[2,6,32,384]{3,2,1,0:T(8,128)(2,1)S(1)}, u32[]{:S(2)}, u32[]{:S(2)}) %collective-permute-start.16) | collective-permute-done | bytes 294944 | tf_op jit(solution)/shard_map/ppermute | solution.py:140
  113.7 7.9 %collective-permute-done.15.got3 = bf16[2,6,32,384]{3,2,1,0:T(8,128)(2,1)S(1)} collective-permute-done((bf16[2,6,32,384]{3,2,1,0:T(8,128)(2,1)}, bf16[2,6,32,384]{3,2,1,0:T(8,128)(2,1)S(1)}, u32[]{:S(2)}, u32[]{:S(2)}) %collective-permute-start.15) | collective-permute-done | bytes 294944 | tf_op jit(solution)/shard_map/ppermute | solution.py:140
  121.6 0.7 shard_map.61
  122.4 1.9 %collective-permute-start.17 = (bf16[2,64,384]{2,1,0:T(8,128)(2,1)S(1)}, bf16[2,64,384]{2,1,0:T(8,128)(2,1)S(1)}, u32[]{:S(2)}, u32[]{:S(2)}) collective-permute-start(bf16[2,64,384]{2,1,0:T(8,128)(2,1)S(1)} %get-tuple-element.36), channel_id=1, source_target_pairs={{0,128},{128,256},{256,0},{384,512},{512,640},{640,384},{1,129},{1... | collective-permute-start | bytes 294920 | tf_op jit(solution)/shard_map/ppermute | solution.py:226
  124.3 4.8 %collective-permute-start.18 = (bf16[2,64,384]{2,1,0:T(8,128)(2,1)S(1)}, bf16[2,64,384]{2,1,0:T(8,128)(2,1)S(1)}, u32[]{:S(2)}, u32[]{:S(2)}) collective-permute-start(bf16[2,64,384]{2,1,0:T(8,128)(2,1)S(1)} %get-tuple-element.37), channel_id=1, source_target_pairs={{0,256},{128,0},{256,128},{384,640},{512,384},{640,512},{1,257},{1... | collective-permute-start | bytes 294920 | tf_op jit(solution)/shard_map/ppermute | solution.py:226
  129.1 1.2 collective-permute-done.17.rest_0_
  130.4 1.0 collective-permute-done.18.rest_1_
  131.3 0.6 shard_map.62
  131.9 1.9 %collective-permute-start.19 = (bf16[64,384]{1,0:T(8,128)(2,1)S(1)}, bf16[64,384]{1,0:T(8,128)(2,1)S(1)}, u32[]{:S(2)}, u32[]{:S(2)}) collective-permute-start(bf16[64,384]{1,0:T(8,128)(2,1)S(1)} %get-tuple-element.39), channel_id=1, source_target_pairs={{0,384},{128,512},{256,640},{384,0},{512,128},{640,256},{1,385},{1... | collective-permute-start | bytes 147464 | tf_op jit(solution)/shard_map/ppermute | solution.py:140
  133.9 0.0 collective-permute-done.12
  133.9 1.7 %add_convert_fusion.2 = bf16[48,3072]{1,0:T(8,128)(2,1)} fusion(f32[48,3072]{1,0:T(8,128)S(1)} %get-tuple-element.28, bf16[48,3072]{1,0:T(8,128)(2,1)} %collective-permute-done.12), kind=kLoop, calls=%fused_computation.2 | loop fusion | flops 442368 | bytes 1179648 | tf_op jit(solution)/shard_map/convert_element_type | solution.py:207
  135.6 4.1 %collective-permute-done.19 = bf16[64,384]{1,0:T(8,128)(2,1)S(1)} collective-permute-done((bf16[64,384]{1,0:T(8,128)(2,1)S(1)}, bf16[64,384]{1,0:T(8,128)(2,1)S(1)}, u32[]{:S(2)}, u32[]{:S(2)}) %collective-permute-start.19) | collective-permute-done | bytes 49184 | tf_op jit(solution)/shard_map/ppermute | solution.py:140
  139.7 0.7 convert_add_fusion
  (8 shorter events, 0.2 us)
Async XLA Ops:
  0.6 34.4 %collective-permute-start = (bf16[48,3072]{1,0:T(8,128)(2,1)}, bf16[48,3072]{1,0:T(8,128)(2,1)S(1)}, u32[]{:S(2)}, u32[]{:S(2)}) collective-permute-start(bf16[48,3072]{1,0:T(8,128)(2,1)} %param.4), channel_id=1, source_target_pairs={{0,642},{2,640},{128,514},{130,512},{256,386},{258,384},{384,258},... | collective-permute-start | bytes 884744 | tf_op jit(solution)/shard_map/ppermute | solution.py:159
  15.2 23.2 %collective-permute-start.1 = (bf16[48,3072]{1,0:T(8,128)(2,1)}, bf16[48,3072]{1,0:T(8,128)(2,1)}, u32[]{:S(2)}, u32[]{:S(2)}) collective-permute-start(bf16[48,3072]{1,0:T(8,128)(2,1)} %param.4), channel_id=1, source_target_pairs={{0,4},{4,8},{8,12},{12,0},{1,5},{5,9},{9,13},{13,1},{2,6},{6,10},{... | collective-permute-start | bytes 884744 | tf_op jit(solution)/shard_map/ppermute | solution.py:140
  17.6 33.9 %collective-permute-start.3 = (bf16[48,3072]{1,0:T(8,128)(2,1)}, bf16[48,3072]{1,0:T(8,128)(2,1)S(1)}, u32[]{:S(2)}, u32[]{:S(2)}) collective-permute-start(bf16[48,3072]{1,0:T(8,128)(2,1)} %param.4), channel_id=1, source_target_pairs={{0,8},{4,12},{8,0},{12,4},{1,9},{5,13},{9,1},{13,5},{2,10},{6,14},... | collective-permute-start | bytes 884744 | tf_op jit(solution)/shard_map/ppermute | solution.py:140
  22.0 29.6 %collective-permute-start.6 = (bf16[48,3072]{1,0:T(8,128)(2,1)}, bf16[48,3072]{1,0:T(8,128)(2,1)S(1)}, u32[]{:S(2)}, u32[]{:S(2)}) collective-permute-start(bf16[48,3072]{1,0:T(8,128)(2,1)} %param.4), channel_id=1, source_target_pairs={{0,12},{4,0},{8,4},{12,8},{1,13},{5,1},{9,5},{13,9},{2,14},{6,2},{... | collective-permute-start | bytes 884744 | tf_op jit(solution)/shard_map/ppermute | solution.py:140
  24.9 30.0 %copy-start = (bf16[3072,384]{1,0:T(8,128)(2,1)S(1)}, bf16[3072,384]{1,0:T(8,128)(2,1)}, u32[]{:S(2)}) copy-start(bf16[3072,384]{1,0:T(8,128)(2,1)} %weight.1) | copy-start | bytes 7077892
  24.9 18.5 %collective-permute-start.5 = (bf16[4,48,384]{2,1,0:T(8,128)(2,1)S(1)}, bf16[4,48,384]{2,1,0:T(8,128)(2,1)S(1)}, u32[]{:S(2)}, u32[]{:S(2)}) collective-permute-start(bf16[4,48,384]{2,1,0:T(8,128)(2,1)S(1)} %get-tuple-element.41), channel_id=1, source_target_pairs={{0,640},{128,512},{256,384},{384,256},{512,128},{640,0},{1,641},{1... | collective-permute-start | bytes 442376 | tf_op jit(solution)/shard_map/ppermute | solution.py:165
  35.0 12.3 %collective-permute-start.4 = (bf16[48,3072]{1,0:T(8,128)(2,1)S(1)}, bf16[48,3072]{1,0:T(8,128)(2,1)S(1)}, u32[]{:S(2)}, u32[]{:S(2)}) collective-permute-start(bf16[48,3072]{1,0:T(8,128)(2,1)S(1)} %collective-permute-done), channel_id=1, source_target_pairs={{0,8},{4,12},{8,0},{12,4},{1,9},{5,13},{9,1},{13,5},{2,10},{6,14},... | collective-permute-start | bytes 884744 | tf_op jit(solution)/shard_map/ppermute | solution.py:140
  38.4 13.1 %collective-permute-start.2 = (bf16[48,3072]{1,0:T(8,128)(2,1)S(1)}, bf16[48,3072]{1,0:T(8,128)(2,1)S(1)}, u32[]{:S(2)}, u32[]{:S(2)}) collective-permute-start(bf16[48,3072]{1,0:T(8,128)(2,1)S(1)} %collective-permute-done), channel_id=1, source_target_pairs={{0,4},{4,8},{8,12},{12,0},{1,5},{5,9},{9,13},{13,1},{2,6},{6,10},{... | collective-permute-start | bytes 884744 | tf_op jit(solution)/shard_map/ppermute | solution.py:140
  43.4 11.5 %collective-permute-start.7 = (bf16[48,3072]{1,0:T(8,128)(2,1)S(1)}, bf16[48,3072]{1,0:T(8,128)(2,1)S(1)}, u32[]{:S(2)}, u32[]{:S(2)}) collective-permute-start(bf16[48,3072]{1,0:T(8,128)(2,1)S(1)} %collective-permute-done), channel_id=1, source_target_pairs={{0,12},{4,0},{8,4},{12,8},{1,13},{5,1},{9,5},{13,9},{2,14},{6,2},{... | collective-permute-start | bytes 884744 | tf_op jit(solution)/shard_map/ppermute | solution.py:140
  54.9 5.5 %copy-start.2 = (f32[128]{0:T(128)S(1)}, f32[128]{0:T(128)}, u32[]{:S(2)}) copy-start(f32[128]{0:T(128)} %param.7) | copy-start | bytes 1540
  56.3 4.0 %collective-permute-start.8 = (f32[384,384]{1,0:T(8,128)S(1)}, f32[384,384]{1,0:T(8,128)}, u32[]{:S(2)}, u32[]{:S(2)}) collective-permute-start(f32[384,384]{1,0:T(8,128)S(1)} %fusion.mine), channel_id=1, source_target_pairs={{0,1},{1,0},{2,3},{3,2},{4,5},{5,4},{6,7},{7,6},{8,9},{9,8},{10,11... | collective-permute-start | bytes 1769480 | tf_op jit(solution)/shard_map/ppermute | solution.py:140
  58.3 13.0 %copy-start.1 = (bf16[3072,384]{1,0:T(8,128)(2,1)S(1)}, bf16[3072,384]{1,0:T(8,128)(2,1)}, u32[]{:S(2)}) copy-start(bf16[3072,384]{1,0:T(8,128)(2,1)} %weight.1) | copy-start | bytes 7077892
  64.0 21.4 %collective-permute-start.14 = (bf16[5,6,32,384]{3,2,1,0:T(8,128)(2,1)S(1)}, bf16[5,6,32,384]{3,2,1,0:T(8,128)(2,1)S(1)}, u32[]{:S(2)}, u32[]{:S(2)}) collective-permute-start(bf16[5,6,32,384]{3,2,1,0:T(8,128)(2,1)S(1)} %get-tuple-element.32), channel_id=1, source_target_pairs={{0,112},{16,0},{32,16},{48,32},{64,48},{80,64},{96,80},{112,96},{1... | collective-permute-start | bytes 2211848 | tf_op jit(solution)/shard_map/ppermute | solution.py:140
  69.4 21.4 %collective-permute-start.13 = (bf16[5,6,32,384]{3,2,1,0:T(8,128)(2,1)S(1)}, bf16[5,6,32,384]{3,2,1,0:T(8,128)(2,1)S(1)}, u32[]{:S(2)}, u32[]{:S(2)}) collective-permute-start(bf16[5,6,32,384]{3,2,1,0:T(8,128)(2,1)S(1)} %get-tuple-element.31), channel_id=1, source_target_pairs={{0,16},{16,32},{32,48},{48,64},{64,80},{80,96},{96,112},{112,0},{1... | collective-permute-start | bytes 2211848 | tf_op jit(solution)/shard_map/ppermute | solution.py:140
  74.3 30.8 %collective-permute-start.10 = (bf16[96,3072]{1,0:T(8,128)(2,1)S(1)}, bf16[96,3072]{1,0:T(8,128)(2,1)S(1)}, u32[]{:S(2)}, u32[]{:S(2)}) collective-permute-start(bf16[96,3072]{1,0:T(8,128)(2,1)S(1)} %get-tuple-element.26), channel_id=1, source_target_pairs={{0,12},{4,0},{8,4},{12,8},{1,13},{5,1},{9,5},{13,9},{2,14},{6,2},{... | collective-permute-start | bytes 1769480 | tf_op jit(solution)/shard_map/ppermute | solution.py:140
  76.3 30.1 %collective-permute-start.11 = (bf16[96,3072]{1,0:T(8,128)(2,1)S(1)}, bf16[96,3072]{1,0:T(8,128)(2,1)S(1)}, u32[]{:S(2)}, u32[]{:S(2)}) collective-permute-start(bf16[96,3072]{1,0:T(8,128)(2,1)S(1)} %get-tuple-element.27), channel_id=1, source_target_pairs={{0,4},{4,8},{8,12},{12,0},{1,5},{5,9},{9,13},{13,1},{2,6},{6,10},{... | collective-permute-start | bytes 1769480 | tf_op jit(solution)/shard_map/ppermute | solution.py:140
  81.4 24.9 %collective-permute-start.9 = (bf16[96,3072]{1,0:T(8,128)(2,1)S(1)}, bf16[96,3072]{1,0:T(8,128)(2,1)S(1)}, u32[]{:S(2)}, u32[]{:S(2)}) collective-permute-start(bf16[96,3072]{1,0:T(8,128)(2,1)S(1)} %get-tuple-element.25), channel_id=1, source_target_pairs={{0,8},{4,12},{8,0},{12,4},{1,9},{5,13},{9,1},{13,5},{2,10},{6,14},... | collective-permute-start | bytes 1769480 | tf_op jit(solution)/shard_map/ppermute | solution.py:140
  91.5 22.2 %collective-permute-start.16 = (bf16[2,6,32,384]{3,2,1,0:T(8,128)(2,1)}, bf16[2,6,32,384]{3,2,1,0:T(8,128)(2,1)S(1)}, u32[]{:S(2)}, u32[]{:S(2)}) collective-permute-start(bf16[2,6,32,384]{3,2,1,0:T(8,128)(2,1)} %add_convert_fusion), channel_id=1, source_target_pairs={{0,80},{16,96},{32,112},{48,0},{64,16},{80,32},{96,48},{112,64},{1... | collective-permute-start | bytes 884744 | tf_op jit(solution)/shard_map/ppermute | solution.py:140
  96.0 25.6 %collective-permute-start.15 = (bf16[2,6,32,384]{3,2,1,0:T(8,128)(2,1)}, bf16[2,6,32,384]{3,2,1,0:T(8,128)(2,1)S(1)}, u32[]{:S(2)}, u32[]{:S(2)}) collective-permute-start(bf16[2,6,32,384]{3,2,1,0:T(8,128)(2,1)} %add_convert_fusion.1), channel_id=1, source_target_pairs={{0,48},{16,64},{32,80},{48,96},{64,112},{80,0},{96,16},{112,32},{1... | collective-permute-start | bytes 884744 | tf_op jit(solution)/shard_map/ppermute | solution.py:140
  106.6 27.2 %collective-permute-start.12 = (bf16[48,3072]{1,0:T(8,128)(2,1)S(1)}, bf16[48,3072]{1,0:T(8,128)(2,1)}, u32[]{:S(2)}, u32[]{:S(2)}) collective-permute-start(bf16[48,3072]{1,0:T(8,128)(2,1)S(1)} %get-tuple-element.29), channel_id=1, source_target_pairs={{0,642},{2,640},{128,514},{130,512},{256,386},{258,384},{384,258},... | collective-permute-start | bytes 884744 | tf_op jit(solution)/shard_map/ppermute | solution.py:159
  122.4 8.0 %collective-permute-start.17 = (bf16[2,64,384]{2,1,0:T(8,128)(2,1)S(1)}, bf16[2,64,384]{2,1,0:T(8,128)(2,1)S(1)}, u32[]{:S(2)}, u32[]{:S(2)}) collective-permute-start(bf16[2,64,384]{2,1,0:T(8,128)(2,1)S(1)} %get-tuple-element.36), channel_id=1, source_target_pairs={{0,128},{128,256},{256,0},{384,512},{512,640},{640,384},{1,129},{1... | collective-permute-start | bytes 294920 | tf_op jit(solution)/shard_map/ppermute | solution.py:226
  124.3 7.1 %collective-permute-start.18 = (bf16[2,64,384]{2,1,0:T(8,128)(2,1)S(1)}, bf16[2,64,384]{2,1,0:T(8,128)(2,1)S(1)}, u32[]{:S(2)}, u32[]{:S(2)}) collective-permute-start(bf16[2,64,384]{2,1,0:T(8,128)(2,1)S(1)} %get-tuple-element.37), channel_id=1, source_target_pairs={{0,256},{128,0},{256,128},{384,640},{512,384},{640,512},{1,257},{1... | collective-permute-start | bytes 294920 | tf_op jit(solution)/shard_map/ppermute | solution.py:226
  131.9 7.8 %collective-permute-start.19 = (bf16[64,384]{1,0:T(8,128)(2,1)S(1)}, bf16[64,384]{1,0:T(8,128)(2,1)S(1)}, u32[]{:S(2)}, u32[]{:S(2)}) collective-permute-start(bf16[64,384]{1,0:T(8,128)(2,1)S(1)} %get-tuple-element.39), channel_id=1, source_target_pairs={{0,384},{128,512},{256,640},{384,0},{512,128},{640,256},{1,385},{1... | collective-permute-start | bytes 147464 | tf_op jit(solution)/shard_map/ppermute | solution.py:140

commit v10 on v9

--- a/solution.py
+++ b/solution.py
@@ -202,7 +202,7 @@
         back_sum_kernel,
         [jax.ShapeDtypeStruct((count, width), t) for t in (F32, BF16)],
         back[0],
-        *[shift(back[k], "x", -k) for k in (2, 1, 3)],
+        *[shift(back[k], "x", -k) for k in (1, 2, 3)],
     )
     input_grad = add(near, mirror(far)).astype(BF16)
 

time: 141 us -> 141 us (level)
  no operation moved by 1% of the time
where the time goes in v10:
time: 141 us; the launch traced here: 140 us
  starting transfers between devices  72.7 us (52%)
  waiting for transfers between devices  49.7 us (35%)
  Pallas kernels  8.22 us (6%)
  other arithmetic  4.15 us (3%)
  local copies, waits for them, and re-layouts  3.17 us (2%)
    ppermute x15, starting transfers between devices, shift(): lax.ppermute(value, axis, [(i, (i + by) % size) for i in range(size)])  44.8 us
    ppermute x15, waiting for transfers between devices, shift(): lax.ppermute(value, axis, [(i, (i + by) % size) for i in range(size)])  40.9 us
    ppermute x2, starting transfers between devices, mirror(): return lax.ppermute(value, ('zl', 'zh'), ends)  18.6 us
    ppermute x2, starting transfers between devices, body(): got.append(lax.ppermute(sends[k - 1], 'zl', hop))  6.74 us
    ppermute x2, waiting for transfers between devices, mirror(): return lax.ppermute(value, ('zl', 'zh'), ends)  6.57 us
    pallas_call x4, Pallas kernels, small_call(): pl.pallas_call(kernel, out_shape=out_shape, in_specs=[pl.BlockSpec(memory...  4.61 us
    pallas_call x1, Pallas kernels, rows_and_chunks(): pl.pallas_call(functools.partial(rows_kernel, sizes, factor), out_shape=[...  3.61 us
  transfers between devices with their start and end apart: 20, of which 14 were waited for; matrix products, arithmetic and copies ran while one was open for 5% of the time, Pallas kernels for 3%

profile of v10, /device:TPU:6, one launch (start us, length us, event | category | flops | bytes accessed | tf_op | source)
XLA Modules:
  0.0 140.4 jit_solution(18409554153727187387)
XLA Ops:
  0.6 14.6 %collective-permute-start = (bf16[48,3072]{1,0:T(8,128)(2,1)}, bf16[48,3072]{1,0:T(8,128)(2,1)S(1)}, u32[]{:S(2)}, u32[]{:S(2)}) collective-permute-start(bf16[48,3072]{1,0:T(8,128)(2,1)} %param.4), channel_id=1, source_target_pairs={{0,642},{2,640},{128,514},{130,512},{256,386},{258,384},{384,258},... | collective-permute-start | bytes 884744 | tf_op jit(solution)/shard_map/ppermute | solution.py:159
  15.2 2.4 %collective-permute-start.1 = (bf16[48,3072]{1,0:T(8,128)(2,1)}, bf16[48,3072]{1,0:T(8,128)(2,1)}, u32[]{:S(2)}, u32[]{:S(2)}) collective-permute-start(bf16[48,3072]{1,0:T(8,128)(2,1)} %param.4), channel_id=1, source_target_pairs={{0,4},{4,8},{8,12},{12,0},{1,5},{5,9},{9,13},{13,1},{2,6},{6,10},{... | collective-permute-start | bytes 884744 | tf_op jit(solution)/shard_map/ppermute | solution.py:140
  17.6 4.3 %collective-permute-start.3 = (bf16[48,3072]{1,0:T(8,128)(2,1)}, bf16[48,3072]{1,0:T(8,128)(2,1)S(1)}, u32[]{:S(2)}, u32[]{:S(2)}) collective-permute-start(bf16[48,3072]{1,0:T(8,128)(2,1)} %param.4), channel_id=1, source_target_pairs={{0,8},{4,12},{8,0},{12,4},{1,9},{5,13},{9,1},{13,5},{2,10},{6,14},... | collective-permute-start | bytes 884744 | tf_op jit(solution)/shard_map/ppermute | solution.py:140
  22.0 1.9 %collective-permute-start.6 = (bf16[48,3072]{1,0:T(8,128)(2,1)}, bf16[48,3072]{1,0:T(8,128)(2,1)S(1)}, u32[]{:S(2)}, u32[]{:S(2)}) collective-permute-start(bf16[48,3072]{1,0:T(8,128)(2,1)} %param.4), channel_id=1, source_target_pairs={{0,12},{4,0},{8,4},{12,8},{1,13},{5,1},{9,5},{13,9},{2,14},{6,2},{... | collective-permute-start | bytes 884744 | tf_op jit(solution)/shard_map/ppermute | solution.py:140
  23.9 1.0 dynamic-slice_bitcast_fusion
  24.9 0.0 copy-start
  24.9 2.6 %collective-permute-start.5 = (bf16[4,48,384]{2,1,0:T(8,128)(2,1)S(1)}, bf16[4,48,384]{2,1,0:T(8,128)(2,1)S(1)}, u32[]{:S(2)}, u32[]{:S(2)}) collective-permute-start(bf16[4,48,384]{2,1,0:T(8,128)(2,1)S(1)} %get-tuple-element.41), channel_id=1, source_target_pairs={{0,640},{128,512},{256,384},{384,256},{512,128},{640,0},{1,641},{1... | collective-permute-start | bytes 442376 | tf_op jit(solution)/shard_map/ppermute | solution.py:165
  27.5 1.0 constant_dynamic-update-slice_fusion.7
  28.5 6.6 %collective-permute-done = bf16[48,3072]{1,0:T(8,128)(2,1)S(1)} collective-permute-done((bf16[48,3072]{1,0:T(8,128)(2,1)}, bf16[48,3072]{1,0:T(8,128)(2,1)S(1)}, u32[]{:S(2)}, u32[]{:S(2)}) %collective-permute-start) | collective-permute-done | bytes 294944 | tf_op jit(solution)/shard_map/ppermute | solution.py:159
  35.0 3.3 %collective-permute-start.4 = (bf16[48,3072]{1,0:T(8,128)(2,1)S(1)}, bf16[48,3072]{1,0:T(8,128)(2,1)S(1)}, u32[]{:S(2)}, u32[]{:S(2)}) collective-permute-start(bf16[48,3072]{1,0:T(8,128)(2,1)S(1)} %collective-permute-done), channel_id=1, source_target_pairs={{0,8},{4,12},{8,0},{12,4},{1,9},{5,13},{9,1},{13,5},{2,10},{6,14},... | collective-permute-start | bytes 884744 | tf_op jit(solution)/shard_map/ppermute | solution.py:140
  38.4 0.0 collective-permute-done.1
  38.4 4.0 %collective-permute-start.2 = (bf16[48,3072]{1,0:T(8,128)(2,1)S(1)}, bf16[48,3072]{1,0:T(8,128)(2,1)S(1)}, u32[]{:S(2)}, u32[]{:S(2)}) collective-permute-start(bf16[48,3072]{1,0:T(8,128)(2,1)S(1)} %collective-permute-done), channel_id=1, source_target_pairs={{0,4},{4,8},{8,12},{12,0},{1,5},{5,9},{9,13},{13,1},{2,6},{6,10},{... | collective-permute-start | bytes 884744 | tf_op jit(solution)/shard_map/ppermute | solution.py:140
  42.4 1.0 constant_dynamic-update-slice_fusion.5
  43.4 0.0 collective-permute-done.5.cot_far
  43.4 1.9 %collective-permute-start.7 = (bf16[48,3072]{1,0:T(8,128)(2,1)S(1)}, bf16[48,3072]{1,0:T(8,128)(2,1)S(1)}, u32[]{:S(2)}, u32[]{:S(2)}) collective-permute-start(bf16[48,3072]{1,0:T(8,128)(2,1)S(1)} %collective-permute-done), channel_id=1, source_target_pairs={{0,12},{4,0},{8,4},{12,8},{1,13},{5,1},{9,5},{13,9},{2,14},{6,2},{... | collective-permute-start | bytes 884744 | tf_op jit(solution)/shard_map/ppermute | solution.py:140
  45.3 2.0 %collective-permute-done.4 = bf16[48,3072]{1,0:T(8,128)(2,1)S(1)} collective-permute-done((bf16[48,3072]{1,0:T(8,128)(2,1)S(1)}, bf16[48,3072]{1,0:T(8,128)(2,1)S(1)}, u32[]{:S(2)}, u32[]{:S(2)}) %collective-permute-start.4) | collective-permute-done | bytes 294944 | tf_op jit(solution)/shard_map/ppermute | solution.py:140
  47.4 4.1 %collective-permute-done.2 = bf16[48,3072]{1,0:T(8,128)(2,1)S(1)} collective-permute-done((bf16[48,3072]{1,0:T(8,128)(2,1)S(1)}, bf16[48,3072]{1,0:T(8,128)(2,1)S(1)}, u32[]{:S(2)}, u32[]{:S(2)}) %collective-permute-start.2) | collective-permute-done | bytes 294944 | tf_op jit(solution)/shard_map/ppermute | solution.py:140
  51.5 0.0 collective-permute-done.3
  51.6 0.0 collective-permute-done.6
  51.6 3.3 %collective-permute-done.7 = bf16[48,3072]{1,0:T(8,128)(2,1)S(1)} collective-permute-done((bf16[48,3072]{1,0:T(8,128)(2,1)S(1)}, bf16[48,3072]{1,0:T(8,128)(2,1)S(1)}, u32[]{:S(2)}, u32[]{:S(2)}) %collective-permute-start.7) | collective-permute-done | bytes 294944 | tf_op jit(solution)/shard_map/ppermute | solution.py:140
  54.9 0.0 copy-done
  54.9 0.0 copy-start.2
  54.9 1.4 fusion.mine
  56.3 1.9 %collective-permute-start.8 = (f32[384,384]{1,0:T(8,128)S(1)}, f32[384,384]{1,0:T(8,128)}, u32[]{:S(2)}, u32[]{:S(2)}) collective-permute-start(f32[384,384]{1,0:T(8,128)S(1)} %fusion.mine), channel_id=1, source_target_pairs={{0,1},{1,0},{2,3},{3,2},{4,5},{5,4},{6,7},{7,6},{8,9},{9,8},{10,11... | collective-permute-start | bytes 1769480 | tf_op jit(solution)/shard_map/ppermute | solution.py:140
  58.3 0.0 copy-start.1
  58.3 0.1 pad_add_fusion.where
  58.4 2.0 %collective-permute-done.8.theirs = f32[384,384]{1,0:T(8,128)} collective-permute-done((f32[384,384]{1,0:T(8,128)S(1)}, f32[384,384]{1,0:T(8,128)}, u32[]{:S(2)}, u32[]{:S(2)}) %collective-permute-start.8) | collective-permute-done | bytes 589856 | tf_op jit(solution)/shard_map/ppermute | solution.py:140
  60.4 0.0 copy-done.2
  60.4 3.6 %rows_and_chunks.1 = (bf16[384,384]{1,0:T(8,128)(2,1)S(1)}, bf16[5,6,32,384]{3,2,1,0:T(8,128)(2,1)S(1)}, bf16[5,6,32,384]{3,2,1,0:T(8,128)(2,1)S(1)}, bf16[2,6,3...) custom-call(s32[2]{0:T(128)S(1)} %pad_add_fusion.where, ...), custom_call_target="tpu_custom_call" | custom-call | tf_op jit(solution)/shard_map/rows_and_chunks/pallas_call | solution.py:69
  64.0 5.4 %collective-permute-start.14 = (bf16[5,6,32,384]{3,2,1,0:T(8,128)(2,1)S(1)}, bf16[5,6,32,384]{3,2,1,0:T(8,128)(2,1)S(1)}, u32[]{:S(2)}, u32[]{:S(2)}) collective-permute-start(bf16[5,6,32,384]{3,2,1,0:T(8,128)(2,1)S(1)} %get-tuple-element.32), channel_id=1, source_target_pairs={{0,112},{16,0},{32,16},{48,32},{64,48},{80,64},{96,80},{112,96},{1... | collective-permute-start | bytes 2211848 | tf_op jit(solution)/shard_map/ppermute | solution.py:140
  69.4 1.9 %collective-permute-start.13 = (bf16[5,6,32,384]{3,2,1,0:T(8,128)(2,1)S(1)}, bf16[5,6,32,384]{3,2,1,0:T(8,128)(2,1)S(1)}, u32[]{:S(2)}, u32[]{:S(2)}) collective-permute-start(bf16[5,6,32,384]{3,2,1,0:T(8,128)(2,1)S(1)} %get-tuple-element.31), channel_id=1, source_target_pairs={{0,16},{16,32},{32,48},{48,64},{64,80},{80,96},{96,112},{112,0},{1... | collective-permute-start | bytes 2211848 | tf_op jit(solution)/shard_map/ppermute | solution.py:140
  71.3 0.0 copy-done.1
  71.3 3.0 %shard_map.59 = (f32[96,3072]{1,0:T(8,128)S(1)}, bf16[96,3072]{1,0:T(8,128)(2,1)S(1)}, bf16[96,3072]{1,0:T(8,128)(2,1)S(1)}, bf16[96,3072]{1,0:T(8,128)(2,1)S(1)}) custom-call(bf16[384,384]{1,0:T(8,128)(2,1)S(1)} %get-tuple-element.23.rows, bf16[3072,384]{1,0:T(8,128)(2,1)S(1)} %copy-done.1), custom_call_target="tpu_custom_call" | custom-call | tf_op jit(solution)/shard_map/pallas_call | solution.py:83
  74.3 2.3 %collective-permute-start.10 = (bf16[96,3072]{1,0:T(8,128)(2,1)S(1)}, bf16[96,3072]{1,0:T(8,128)(2,1)S(1)}, u32[]{:S(2)}, u32[]{:S(2)}) collective-permute-start(bf16[96,3072]{1,0:T(8,128)(2,1)S(1)} %get-tuple-element.26), channel_id=1, source_target_pairs={{0,8},{4,12},{8,0},{12,4},{1,9},{5,13},{9,1},{13,5},{2,10},{6,14},... | collective-permute-start | bytes 1769480 | tf_op jit(solution)/shard_map/ppermute | solution.py:140
  76.7 3.9 %collective-permute-start.11 = (bf16[96,3072]{1,0:T(8,128)(2,1)S(1)}, bf16[96,3072]{1,0:T(8,128)(2,1)S(1)}, u32[]{:S(2)}, u32[]{:S(2)}) collective-permute-start(bf16[96,3072]{1,0:T(8,128)(2,1)S(1)} %get-tuple-element.27), channel_id=1, source_target_pairs={{0,4},{4,8},{8,12},{12,0},{1,5},{5,9},{9,13},{13,1},{2,6},{6,10},{... | collective-permute-start | bytes 1769480 | tf_op jit(solution)/shard_map/ppermute | solution.py:140
  80.6 1.9 %collective-permute-start.9 = (bf16[96,3072]{1,0:T(8,128)(2,1)S(1)}, bf16[96,3072]{1,0:T(8,128)(2,1)S(1)}, u32[]{:S(2)}, u32[]{:S(2)}) collective-permute-start(bf16[96,3072]{1,0:T(8,128)(2,1)S(1)} %get-tuple-element.25), channel_id=1, source_target_pairs={{0,12},{4,0},{8,4},{12,8},{1,13},{5,1},{9,5},{13,9},{2,14},{6,2},{... | collective-permute-start | bytes 1769480 | tf_op jit(solution)/shard_map/ppermute | solution.py:140
  82.6 2.9 %collective-permute-done.14.down = bf16[5,6,32,384]{3,2,1,0:T(8,128)(2,1)S(1)} collective-permute-done((bf16[5,6,32,384]{3,2,1,0:T(8,128)(2,1)S(1)}, bf16[5,6,32,384]{3,2,1,0:T(8,128)(2,1)S(1)}, u32[]{:S(2)}, u32[]{:S(2)}) %collective-permute-start.14) | collective-permute-done | bytes 737312 | tf_op jit(solution)/shard_map/ppermute | solution.py:140
  85.4 5.3 %collective-permute-done.13.up = bf16[5,6,32,384]{3,2,1,0:T(8,128)(2,1)S(1)} collective-permute-done((bf16[5,6,32,384]{3,2,1,0:T(8,128)(2,1)S(1)}, bf16[5,6,32,384]{3,2,1,0:T(8,128)(2,1)S(1)}, u32[]{:S(2)}, u32[]{:S(2)}) %collective-permute-start.13) | collective-permute-done | bytes 737312 | tf_op jit(solution)/shard_map/ppermute | solution.py:140
  90.7 0.8 add_convert_fusion
  91.5 3.6 %collective-permute-start.16 = (bf16[2,6,32,384]{3,2,1,0:T(8,128)(2,1)}, bf16[2,6,32,384]{3,2,1,0:T(8,128)(2,1)S(1)}, u32[]{:S(2)}, u32[]{:S(2)}) collective-permute-start(bf16[2,6,32,384]{3,2,1,0:T(8,128)(2,1)} %add_convert_fusion), channel_id=1, source_target_pairs={{0,80},{16,96},{32,112},{48,0},{64,16},{80,32},{96,48},{112,64},{1... | collective-permute-start | bytes 884744 | tf_op jit(solution)/shard_map/ppermute | solution.py:140
  95.2 0.8 add_convert_fusion.1
  96.0 4.0 %collective-permute-start.15 = (bf16[2,6,32,384]{3,2,1,0:T(8,128)(2,1)}, bf16[2,6,32,384]{3,2,1,0:T(8,128)(2,1)S(1)}, u32[]{:S(2)}, u32[]{:S(2)}) collective-permute-start(bf16[2,6,32,384]{3,2,1,0:T(8,128)(2,1)} %add_convert_fusion.1), channel_id=1, source_target_pairs={{0,48},{16,64},{32,80},{48,96},{64,112},{80,0},{96,16},{112,32},{1... | collective-permute-start | bytes 884744 | tf_op jit(solution)/shard_map/ppermute | solution.py:140
  100.0 0.0 collective-permute-done.10.rest_1_
  100.0 2.4 %collective-permute-done.11.rest_2_ = bf16[96,3072]{1,0:T(8,128)(2,1)S(1)} collective-permute-done((bf16[96,3072]{1,0:T(8,128)(2,1)S(1)}, bf16[96,3072]{1,0:T(8,128)(2,1)S(1)}, u32[]{:S(2)}, u32[]{:S(2)}) %collective-permute-start.11) | collective-permute-done | bytes 589856 | tf_op jit(solution)/shard_map/ppermute | solution.py:140
  102.4 3.1 %collective-permute-done.9.rest_0_ = bf16[96,3072]{1,0:T(8,128)(2,1)S(1)} collective-permute-done((bf16[96,3072]{1,0:T(8,128)(2,1)S(1)}, bf16[96,3072]{1,0:T(8,128)(2,1)S(1)}, u32[]{:S(2)}, u32[]{:S(2)}) %collective-permute-start.9) | collective-permute-done | bytes 589856 | tf_op jit(solution)/shard_map/ppermute | solution.py:140
  105.5 0.3 shard_map.60
  105.8 4.0 %collective-permute-start.12 = (bf16[48,3072]{1,0:T(8,128)(2,1)S(1)}, bf16[48,3072]{1,0:T(8,128)(2,1)}, u32[]{:S(2)}, u32[]{:S(2)}) collective-permute-start(bf16[48,3072]{1,0:T(8,128)(2,1)S(1)} %get-tuple-element.29), channel_id=1, source_target_pairs={{0,642},{2,640},{128,514},{130,512},{256,386},{258,384},{384,258},... | collective-permute-start | bytes 884744 | tf_op jit(solution)/shard_map/ppermute | solution.py:159
  109.8 0.1 pad_add_fusion.1.where
  109.8 3.9 %collective-permute-done.16.got5 = bf16[2,6,32,384]{3,2,1,0:T(8,128)(2,1)S(1)} collective-permute-done((bf16[2,6,32,384]{3,2,1,0:T(8,128)(2,1)}, bf16[2,6,32,384]{3,2,1,0:T(8,128)(2,1)S(1)}, u32[]{:S(2)}, u32[]{:S(2)}) %collective-permute-start.16) | collective-permute-done | bytes 294944 | tf_op jit(solution)/shard_map/ppermute | solution.py:140
  113.7 7.9 %collective-permute-done.15.got3 = bf16[2,6,32,384]{3,2,1,0:T(8,128)(2,1)S(1)} collective-permute-done((bf16[2,6,32,384]{3,2,1,0:T(8,128)(2,1)}, bf16[2,6,32,384]{3,2,1,0:T(8,128)(2,1)S(1)}, u32[]{:S(2)}, u32[]{:S(2)}) %collective-permute-start.15) | collective-permute-done | bytes 294944 | tf_op jit(solution)/shard_map/ppermute | solution.py:140
  121.6 0.7 shard_map.61
  122.4 1.9 %collective-permute-start.17 = (bf16[2,64,384]{2,1,0:T(8,128)(2,1)S(1)}, bf16[2,64,384]{2,1,0:T(8,128)(2,1)S(1)}, u32[]{:S(2)}, u32[]{:S(2)}) collective-permute-start(bf16[2,64,384]{2,1,0:T(8,128)(2,1)S(1)} %get-tuple-element.36), channel_id=1, source_target_pairs={{0,128},{128,256},{256,0},{384,512},{512,640},{640,384},{1,129},{1... | collective-permute-start | bytes 294920 | tf_op jit(solution)/shard_map/ppermute | solution.py:226
  124.3 4.8 %collective-permute-start.18 = (bf16[2,64,384]{2,1,0:T(8,128)(2,1)S(1)}, bf16[2,64,384]{2,1,0:T(8,128)(2,1)S(1)}, u32[]{:S(2)}, u32[]{:S(2)}) collective-permute-start(bf16[2,64,384]{2,1,0:T(8,128)(2,1)S(1)} %get-tuple-element.37), channel_id=1, source_target_pairs={{0,256},{128,0},{256,128},{384,640},{512,384},{640,512},{1,257},{1... | collective-permute-start | bytes 294920 | tf_op jit(solution)/shard_map/ppermute | solution.py:226
  129.1 1.2 collective-permute-done.17.rest_0_
  130.4 1.0 collective-permute-done.18.rest_1_
  131.3 0.6 shard_map.62
  131.9 1.9 %collective-permute-start.19 = (bf16[64,384]{1,0:T(8,128)(2,1)S(1)}, bf16[64,384]{1,0:T(8,128)(2,1)S(1)}, u32[]{:S(2)}, u32[]{:S(2)}) collective-permute-start(bf16[64,384]{1,0:T(8,128)(2,1)S(1)} %get-tuple-element.39), channel_id=1, source_target_pairs={{0,384},{128,512},{256,640},{384,0},{512,128},{640,256},{1,385},{1... | collective-permute-start | bytes 147464 | tf_op jit(solution)/shard_map/ppermute | solution.py:140
  133.9 0.0 collective-permute-done.12
  133.9 1.7 %add_convert_fusion.2 = bf16[48,3072]{1,0:T(8,128)(2,1)} fusion(f32[48,3072]{1,0:T(8,128)S(1)} %get-tuple-element.28, bf16[48,3072]{1,0:T(8,128)(2,1)} %collective-permute-done.12), kind=kLoop, calls=%fused_computation.2 | loop fusion | flops 442368 | bytes 1179648 | tf_op jit(solution)/shard_map/convert_element_type | solution.py:207
  135.6 4.1 %collective-permute-done.19 = bf16[64,384]{1,0:T(8,128)(2,1)S(1)} collective-permute-done((bf16[64,384]{1,0:T(8,128)(2,1)S(1)}, bf16[64,384]{1,0:T(8,128)(2,1)S(1)}, u32[]{:S(2)}, u32[]{:S(2)}) %collective-permute-start.19) | collective-permute-done | bytes 49184 | tf_op jit(solution)/shard_map/ppermute | solution.py:140
  139.7 0.7 convert_add_fusion
  (8 shorter events, 0.2 us)
Async XLA Ops:
  0.6 34.4 %collective-permute-start = (bf16[48,3072]{1,0:T(8,128)(2,1)}, bf16[48,3072]{1,0:T(8,128)(2,1)S(1)}, u32[]{:S(2)}, u32[]{:S(2)}) collective-permute-start(bf16[48,3072]{1,0:T(8,128)(2,1)} %param.4), channel_id=1, source_target_pairs={{0,642},{2,640},{128,514},{130,512},{256,386},{258,384},{384,258},... | collective-permute-start | bytes 884744 | tf_op jit(solution)/shard_map/ppermute | solution.py:159
  15.2 23.2 %collective-permute-start.1 = (bf16[48,3072]{1,0:T(8,128)(2,1)}, bf16[48,3072]{1,0:T(8,128)(2,1)}, u32[]{:S(2)}, u32[]{:S(2)}) collective-permute-start(bf16[48,3072]{1,0:T(8,128)(2,1)} %param.4), channel_id=1, source_target_pairs={{0,4},{4,8},{8,12},{12,0},{1,5},{5,9},{9,13},{13,1},{2,6},{6,10},{... | collective-permute-start | bytes 884744 | tf_op jit(solution)/shard_map/ppermute | solution.py:140
  17.6 33.9 %collective-permute-start.3 = (bf16[48,3072]{1,0:T(8,128)(2,1)}, bf16[48,3072]{1,0:T(8,128)(2,1)S(1)}, u32[]{:S(2)}, u32[]{:S(2)}) collective-permute-start(bf16[48,3072]{1,0:T(8,128)(2,1)} %param.4), channel_id=1, source_target_pairs={{0,8},{4,12},{8,0},{12,4},{1,9},{5,13},{9,1},{13,5},{2,10},{6,14},... | collective-permute-start | bytes 884744 | tf_op jit(solution)/shard_map/ppermute | solution.py:140
  22.0 29.6 %collective-permute-start.6 = (bf16[48,3072]{1,0:T(8,128)(2,1)}, bf16[48,3072]{1,0:T(8,128)(2,1)S(1)}, u32[]{:S(2)}, u32[]{:S(2)}) collective-permute-start(bf16[48,3072]{1,0:T(8,128)(2,1)} %param.4), channel_id=1, source_target_pairs={{0,12},{4,0},{8,4},{12,8},{1,13},{5,1},{9,5},{13,9},{2,14},{6,2},{... | collective-permute-start | bytes 884744 | tf_op jit(solution)/shard_map/ppermute | solution.py:140
  24.9 30.0 %copy-start = (bf16[3072,384]{1,0:T(8,128)(2,1)S(1)}, bf16[3072,384]{1,0:T(8,128)(2,1)}, u32[]{:S(2)}) copy-start(bf16[3072,384]{1,0:T(8,128)(2,1)} %weight.1) | copy-start | bytes 7077892
  24.9 18.5 %collective-permute-start.5 = (bf16[4,48,384]{2,1,0:T(8,128)(2,1)S(1)}, bf16[4,48,384]{2,1,0:T(8,128)(2,1)S(1)}, u32[]{:S(2)}, u32[]{:S(2)}) collective-permute-start(bf16[4,48,384]{2,1,0:T(8,128)(2,1)S(1)} %get-tuple-element.41), channel_id=1, source_target_pairs={{0,640},{128,512},{256,384},{384,256},{512,128},{640,0},{1,641},{1... | collective-permute-start | bytes 442376 | tf_op jit(solution)/shard_map/ppermute | solution.py:165
  35.0 12.3 %collective-permute-start.4 = (bf16[48,3072]{1,0:T(8,128)(2,1)S(1)}, bf16[48,3072]{1,0:T(8,128)(2,1)S(1)}, u32[]{:S(2)}, u32[]{:S(2)}) collective-permute-start(bf16[48,3072]{1,0:T(8,128)(2,1)S(1)} %collective-permute-done), channel_id=1, source_target_pairs={{0,8},{4,12},{8,0},{12,4},{1,9},{5,13},{9,1},{13,5},{2,10},{6,14},... | collective-permute-start | bytes 884744 | tf_op jit(solution)/shard_map/ppermute | solution.py:140
  38.4 13.1 %collective-permute-start.2 = (bf16[48,3072]{1,0:T(8,128)(2,1)S(1)}, bf16[48,3072]{1,0:T(8,128)(2,1)S(1)}, u32[]{:S(2)}, u32[]{:S(2)}) collective-permute-start(bf16[48,3072]{1,0:T(8,128)(2,1)S(1)} %collective-permute-done), channel_id=1, source_target_pairs={{0,4},{4,8},{8,12},{12,0},{1,5},{5,9},{9,13},{13,1},{2,6},{6,10},{... | collective-permute-start | bytes 884744 | tf_op jit(solution)/shard_map/ppermute | solution.py:140
  43.4 11.5 %collective-permute-start.7 = (bf16[48,3072]{1,0:T(8,128)(2,1)S(1)}, bf16[48,3072]{1,0:T(8,128)(2,1)S(1)}, u32[]{:S(2)}, u32[]{:S(2)}) collective-permute-start(bf16[48,3072]{1,0:T(8,128)(2,1)S(1)} %collective-permute-done), channel_id=1, source_target_pairs={{0,12},{4,0},{8,4},{12,8},{1,13},{5,1},{9,5},{13,9},{2,14},{6,2},{... | collective-permute-start | bytes 884744 | tf_op jit(solution)/shard_map/ppermute | solution.py:140
  54.9 5.5 %copy-start.2 = (f32[128]{0:T(128)S(1)}, f32[128]{0:T(128)}, u32[]{:S(2)}) copy-start(f32[128]{0:T(128)} %param.7) | copy-start | bytes 1540
  56.3 4.0 %collective-permute-start.8 = (f32[384,384]{1,0:T(8,128)S(1)}, f32[384,384]{1,0:T(8,128)}, u32[]{:S(2)}, u32[]{:S(2)}) collective-permute-start(f32[384,384]{1,0:T(8,128)S(1)} %fusion.mine), channel_id=1, source_target_pairs={{0,1},{1,0},{2,3},{3,2},{4,5},{5,4},{6,7},{7,6},{8,9},{9,8},{10,11... | collective-permute-start | bytes 1769480 | tf_op jit(solution)/shard_map/ppermute | solution.py:140
  58.3 13.0 %copy-start.1 = (bf16[3072,384]{1,0:T(8,128)(2,1)S(1)}, bf16[3072,384]{1,0:T(8,128)(2,1)}, u32[]{:S(2)}) copy-start(bf16[3072,384]{1,0:T(8,128)(2,1)} %weight.1) | copy-start | bytes 7077892
  64.0 21.4 %collective-permute-start.14 = (bf16[5,6,32,384]{3,2,1,0:T(8,128)(2,1)S(1)}, bf16[5,6,32,384]{3,2,1,0:T(8,128)(2,1)S(1)}, u32[]{:S(2)}, u32[]{:S(2)}) collective-permute-start(bf16[5,6,32,384]{3,2,1,0:T(8,128)(2,1)S(1)} %get-tuple-element.32), channel_id=1, source_target_pairs={{0,112},{16,0},{32,16},{48,32},{64,48},{80,64},{96,80},{112,96},{1... | collective-permute-start | bytes 2211848 | tf_op jit(solution)/shard_map/ppermute | solution.py:140
  69.4 21.4 %collective-permute-start.13 = (bf16[5,6,32,384]{3,2,1,0:T(8,128)(2,1)S(1)}, bf16[5,6,32,384]{3,2,1,0:T(8,128)(2,1)S(1)}, u32[]{:S(2)}, u32[]{:S(2)}) collective-permute-start(bf16[5,6,32,384]{3,2,1,0:T(8,128)(2,1)S(1)} %get-tuple-element.31), channel_id=1, source_target_pairs={{0,16},{16,32},{32,48},{48,64},{64,80},{80,96},{96,112},{112,0},{1... | collective-permute-start | bytes 2211848 | tf_op jit(solution)/shard_map/ppermute | solution.py:140
  74.3 25.7 %collective-permute-start.10 = (bf16[96,3072]{1,0:T(8,128)(2,1)S(1)}, bf16[96,3072]{1,0:T(8,128)(2,1)S(1)}, u32[]{:S(2)}, u32[]{:S(2)}) collective-permute-start(bf16[96,3072]{1,0:T(8,128)(2,1)S(1)} %get-tuple-element.26), channel_id=1, source_target_pairs={{0,8},{4,12},{8,0},{12,4},{1,9},{5,13},{9,1},{13,5},{2,10},{6,14},... | collective-permute-start | bytes 1769480 | tf_op jit(solution)/shard_map/ppermute | solution.py:140
  76.7 25.7 %collective-permute-start.11 = (bf16[96,3072]{1,0:T(8,128)(2,1)S(1)}, bf16[96,3072]{1,0:T(8,128)(2,1)S(1)}, u32[]{:S(2)}, u32[]{:S(2)}) collective-permute-start(bf16[96,3072]{1,0:T(8,128)(2,1)S(1)} %get-tuple-element.27), channel_id=1, source_target_pairs={{0,4},{4,8},{8,12},{12,0},{1,5},{5,9},{9,13},{13,1},{2,6},{6,10},{... | collective-permute-start | bytes 1769480 | tf_op jit(solution)/shard_map/ppermute | solution.py:140
  80.6 24.8 %collective-permute-start.9 = (bf16[96,3072]{1,0:T(8,128)(2,1)S(1)}, bf16[96,3072]{1,0:T(8,128)(2,1)S(1)}, u32[]{:S(2)}, u32[]{:S(2)}) collective-permute-start(bf16[96,3072]{1,0:T(8,128)(2,1)S(1)} %get-tuple-element.25), channel_id=1, source_target_pairs={{0,12},{4,0},{8,4},{12,8},{1,13},{5,1},{9,5},{13,9},{2,14},{6,2},{... | collective-permute-start | bytes 1769480 | tf_op jit(solution)/shard_map/ppermute | solution.py:140
  91.5 22.2 %collective-permute-start.16 = (bf16[2,6,32,384]{3,2,1,0:T(8,128)(2,1)}, bf16[2,6,32,384]{3,2,1,0:T(8,128)(2,1)S(1)}, u32[]{:S(2)}, u32[]{:S(2)}) collective-permute-start(bf16[2,6,32,384]{3,2,1,0:T(8,128)(2,1)} %add_convert_fusion), channel_id=1, source_target_pairs={{0,80},{16,96},{32,112},{48,0},{64,16},{80,32},{96,48},{112,64},{1... | collective-permute-start | bytes 884744 | tf_op jit(solution)/shard_map/ppermute | solution.py:140
  96.0 25.6 %collective-permute-start.15 = (bf16[2,6,32,384]{3,2,1,0:T(8,128)(2,1)}, bf16[2,6,32,384]{3,2,1,0:T(8,128)(2,1)S(1)}, u32[]{:S(2)}, u32[]{:S(2)}) collective-permute-start(bf16[2,6,32,384]{3,2,1,0:T(8,128)(2,1)} %add_convert_fusion.1), channel_id=1, source_target_pairs={{0,48},{16,64},{32,80},{48,96},{64,112},{80,0},{96,16},{112,32},{1... | collective-permute-start | bytes 884744 | tf_op jit(solution)/shard_map/ppermute | solution.py:140
  105.8 28.1 %collective-permute-start.12 = (bf16[48,3072]{1,0:T(8,128)(2,1)S(1)}, bf16[48,3072]{1,0:T(8,128)(2,1)}, u32[]{:S(2)}, u32[]{:S(2)}) collective-permute-start(bf16[48,3072]{1,0:T(8,128)(2,1)S(1)} %get-tuple-element.29), channel_id=1, source_target_pairs={{0,642},{2,640},{128,514},{130,512},{256,386},{258,384},{384,258},... | collective-permute-start | bytes 884744 | tf_op jit(solution)/shard_map/ppermute | solution.py:159
  122.4 8.0 %collective-permute-start.17 = (bf16[2,64,384]{2,1,0:T(8,128)(2,1)S(1)}, bf16[2,64,384]{2,1,0:T(8,128)(2,1)S(1)}, u32[]{:S(2)}, u32[]{:S(2)}) collective-permute-start(bf16[2,64,384]{2,1,0:T(8,128)(2,1)S(1)} %get-tuple-element.36), channel_id=1, source_target_pairs={{0,128},{128,256},{256,0},{384,512},{512,640},{640,384},{1,129},{1... | collective-permute-start | bytes 294920 | tf_op jit(solution)/shard_map/ppermute | solution.py:226
  124.3 7.1 %collective-permute-start.18 = (bf16[2,64,384]{2,1,0:T(8,128)(2,1)S(1)}, bf16[2,64,384]{2,1,0:T(8,128)(2,1)S(1)}, u32[]{:S(2)}, u32[]{:S(2)}) collective-permute-start(bf16[2,64,384]{2,1,0:T(8,128)(2,1)S(1)} %get-tuple-element.37), channel_id=1, source_target_pairs={{0,256},{128,0},{256,128},{384,640},{512,384},{640,512},{1,257},{1... | collective-permute-start | bytes 294920 | tf_op jit(solution)/shard_map/ppermute | solution.py:226
  131.9 7.8 %collective-permute-start.19 = (bf16[64,384]{1,0:T(8,128)(2,1)S(1)}, bf16[64,384]{1,0:T(8,128)(2,1)S(1)}, u32[]{:S(2)}, u32[]{:S(2)}) collective-permute-start(bf16[64,384]{1,0:T(8,128)(2,1)S(1)} %get-tuple-element.39), channel_id=1, source_target_pairs={{0,384},{128,512},{256,640},{384,0},{512,128},{640,256},{1,385},{1... | collective-permute-start | bytes 147464 | tf_op jit(solution)/shard_map/ppermute | solution.py:140
